TPU v7x, 32 devices: a whole 2x2x4 slice. The times are simulated.
32 devices in a mesh: section: 2 (over x), dp: 16 (over z, y, core).
Axes of the slice: x: 2, y: 2, z: 4, core: 2. Of those that a mesh axis runs over, the one named last changes fastest.
Arguments:
- block_input: bfloat16 [2, 2560, 1024], P(None, 'dp'), may hold values from -6 to 6
- conditioning: bfloat16 [2, 2, 1024], replicated, may hold values from -6 to 6
- text_embed: bfloat16 [2, 160, 1024], P(None, 'dp'), may hold values from -6 to 6
- text_keep: int32 [2, 2], replicated, may hold values 0 or 1
- cotangent: bfloat16 [2, 2560, 1024], P(None, 'dp'), may hold values from -6 to 6
- self_input: float32 [2, 1024, 3072], P('section', 'dp'), may hold values from -0.1875 to 0.1875
- self_output: float32 [2, 1024, 1024], P('section', 'dp'), may hold values from -0.75 to 0.75
- cross_query: float32 [2, 1024, 1024], P('section', 'dp'), may hold values from -0.1875 to 0.1875
- cross_memory: float32 [2, 1024, 2048], P('section', 'dp'), may hold values from -0.1875 to 0.1875
- cross_output: float32 [2, 1024, 1024], P('section', 'dp'), may hold values from -0.5 to 0.5
- up_weight: float32 [2, 1024, 4096], P('section', 'dp'), may hold values from -0.1875 to 0.1875
- down_weight: float32 [2, 4096, 1024], P('section', 'dp'), may hold values from -0.09375 to 0.09375
- modulation: float32 [2, 1024, 6144], P('section', 'dp'), may hold values from -0.1875 to 0.1875
- modulation_bias: float32 [2, 6144], P('section'), may hold values from -3 to 3
- position_bias: float32 [2, 16, 71], P('section'), may hold values from -4 to 4
Outputs:
- block_outputs: bfloat16 [2, 2, 2560, 1024], P('section', None, 'dp')
- input_grads: bfloat16 [2, 2, 2560, 1024], P('section', None, 'dp')
- grad_self_input: float32 [2, 1024, 3072], P('section', 'dp')
- grad_self_output: float32 [2, 1024, 1024], P('section', 'dp')
- grad_cross_query: float32 [2, 1024, 1024], P('section', 'dp')
- grad_cross_memory: float32 [2, 1024, 2048], P('section', 'dp')
- grad_cross_output: float32 [2, 1024, 1024], P('section', 'dp')
- grad_up_weight: float32 [2, 1024, 4096], P('section', 'dp')
- grad_down_weight: float32 [2, 4096, 1024], P('section', 'dp')
- grad_modulation: float32 [2, 1024, 6144], P('section', 'dp')
- grad_modulation_bias: float32 [2, 6144], P('section')
- grad_position_bias: float32 [2, 16, 71], P('section')
All inputs are finite; a program needn't handle non-finite values.
Results may differ from a plain program's by a relative error of at most 0.024.
The roundings to bfloat16 on the way count: a program that leaves them out, or rounds other values in their place, can miss the bound.
Values may be sent and summed in bfloat16 or wider, within the bound.
No kernel may reach another device: no remote copies, remote signals or barrier semaphores. Data moves between devices by JAX's collectives and lax.ppermute only.
A program may use at most 384 MiB of HBM per device.

v0:
```python
import jax
import jax.numpy as jnp
from jax import lax
from jax.sharding import PartitionSpec as P

D = 1024
HEADS = 16
HEAD = 64
FRAMES = 5
BH = 8
BW = 4
ROWS = 160
REL = 71


EPSILON = 1e-06
NEGATIVE = -1e30


def swapped(x, axis, bit):
    return lax.ppermute(x, axis, [(i, i ^ 1 << bit) for i in range(lax.axis_size(axis))])


def shortened(x):

    def short(part):
        return part.astype(jnp.bfloat16) if part.dtype == jnp.float32 else part

    return jax.tree.map(short, x)


def from_behind(block, axis, distance):
    devices = range(lax.axis_size(axis))
    route = [(i - distance, i) for i in devices if i - distance in devices]
    return lax.ppermute(block, axis, route)


def layer_mod(inputs, offset, factor):
    average = jnp.mean(inputs, axis=-1, keepdims=True)
    centred = inputs - average
    spread = jnp.mean(centred * centred, axis=-1, keepdims=True)
    return centred * lax.rsqrt(spread + EPSILON) * (1.0 + factor) + offset


def places_of(member, within):
    frame_id = within // (BH * BW)
    cell_id = within % (BH * BW)
    row_at = member // 4 * BH + cell_id // BW
    col_at = member % 4 * BW + cell_id % BW
    return (member, frame_id, row_at, col_at)


def bias_hot(query_places, key_places):
    time_index = query_places[1][:, None] - key_places[1][None, :] + FRAMES - 1
    row_index = query_places[2][:, None] - key_places[2][None, :] + 2 * BH - 1 + 2 * FRAMES - 1
    col_index = (
        query_places[3][:, None] - key_places[3][None, :] + 4 * BW - 1 + 2 * FRAMES - 1 + 4 * BH - 1
    )
    buckets = jnp.arange(REL)[None, None, :]
    hits = (
        (time_index[:, :, None] == buckets)
        | (row_index[:, :, None] == buckets)
        | (col_index[:, :, None] == buckets)
    )
    return hits.astype(jnp.float32)


def collect(pieces, member):
    for bit_level in range(3):
        others = swapped((pieces[0], pieces[1], pieces[2], pieces[3]), "dp", bit_level)
        upper_half = member >> bit_level & 1 == 1
        pieces = tuple(
            (
                jnp.where(
                    upper_half,
                    jnp.concatenate([peer_part, mine_part], 0),
                    jnp.concatenate([mine_part, peer_part], 0),
                )
                for mine_part, peer_part in zip(pieces, others)
            )
        )
    return pieces


def spread_back(grads, member):
    for bit_level in (2, 1, 0):
        upper_half = member >> bit_level & 1 == 1
        kept_parts = tuple(
            (
                jnp.where(
                    upper_half,
                    grad_part[grad_part.shape[0] // 2 :],
                    grad_part[: grad_part.shape[0] // 2],
                )
                for grad_part in grads
            )
        )
        sent_parts = tuple(
            (
                jnp.where(
                    upper_half,
                    grad_part[: grad_part.shape[0] // 2],
                    grad_part[grad_part.shape[0] // 2 :],
                )
                for grad_part in grads
            )
        )
        arrived = swapped(
            (
                shortened(sent_parts[0]),
                shortened(sent_parts[1]),
                shortened(sent_parts[2]),
                shortened(sent_parts[3]),
            ),
            "dp",
            bit_level,
        )
        grads = tuple(
            (kept_part + arrived_part for kept_part, arrived_part in zip(kept_parts, arrived))
        )
    return grads


def attend(queries, key_rows, values, additive, window):
    row_count = queries.shape[0]
    query_heads = queries.reshape(row_count, HEADS, HEAD)
    key_heads = key_rows.reshape(key_rows.shape[0], HEADS, HEAD)
    value_heads = values.reshape(values.shape[0], HEADS, HEAD)
    scores = jnp.einsum("qhd,khd->hqk", query_heads, key_heads, preferred_element_type=jnp.float32)
    scores = scores * HEAD ** (-0.5) + additive
    if window is not None:
        scores = jnp.where(window[None], scores, NEGATIVE)
    highest = jnp.max(scores, axis=-1, keepdims=True)
    exponent = jnp.exp(scores - highest)
    softmaxed = exponent / jnp.sum(exponent, axis=-1, keepdims=True)
    mixture = jnp.einsum(
        "hqk,khd->qhd",
        softmaxed.astype(jnp.bfloat16),
        value_heads,
        preferred_element_type=jnp.float32,
    )
    return (mixture.reshape(row_count, HEADS * HEAD).astype(jnp.bfloat16), softmaxed)


def attend_back(queries, key_rows, values, softmaxed, grad_mixture):
    row_count = queries.shape[0]
    query_heads = queries.reshape(row_count, HEADS, HEAD)
    key_heads = key_rows.reshape(key_rows.shape[0], HEADS, HEAD)
    value_heads = values.reshape(values.shape[0], HEADS, HEAD)
    grad_heads = grad_mixture.reshape(row_count, HEADS, HEAD)
    grad_values = jnp.einsum(
        "hqk,qhd->khd",
        softmaxed.astype(jnp.bfloat16),
        grad_heads,
        preferred_element_type=jnp.float32,
    )
    grad_soft = jnp.einsum(
        "qhd,khd->hqk", grad_heads, value_heads, preferred_element_type=jnp.float32
    )
    grad_scores = softmaxed * (grad_soft - jnp.sum(softmaxed * grad_soft, axis=-1, keepdims=True))
    grad_raw = (grad_scores * HEAD ** (-0.5)).astype(jnp.bfloat16)
    grad_queries = jnp.einsum(
        "hqk,khd->qhd", grad_raw, key_heads, preferred_element_type=jnp.float32
    )
    grad_keys = jnp.einsum(
        "hqk,qhd->khd", grad_raw, query_heads, preferred_element_type=jnp.float32
    )
    return (
        grad_queries.reshape(row_count, D),
        grad_keys.reshape(-1, D),
        grad_values.reshape(-1, D),
        grad_scores,
    )


def per_device(
    block_input,
    conditioning,
    text_embed,
    text_keep,
    cotangent,
    self_input,
    self_output,
    cross_query,
    cross_memory,
    cross_output,
    up_weight,
    down_weight,
    modulation,
    modulation_bias,
    position_bias,
):
    section_id = lax.axis_index("section")
    device_id = lax.axis_index("dp")
    member = device_id % 8
    clip_id = device_id // 8
    micro_count = block_input.shape[0]
    gain_bias = modulation_bias[0]
    cond_low = jax.nn.silu(conditioning.astype(jnp.float32)).astype(jnp.bfloat16)
    all_eight = (
        lax.all_gather(self_input[0].astype(jnp.bfloat16), "dp", axis=0, tiled=True),
        lax.all_gather(self_output[0].astype(jnp.bfloat16), "dp", axis=0, tiled=True),
        lax.all_gather(cross_query[0].astype(jnp.bfloat16), "dp", axis=0, tiled=True),
        lax.all_gather(cross_memory[0].astype(jnp.bfloat16), "dp", axis=0, tiled=True),
        lax.all_gather(cross_output[0].astype(jnp.bfloat16), "dp", axis=0, tiled=True),
        lax.all_gather(up_weight[0].astype(jnp.bfloat16), "dp", axis=0, tiled=True),
        lax.all_gather(down_weight[0].astype(jnp.bfloat16), "dp", axis=0, tiled=True),
        lax.all_gather(modulation[0].astype(jnp.bfloat16), "dp", axis=0, tiled=True),
    )
    gathered_weights = all_eight[:7]
    mod_table = (
        jnp.dot(cond_low[:, clip_id], all_eight[7], preferred_element_type=jnp.float32) + gain_bias
    )
    within = jnp.arange(ROWS)
    query_places = places_of(member + 0 * within, within)
    key_order = jnp.arange(8 * ROWS)
    key_places = places_of(key_order // ROWS, key_order % ROWS)
    hot_table = bias_hot(query_places, key_places)
    relative = jnp.einsum(
        "qkn,hn->hqk", hot_table, position_bias[0], precision=lax.Precision.HIGHEST
    )
    same_frame = query_places[1][:, None] == key_places[1][None, :]
    same_pair = (query_places[0] // 2)[:, None] == (key_places[0] // 2)[None, :]
    window = jnp.where(section_id == 0, same_frame, same_pair)

    def forward(weights, inputs, micro_id):
        w_joint, w_self_out, w_query, w_memory, w_cross_out, w_upper, w_lower = weights
        cond_row = cond_low[micro_id, clip_id]
        mod_parts = mod_table[micro_id].reshape(6, D)
        text_part = text_embed[micro_id] * text_keep[micro_id, clip_id].astype(jnp.bfloat16)
        hidden_low = layer_mod(inputs, mod_parts[0], mod_parts[1]).astype(jnp.bfloat16)
        joint_rows = jnp.dot(hidden_low, w_joint, preferred_element_type=jnp.float32).astype(
            jnp.bfloat16
        )
        text_query = jnp.dot(hidden_low, w_query, preferred_element_type=jnp.float32).astype(
            jnp.bfloat16
        )
        memory = jnp.dot(text_part, w_memory, preferred_element_type=jnp.float32).astype(
            jnp.bfloat16
        )
        gathered = collect(
            (joint_rows[:, D : 2 * D], joint_rows[:, 2 * D :], memory[:, :D], memory[:, D:]), member
        )
        mixture, soft_self = attend(joint_rows[:, :D], gathered[0], gathered[1], relative, window)
        mixture_text, soft_text = attend(text_query, gathered[2], gathered[3], 0.0, None)
        branch = jnp.dot(mixture, w_self_out, preferred_element_type=jnp.float32) + jnp.dot(
            mixture_text, w_cross_out, preferred_element_type=jnp.float32
        )
        middle = inputs + mod_parts[2] * branch
        second_low = layer_mod(middle, mod_parts[3], mod_parts[4]).astype(jnp.bfloat16)
        upper_pre = jnp.dot(second_low, w_upper, preferred_element_type=jnp.float32)
        active_low = jax.nn.gelu(upper_pre).astype(jnp.bfloat16)
        feed_out = jnp.dot(active_low, w_lower, preferred_element_type=jnp.float32)
        result = middle + mod_parts[5] * feed_out
        saved = (
            cond_row,
            mod_parts,
            text_part,
            hidden_low,
            joint_rows,
            text_query,
            gathered,
            mixture,
            soft_self,
            mixture_text,
            soft_text,
            branch,
            middle,
            second_low,
            upper_pre,
            active_low,
            feed_out,
        )
        return (result, saved)

    kept_inputs = []
    block_results = []
    received = jnp.zeros((ROWS, D), jnp.bfloat16)
    for clock_step in range(micro_count + 1):
        micro_id = jnp.clip(clock_step - section_id, 0, micro_count - 1)
        current = jnp.where(
            section_id == 0, block_input[min(clock_step, micro_count - 1)], received
        )
        kept_inputs.append(current)
        result = forward(gathered_weights, current.astype(jnp.float32), micro_id)[0]
        sending = result.astype(jnp.bfloat16)
        block_results.append(sending)
        if clock_step < micro_count:
            received = from_behind(sending, "section", 1)
    kept_stack = jnp.stack(kept_inputs)
    grad_received = jnp.zeros((ROWS, D), jnp.bfloat16)
    input_list = []
    totals = None
    score_total = jnp.zeros((HEADS, ROWS, 8 * ROWS), jnp.float32)
    parts_total = jnp.zeros((6 * D,), jnp.float32)
    for clock_step in range(micro_count + 1):
        raw_id = micro_count - clock_step - section_id
        active_flag = ((raw_id >= 0) & (raw_id < micro_count)).astype(jnp.float32)
        micro_id = jnp.clip(raw_id, 0, micro_count - 1)
        incoming = jnp.where(
            section_id == 1, cotangent[max(micro_count - 1 - clock_step, 0)], grad_received
        )
        stored = kept_stack[micro_id + section_id].astype(jnp.float32)
        saved = forward(gathered_weights, stored, micro_id)[1]
        grad_result = incoming.astype(jnp.float32)
        (
            backward_w_joint,
            backward_w_self_out,
            backward_w_query,
            backward_w_memory,
            backward_w_cross_out,
            backward_w_upper,
            backward_w_lower,
        ) = gathered_weights
        (
            backward_cond_row,
            backward_mod_parts,
            backward_text_part,
            backward_hidden_low,
            backward_joint_rows,
            backward_text_query,
            backward_gathered,
            backward_mixture,
            backward_soft_self,
            backward_mixture_text,
            backward_soft_text,
            backward_branch,
            backward_middle,
            backward_second_low,
            backward_upper_pre,
            backward_active_low,
            backward_feed_out,
        ) = saved
        grad_gate_two = jnp.sum(grad_result * backward_feed_out, 0)
        grad_feed = (backward_mod_parts[5] * grad_result).astype(jnp.bfloat16)
        grad_lower = jnp.dot(backward_active_low.T, grad_feed, preferred_element_type=jnp.float32)
        grad_active = jnp.dot(grad_feed, backward_w_lower.T, preferred_element_type=jnp.float32)
        grad_upper_pre = jax.vjp(jax.nn.gelu, backward_upper_pre)[1](grad_active)[0].astype(
            jnp.bfloat16
        )
        grad_upper = jnp.dot(
            backward_second_low.T, grad_upper_pre, preferred_element_type=jnp.float32
        )
        grad_second = jnp.dot(
            grad_upper_pre, backward_w_upper.T, preferred_element_type=jnp.float32
        )
        grad_middle_norm, grad_shift_two, grad_scale_two = jax.vjp(
            layer_mod, backward_middle, backward_mod_parts[3], backward_mod_parts[4]
        )[1](grad_second)
        grad_middle = grad_result + grad_middle_norm
        grad_gate_one = jnp.sum(grad_middle * backward_branch, 0)
        grad_branch = (backward_mod_parts[2] * grad_middle).astype(jnp.bfloat16)
        grad_self_out = jnp.dot(backward_mixture.T, grad_branch, preferred_element_type=jnp.float32)
        grad_cross_out = jnp.dot(
            backward_mixture_text.T, grad_branch, preferred_element_type=jnp.float32
        )
        grad_mixture = jnp.dot(
            grad_branch, backward_w_self_out.T, preferred_element_type=jnp.float32
        ).astype(jnp.bfloat16)
        grad_mixture_text = jnp.dot(
            grad_branch, backward_w_cross_out.T, preferred_element_type=jnp.float32
        ).astype(jnp.bfloat16)
        grad_q_self, grad_keys, grad_values, grad_scores = attend_back(
            backward_joint_rows[:, :D],
            backward_gathered[0],
            backward_gathered[1],
            backward_soft_self,
            grad_mixture,
        )
        grad_q_text, grad_text_keys, grad_text_values, unused = attend_back(
            backward_text_query,
            backward_gathered[2],
            backward_gathered[3],
            backward_soft_text,
            grad_mixture_text,
        )
        owned_grads = spread_back(
            (grad_keys, grad_values, grad_text_keys, grad_text_values), member
        )
        grad_joint = jnp.concatenate([grad_q_self, owned_grads[0], owned_grads[1]], 1).astype(
            jnp.bfloat16
        )
        grad_memory = jnp.concatenate([owned_grads[2], owned_grads[3]], 1).astype(jnp.bfloat16)
        grad_asked = grad_q_text.astype(jnp.bfloat16)
        grad_joint_w = jnp.dot(
            backward_hidden_low.T, grad_joint, preferred_element_type=jnp.float32
        )
        grad_query_w = jnp.dot(
            backward_hidden_low.T, grad_asked, preferred_element_type=jnp.float32
        )
        grad_memory_w = jnp.dot(
            backward_text_part.T, grad_memory, preferred_element_type=jnp.float32
        )
        grad_hidden = jnp.dot(
            grad_joint, backward_w_joint.T, preferred_element_type=jnp.float32
        ) + jnp.dot(grad_asked, backward_w_query.T, preferred_element_type=jnp.float32)
        grad_inputs_norm, grad_shift_one, grad_scale_one = jax.vjp(
            layer_mod, stored, backward_mod_parts[0], backward_mod_parts[1]
        )[1](grad_hidden)
        grad_inputs = grad_middle + grad_inputs_norm
        grad_parts = jnp.concatenate(
            [
                grad_shift_one,
                grad_scale_one,
                grad_gate_one,
                grad_shift_two,
                grad_scale_two,
                grad_gate_two,
            ]
        )
        base_terms = (
            grad_joint_w,
            grad_self_out,
            grad_query_w,
            grad_memory_w,
            grad_cross_out,
            grad_upper,
            grad_lower,
        )
        grad_modul = backward_cond_row.astype(jnp.float32)[:, None] * grad_parts[None, :]
        weight_terms = base_terms + (grad_modul,)
        grad_inputs, weight_terms, grad_parts, grad_scores = (
            grad_inputs,
            weight_terms,
            grad_parts,
            grad_scores,
        )
        weight_terms = tuple((weight_term * active_flag for weight_term in weight_terms))
        totals = (
            weight_terms
            if totals is None
            else tuple(
                (left_part + right_part for left_part, right_part in zip(totals, weight_terms))
            )
        )
        score_total = score_total + grad_scores * active_flag
        parts_total = parts_total + grad_parts * active_flag
        sending = grad_inputs.astype(jnp.bfloat16)
        input_list.append(sending)
        if clock_step < micro_count:
            grad_received = from_behind(sending, "section", -1)
    shards = (
        lax.psum_scatter(totals[0], "dp", scatter_dimension=0, tiled=True),
        lax.psum_scatter(totals[1], "dp", scatter_dimension=0, tiled=True),
        lax.psum_scatter(totals[2], "dp", scatter_dimension=0, tiled=True),
        lax.psum_scatter(totals[3], "dp", scatter_dimension=0, tiled=True),
        lax.psum_scatter(totals[4], "dp", scatter_dimension=0, tiled=True),
        lax.psum_scatter(totals[5], "dp", scatter_dimension=0, tiled=True),
        lax.psum_scatter(totals[6], "dp", scatter_dimension=0, tiled=True),
        lax.psum_scatter(totals[7], "dp", scatter_dimension=0, tiled=True),
    )
    modul_shard = shards[7]
    table_grad = jnp.einsum("hqk,qkn->hn", score_total, hot_table, precision=lax.Precision.HIGHEST)
    table_sum, bias_sum = lax.psum((table_grad, parts_total), "dp")
    outputs = jnp.stack(
        [
            jnp.where(section_id == 0, block_results[micro_index], block_results[micro_index + 1])
            for micro_index in range(micro_count)
        ]
    )
    input_grads = jnp.stack(
        [
            jnp.where(
                section_id == 1,
                input_list[micro_count - 1 - micro_index],
                input_list[micro_count - micro_index],
            )
            for micro_index in range(micro_count)
        ]
    )
    return (
        outputs[None],
        input_grads[None],
        shards[0][None],
        shards[1][None],
        shards[2][None],
        shards[3][None],
        shards[4][None],
        shards[5][None],
        shards[6][None],
        modul_shard[None],
        bias_sum[None],
        table_sum[None],
    )


def solution(mesh):
    return jax.shard_map(
        per_device,
        mesh=mesh,
        in_specs=(
            P(None, "dp", None),
            P(),
            P(None, "dp", None),
            P(),
            P(None, "dp", None),
            P("section", "dp", None),
            P("section", "dp", None),
            P("section", "dp", None),
            P("section", "dp", None),
            P("section", "dp", None),
            P("section", "dp", None),
            P("section", "dp", None),
            P("section", "dp", None),
            P("section", None),
            P("section", None, None),
        ),
        out_specs=(
            P("section", None, "dp", None),
            P("section", None, "dp", None),
            P("section", "dp", None),
            P("section", "dp", None),
            P("section", "dp", None),
            P("section", "dp", None),
            P("section", "dp", None),
            P("section", "dp", None),
            P("section", "dp", None),
            P("section", "dp", None),
            P("section", None),
            P("section", None, None),
        ),
        check_vma=False,
    )
```

profile of v0, /device:TPU:0, one launch (start us, length us, event | category | flops | bytes accessed | tf_op | source)
XLA Modules:
  0.0 2580.8 jit_solution(16860438059901379923)
XLA Ops:
  23.8 28.9 %fusion.22 = f32[160,1280,16]{1,2,0:T(8,128)} fusion(s32[160,1280]{1,0:T(8,128)S(1)} %subtract_add_fusion, s32[160,1280]{1,0:T(8,128)S(1)} %subtract_add_fusion.1, s32[160,1280]{1,0:T(8,128)S(1)} %subtract_add_fusion.2, f32[1,16,71]{2,1,0:T(8,128)S(1)} %copy-done), kind=kOutput, calls=%fused_computation.24 | convolution fusion | flops 2864537600 | bytes 15569344 | tf_op jit(solution)/shard_map/qkn,hn->hqk/dot_general | solution.py:219
  52.7 11.5 all-gather.23.cloned.1.call-done
  80.6 85.8 %all-gather.17.cloned.1.call-done = bf16[1,1024,6144]{2,1,0:T(8,128)(2,1)} async-done(((bf16[1,64,6144]{2,1,0:T(8,128)(2,1)}), bf16[1,1024,6144]{2,1,0:T(8,128)(2,1)}) %all-gather.17.cloned.1.call-update) | async-done | bytes 12582928 | tf_op jit(solution)/shard_map/all_gather | solution.py:208
  173.6 55.7 %all-gather.19.cloned.1.call-done = bf16[1,1024,3072]{2,1,0:T(8,128)(2,1)} async-done(((bf16[1,64,3072]{2,1,0:T(8,128)(2,1)}), bf16[1,1024,3072]{2,1,0:T(8,128)(2,1)}) %all-gather.19.cloned.1.call-update) | async-done | bytes 6291472 | tf_op jit(solution)/shard_map/all_gather | solution.py:201
  255.3 21.5 all-gather.25.cloned.1.call-done
  294.3 29.6 %all-gather.27.cloned.1.call-done = bf16[1,1024,1024]{2,1,0:T(8,128)(2,1)} async-done(((bf16[1,64,1024]{2,1,0:T(8,128)(2,1)}), bf16[1,1024,1024]{2,1,0:T(8,128)(2,1)}) %all-gather.27.cloned.1.call-update) | async-done | bytes 2097168 | tf_op jit(solution)/shard_map/all_gather | solution.py:205
  345.7 21.3 collective-permute-done.2
  369.5 14.9 fusion.24
  384.4 11.1 fusion.819
  395.5 15.4 fusion.344
  413.6 35.9 %all-gather.31.cloned.1.call-done = bf16[1,4096,1024]{2,1,0:T(8,128)(2,1)} async-done(((bf16[1,256,1024]{2,1,0:T(8,128)(2,1)}), bf16[1,4096,1024]{2,1,0:T(8,128)(2,1)}) %all-gather.31.cloned.1.call-update) | async-done | bytes 8388624 | tf_op jit(solution)/shard_map/all_gather | solution.py:207
  449.5 75.2 %all-gather.29.cloned.1.call-done = bf16[1,1024,4096]{2,1,0:T(8,128)(2,1)} async-done(((bf16[1,64,4096]{2,1,0:T(8,128)(2,1)}), bf16[1,1024,4096]{2,1,0:T(8,128)(2,1)}) %all-gather.29.cloned.1.call-update) | async-done | bytes 8388624 | tf_op jit(solution)/shard_map/all_gather | solution.py:206
  524.7 9.3 fusion.468
  626.5 20.5 fusion.25
  646.9 11.1 fusion.822
  660.5 16.2 fusion.343
  680.3 10.3 fusion.471
  726.3 10.1 collective-permute-done.42
  779.9 20.6 fusion.27
  800.5 15.7 fusion.828
  818.6 15.9 fusion.333
  842.6 8.4 fusion.141
  860.3 16.0 convolution_bitcast_fusion.4
  882.1 20.1 subtract_multiply_fusion.2
  939.6 9.3 collective-permute-done.47
  951.6 22.7 collective-permute-done.44
  979.7 10.8 collective-permute-done.45
  1087.1 9.0 collective-permute-done.68
  1122.5 20.5 fusion.28
  1143.1 15.7 fusion.832
  1158.8 20.8 collective-permute-done.69
  1182.0 13.9 fusion.29
  1198.5 15.5 fusion.336
  1214.0 15.5 fusion.830
  1232.0 15.7 fusion.339
  1278.3 15.8 convolution_bitcast_fusion.2
  1301.5 19.2 subtract_multiply_fusion.1
  1343.8 9.6 fusion.331
  1356.0 11.5 collective-permute-done.57
  1372.9 10.5 collective-permute-done.58
  1405.0 10.8 collective-permute-done.63
  1566.9 10.7 multiply_add_fusion.5
  1578.3 14.8 convolution_bitcast_fusion
  1597.7 33.6 %multiply_add_fusion.3 = (f32[16,160,1280]{2,1,0:T(8,128)}, f32[16,160,1280]{2,1,0:T(8,128)}) fusion(f32[16,160,1280]{2,1,0:T(8,128)} %subtract_multiply_fusion.1, f32[16,160,1280]{2,1,0:T(8,128)} %subtract_multiply_fusion.2, f32[]{:T(128)S(6)} %convert_element_type.995, f32[]{:T(128)S(6)} %convert_element_type.994, f32[]{:T(128)S(6)} %convert_element_type.993, ...), kind=kOutput, calls=%fused_computation.41 | convolution fusion | flops 895225600 | bytes 68495376 | tf_op jit(solution)/shard_map/sub | solution.py:160
  1662.4 19.8 collective-permute-done.70
  1710.5 14.9 multiply_add_fusion.4
  1726.4 9.7 fusion.787
  1736.2 8.4 fusion.788
  1744.6 19.3 multiply_add_fusion.2
  1765.0 10.1 fusion.636
  1783.4 23.3 multiply_add_fusion.1
  1830.1 12.6 multiply_add_fusion
  1863.2 12.3 collective-permute-done.30
  1881.3 18.5 collective-permute-done.27
  1930.5 31.3 %collective-permute-done.28 = bf16[640,1024]{1,0:T(8,128)(2,1)} collective-permute-done((bf16[640,1024]{1,0:T(8,128)(2,1)}, bf16[640,1024]{1,0:T(8,128)(2,1)}, u32[]{:S(2)}, u32[]{:S(2)}) %collective-permute-start.28) | collective-permute-done | bytes 1310752 | tf_op jit(solution)/shard_map/ppermute | solution.py:21
  1964.3 14.9 fusion.26
  1979.2 15.2 fusion.825
  1994.5 15.9 fusion.342
  2013.4 9.8 fusion.489
  2024.1 40.4 %fusion.492 = f32[1,16,71]{2,1,0:T(8,128)S(1)} fusion(s32[160,1280]{1,0:T(8,128)} %copy-done.186, s32[160,1280]{1,0:T(8,128)} %copy-done.187, s32[160,1280]{1,0:T(8,128)} %copy-done.185, f32[16,160,1280]{2,1,0:T(8,128)} %get-tuple-element.152), kind=kOutput, calls=%fused_computation.487 | convolution fusion | flops 2864537600 | bytes 15569344 | tf_op jit(solution)/shard_map/hqk,qkn->hn/dot_general | solution.py:453
  2064.5 61.2 %all-reduce = (f32[1,6144]{1,0:T(1,128)}, f32[1,16,71]{2,1,0:T(8,128)}) all-reduce(f32[1,6144]{1,0:T(1,128)S(1)} %bitcast.1025, f32[1,16,71]{2,1,0:T(8,128)S(1)} %fusion.492), channel_id=1, replica_groups=mesh['section'=2,'dp'=16] {'dp'}, use_global_device_ids=true, to_apply=%region_92.93 | all-reduce | flops 7280 | bytes 58240 | tf_op jit(solution)/shard_map/psum | solution.py:454
  2127.1 16.3 reduce-scatter.19.cloned.1.call-done
  2143.4 182.6 %reduce-scatter.21.cloned.1.call-done = f32[256,1024]{1,0:T(8,128)} async-done(((f32[4096,1024]{1,0:T(8,128)}), f32[256,1024]{1,0:T(8,128)}) %reduce-scatter.21.cloned.1.call-update) | async-done | bytes 1048592 | tf_op jit(solution)/shard_map/reduce_scatter | solution.py:449
  2326.0 248.0 %reduce-scatter.23.cloned.1.call-done = f32[64,6144]{1,0:T(8,128)} async-done(((f32[1024,6144]{1,0:T(8,128)}), f32[64,6144]{1,0:T(8,128)}) %reduce-scatter.23.cloned.1.call-update) | async-done | bytes 1572880 | tf_op jit(solution)/shard_map/reduce_scatter | solution.py:450
  (1388 shorter events, 888.4 us)
Async XLA Ops:
  7.2 57.0 %all-gather.23.cloned.1.call-start = ((), (), s32[]{:S(2)}) async-start(), calls=%async_computation.19 | async-start | bytes 4456448 | tf_op jit(solution)/shard_map/all_gather | solution.py:204
  9.1 157.2 %all-gather.17.cloned.1.call-start = ((), (), s32[]{:S(2)}) async-start(), calls=%async_computation.16 | async-start | bytes 13369344 | tf_op jit(solution)/shard_map/all_gather | solution.py:208
  11.7 217.6 %all-gather.19.cloned.1.call-start = ((), (), s32[]{:S(2)}) async-start(), calls=%async_computation.17 | async-start | bytes 6684672 | tf_op jit(solution)/shard_map/all_gather | solution.py:201
  12.6 264.2 %all-gather.25.cloned.1.call-start = ((), (), s32[]{:S(2)}) async-start(), calls=%async_computation.20 | async-start | bytes 2228224 | tf_op jit(solution)/shard_map/all_gather | solution.py:203
  13.3 310.6 %all-gather.27.cloned.1.call-start = ((), (), s32[]{:S(2)}) async-start(), calls=%async_computation.21 | async-start | bytes 2228224 | tf_op jit(solution)/shard_map/all_gather | solution.py:205
  14.1 396.8 %all-gather.21.cloned.1.call-start = ((), (), s32[]{:S(2)}) async-start(), calls=%async_computation.18 | async-start | bytes 2228224 | tf_op jit(solution)/shard_map/all_gather | solution.py:202
  15.8 433.6 %all-gather.31.cloned.1.call-start = ((), (), s32[]{:S(2)}) async-start(), calls=%async_computation.23 | async-start | bytes 8912896 | tf_op jit(solution)/shard_map/all_gather | solution.py:207
  16.8 507.9 %all-gather.29.cloned.1.call-start = ((), (), s32[]{:S(2)}) async-start(), calls=%async_computation.22 | async-start | bytes 8912896 | tf_op jit(solution)/shard_map/all_gather | solution.py:206
  17.7 2109.4 %reduce-scatter.11.cloned.1.call-start = ((), (), s32[]{:S(2)}) async-start(), calls=%async_computation.9 | async-start | bytes 4456448 | tf_op jit(solution)/shard_map/reduce_scatter | solution.py:444
  71.2 164.3 %collective-permute-start.20 = (bf16[20,1024]{1,0:T(8,128)(2,1)S(1)}, bf16[20,1024]{1,0:T(8,128)(2,1)S(1)}, u32[]{:S(2)}, u32[]{:S(2)}) collective-permute-start(bf16[20,1024]{1,0:T(8,128)(2,1)S(1)} %maximum_select_fusion.104), channel_id=1, source_target_pairs={{0,2},{1,3},{2,0},{3,1},{4,6},{5,7},{6,4},{7,5},{8,10},{9,11},{10,... | collective-permute-start | bytes 122888 | tf_op jit(solution)/shard_map/ppermute | solution.py:21
  74.1 463.6 %collective-permute-start.23 = (bf16[20,1024]{1,0:T(8,128)(2,1)S(1)}, bf16[20,1024]{1,0:T(8,128)(2,1)}, u32[]{:S(2)}, u32[]{:S(2)}) collective-permute-start(bf16[20,1024]{1,0:T(8,128)(2,1)S(1)} %maximum_select_fusion.105), channel_id=1, source_target_pairs={{0,2},{1,3},{2,0},{3,1},{4,6},{5,7},{6,4},{7,5},{8,10},{9,11},{10,... | collective-permute-start | bytes 122888 | tf_op jit(solution)/shard_map/ppermute | solution.py:21
  76.2 463.9 %collective-permute-start.33 = (bf16[20,1024]{1,0:T(8,128)(2,1)S(1)}, bf16[20,1024]{1,0:T(8,128)(2,1)}, u32[]{:S(2)}, u32[]{:S(2)}) collective-permute-start(bf16[20,1024]{1,0:T(8,128)(2,1)S(1)} %maximum_select_fusion.106), channel_id=1, source_target_pairs={{0,2},{1,3},{2,0},{3,1},{4,6},{5,7},{6,4},{7,5},{8,10},{9,11},{10,... | collective-permute-start | bytes 122888 | tf_op jit(solution)/shard_map/ppermute | solution.py:21
  243.5 37.5 %collective-permute-start.4 = (bf16[320,1024]{1,0:T(8,128)(2,1)}, bf16[320,1024]{1,0:T(8,128)(2,1)S(1)}, u32[]{:S(2)}, u32[]{:S(2)}) collective-permute-start(bf16[320,1024]{1,0:T(8,128)(2,1)} %maximum_select_fusion.61), channel_id=1, source_target_pairs={{0,2},{1,3},{2,0},{3,1},{4,6},{5,7},{6,4},{7,5},{8,10},{9,11},{10,... | collective-permute-start | bytes 1966088 | tf_op jit(solution)/shard_map/ppermute | solution.py:21
  245.1 41.0 %collective-permute-start.1 = (bf16[320,1024]{1,0:T(8,128)(2,1)}, bf16[320,1024]{1,0:T(8,128)(2,1)S(1)}, u32[]{:S(2)}, u32[]{:S(2)}) collective-permute-start(bf16[320,1024]{1,0:T(8,128)(2,1)} %maximum_select_fusion.60), channel_id=1, source_target_pairs={{0,2},{1,3},{2,0},{3,1},{4,6},{5,7},{6,4},{7,5},{8,10},{9,11},{10,... | collective-permute-start | bytes 1966088 | tf_op jit(solution)/shard_map/ppermute | solution.py:21
  248.8 294.0 %collective-permute-start.36 = (bf16[20,1024]{1,0:T(8,128)(2,1)}, bf16[20,1024]{1,0:T(8,128)(2,1)}, u32[]{:S(2)}, u32[]{:S(2)}) collective-permute-start(bf16[20,1024]{1,0:T(8,128)(2,1)} %maximum_select_fusion.107), channel_id=1, source_target_pairs={{0,2},{1,3},{2,0},{3,1},{4,6},{5,7},{6,4},{7,5},{8,10},{9,11},{10,... | collective-permute-start | bytes 122888 | tf_op jit(solution)/shard_map/ppermute | solution.py:21
  283.9 56.5 %collective-permute-start.5 = (bf16[640,1024]{1,0:T(8,128)(2,1)}, bf16[640,1024]{1,0:T(8,128)(2,1)}, u32[]{:S(2)}, u32[]{:S(2)}) collective-permute-start(bf16[640,1024]{1,0:T(8,128)(2,1)} %maximum_select_fusion.20), channel_id=1, source_target_pairs={{0,4},{1,5},{2,6},{3,7},{4,0},{5,1},{6,2},{7,3},{8,12},{9,13},{10,... | collective-permute-start | bytes 3932168 | tf_op jit(solution)/shard_map/ppermute | solution.py:21
  289.0 78.0 %collective-permute-start.2 = (bf16[640,1024]{1,0:T(8,128)(2,1)}, bf16[640,1024]{1,0:T(8,128)(2,1)}, u32[]{:S(2)}, u32[]{:S(2)}) collective-permute-start(bf16[640,1024]{1,0:T(8,128)(2,1)} %maximum_select_fusion.18), channel_id=1, source_target_pairs={{0,4},{1,5},{2,6},{3,7},{4,0},{5,1},{6,2},{7,3},{8,12},{9,13},{10,... | collective-permute-start | bytes 3932168 | tf_op jit(solution)/shard_map/ppermute | solution.py:21
  340.4 217.2 %collective-permute-start.21 = (bf16[40,1024]{1,0:T(8,128)(2,1)}, bf16[40,1024]{1,0:T(8,128)(2,1)}, u32[]{:S(2)}, u32[]{:S(2)}) collective-permute-start(bf16[40,1024]{1,0:T(8,128)(2,1)} %maximum_select_fusion.94), channel_id=1, source_target_pairs={{0,4},{1,5},{2,6},{3,7},{4,0},{5,1},{6,2},{7,3},{8,12},{9,13},{10,... | collective-permute-start | bytes 245768 | tf_op jit(solution)/shard_map/ppermute | solution.py:21
  539.2 24.1 collective-permute-start.24
  541.6 152.7 %collective-permute-start.34 = (bf16[40,1024]{1,0:T(8,128)(2,1)}, bf16[40,1024]{1,0:T(8,128)(2,1)}, u32[]{:S(2)}, u32[]{:S(2)}) collective-permute-start(bf16[40,1024]{1,0:T(8,128)(2,1)} %maximum_select_fusion.98), channel_id=1, source_target_pairs={{0,4},{1,5},{2,6},{3,7},{4,0},{5,1},{6,2},{7,3},{8,12},{9,13},{10,... | collective-permute-start | bytes 245768 | tf_op jit(solution)/shard_map/ppermute | solution.py:21
  544.4 151.0 %collective-permute-start.37 = (bf16[40,1024]{1,0:T(8,128)(2,1)}, bf16[40,1024]{1,0:T(8,128)(2,1)}, u32[]{:S(2)}, u32[]{:S(2)}) collective-permute-start(bf16[40,1024]{1,0:T(8,128)(2,1)} %maximum_select_fusion.100), channel_id=1, source_target_pairs={{0,4},{1,5},{2,6},{3,7},{4,0},{5,1},{6,2},{7,3},{8,12},{9,13},{10,... | collective-permute-start | bytes 245768 | tf_op jit(solution)/shard_map/ppermute | solution.py:21
  567.4 17.4 collective-permute-start.17
  588.3 35.8 %collective-permute-start.18 = (bf16[640,1024]{1,0:T(8,128)(2,1)}, bf16[640,1024]{1,0:T(8,128)(2,1)}, u32[]{:S(2)}, u32[]{:S(2)}) collective-permute-start(bf16[640,1024]{1,0:T(8,128)(2,1)} %maximum_select_fusion.24), channel_id=1, source_target_pairs={{0,4},{1,5},{2,6},{3,7},{4,0},{5,1},{6,2},{7,3},{8,12},{9,13},{10,... | collective-permute-start | bytes 3932168 | tf_op jit(solution)/shard_map/ppermute | solution.py:21
  590.5 18.1 collective-permute-start.14
  612.0 46.0 %collective-permute-start.15 = (bf16[640,1024]{1,0:T(8,128)(2,1)}, bf16[640,1024]{1,0:T(8,128)(2,1)}, u32[]{:S(2)}, u32[]{:S(2)}) collective-permute-start(bf16[640,1024]{1,0:T(8,128)(2,1)} %maximum_select_fusion.22), channel_id=1, source_target_pairs={{0,4},{1,5},{2,6},{3,7},{4,0},{5,1},{6,2},{7,3},{8,12},{9,13},{10,... | collective-permute-start | bytes 3932168 | tf_op jit(solution)/shard_map/ppermute | solution.py:21
  716.8 24.1 collective-permute-start.38
  719.4 17.0 collective-permute-start.42
  739.8 37.6 %collective-permute-start.43 = (bf16[640,1024]{1,0:T(8,128)(2,1)}, bf16[640,1024]{1,0:T(8,128)(2,1)}, u32[]{:S(2)}, u32[]{:S(2)}) collective-permute-start(bf16[640,1024]{1,0:T(8,128)(2,1)} %maximum_select_fusion.32), channel_id=1, source_target_pairs={{0,4},{1,5},{2,6},{3,7},{4,0},{5,1},{6,2},{7,3},{8,12},{9,13},{10,... | collective-permute-start | bytes 3932168 | tf_op jit(solution)/shard_map/ppermute | solution.py:21
  743.0 18.8 collective-permute-start.39
  765.3 50.8 %collective-permute-start.40 = (bf16[640,1024]{1,0:T(8,128)(2,1)}, bf16[640,1024]{1,0:T(8,128)(2,1)}, u32[]{:S(2)}, u32[]{:S(2)}) collective-permute-start(bf16[640,1024]{1,0:T(8,128)(2,1)} %maximum_select_fusion.30), channel_id=1, source_target_pairs={{0,4},{1,5},{2,6},{3,7},{4,0},{5,1},{6,2},{7,3},{8,12},{9,13},{10,... | collective-permute-start | bytes 3932168 | tf_op jit(solution)/shard_map/ppermute | solution.py:21
  916.9 32.0 %collective-permute-start.47 = (bf16[640,1024]{1,0:T(8,128)(2,1)}, bf16[640,1024]{1,0:T(8,128)(2,1)}, u32[]{:S(2)}, u32[]{:S(2)}) collective-permute-start(bf16[640,1024]{1,0:T(8,128)(2,1)} %copy.465), channel_id=1, source_target_pairs={{0,4},{1,5},{2,6},{3,7},{4,0},{5,1},{6,2},{7,3},{8,12},{9,13},{10,... | collective-permute-start | bytes 3932168 | tf_op jit(solution)/shard_map/ppermute | solution.py:21
  923.7 50.6 %collective-permute-start.44 = (bf16[640,1024]{1,0:T(8,128)(2,1)}, bf16[640,1024]{1,0:T(8,128)(2,1)}, u32[]{:S(2)}, u32[]{:S(2)}) collective-permute-start(bf16[640,1024]{1,0:T(8,128)(2,1)} %copy.462), channel_id=1, source_target_pairs={{0,4},{1,5},{2,6},{3,7},{4,0},{5,1},{6,2},{7,3},{8,12},{9,13},{10,... | collective-permute-start | bytes 3932168 | tf_op jit(solution)/shard_map/ppermute | solution.py:21
  951.0 27.5 %collective-permute-start.48 = (bf16[320,1024]{1,0:T(8,128)(2,1)S(1)}, bf16[320,1024]{1,0:T(8,128)(2,1)S(1)}, u32[]{:S(2)}, u32[]{:S(2)}) collective-permute-start(bf16[320,1024]{1,0:T(8,128)(2,1)S(1)} %select_convert_fusion.10), channel_id=1, source_target_pairs={{0,2},{1,3},{2,0},{3,1},{4,6},{5,7},{6,4},{7,5},{8,10},{9,11},{10,... | collective-permute-start | bytes 1966088 | tf_op jit(solution)/shard_map/ppermute | solution.py:21
  979.6 17.6 collective-permute-start.49
  1018.1 27.1 %collective-permute-start.51 = (bf16[160,1024]{1,0:T(8,128)(2,1)S(1)}, bf16[160,1024]{1,0:T(8,128)(2,1)}, u32[]{:S(2)}, u32[]{:S(2)}) collective-permute-start(bf16[160,1024]{1,0:T(8,128)(2,1)S(1)} %get-tuple-element.71), channel_id=1, source_target_pairs={{0,1},{1,0},{2,3},{3,2},{4,5},{5,4},{6,7},{7,6},{8,9},{9,8},{10,11... | collective-permute-start | bytes 983048 | tf_op jit(solution)/shard_map/ppermute | solution.py:21
  1030.0 19.0 collective-permute-start.64
  1030.5 21.4 collective-permute-start.67
  1036.5 25.5 collective-permute-start.55
  1047.6 30.0 %collective-permute-start.52 = (bf16[320,1024]{1,0:T(8,128)(2,1)}, bf16[320,1024]{1,0:T(8,128)(2,1)}, u32[]{:S(2)}, u32[]{:S(2)}) collective-permute-start(bf16[320,1024]{1,0:T(8,128)(2,1)} %maximum_select_fusion.68), channel_id=1, source_target_pairs={{0,2},{1,3},{2,0},{3,1},{4,6},{5,7},{6,4},{7,5},{8,10},{9,11},{10,... | collective-permute-start | bytes 1966088 | tf_op jit(solution)/shard_map/ppermute | solution.py:21
  1051.4 31.1 %collective-permute-start.65 = (bf16[320,1024]{1,0:T(8,128)(2,1)}, bf16[320,1024]{1,0:T(8,128)(2,1)}, u32[]{:S(2)}, u32[]{:S(2)}) collective-permute-start(bf16[320,1024]{1,0:T(8,128)(2,1)} %maximum_select_fusion.70), channel_id=1, source_target_pairs={{0,2},{1,3},{2,0},{3,1},{4,6},{5,7},{6,4},{7,5},{8,10},{9,11},{10,... | collective-permute-start | bytes 1966088 | tf_op jit(solution)/shard_map/ppermute | solution.py:21
  1054.4 41.8 %collective-permute-start.68 = (bf16[320,1024]{1,0:T(8,128)(2,1)}, bf16[320,1024]{1,0:T(8,128)(2,1)}, u32[]{:S(2)}, u32[]{:S(2)}) collective-permute-start(bf16[320,1024]{1,0:T(8,128)(2,1)} %maximum_select_fusion.71), channel_id=1, source_target_pairs={{0,2},{1,3},{2,0},{3,1},{4,6},{5,7},{6,4},{7,5},{8,10},{9,11},{10,... | collective-permute-start | bytes 1966088 | tf_op jit(solution)/shard_map/ppermute | solution.py:21
  1064.9 54.7 %collective-permute-start.56 = (bf16[640,1024]{1,0:T(8,128)(2,1)}, bf16[640,1024]{1,0:T(8,128)(2,1)}, u32[]{:S(2)}, u32[]{:S(2)}) collective-permute-start(bf16[640,1024]{1,0:T(8,128)(2,1)} %maximum_select_fusion.36), channel_id=1, source_target_pairs={{0,4},{1,5},{2,6},{3,7},{4,0},{5,1},{6,2},{7,3},{8,12},{9,13},{10,... | collective-permute-start | bytes 3932168 | tf_op jit(solution)/shard_map/ppermute | solution.py:21
  1081.0 115.0 %collective-permute-start.53 = (bf16[640,1024]{1,0:T(8,128)(2,1)}, bf16[640,1024]{1,0:T(8,128)(2,1)}, u32[]{:S(2)}, u32[]{:S(2)}) collective-permute-start(bf16[640,1024]{1,0:T(8,128)(2,1)} %maximum_select_fusion.34), channel_id=1, source_target_pairs={{0,4},{1,5},{2,6},{3,7},{4,0},{5,1},{6,2},{7,3},{8,12},{9,13},{10,... | collective-permute-start | bytes 3932168 | tf_op jit(solution)/shard_map/ppermute | solution.py:21
  1086.0 143.5 %collective-permute-start.66 = (bf16[640,1024]{1,0:T(8,128)(2,1)}, bf16[640,1024]{1,0:T(8,128)(2,1)}, u32[]{:S(2)}, u32[]{:S(2)}) collective-permute-start(bf16[640,1024]{1,0:T(8,128)(2,1)} %maximum_select_fusion.38), channel_id=1, source_target_pairs={{0,4},{1,5},{2,6},{3,7},{4,0},{5,1},{6,2},{7,3},{8,12},{9,13},{10,... | collective-permute-start | bytes 3932168 | tf_op jit(solution)/shard_map/ppermute | solution.py:21
  1099.6 80.0 %collective-permute-start.69 = (bf16[640,1024]{1,0:T(8,128)(2,1)}, bf16[640,1024]{1,0:T(8,128)(2,1)}, u32[]{:S(2)}, u32[]{:S(2)}) collective-permute-start(bf16[640,1024]{1,0:T(8,128)(2,1)} %maximum_select_fusion.40), channel_id=1, source_target_pairs={{0,4},{1,5},{2,6},{3,7},{4,0},{5,1},{6,2},{7,3},{8,12},{9,13},{10,... | collective-permute-start | bytes 3932168 | tf_op jit(solution)/shard_map/ppermute | solution.py:21
  1300.3 53.0 %collective-permute-start.60 = (bf16[640,1024]{1,0:T(8,128)(2,1)}, bf16[640,1024]{1,0:T(8,128)(2,1)}, u32[]{:S(2)}, u32[]{:S(2)}) collective-permute-start(bf16[640,1024]{1,0:T(8,128)(2,1)} %copy.494), channel_id=1, source_target_pairs={{0,4},{1,5},{2,6},{3,7},{4,0},{5,1},{6,2},{7,3},{8,12},{9,13},{10,... | collective-permute-start | bytes 3932168 | tf_op jit(solution)/shard_map/ppermute | solution.py:21
  1339.2 28.3 %collective-permute-start.57 = (bf16[640,1024]{1,0:T(8,128)(2,1)}, bf16[640,1024]{1,0:T(8,128)(2,1)}, u32[]{:S(2)}, u32[]{:S(2)}) collective-permute-start(bf16[640,1024]{1,0:T(8,128)(2,1)} %copy.491), channel_id=1, source_target_pairs={{0,4},{1,5},{2,6},{3,7},{4,0},{5,1},{6,2},{7,3},{8,12},{9,13},{10,... | collective-permute-start | bytes 3932168 | tf_op jit(solution)/shard_map/ppermute | solution.py:21
  1372.9 18.2 collective-permute-start.62
  1433.0 694.1 %reduce-scatter.13.cloned.1.call-start = ((), (), s32[]{:S(2)}) async-start(), calls=%async_computation.10 | async-start | bytes 4456448 | tf_op jit(solution)/shard_map/reduce_scatter | solution.py:445
  1438.3 23.9 collective-permute-start.79
  1463.2 29.5 %collective-permute-start.80 = (bf16[20,1024]{1,0:T(8,128)(2,1)S(1)}, bf16[20,1024]{1,0:T(8,128)(2,1)}, u32[]{:S(2)}, u32[]{:S(2)}) collective-permute-start(bf16[20,1024]{1,0:T(8,128)(2,1)S(1)} %select_convert_fusion.28), channel_id=1, source_target_pairs={{0,2},{1,3},{2,0},{3,1},{4,6},{5,7},{6,4},{7,5},{8,10},{9,11},{10,... | collective-permute-start | bytes 122888 | tf_op jit(solution)/shard_map/ppermute | solution.py:21
  1490.7 636.4 %reduce-scatter.17.cloned.1.call-start = ((), (), s32[]{:S(2)}) async-start(), calls=%async_computation.12 | async-start | bytes 4456448 | tf_op jit(solution)/shard_map/reduce_scatter | solution.py:447
  1532.3 594.8 %reduce-scatter.15.cloned.1.call-start = ((), (), s32[]{:S(2)}) async-start(), calls=%async_computation.11 | async-start | bytes 8912896 | tf_op jit(solution)/shard_map/reduce_scatter | solution.py:446
  1577.7 549.5 %reduce-scatter.9.cloned.1.call-start = ((), (), s32[]{:S(2)}) async-start(), calls=%async_computation.8 | async-start | bytes 13369344 | tf_op jit(solution)/shard_map/reduce_scatter | solution.py:443
  1597.6 61.0 %collective-permute-start.73 = (bf16[640,1024]{1,0:T(8,128)(2,1)}, bf16[640,1024]{1,0:T(8,128)(2,1)}, u32[]{:S(2)}, u32[]{:S(2)}) collective-permute-start(bf16[640,1024]{1,0:T(8,128)(2,1)} %copy.523), channel_id=1, source_target_pairs={{0,4},{1,5},{2,6},{3,7},{4,0},{5,1},{6,2},{7,3},{8,12},{9,13},{10,... | collective-permute-start | bytes 3932168 | tf_op jit(solution)/shard_map/ppermute | solution.py:21
  1641.5 40.7 %collective-permute-start.70 = (bf16[640,1024]{1,0:T(8,128)(2,1)}, bf16[640,1024]{1,0:T(8,128)(2,1)S(1)}, u32[]{:S(2)}, u32[]{:S(2)}) collective-permute-start(bf16[640,1024]{1,0:T(8,128)(2,1)} %copy.520), channel_id=1, source_target_pairs={{0,4},{1,5},{2,6},{3,7},{4,0},{5,1},{6,2},{7,3},{8,12},{9,13},{10,... | collective-permute-start | bytes 3932168 | tf_op jit(solution)/shard_map/ppermute | solution.py:21
  1661.5 29.6 %collective-permute-start.74 = (bf16[320,1024]{1,0:T(8,128)(2,1)S(1)}, bf16[320,1024]{1,0:T(8,128)(2,1)S(1)}, u32[]{:S(2)}, u32[]{:S(2)}) collective-permute-start(bf16[320,1024]{1,0:T(8,128)(2,1)S(1)} %select_convert_fusion.6), channel_id=1, source_target_pairs={{0,2},{1,3},{2,0},{3,1},{4,6},{5,7},{6,4},{7,5},{8,10},{9,11},{10,... | collective-permute-start | bytes 1966088 | tf_op jit(solution)/shard_map/ppermute | solution.py:21
  1725.5 418.0 %reduce-scatter.19.cloned.1.call-start = ((), (), s32[]{:S(2)}) async-start(), calls=%async_computation.13 | async-start | bytes 17825792 | tf_op jit(solution)/shard_map/reduce_scatter | solution.py:448
  1764.0 562.1 %reduce-scatter.21.cloned.1.call-start = ((), (), s32[]{:S(2)}) async-start(), calls=%async_computation.14 | async-start | bytes 17825792 | tf_op jit(solution)/shard_map/reduce_scatter | solution.py:449
  1806.8 767.3 %reduce-scatter.23.cloned.1.call-start = ((), (), s32[]{:S(2)}) async-start(), calls=%async_computation.15 | async-start | bytes 26738688 | tf_op jit(solution)/shard_map/reduce_scatter | solution.py:450
  1851.7 23.8 collective-permute-start.30
  1853.8 46.1 %collective-permute-start.27 = (bf16[320,1024]{1,0:T(8,128)(2,1)}, bf16[320,1024]{1,0:T(8,128)(2,1)}, u32[]{:S(2)}, u32[]{:S(2)}) collective-permute-start(bf16[320,1024]{1,0:T(8,128)(2,1)} %maximum_select_fusion.64), channel_id=1, source_target_pairs={{0,2},{1,3},{2,0},{3,1},{4,6},{5,7},{6,4},{7,5},{8,10},{9,11},{10,... | collective-permute-start | bytes 1966088 | tf_op jit(solution)/shard_map/ppermute | solution.py:21
  1878.9 49.1 %collective-permute-start.31 = (bf16[640,1024]{1,0:T(8,128)(2,1)}, bf16[640,1024]{1,0:T(8,128)(2,1)}, u32[]{:S(2)}, u32[]{:S(2)}) collective-permute-start(bf16[640,1024]{1,0:T(8,128)(2,1)} %maximum_select_fusion.28), channel_id=1, source_target_pairs={{0,4},{1,5},{2,6},{3,7},{4,0},{5,1},{6,2},{7,3},{8,12},{9,13},{10,... | collective-permute-start | bytes 3932168 | tf_op jit(solution)/shard_map/ppermute | solution.py:21
  1903.5 58.3 %collective-permute-start.28 = (bf16[640,1024]{1,0:T(8,128)(2,1)}, bf16[640,1024]{1,0:T(8,128)(2,1)}, u32[]{:S(2)}, u32[]{:S(2)}) collective-permute-start(bf16[640,1024]{1,0:T(8,128)(2,1)} %maximum_select_fusion.26), channel_id=1, source_target_pairs={{0,4},{1,5},{2,6},{3,7},{4,0},{5,1},{6,2},{7,3},{8,12},{9,13},{10,... | collective-permute-start | bytes 3932168 | tf_op jit(solution)/shard_map/ppermute | solution.py:21
  (385 other events, 11549.0 us)
Sparse Core Ops, SparseCore 0:
  10.8 53.4 all-gather.22
  67.1 99.2 all-gather.16
  169.2 60.0 all-gather.18
  231.9 44.8 all-gather.24
  278.8 45.0 all-gather.26
  325.9 47.3 all-gather.20
  375.4 73.9 all-gather.30
  451.6 73.0 all-gather.28
  1433.1 71.9 reduce-scatter.10
  1509.9 71.7 reduce-scatter.12
  1586.2 82.0 reduce-scatter.16
  1673.4 106.0 reduce-scatter.14
  1784.6 173.4 reduce-scatter.8
  1963.2 180.1 reduce-scatter.18
  2148.5 177.4 reduce-scatter.20
  2331.1 242.8 reduce-scatter.22
where the time goes:
time: 2590 us; the launch traced here: 2580 us
  waiting for transfers between devices  1020 us (39%)
  matrix products  835 us (32%)
  other arithmetic  344 us (13%)
  local copies, waits for them, and re-layouts  215 us (8%)
  starting transfers between devices  78.9 us (3%)
  blocking collectives  61.2 us (2%)
    ppermute x90, waiting for transfers between devices, swapped(): lax.ppermute(x, axis, [(i, i ^ 1 << bit) for i in range(lax.axis_size(axi...  251 us
    reduce_scatter x1, waiting for transfers between devices, per_device(): lax.psum_scatter(totals[7], 'dp', scatter_dimension=0, tiled=True)  248 us
    reduce_scatter x1, waiting for transfers between devices, per_device(): lax.psum_scatter(totals[6], 'dp', scatter_dimension=0, tiled=True)  183 us
    select_n x74, other arithmetic, collect(): jnp.where(upper_half, jnp.concatenate([peer_part, mine_part], 0), jnp.con...  149 us
    dot_general x6, matrix products, attend(): jnp.einsum('qhd,khd->hqk', query_heads, key_heads, preferred_element_type...  105 us
    dot_general x12, matrix products, attend(): jnp.einsum('hqk,khd->qhd', softmaxed.astype(jnp.bfloat16), value_heads, p...  103 us
    all_gather x1, waiting for transfers between devices, per_device(): lax.all_gather(modulation[0].astype(jnp.bfloat16), 'dp', axis=0, tiled=True)  85.8 us
    sub x6, other arithmetic, attend(): exponent = jnp.exp(scores - highest)  84.3 us
  transfers between devices with their start and end apart: 110, of which 40 were waited for; matrix products, arithmetic and copies ran while one was open for 45% of the time, Pallas kernels for 0%

commit v1 on v0

v1 whole, which is shorter than its diff:
```python
import functools

import jax
import jax.numpy as jnp
import numpy as np
from jax import lax
from jax.experimental import pallas as pl
from jax.experimental.pallas import tpu as pltpu
from jax.sharding import PartitionSpec as P

D = 1024
HEADS = 16
HEAD = 64
FF = 4096
FRAMES = 5
BH = 8
BW = 4
CELLS = BH * BW
ROWS = 160
REL = 71
MEMBERS = 8
PAIR = 2 * HEAD
TEXT_PAD = 16
EPSILON = 1e-06
NEGATIVE = -1e30
LOW = jnp.bfloat16
HIGH = jnp.float32
MIB = 1024 * 1024


def dot(left, right):
    return lax.dot_general(left, right, (((1,), (0,)), ((), ())), preferred_element_type=HIGH)


def dot_right_t(left, right):
    return lax.dot_general(left, right, (((1,), (1,)), ((), ())), preferred_element_type=HIGH)


def dot_left_t(left, right):
    return lax.dot_general(left, right, (((0,), (0,)), ((), ())), preferred_element_type=HIGH)


def low(v):
    return v.astype(LOW)


def high(v):
    return v.astype(HIGH)


def layer_mod(inputs, offset, factor):
    average = jnp.mean(inputs, axis=-1, keepdims=True)
    centred = inputs - average
    spread = jnp.mean(centred * centred, axis=-1, keepdims=True)
    return centred * lax.rsqrt(spread + EPSILON) * (1.0 + factor) + offset


def swap(x, bits, sections=(0, 1)):
    count = lax.axis_size("dp")
    route = [(s * count + i, s * count + (i ^ bits)) for s in sections for i in range(count)]
    return lax.ppermute(x, ("section", "dp"), route)


def xor_blocks(x, axis, block, member, parts=1):
    stride = x.shape[axis] // parts
    pieces = [
        lax.dynamic_slice_in_dim(x, part * stride + block * (member ^ k), block, axis)
        for k in range(MEMBERS)
        for part in range(parts)
    ]
    return jnp.concatenate(pieces, axis)


def xor_blocks_back(x, axis, block, member, parts):
    pieces = [
        lax.dynamic_slice_in_dim(x, block * (parts * (member ^ k) + part), block, axis)
        for part in range(parts)
        for k in range(MEMBERS)
    ]
    return jnp.concatenate(pieces, axis)


def head_masks(dtype):
    lane = lax.broadcasted_iota(jnp.int32, (1, PAIR), 1)
    first = (lane < HEAD).astype(dtype)
    return first, 1 - first


def soft_rows(queries, keys, bias):
    scores = dot_right_t(queries, keys) * HEAD ** (-0.5) + bias
    exponent = jnp.exp(scores - jnp.max(scores, axis=-1, keepdims=True))
    return exponent * (1.0 / jnp.sum(exponent, axis=-1, keepdims=True))


def attend_kernel(shared, q_ref, k_ref, v_ref, bias_ref, o_ref):
    masks = head_masks(LOW)
    q, k, v = q_ref[0], k_ref[0], v_ref[0]
    mixed = []
    for a in range(2):
        soft = soft_rows(q * masks[a], k, bias_ref[0 if shared else a])
        mixed.append(dot(low(soft), v))
    lane = lax.broadcasted_iota(jnp.int32, (1, PAIR), 1)
    o_ref[0] = low(jnp.where(lane < HEAD, mixed[0], mixed[1]))


def attend_back_kernel(shared, q_ref, k_ref, v_ref, bias_ref, do_ref, dq_ref, dk_ref, dv_ref, *rest):
    masks = head_masks(LOW)
    q, k, v, do = q_ref[0], k_ref[0], v_ref[0], do_ref[0]
    lane = lax.broadcasted_iota(jnp.int32, (1, PAIR), 1)
    dq, dk, dv = [], [], []
    for a in range(2):
        soft = soft_rows(q * masks[a], k, bias_ref[0 if shared else a])
        dv.append(dot_left_t(low(soft), do))
        grad = dot_right_t(do * masks[a], v)
        grad = soft * (grad - jnp.sum(soft * grad, axis=-1, keepdims=True))
        if rest:
            dbias_ref = rest[0]

            @pl.when(pl.program_id(1) == 0)
            def _():
                dbias_ref[a] = grad

            @pl.when(pl.program_id(1) > 0)
            def _():
                dbias_ref[a] += grad

        raw = low(grad * HEAD ** (-0.5))
        dq.append(dot(raw, k))
        dk.append(dot_left_t(raw, q))
    dq_ref[0] = low(jnp.where(lane < HEAD, dq[0], dq[1]))
    dk_ref[0] = low(jnp.where(lane < HEAD, dk[0], dk[1]))
    dv_ref[0] = low(jnp.where(lane < HEAD, dv[0], dv[1]))


def column_spec(rows, first):
    return pl.BlockSpec((1, rows, PAIR), lambda h, w: (w, 0, first + h))


def attend_shapes(q, k, heads):
    pairs = heads // 2
    return q[0].shape[0], q[0].shape[1], k[0].shape[1], pairs


def attend(q, k, v, bias, heads):
    windows, rows, keys, pairs = attend_shapes(q, k, heads)
    shared = bias.shape[0] == 1
    if shared:
        bias_spec = pl.BlockSpec((1,) + bias.shape[1:], lambda h, w: (0, 0, 0))
    else:
        bias_spec = pl.BlockSpec((2,) + bias.shape[1:], lambda h, w: (h, 0, 0))
    return pl.pallas_call(
        functools.partial(attend_kernel, shared),
        grid=(pairs, windows),
        in_specs=[
            column_spec(rows, q[1]),
            column_spec(keys, k[1]),
            column_spec(keys, v[1]),
            bias_spec,
        ],
        out_specs=column_spec(rows, 0),
        out_shape=jax.ShapeDtypeStruct((windows, rows, pairs * PAIR), LOW),
        cost_estimate=pl.CostEstimate(
            flops=8 * windows * pairs * rows * keys * PAIR,
            bytes_accessed=windows * pairs * PAIR * 4 * (rows + keys),
            transcendentals=2 * windows * pairs * rows * keys,
        ),
        compiler_params=pltpu.CompilerParams(vmem_limit_bytes=32 * MIB),
    )(q[0], k[0], v[0], bias)


def attend_back(q, k, v, bias, do, heads):
    windows, rows, keys, pairs = attend_shapes(q, k, heads)
    shared = bias.shape[0] == 1
    if shared:
        bias_spec = pl.BlockSpec((1,) + bias.shape[1:], lambda h, w: (0, 0, 0))
    else:
        bias_spec = pl.BlockSpec((2,) + bias.shape[1:], lambda h, w: (h, 0, 0))
    out_specs = [column_spec(rows, 0), column_spec(keys, 0), column_spec(keys, 0)]
    out_shape = [
        jax.ShapeDtypeStruct((windows, rows, pairs * PAIR), LOW),
        jax.ShapeDtypeStruct((windows, keys, pairs * PAIR), LOW),
        jax.ShapeDtypeStruct((windows, keys, pairs * PAIR), LOW),
    ]
    if not shared:
        out_specs.append(pl.BlockSpec((2, rows, keys), lambda h, w: (h, 0, 0)))
        out_shape.append(jax.ShapeDtypeStruct((heads, rows, keys), HIGH))
    return pl.pallas_call(
        functools.partial(attend_back_kernel, shared),
        grid=(pairs, windows),
        in_specs=[
            column_spec(rows, q[1]),
            column_spec(keys, k[1]),
            column_spec(keys, v[1]),
            bias_spec,
            column_spec(rows, do[1]),
        ],
        out_specs=out_specs,
        out_shape=out_shape,
        cost_estimate=pl.CostEstimate(
            flops=20 * windows * pairs * rows * keys * PAIR,
            bytes_accessed=windows * pairs * PAIR * 6 * (rows + keys),
            transcendentals=2 * windows * pairs * rows * keys,
        ),
        compiler_params=pltpu.CompilerParams(vmem_limit_bytes=32 * MIB),
    )(q[0], k[0], v[0], bias, do[0])


SPANS = ((FRAMES, FRAMES - 1), (2 * BH, 2 * FRAMES - 1 + 2 * BH - 1), (4 * BW, 2 * FRAMES - 1 + 4 * BH - 1 + 4 * BW - 1))
SPAN = sum(size for size, _ in SPANS)


def table_picks():
    picks = np.zeros((SPAN, SPAN, REL), np.float32)
    start = 0
    for size, middle in SPANS:
        for i in range(size):
            for j in range(size):
                picks[start + i, start + j, middle + i - j] = 1
        start += size
    return picks


def place_hot(frame, row, column):
    marks = []
    for (size, _), place in zip(SPANS, (frame, row, column)):
        marks.append(place[:, None] == jnp.arange(size)[None, :])
    return jnp.concatenate(marks, 1).astype(HIGH)


def places_of(member, within):
    cell = within % CELLS
    return (
        within // CELLS + 0 * member,
        member // 4 * BH + cell // BW,
        member % 4 * BW + cell % BW,
    )


def bias_of(table, hot_q, hot_k):
    exact = lax.Precision.HIGHEST
    blocks = jnp.einsum("hn,abn->hab", table, table_picks(), precision=exact)
    left = jnp.einsum("ia,hab->hib", hot_q, blocks, precision=exact)
    return jnp.einsum("hib,jb->hij", left, hot_k, precision=exact)


def bias_grad(grad, hot_q, hot_k):
    exact = lax.Precision.HIGHEST
    right = jnp.einsum("hij,jb->hib", grad, hot_k, precision=exact)
    blocks = jnp.einsum("ia,hib->hab", hot_q, right, precision=exact)
    return jnp.einsum("hab,abn->hn", blocks, table_picks(), precision=exact)


def ring_sums(rights, lefts):
    count = lax.axis_size("dp")
    if count != 16:
        done = [
            high(lax.psum_scatter(x, "dp", scatter_dimension=0, tiled=True)) for x in rights + lefts
        ]
        return done[: len(rights)], done[len(rights) :]
    chips = count // 2
    order = [0, 2, 4, 6, 7, 5, 3, 1]
    chip_at = jnp.array(order, jnp.int32)
    place_of = jnp.array([order.index(i) for i in range(chips)], jnp.int32)
    device = lax.axis_index("dp")
    core = device % 2
    place = place_of[device // 2]

    def hop(x, way):
        route = []
        for s in range(2):
            for i in range(chips):
                for c in range(2):
                    route.append((s * count + order[i] * 2 + c, s * count + order[(i + way) % chips] * 2 + c))
        return lax.ppermute(x, ("section", "dp"), route)

    def prepare(x):
        x = x.reshape(chips, 2, x.shape[0] // count, x.shape[1])
        mine = lax.dynamic_index_in_dim(x, core, 1, keepdims=False)
        other = swap(lax.dynamic_index_in_dim(x, 1 - core, 1, keepdims=False), 1)
        return mine, other

    def at(pair, spot):
        chip = chip_at[spot % chips]
        return sum(high(lax.dynamic_index_in_dim(x, chip, 0, keepdims=False)) for x in pair)

    ways = [(prepare(x), 1) for x in rights] + [(prepare(x), -1) for x in lefts]
    totals = [at(pair, place - way + chips) for pair, way in ways]
    for step in range(1, chips):
        totals = [
            high(hop(low(total), way)) + at(pair, place - way * (step + 1) + 2 * chips)
            for total, (pair, way) in zip(totals, ways)
        ]
    return totals[: len(rights)], totals[len(rights) :]


def per_device(
    block_input,
    conditioning,
    text_embed,
    text_keep,
    cotangent,
    self_input,
    self_output,
    cross_query,
    cross_memory,
    cross_output,
    up_weight,
    down_weight,
    modulation,
    modulation_bias,
    position_bias,
):
    section = lax.axis_index("section")
    device = lax.axis_index("dp")
    count = lax.axis_size("dp")
    member = device % MEMBERS
    clip = device // MEMBERS
    clips = count // MEMBERS
    micro = block_input.shape[0]
    tokens = micro * ROWS
    shard = D // count
    members = [list(range(c * MEMBERS, (c + 1) * MEMBERS)) for c in range(clips)]

    def chosen(first, second):
        return jnp.where(section == 1, second, first)

    cond_low = low(jax.nn.silu(high(conditioning)))
    cond_rows = lax.dynamic_slice_in_dim(cond_low, device * shard, shard, 2)
    sums = jnp.einsum("bck,kn->cbn", cond_rows, low(modulation[0]), preferred_element_type=HIGH)
    bit = clips // 2
    while bit:
        upper = clip // bit % 2 == 1
        halves = (sums[:bit], sums[bit:])
        sums = jnp.where(upper, halves[1], halves[0]) + swap(
            jnp.where(upper, halves[0], halves[1]), bit * MEMBERS
        )
        bit //= 2
    sums = sums[0]
    for bit in (1, 2, 4):
        sums = sums + swap(sums, bit)
    mods = (sums + modulation_bias[0]).reshape(micro, 6, 1, D)
    shift1, scale1, gate1, shift2, scale2, gate2 = [mods[:, i] for i in range(6)]

    def gathered(x):
        return lax.all_gather(low(x[0]), "dp", axis=0, tiled=True)

    w_in = gathered(self_input)
    w_query = gathered(cross_query)
    w_self_out = gathered(self_output)
    w_cross_out = gathered(cross_output)
    w_up = gathered(up_weight)
    w_down = gathered(down_weight)
    w_in_x = xor_blocks(w_in, 1, PAIR, member, 3)
    w_self_out_x = xor_blocks(w_self_out, 0, PAIR, member)

    keep = lax.dynamic_index_in_dim(text_keep, clip, 1, keepdims=False).astype(LOW)
    text = text_embed * keep[:, None, None]
    text = jnp.pad(text, ((0, 0), (0, TEXT_PAD - text.shape[1]), (0, 0)))
    real = jnp.arange(TEXT_PAD * MEMBERS) % TEXT_PAD < text_embed.shape[1]
    text_mask = jnp.where(real, 0.0, NEGATIVE).astype(HIGH).reshape(1, 1, -1)

    def collect(x):
        parts = jnp.stack([x] + [swap(x, k) for k in range(1, MEMBERS)])
        return parts[member ^ jnp.arange(MEMBERS)]

    text_all = jnp.swapaxes(collect(text), 0, 1).reshape(micro * MEMBERS * TEXT_PAD, D)
    w_memory = low(cross_memory[0]).reshape(shard, 2, MEMBERS, PAIR)
    w_memory = jnp.transpose(w_memory, (2, 0, 1, 3)).reshape(MEMBERS, shard, 2 * PAIR)
    w_memory = lax.all_to_all(jnp.tile(w_memory, (clips, 1, 1)), "dp", 0, 0, tiled=True)
    w_memory = w_memory.reshape(D, 2 * PAIR)
    memory = low(dot(text_all, w_memory)).reshape(micro, MEMBERS * TEXT_PAD, 2 * PAIR)
    memory = collect(memory).reshape(MEMBERS, micro, MEMBERS * TEXT_PAD, 2, PAIR)
    memory = jnp.transpose(memory, (1, 2, 3, 0, 4)).reshape(micro, MEMBERS * TEXT_PAD, 2 * D)

    within = jnp.arange(ROWS)
    mine, partner = places_of(member, within), places_of(member ^ 1, within)
    hot_q1 = place_hot(*mine)
    hot_k1 = jnp.concatenate([hot_q1, place_hot(*partner)])
    bias1 = bias_of(position_bias[0], hot_q1, hot_k1)
    spread = jnp.arange(MEMBERS * CELLS)
    frame_places = places_of(member ^ (spread // CELLS), spread % CELLS)
    hot0 = place_hot(*frame_places)
    own_table = lax.dynamic_slice_in_dim(position_bias[0], 2 * member, 2, 0)
    bias0 = bias_of(own_table, hot0, hot0)

    def heads_of_frames(x):
        width = x.shape[1] // MEMBERS
        parts = [x[:, k * width : (k + 1) * width] for k in range(MEMBERS)]
        parts = [parts[0]] + [swap(parts[k], k, (0,)) for k in range(1, MEMBERS)]
        parts = [part.reshape(micro * FRAMES, CELLS, width) for part in parts]
        return jnp.concatenate(parts, 1)

    def heads_back(x):
        width = x.shape[2]
        parts = [x[:, k * CELLS : (k + 1) * CELLS].reshape(tokens, width) for k in range(MEMBERS)]
        parts = [parts[0]] + [swap(parts[k], k, (0,)) for k in range(1, MEMBERS)]
        return jnp.concatenate(parts, 1)

    def forward(which, inputs):
        kept = {"x": inputs}
        hidden = low(layer_mod(inputs, shift1, scale1)).reshape(tokens, D)
        kept["hidden"] = hidden
        asked = low(dot(hidden, w_query)).reshape(micro, ROWS, D)
        kept["asked"] = asked
        if which == 0:
            joint = heads_of_frames(low(dot(hidden, w_in_x)))
            kept["joint"] = joint
            mixture = heads_back(attend((joint, 0), (joint, 1), (joint, 2), bias0, 2))
            w_out = w_self_out_x
        else:
            joint = low(dot(hidden, w_in)).reshape(micro, ROWS, 3 * D)
            pair = joint[:, :, D:]
            pair = jnp.concatenate([pair, swap(pair, 1, (1,))], 1)
            kept["joint"] = joint
            kept["pair"] = pair
            mixture = attend((joint, 0), (pair, 0), (pair, MEMBERS), bias1, HEADS).reshape(tokens, D)
            w_out = w_self_out
        mixture_text = attend((asked, 0), (memory, 0), (memory, MEMBERS), text_mask, HEADS)
        mixture_text = mixture_text.reshape(tokens, D)
        branch = (dot(mixture, w_out) + dot(mixture_text, w_cross_out)).reshape(micro, ROWS, D)
        middle = inputs + gate1 * branch
        second = low(layer_mod(middle, shift2, scale2)).reshape(tokens, D)
        upper = dot(second, w_up)
        active = low(jax.nn.gelu(upper))
        feed = dot(active, w_down).reshape(micro, ROWS, D)
        result = low(middle + gate2 * feed)
        kept.update(
            mixture=mixture,
            mixture_text=mixture_text,
            branch=branch,
            middle=middle,
            second=second,
            upper=upper,
            active=active,
            feed=feed,
        )
        return result, kept

    def back_feed(which, kept, grad_result):
        out = {}
        gate2_grad = jnp.sum(grad_result * kept["feed"], 1)
        feed_grad = low(gate2 * grad_result).reshape(tokens, D)
        active_grad = dot_right_t(feed_grad, w_down)
        upper_grad = low(jax.vjp(jax.nn.gelu, kept["upper"])[1](active_grad)[0])
        second_grad = dot_right_t(upper_grad, w_up).reshape(micro, ROWS, D)
        middle_norm, shift2_grad, scale2_grad = jax.vjp(layer_mod, kept["middle"], shift2, scale2)[1](second_grad)
        out["feed_grad"] = feed_grad
        out["upper_grad"] = upper_grad
        out["middle_grad"] = grad_result + middle_norm
        out["late"] = [shift2_grad[:, 0], scale2_grad[:, 0], gate2_grad]
        return out

    def back_attention(which, kept, out):
        middle_grad = out["middle_grad"]
        gate1_grad = jnp.sum(middle_grad * kept["branch"], 1)
        branch_grad = low(gate1 * middle_grad).reshape(tokens, D)
        out["branch_grad"] = branch_grad
        text_grad = low(dot_right_t(branch_grad, w_cross_out)).reshape(micro, ROWS, D)
        if which == 0:
            mixture_grad = heads_of_frames(low(dot_right_t(branch_grad, w_self_out_x)))
            joint = kept["joint"]
            dq, dk, dv, dbias = attend_back(
                (joint, 0), (joint, 1), (joint, 2), bias0, (mixture_grad, 0), 2
            )
            joint_grad = heads_back(jnp.concatenate([dq, dk, dv], 2))
            hidden_grad = dot_right_t(joint_grad, w_in_x)
            out["joint_grad"] = xor_blocks_back(joint_grad, 1, PAIR, member, 3)
            table = bias_grad(dbias, hot0, hot0)
            out["table"] = lax.dynamic_update_slice_in_dim(
                jnp.zeros((HEADS, REL), HIGH), table, 2 * member, 0
            )
            out["mixture"] = xor_blocks(kept["mixture"], 1, PAIR, member)
        else:
            mixture_grad = low(dot_right_t(branch_grad, w_self_out)).reshape(micro, ROWS, D)
            joint, pair = kept["joint"], kept["pair"]
            dq, dk, dv, dbias = attend_back(
                (joint, 0), (pair, 0), (pair, MEMBERS), bias1, (mixture_grad, 0), HEADS
            )
            pair_grad = jnp.concatenate([dk, dv], 2)
            arrived = swap(pair_grad[:, ROWS:], 1, (1,))
            own = low(high(pair_grad[:, :ROWS]) + high(arrived))
            joint_grad = jnp.concatenate([dq, own], 2).reshape(tokens, 3 * D)
            hidden_grad = dot_right_t(joint_grad, w_in)
            out["joint_grad"] = joint_grad
            out["table"] = bias_grad(dbias, hot_q1, hot_k1)
            out["mixture"] = kept["mixture"]
        dqt, dkt, dvt = attend_back(
            (kept["asked"], 0), (memory, 0), (memory, MEMBERS), text_mask, (text_grad, 0), HEADS
        )
        asked_grad = dqt.reshape(tokens, D)
        out["asked_grad"] = asked_grad
        out["memory_grad"] = jnp.concatenate([dkt, dvt], 2)
        hidden_grad = hidden_grad + dot_right_t(asked_grad, w_query)
        inputs_norm, shift1_grad, scale1_grad = jax.vjp(layer_mod, kept["x"], shift1, scale1)[1](
            hidden_grad.reshape(micro, ROWS, D)
        )
        out["mods"] = jnp.concatenate(
            [shift1_grad[:, 0], scale1_grad[:, 0], gate1_grad] + out["late"], 1
        )
        return low(middle_grad + inputs_norm)

    first_result, first_kept = forward(0, high(block_input))
    received = lax.ppermute(first_result, "section", [(0, 1)])
    second_result, second_kept = forward(1, high(received))
    second_out = back_feed(1, second_kept, high(cotangent))
    second_grad = back_attention(1, second_kept, second_out)
    returned = lax.ppermute(second_grad, "section", [(1, 0)])
    first_out = back_feed(0, first_kept, high(returned))

    def both(name):
        if name in first_out:
            return chosen(first_out[name], second_out[name])
        return chosen(first_kept[name], second_kept[name])

    def outer(left, right):
        return low(dot_left_t(left, right))

    grad_up = outer(both("second"), both("upper_grad"))
    grad_down = outer(both("active"), both("feed_grad"))
    (up_shard,), (down_shard,) = ring_sums([grad_up], [grad_down])

    first_grad = back_attention(0, first_kept, first_out)
    branch_grad = both("branch_grad")
    hidden = both("hidden")
    grad_self_out = outer(both("mixture"), branch_grad)
    grad_cross_out = outer(both("mixture_text"), branch_grad)
    grad_in = outer(hidden, both("joint_grad"))
    grad_query = outer(hidden, both("asked_grad"))
    (in_shard,), (out_shard, cross_shard, query_shard) = ring_sums(
        [grad_in], [grad_self_out, grad_cross_out, grad_query]
    )

    memory_grad = both("memory_grad").reshape(micro, MEMBERS * TEXT_PAD, 2, MEMBERS, PAIR)
    memory_grad = jnp.transpose(memory_grad, (3, 0, 1, 2, 4)).reshape(MEMBERS, -1, 2 * PAIR)
    memory_grad = lax.all_to_all(memory_grad, "dp", 0, 0, tiled=True, axis_index_groups=members)
    memory_grad = low(jnp.sum(high(memory_grad), 0))
    grad_memory = outer(text_all, memory_grad).reshape(count, shard, 2 * PAIR)
    grad_memory = lax.all_to_all(grad_memory, "dp", 0, 0, tiled=True)
    grad_memory = jnp.sum(high(grad_memory).reshape(clips, MEMBERS, shard, 2, PAIR), 0)
    memory_shard = jnp.transpose(grad_memory, (1, 2, 0, 3)).reshape(shard, 2 * D)

    mods_grad = both("mods").reshape(micro * 6 * D)
    table_grad = both("table").reshape(HEADS * REL)
    small = jnp.concatenate([mods_grad, table_grad])
    small = jnp.pad(small, (0, -small.shape[0] % 1024)).reshape(-1, 128)
    small = lax.all_gather(small, "dp", axis=0, tiled=False).reshape(count, -1)
    mods_all = small[:, : micro * 6 * D].reshape(count, micro, 6 * D)
    table_sum = jnp.sum(small[:, micro * 6 * D : micro * 6 * D + HEADS * REL], 0).reshape(HEADS, REL)
    conds = jnp.repeat(jnp.swapaxes(cond_rows, 0, 1), MEMBERS, axis=0)
    modul_shard = jnp.einsum(
        "nbk,nbc->kc", high(conds), mods_all, precision=lax.Precision.HIGHEST
    )
    bias_sum = jnp.sum(mods_all, (0, 1))

    outputs = chosen(first_result, second_result)
    input_grads = chosen(first_grad, second_grad)
    return tuple(
        x[None]
        for x in (
            outputs,
            input_grads,
            in_shard,
            out_shard,
            query_shard,
            memory_shard,
            cross_shard,
            up_shard,
            down_shard,
            modul_shard,
            bias_sum,
            table_sum,
        )
    )


def solution(mesh):
    weights = P("section", "dp", None)
    return jax.shard_map(
        per_device,
        mesh=mesh,
        in_specs=(
            P(None, "dp", None),
            P(),
            P(None, "dp", None),
            P(),
            P(None, "dp", None),
        )
        + (weights,) * 8
        + (P("section", None), P("section", None, None)),
        out_specs=(P("section", None, "dp", None),) * 2
        + (weights,) * 8
        + (P("section", None), P("section", None, None)),
        check_vma=False,
    )
```

time: 2590 us -> 1060 us (0.41)
  waiting for transfers between devices: 1020 us -> 322 us
  matrix products: 835 us -> 147 us
  other arithmetic: 344 us -> 103 us
  Pallas kernels: 0 us -> 136 us
  local copies, waits for them, and re-layouts: 215 us -> 108 us
  starting transfers between devices: 78.9 us -> 156 us
  blocking collectives: 61.2 us -> 22.5 us
  between operations: 21 us -> 57.4 us
    dot_general x117 -> x46, matrix products: 747 us -> 147 us  [the longest x12 55 us: dot_right_t(): lax.dot_general(left, right, (((1,), (1,)), ((), ())), preferred_element_...]
    reduce_scatter x8 -> x0, waiting for transfers between devices: 447 us -> none  [the longest x1 248 us: per_device(): lax.psum_scatter(totals[7], 'dp', scatter_dimension=0, tiled=True)]
    all_gather x8 -> x6, waiting for transfers between devices: 315 us -> 84.2 us  [gathered(): return lax.all_gather(low(x[0]), 'dp', axis=0, tiled=True)]
    select_n x91 -> x5, other arithmetic: 179 us -> 0.7 us  [the longest x1 0.67 us: per_device(): jnp.where(upper, halves[0], halves[1])]
    pallas_call x0 -> x8, Pallas kernels: none -> 136 us  [the longest x4 84.1 us: attend_back(): pl.pallas_call(functools.partial(attend_back_kernel, shared), grid=(pairs...]
    sub x9 -> x0, matrix products: 88.4 us -> none  [the longest x3 72.9 us: attend_back(): grad_soft - jnp.sum(softmaxed * grad_soft, axis=-1, keepdims=True)]
    sub x9 -> x0, other arithmetic: 84.7 us -> none  [the longest x6 84.3 us: attend(): exponent = jnp.exp(scores - highest)]
    ppermute x94 -> x98, starting transfers between devices: 76.8 us -> 144 us  [the longest x54 102 us: swap(): return lax.ppermute(x, ('section', 'dp'), route)]
  transfers between devices with their start and end apart: 110 -> 107, of which waited for: 40 -> 54; matrix products, arithmetic and copies ran while one was open for 45% -> 23% of each run, Pallas kernels for 0% -> 9%
where the time goes in v1:
time: 1060 us; the launch traced here: 1050 us
  waiting for transfers between devices  322 us (30%)
  starting transfers between devices  156 us (15%)
  matrix products  147 us (14%)
  Pallas kernels  136 us (13%)
  local copies, waits for them, and re-layouts  108 us (10%)
  other arithmetic  103 us (10%)
  between operations  57.4 us (5%)
  blocking collectives  22.5 us (2%)
    ppermute x42, waiting for transfers between devices, hop(): return lax.ppermute(x, ('section', 'dp'), route)  121 us
    ppermute x54, starting transfers between devices, swap(): return lax.ppermute(x, ('section', 'dp'), route)  102 us
    ppermute x54, waiting for transfers between devices, swap(): return lax.ppermute(x, ('section', 'dp'), route)  86.5 us
    all_gather x6, waiting for transfers between devices, gathered(): return lax.all_gather(low(x[0]), 'dp', axis=0, tiled=True)  84.2 us
    pallas_call x4, Pallas kernels, attend_back(): pl.pallas_call(functools.partial(attend_back_kernel, shared), grid=(pairs...  84.1 us
    unnamed x460, local copies, waits for them, and re-layouts  63.5 us
    convert_element_type x56, other arithmetic, low(): return v.astype(LOW)  62.6 us
    dot_general x12, matrix products, dot_right_t(): lax.dot_general(left, right, (((1,), (1,)), ((), ())), preferred_element_...  55 us
  transfers between devices with their start and end apart: 107, of which 54 were waited for; matrix products, arithmetic and copies ran while one was open for 23% of the time, Pallas kernels for 9%

profile of v1, /device:TPU:0, one launch (start us, length us, event | category | flops | bytes accessed | tf_op | source)
XLA Modules:
  0.0 1052.2 jit_solution(2920834315846345798)
XLA Ops:
  26.4 3.7 all-to-all-start
  93.4 3.8 collective-permute-done.2
  98.7 4.8 collective-permute-done.3
  117.4 5.2 collective-permute-done.30
  132.0 13.3 %shard_map.311 = bf16[2,160,1024]{2,1,0:T(8,128)(2,1)S(1)} custom-call(bf16[2,160,1024]{2,1,0:T(8,128)(2,1)S(1)} %bitcast.796, bf16[2,128,2048]{2,1,0:T(8,128)(2,1)S(1)} %reshape.1037.k_ref.v_ref, bf16[2,128,2048]{2,1,0:T(8,128)(2,1)S(1)} %reshape.1037.k_ref.v_ref, f32[1,1,128]{2,1,0:T(1,128)S(1)} %compare_select_fusion.1.bias_ref), custom_call_target="tpu_custom_call" | custom-call | flops 335544320 | bytes 2359296 | tf_op jit(solution)/shard_map/pallas_call | solution.py:151
  156.4 3.6 fusion.55
  160.0 52.7 %all-gather.13.cloned.1.call-done = bf16[1,1024,3072]{2,1,0:T(8,128)(2,1)} async-done(((bf16[1,64,3072]{2,1,0:T(8,128)(2,1)}), bf16[1,1024,3072]{2,1,0:T(8,128)(2,1)}) %all-gather.13.cloned.1.call-update) | async-done | bytes 6291472 | tf_op jit(solution)/shard_map/all_gather | solution.py:345
  243.4 3.4 collective-permute-start.7
  249.2 3.4 collective-permute-start.9
  255.7 11.3 %collective-permute-done.7 = bf16[320,384]{1,0:T(8,128)(2,1)S(1)} collective-permute-done((bf16[320,384]{1,0:T(8,128)(2,1)S(1)}, bf16[320,384]{1,0:T(8,128)(2,1)S(1)}, u32[]{:S(2)}, u32[]{:S(2)}) %collective-permute-start.7) | collective-permute-done | bytes 245792 | tf_op jit(solution)/shard_map/ppermute | solution.py:61
  267.1 12.0 %collective-permute-done.8 = bf16[320,384]{1,0:T(8,128)(2,1)S(1)} collective-permute-done((bf16[320,384]{1,0:T(8,128)(2,1)S(1)}, bf16[320,384]{1,0:T(8,128)(2,1)S(1)}, u32[]{:S(2)}, u32[]{:S(2)}) %collective-permute-start.8) | collective-permute-done | bytes 245792 | tf_op jit(solution)/shard_map/ppermute | solution.py:61
  279.1 14.5 %collective-permute-done.9 = bf16[320,384]{1,0:T(8,128)(2,1)S(1)} collective-permute-done((bf16[320,384]{1,0:T(8,128)(2,1)S(1)}, bf16[320,384]{1,0:T(8,128)(2,1)S(1)}, u32[]{:S(2)}, u32[]{:S(2)}) %collective-permute-start.9) | collective-permute-done | bytes 245792 | tf_op jit(solution)/shard_map/ppermute | solution.py:61
  293.6 9.3 collective-permute-done.10
  302.9 9.7 shard_map.310
  314.9 3.4 collective-permute-start.12
  322.4 3.7 collective-permute-start.15
  336.0 4.0 collective-permute-done.16
  346.8 8.4 fusion.14
  355.2 31.4 %all-gather.23.cloned.1.call-done = bf16[1,4096,1024]{2,1,0:T(8,128)(2,1)} async-done(((bf16[1,256,1024]{2,1,0:T(8,128)(2,1)}), bf16[1,4096,1024]{2,1,0:T(8,128)(2,1)}) %all-gather.23.cloned.1.call-update) | async-done | bytes 8388624 | tf_op jit(solution)/shard_map/all_gather | solution.py:345
  386.6 8.4 fusion.6
  396.1 3.7 collective-permute-start.32
  402.0 12.1 %collective-permute-done.32 = bf16[2,160,1024]{2,1,0:T(8,128)(2,1)S(1)} collective-permute-done((bf16[2,160,1024]{2,1,0:T(8,128)(2,1)S(1)}, bf16[2,160,1024]{2,1,0:T(8,128)(2,1)S(1)}, u32[]{:S(2)}, u32[]{:S(2)}) %collective-permute-start.32) | collective-permute-done | bytes 655392 | tf_op jit(solution)/shard_map/ppermute | solution.py:503
  419.8 13.5 %shard_map.313 = bf16[2,160,1024]{2,1,0:T(8,128)(2,1)S(1)} custom-call(bf16[2,160,1024]{2,1,0:T(8,128)(2,1)S(1)} %bitcast.798, bf16[2,128,2048]{2,1,0:T(8,128)(2,1)S(1)} %reshape.1037.k_ref.v_ref, bf16[2,128,2048]{2,1,0:T(8,128)(2,1)S(1)} %reshape.1037.k_ref.v_ref, f32[1,1,128]{2,1,0:T(1,128)S(1)} %compare_select_fusion.1.bias_ref), custom_call_target="tpu_custom_call" | custom-call | flops 335544320 | bytes 2359296 | tf_op jit(solution)/shard_map/pallas_call | solution.py:151
  434.6 15.3 %shard_map.312 = bf16[2,160,1024]{2,1,0:T(8,128)(2,1)S(1)} custom-call(bf16[2,160,3072]{2,1,0:T(8,128)(2,1)S(1)} %bitcast.793, bf16[2,320,2048]{2,1,0:T(8,128)(2,1)S(1)} %pad_maximum_fusion.k_ref.v_ref, bf16[2,320,2048]{2,1,0:T(8,128)(2,1)S(1)} %pad_maximum_fusion.k_ref.v_ref, f32[16,160,320]{2,1,0:T(8,128)S(1)} %fusion.256.bias_ref), custom_call_target="tpu_custom_call" | custom-call | flops 838860800 | bytes 3932160 | tf_op jit(solution)/shard_map/pallas_call | solution.py:151
  453.2 4.6 fusion.12
  457.8 13.1 %fusion.33 = bf16[320,4096]{1,0:T(8,128)(2,1)} fusion(f32[320,4096]{1,0:T(8,128)} %fusion.12, bf16[320,1024]{1,0:T(8,128)(2,1)S(1)} %bitcast.914, bf16[1,4096,1024]{2,1,0:T(8,128)(2,1)} %all-gather.23.cloned.1.call-done), kind=kOutput, calls=%fused_computation.44 | convolution fusion | flops 2710568960 | bytes 16908288 | tf_op jit(solution)/shard_map/dot_general | solution.py:36
  470.9 4.6 fusion.10
  479.0 29.6 %shard_map.314 = (bf16[2,160,1024]{2,1,0:T(8,128)(2,1)S(1)}, bf16[2,320,1024]{2,1,0:T(8,128)(2,1)S(1)}, bf16[2,320,1024]{2,1,0:T(8,128)(2,1)S(1)}, f32[16,160,320]{2,1,0:T(8,128)S(1)}) custom-call(bf16[2,160,3072]{2,1,0:T(8,128)(2,1)S(1)} %bitcast.794, bf16[2,320,2048]{2,1,0:T(8,128)(2,1)S(1)} %pad_maximum_fusion.k_ref.v_ref, ...), custom_call_target="tpu_custom_call" | custom-call | flops 2097152000 | bytes 5898240 | tf_op jit(solution)/shard_map/pallas_call | solution.py:187
  512.8 18.7 %shard_map.315 = (bf16[2,160,1024]{2,1,0:T(8,128)(2,1)S(1)}, bf16[2,128,1024]{2,1,0:T(8,128)(2,1)S(1)}, bf16[2,128,1024]{2,1,0:T(8,128)(2,1)S(1)}) custom-call(bf16[2,160,1024]{2,1,0:T(8,128)(2,1)S(1)} %bitcast.799, bf16[2,128,2048]{2,1,0:T(8,128)(2,1)S(1)} %reshape.1037.k_ref.v_ref, bf16[2,128,2048]{2,1,0:T(8,128)(2,1)S(1)} %reshape.1037.k_ref.v_ref, ...), custom_call_target="tpu_custom_call" | custom-call | flops 838860800 | bytes 3538944 | tf_op jit(solution)/shard_map/pallas_call | solution.py:187
  542.6 8.4 fusion.4
  563.8 18.8 %collective-permute-done.35 = bf16[2,160,1024]{2,1,0:T(8,128)(2,1)S(1)} collective-permute-done((bf16[2,160,1024]{2,1,0:T(8,128)(2,1)S(1)}, bf16[2,160,1024]{2,1,0:T(8,128)(2,1)S(1)}, u32[]{:S(2)}, u32[]{:S(2)}) %collective-permute-start.35) | collective-permute-done | bytes 655392 | tf_op jit(solution)/shard_map/ppermute | solution.py:507
  582.7 9.5 convolution_convert_fusion
  592.3 10.7 %fusion.26 = bf16[320,4096]{1,0:T(8,128)(2,1)} fusion(f32[320,4096]{1,0:T(8,128)} %fusion.14, bf16[320,1024]{1,0:T(8,128)(2,1)S(1)} %bitcast.919, bf16[1,4096,1024]{2,1,0:T(8,128)(2,1)S(1)} %bitcast.1012), kind=kOutput, calls=%fused_computation.37 | convolution fusion | flops 2710568960 | bytes 16908288 | tf_op jit(solution)/shard_map/dot_general | solution.py:36
  603.0 6.5 convolution_convert_fusion.1
  609.6 9.6 fusion.8
  643.4 18.3 %shard_map.317 = (bf16[2,160,1024]{2,1,0:T(8,128)(2,1)S(1)}, bf16[2,128,1024]{2,1,0:T(8,128)(2,1)S(1)}, bf16[2,128,1024]{2,1,0:T(8,128)(2,1)S(1)}) custom-call(bf16[2,160,1024]{2,1,0:T(8,128)(2,1)S(1)} %bitcast.797, bf16[2,128,2048]{2,1,0:T(8,128)(2,1)S(1)} %reshape.1037.k_ref.v_ref, bf16[2,128,2048]{2,1,0:T(8,128)(2,1)S(1)} %reshape.1037.k_ref.v_ref, ...), custom_call_target="tpu_custom_call" | custom-call | flops 838860800 | bytes 3538944 | tf_op jit(solution)/shard_map/pallas_call | solution.py:187
  669.8 5.3 fusion.116
  677.7 4.4 all-to-all-start.1
  693.0 4.8 collective-permute-start.41
  706.3 17.5 %shard_map.316 = (bf16[10,256,128]{2,1,0:T(8,128)(2,1)S(1)}, bf16[10,256,128]{2,1,0:T(8,128)(2,1)S(1)}, bf16[10,256,128]{2,1,0:T(8,128)(2,1)S(1)}, f32[2,256,256]{2,1,0:T(8,128)S(1)}) custom-call(bf16[10,256,384]{2,1,0:T(8,128)(2,1)S(1)} %copy-done.3, bf16[10,256,384]{2,1,0:T(8,128)(2,1)S(1)} %copy-done.3, bf16[10,256,384]{2,1,0:T(8,128)(2,1)S(1)} %copy-done.3, ...), custom_call_target="tpu_custom_call" | custom-call | flops 1677721600 | bytes 3932160 | tf_op jit(solution)/shard_map/pallas_call | solution.py:187
  743.3 3.6 collective-permute-start.48
  753.3 4.3 collective-permute-done.48
  758.4 3.8 collective-permute-done.49
  763.1 6.0 convolution_add_fusion.1
  770.6 22.5 %all_gather.27 = f32[16,112,128]{2,1,0:T(8,128)S(1)} all-gather(f32[1,112,128]{2,1,0:T(8,128)S(1)} %fusion.228), channel_id=1, replica_groups=mesh['section'=2,'dp'=16] {'dp'}, dimensions={0}, use_global_device_ids=true | all-gather | bytes 974848 | tf_op jit(solution)/shard_map/all_gather | solution.py:546
  798.4 6.0 bitcast_convert_fusion
  810.7 3.9 dynamic-slice_bitcast_fusion.2
  818.0 4.2 collective-permute-done.75
  868.0 4.2 all-to-all-start.2
  877.6 9.3 collective-permute-done.64
  910.8 5.2 collective-permute-done.51
  921.1 6.1 collective-permute-done.83
  930.8 4.9 collective-permute-done.52
  940.6 6.3 collective-permute-done.84
  950.4 4.9 collective-permute-done.53
  960.2 6.3 collective-permute-done.85
  970.1 4.9 collective-permute-done.54
  979.9 6.3 collective-permute-done.86
  989.7 4.9 collective-permute-done.55
  999.6 6.3 collective-permute-done.87
  1009.4 4.9 collective-permute-done.56
  1019.2 6.3 collective-permute-done.88
  1029.1 4.9 collective-permute-done.57
  1038.5 3.9 collective-permute-done.89
  (867 shorter events, 411.8 us)
Async XLA Ops:
  7.2 122.3 %all-gather.17.cloned.1.call-start = ((), (), s32[]{:S(2)}) async-start(), calls=%async_computation.5 | async-start | bytes 2228224 | tf_op jit(solution)/shard_map/all_gather | solution.py:345
  9.0 137.2 %all-gather.15.cloned.1.call-start = ((), (), s32[]{:S(2)}) async-start(), calls=%async_computation.4 | async-start | bytes 2228224 | tf_op jit(solution)/shard_map/all_gather | solution.py:345
  10.8 145.6 %all-gather.19.cloned.1.call-start = ((), (), s32[]{:S(2)}) async-start(), calls=%async_computation.6 | async-start | bytes 2228224 | tf_op jit(solution)/shard_map/all_gather | solution.py:345
  12.5 200.2 %all-gather.13.cloned.1.call-start = ((), (), s32[]{:S(2)}) async-start(), calls=%async_computation.3 | async-start | bytes 6684672 | tf_op jit(solution)/shard_map/all_gather | solution.py:345
  13.3 332.6 %all-gather.21.cloned.1.call-start = ((), (), s32[]{:S(2)}) async-start(), calls=%async_computation.7 | async-start | bytes 8912896 | tf_op jit(solution)/shard_map/all_gather | solution.py:345
  15.3 69.5 %collective-permute-start.18 = (bf16[2,16,1024]{2,0,1:T(2,128)(2,1)}, bf16[2,16,1024]{2,0,1:T(2,128)(2,1)}, u32[]{:S(2)}, u32[]{:S(2)}) collective-permute-start(bf16[2,16,1024]{2,0,1:T(2,128)(2,1)} %pad.8), channel_id=1, source_target_pairs={{0,1},{1,0},{2,3},{3,2},{4,5},{5,4},{6,7},{7,6},{8,9},{9,8},{10,11... | collective-permute-start | bytes 196616 | tf_op jit(solution)/shard_map/ppermute | solution.py:61
  15.7 71.5 %collective-permute-start.19 = (bf16[2,16,1024]{2,0,1:T(2,128)(2,1)}, bf16[2,16,1024]{2,0,1:T(2,128)(2,1)}, u32[]{:S(2)}, u32[]{:S(2)}) collective-permute-start(bf16[2,16,1024]{2,0,1:T(2,128)(2,1)} %pad.8), channel_id=1, source_target_pairs={{0,2},{1,3},{2,0},{3,1},{4,6},{5,7},{6,4},{7,5},{8,10},{9,11},{10,... | collective-permute-start | bytes 196616 | tf_op jit(solution)/shard_map/ppermute | solution.py:61
  18.2 71.1 %collective-permute-start.20 = (bf16[2,16,1024]{2,0,1:T(2,128)(2,1)}, bf16[2,16,1024]{2,0,1:T(2,128)(2,1)}, u32[]{:S(2)}, u32[]{:S(2)}) collective-permute-start(bf16[2,16,1024]{2,0,1:T(2,128)(2,1)} %pad.8), channel_id=1, source_target_pairs={{0,3},{1,2},{2,1},{3,0},{4,7},{5,6},{6,5},{7,4},{8,11},{9,10},{10,... | collective-permute-start | bytes 196616 | tf_op jit(solution)/shard_map/ppermute | solution.py:61
  18.4 72.4 %collective-permute-start.21 = (bf16[2,16,1024]{2,0,1:T(2,128)(2,1)}, bf16[2,16,1024]{2,0,1:T(2,128)(2,1)}, u32[]{:S(2)}, u32[]{:S(2)}) collective-permute-start(bf16[2,16,1024]{2,0,1:T(2,128)(2,1)} %pad.8), channel_id=1, source_target_pairs={{0,4},{1,5},{2,6},{3,7},{4,0},{5,1},{6,2},{7,3},{8,12},{9,13},{10,... | collective-permute-start | bytes 196616 | tf_op jit(solution)/shard_map/ppermute | solution.py:61
  21.4 60.8 %collective-permute-start = (f32[1,2,6144]{2,0,1:T(1,128)}, f32[1,2,6144]{2,0,1:T(1,128)}, u32[]{:S(2)}, u32[]{:S(2)}) collective-permute-start(f32[1,2,6144]{2,0,1:T(1,128)} %broadcast_select_fusion.7), channel_id=1, source_target_pairs={{0,8},{1,9},{2,10},{3,11},{4,12},{5,13},{6,14},{7,15},{8,0},{9,1},... | collective-permute-start | bytes 147464 | tf_op jit(solution)/shard_map/ppermute | solution.py:61
  26.4 77.8 %all-to-all-start = ((bf16[16,64,256]{2,1,0:T(8,128)(2,1)}), bf16[16,64,256]{2,1,0:T(8,128)(2,1)S(1)}, u32[]{:S(2)}, u32[]{:S(2)}) async-start(bf16[16,64,256]{2,1,0:T(8,128)(2,1)} %bitcast.71), calls=%async_computation | async-start | bytes 1048576 | tf_op jit(solution)/shard_map/all_to_all | solution.py:369
  30.1 356.5 %all-gather.23.cloned.1.call-start = ((), (), s32[]{:S(2)}) async-start(), calls=%async_computation.8 | async-start | bytes 8912896 | tf_op jit(solution)/shard_map/all_gather | solution.py:345
  232.4 16.7 %collective-permute-start.4 = (bf16[320,384]{1,0:T(8,128)(2,1)S(1)}, bf16[320,384]{1,0:T(8,128)(2,1)S(1)}, u32[]{:S(2)}, u32[]{:S(2)}) collective-permute-start(bf16[320,384]{1,0:T(8,128)(2,1)S(1)} %get-tuple-element.104), channel_id=1, source_target_pairs={{0,1},{1,0},{2,3},{3,2},{4,5},{5,4},{6,7},{7,6},{8,9},{9,8},{10,11... | collective-permute-start | bytes 737288 | tf_op jit(solution)/shard_map/ppermute | solution.py:61
  236.3 16.3 %collective-permute-start.5 = (bf16[320,384]{1,0:T(8,128)(2,1)S(1)}, bf16[320,384]{1,0:T(8,128)(2,1)S(1)}, u32[]{:S(2)}, u32[]{:S(2)}) collective-permute-start(bf16[320,384]{1,0:T(8,128)(2,1)S(1)} %get-tuple-element.103), channel_id=1, source_target_pairs={{0,2},{1,3},{2,0},{3,1},{4,6},{5,7},{6,4},{7,5},{8,10},{9,11},{10,... | collective-permute-start | bytes 737288 | tf_op jit(solution)/shard_map/ppermute | solution.py:61
  240.5 15.2 %collective-permute-start.6 = (bf16[320,384]{1,0:T(8,128)(2,1)S(1)}, bf16[320,384]{1,0:T(8,128)(2,1)S(1)}, u32[]{:S(2)}, u32[]{:S(2)}) collective-permute-start(bf16[320,384]{1,0:T(8,128)(2,1)S(1)} %get-tuple-element.102), channel_id=1, source_target_pairs={{0,3},{1,2},{2,1},{3,0},{4,7},{5,6},{6,5},{7,4},{8,11},{9,10},{10,... | collective-permute-start | bytes 737288 | tf_op jit(solution)/shard_map/ppermute | solution.py:61
  243.4 23.6 %collective-permute-start.7 = (bf16[320,384]{1,0:T(8,128)(2,1)S(1)}, bf16[320,384]{1,0:T(8,128)(2,1)S(1)}, u32[]{:S(2)}, u32[]{:S(2)}) collective-permute-start(bf16[320,384]{1,0:T(8,128)(2,1)S(1)} %get-tuple-element.101), channel_id=1, source_target_pairs={{0,4},{1,5},{2,6},{3,7},{4,0},{5,1},{6,2},{7,3},{8,12},{9,13},{10,... | collective-permute-start | bytes 737288 | tf_op jit(solution)/shard_map/ppermute | solution.py:61
  246.8 32.3 %collective-permute-start.8 = (bf16[320,384]{1,0:T(8,128)(2,1)S(1)}, bf16[320,384]{1,0:T(8,128)(2,1)S(1)}, u32[]{:S(2)}, u32[]{:S(2)}) collective-permute-start(bf16[320,384]{1,0:T(8,128)(2,1)S(1)} %get-tuple-element.100), channel_id=1, source_target_pairs={{0,5},{1,4},{2,7},{3,6},{4,1},{5,0},{6,3},{7,2},{8,13},{9,12},{10,... | collective-permute-start | bytes 737288 | tf_op jit(solution)/shard_map/ppermute | solution.py:61
  249.2 44.4 %collective-permute-start.9 = (bf16[320,384]{1,0:T(8,128)(2,1)S(1)}, bf16[320,384]{1,0:T(8,128)(2,1)S(1)}, u32[]{:S(2)}, u32[]{:S(2)}) collective-permute-start(bf16[320,384]{1,0:T(8,128)(2,1)S(1)} %get-tuple-element.99), channel_id=1, source_target_pairs={{0,6},{1,7},{2,4},{3,5},{4,2},{5,3},{6,0},{7,1},{8,14},{9,15},{10,... | collective-permute-start | bytes 737288 | tf_op jit(solution)/shard_map/ppermute | solution.py:61
  252.6 50.3 %collective-permute-start.10 = (bf16[320,384]{1,0:T(8,128)(2,1)S(1)}, bf16[320,384]{1,0:T(8,128)(2,1)S(1)}, u32[]{:S(2)}, u32[]{:S(2)}) collective-permute-start(bf16[320,384]{1,0:T(8,128)(2,1)S(1)} %get-tuple-element.98), channel_id=1, source_target_pairs={{0,7},{1,6},{2,5},{3,4},{4,3},{5,2},{6,1},{7,0},{8,15},{9,14},{10,... | collective-permute-start | bytes 737288 | tf_op jit(solution)/shard_map/ppermute | solution.py:61
  312.7 13.4 %collective-permute-start.11 = (bf16[320,128]{1,0:T(8,128)(2,1)S(1)}, bf16[320,128]{1,0:T(8,128)(2,1)S(1)}, u32[]{:S(2)}, u32[]{:S(2)}) collective-permute-start(bf16[320,128]{1,0:T(8,128)(2,1)S(1)} %bitcast.1003), channel_id=1, source_target_pairs={{0,1},{1,0},{2,3},{3,2},{4,5},{5,4},{6,7},{7,6},{8,9},{9,8},{10,11... | collective-permute-start | bytes 245768 | tf_op jit(solution)/shard_map/ppermute | solution.py:61
  314.9 14.4 %collective-permute-start.12 = (bf16[320,128]{1,0:T(8,128)(2,1)S(1)}, bf16[320,128]{1,0:T(8,128)(2,1)S(1)}, u32[]{:S(2)}, u32[]{:S(2)}) collective-permute-start(bf16[320,128]{1,0:T(8,128)(2,1)S(1)} %bitcast.1002), channel_id=1, source_target_pairs={{0,2},{1,3},{2,0},{3,1},{4,6},{5,7},{6,4},{7,5},{8,10},{9,11},{10,... | collective-permute-start | bytes 245768 | tf_op jit(solution)/shard_map/ppermute | solution.py:61
  318.3 14.3 %collective-permute-start.13 = (bf16[320,128]{1,0:T(8,128)(2,1)S(1)}, bf16[320,128]{1,0:T(8,128)(2,1)S(1)}, u32[]{:S(2)}, u32[]{:S(2)}) collective-permute-start(bf16[320,128]{1,0:T(8,128)(2,1)S(1)} %bitcast.1001), channel_id=1, source_target_pairs={{0,3},{1,2},{2,1},{3,0},{4,7},{5,6},{6,5},{7,4},{8,11},{9,10},{10,... | collective-permute-start | bytes 245768 | tf_op jit(solution)/shard_map/ppermute | solution.py:61
  322.4 13.6 %collective-permute-start.15 = (bf16[320,128]{1,0:T(8,128)(2,1)S(1)}, bf16[320,128]{1,0:T(8,128)(2,1)S(1)}, u32[]{:S(2)}, u32[]{:S(2)}) collective-permute-start(bf16[320,128]{1,0:T(8,128)(2,1)S(1)} %bitcast.999), channel_id=1, source_target_pairs={{0,5},{1,4},{2,7},{3,6},{4,1},{5,0},{6,3},{7,2},{8,13},{9,12},{10,... | collective-permute-start | bytes 245768 | tf_op jit(solution)/shard_map/ppermute | solution.py:61
  326.1 13.9 %collective-permute-start.16 = (bf16[320,128]{1,0:T(8,128)(2,1)S(1)}, bf16[320,128]{1,0:T(8,128)(2,1)S(1)}, u32[]{:S(2)}, u32[]{:S(2)}) collective-permute-start(bf16[320,128]{1,0:T(8,128)(2,1)S(1)} %bitcast.998), channel_id=1, source_target_pairs={{0,6},{1,7},{2,4},{3,5},{4,2},{5,3},{6,0},{7,1},{8,14},{9,15},{10,... | collective-permute-start | bytes 245768 | tf_op jit(solution)/shard_map/ppermute | solution.py:61
  396.1 18.0 %collective-permute-start.32 = (bf16[2,160,1024]{2,1,0:T(8,128)(2,1)S(1)}, bf16[2,160,1024]{2,1,0:T(8,128)(2,1)S(1)}, u32[]{:S(2)}, u32[]{:S(2)}) collective-permute-start(bf16[2,160,1024]{2,1,0:T(8,128)(2,1)S(1)} %get-tuple-element.139), channel_id=1, source_target_pairs={{0,16},{1,17},{2,18},{3,19},{4,20},{5,21},{6,22},{7,23},{8,24},{9,... | collective-permute-start | bytes 1966088 | tf_op jit(solution)/shard_map/ppermute | solution.py:503
  417.5 16.8 %collective-permute-start.33 = (bf16[2,160,2048]{2,1,0:T(8,128)(2,1)S(1)}, bf16[2,160,2048]{2,1,0:T(8,128)(2,1)S(1)}, u32[]{:S(2)}, u32[]{:S(2)}) collective-permute-start(bf16[2,160,2048]{2,1,0:T(8,128)(2,1)S(1)} %slice.208), channel_id=1, source_target_pairs={{16,17},{17,16},{18,19},{19,18},{20,21},{21,20},{22,23},{23,22},{2... | collective-permute-start | bytes 3932168 | tf_op jit(solution)/shard_map/ppermute | solution.py:61
  510.1 43.9 %collective-permute-start.34 = (bf16[2,160,2048]{2,1,0:T(8,128)(2,1)}, bf16[2,160,2048]{2,1,0:T(8,128)(2,1)}, u32[]{:S(2)}, u32[]{:S(2)}) collective-permute-start(bf16[2,160,2048]{2,1,0:T(8,128)(2,1)} %slice.210), channel_id=1, source_target_pairs={{16,17},{17,16},{18,19},{19,18},{20,21},{21,20},{22,23},{23,22},{2... | collective-permute-start | bytes 3932168 | tf_op jit(solution)/shard_map/ppermute | solution.py:61
  562.2 20.3 %collective-permute-start.35 = (bf16[2,160,1024]{2,1,0:T(8,128)(2,1)S(1)}, bf16[2,160,1024]{2,1,0:T(8,128)(2,1)S(1)}, u32[]{:S(2)}, u32[]{:S(2)}) collective-permute-start(bf16[2,160,1024]{2,1,0:T(8,128)(2,1)S(1)} %get-tuple-element.65), channel_id=1, source_target_pairs={{16,0},{17,1},{18,2},{19,3},{20,4},{21,5},{22,6},{23,7},{24,8},{25... | collective-permute-start | bytes 1966088 | tf_op jit(solution)/shard_map/ppermute | solution.py:507
  629.3 63.7 %collective-permute-start.36 = (bf16[320,128]{1,0:T(8,128)(2,1)}, bf16[320,128]{1,0:T(8,128)(2,1)}, u32[]{:S(2)}, u32[]{:S(2)}) collective-permute-start(bf16[320,128]{1,0:T(8,128)(2,1)} %get-tuple-element.122), channel_id=1, source_target_pairs={{0,1},{1,0},{2,3},{3,2},{4,5},{5,4},{6,7},{7,6},{8,9},{9,8},{10,11... | collective-permute-start | bytes 245768 | tf_op jit(solution)/shard_map/ppermute | solution.py:61
  631.2 67.5 %collective-permute-start.37 = (bf16[320,128]{1,0:T(8,128)(2,1)}, bf16[320,128]{1,0:T(8,128)(2,1)}, u32[]{:S(2)}, u32[]{:S(2)}) collective-permute-start(bf16[320,128]{1,0:T(8,128)(2,1)} %get-tuple-element.121), channel_id=1, source_target_pairs={{0,2},{1,3},{2,0},{3,1},{4,6},{5,7},{6,4},{7,5},{8,10},{9,11},{10,... | collective-permute-start | bytes 245768 | tf_op jit(solution)/shard_map/ppermute | solution.py:61
  633.7 67.9 %collective-permute-start.38 = (bf16[320,128]{1,0:T(8,128)(2,1)}, bf16[320,128]{1,0:T(8,128)(2,1)}, u32[]{:S(2)}, u32[]{:S(2)}) collective-permute-start(bf16[320,128]{1,0:T(8,128)(2,1)} %get-tuple-element.120), channel_id=1, source_target_pairs={{0,3},{1,2},{2,1},{3,0},{4,7},{5,6},{6,5},{7,4},{8,11},{9,10},{10,... | collective-permute-start | bytes 245768 | tf_op jit(solution)/shard_map/ppermute | solution.py:61
  636.9 65.8 %collective-permute-start.39 = (bf16[320,128]{1,0:T(8,128)(2,1)}, bf16[320,128]{1,0:T(8,128)(2,1)}, u32[]{:S(2)}, u32[]{:S(2)}) collective-permute-start(bf16[320,128]{1,0:T(8,128)(2,1)} %get-tuple-element.119), channel_id=1, source_target_pairs={{0,4},{1,5},{2,6},{3,7},{4,0},{5,1},{6,2},{7,3},{8,12},{9,13},{10,... | collective-permute-start | bytes 245768 | tf_op jit(solution)/shard_map/ppermute | solution.py:61
  639.7 64.4 %collective-permute-start.40 = (bf16[320,128]{1,0:T(8,128)(2,1)}, bf16[320,128]{1,0:T(8,128)(2,1)}, u32[]{:S(2)}, u32[]{:S(2)}) collective-permute-start(bf16[320,128]{1,0:T(8,128)(2,1)} %get-tuple-element.118), channel_id=1, source_target_pairs={{0,5},{1,4},{2,7},{3,6},{4,1},{5,0},{6,3},{7,2},{8,13},{9,12},{10,... | collective-permute-start | bytes 245768 | tf_op jit(solution)/shard_map/ppermute | solution.py:61
  677.7 187.7 %all-to-all-start.1 = ((bf16[8,256,256]{2,1,0:T(8,128)(2,1)}), bf16[8,256,256]{2,1,0:T(8,128)(2,1)}, u32[]{:S(2)}, u32[]{:S(2)}) async-start(bf16[8,256,256]{2,1,0:T(8,128)(2,1)} %reshape.1083), calls=%async_computation.1 | async-start | bytes 2097152 | tf_op jit(solution)/shard_map/all_to_all | solution.py:535
  701.6 204.4 %collective-permute-start.90 = (bf16[8,256,1024]{2,1,0:T(8,128)(2,1)}, bf16[8,256,1024]{2,1,0:T(8,128)(2,1)}, u32[]{:S(2)}, u32[]{:S(2)}) collective-permute-start(bf16[8,256,1024]{2,1,0:T(8,128)(2,1)} %dynamic-slice_bitcast_fusion), channel_id=1, source_target_pairs={{0,1},{1,0},{2,3},{3,2},{4,5},{5,4},{6,7},{7,6},{8,9},{9,8},{10,11... | collective-permute-start | bytes 12582920 | tf_op jit(solution)/shard_map/ppermute | solution.py:61
  702.7 204.7 %collective-permute-start.82 = (bf16[8,64,4096]{2,1,0:T(8,128)(2,1)}, bf16[8,64,4096]{2,1,0:T(8,128)(2,1)}, u32[]{:S(2)}, u32[]{:S(2)}) collective-permute-start(bf16[8,64,4096]{2,1,0:T(8,128)(2,1)} %dynamic-slice_bitcast_fusion.1), channel_id=1, source_target_pairs={{0,1},{1,0},{2,3},{3,2},{4,5},{5,4},{6,7},{7,6},{8,9},{9,8},{10,11... | collective-permute-start | bytes 12582920 | tf_op jit(solution)/shard_map/ppermute | solution.py:61
  743.3 14.3 %collective-permute-start.48 = (bf16[320,384]{1,0:T(8,128)(2,1)S(1)}, bf16[320,384]{1,0:T(8,128)(2,1)S(1)}, u32[]{:S(2)}, u32[]{:S(2)}) collective-permute-start(bf16[320,384]{1,0:T(8,128)(2,1)S(1)} %bitcast.986), channel_id=1, source_target_pairs={{0,6},{1,7},{2,4},{3,5},{4,2},{5,3},{6,0},{7,1},{8,14},{9,15},{10,... | collective-permute-start | bytes 737288 | tf_op jit(solution)/shard_map/ppermute | solution.py:61
  747.6 14.6 %collective-permute-start.49 = (bf16[320,384]{1,0:T(8,128)(2,1)S(1)}, bf16[320,384]{1,0:T(8,128)(2,1)S(1)}, u32[]{:S(2)}, u32[]{:S(2)}) collective-permute-start(bf16[320,384]{1,0:T(8,128)(2,1)S(1)} %bitcast.985), channel_id=1, source_target_pairs={{0,7},{1,6},{2,5},{3,4},{4,3},{5,2},{6,1},{7,0},{8,15},{9,14},{10,... | collective-permute-start | bytes 737288 | tf_op jit(solution)/shard_map/ppermute | solution.py:61
  751.3 63.3 %collective-permute-start.74 = (bf16[8,64,1024]{2,1,0:T(8,128)(2,1)}, bf16[8,64,1024]{2,1,0:T(8,128)(2,1)}, u32[]{:S(2)}, u32[]{:S(2)}) collective-permute-start(bf16[8,64,1024]{2,1,0:T(8,128)(2,1)} %dynamic-slice_bitcast_fusion.3), channel_id=1, source_target_pairs={{0,1},{1,0},{2,3},{3,2},{4,5},{5,4},{6,7},{7,6},{8,9},{9,8},{10,11... | collective-permute-start | bytes 3145736 | tf_op jit(solution)/shard_map/ppermute | solution.py:61
  757.6 58.3 %collective-permute-start.66 = (bf16[8,64,1024]{2,1,0:T(8,128)(2,1)}, bf16[8,64,1024]{2,1,0:T(8,128)(2,1)}, u32[]{:S(2)}, u32[]{:S(2)}) collective-permute-start(bf16[8,64,1024]{2,1,0:T(8,128)(2,1)} %dynamic-slice_bitcast_fusion.4), channel_id=1, source_target_pairs={{0,1},{1,0},{2,3},{3,2},{4,5},{5,4},{6,7},{7,6},{8,9},{9,8},{10,11... | collective-permute-start | bytes 3145736 | tf_op jit(solution)/shard_map/ppermute | solution.py:61
  762.2 54.8 %collective-permute-start.58 = (bf16[8,64,1024]{2,1,0:T(8,128)(2,1)}, bf16[8,64,1024]{2,1,0:T(8,128)(2,1)}, u32[]{:S(2)}, u32[]{:S(2)}) collective-permute-start(bf16[8,64,1024]{2,1,0:T(8,128)(2,1)} %dynamic-slice_bitcast_fusion.5), channel_id=1, source_target_pairs={{0,1},{1,0},{2,3},{3,2},{4,5},{5,4},{6,7},{7,6},{8,9},{9,8},{10,11... | collective-permute-start | bytes 3145736 | tf_op jit(solution)/shard_map/ppermute | solution.py:61
  814.6 88.1 %collective-permute-start.50 = (bf16[8,64,3072]{2,1,0:T(8,128)(2,1)}, bf16[8,64,3072]{2,1,0:T(8,128)(2,1)}, u32[]{:S(2)}, u32[]{:S(2)}) collective-permute-start(bf16[8,64,3072]{2,1,0:T(8,128)(2,1)} %dynamic-slice_bitcast_fusion.2), channel_id=1, source_target_pairs={{0,1},{1,0},{2,3},{3,2},{4,5},{5,4},{6,7},{7,6},{8,9},{9,8},{10,11... | collective-permute-start | bytes 9437192 | tf_op jit(solution)/shard_map/ppermute | solution.py:61
  868.0 30.9 %all-to-all-start.2 = ((bf16[16,64,256]{2,1,0:T(8,128)(2,1)}), bf16[16,64,256]{2,1,0:T(8,128)(2,1)}, u32[]{:S(2)}, u32[]{:S(2)}) async-start(bf16[16,64,256]{2,1,0:T(8,128)(2,1)} %bitcast.262), calls=%async_computation.2 | async-start | bytes 1048576 | tf_op jit(solution)/shard_map/all_to_all | solution.py:538
  872.2 14.7 %collective-permute-start.64 = (bf16[64,1024]{1,0:T(8,128)(2,1)S(1)}, bf16[64,1024]{1,0:T(8,128)(2,1)S(1)}, u32[]{:S(2)}, u32[]{:S(2)}) collective-permute-start(bf16[64,1024]{1,0:T(8,128)(2,1)S(1)} %fusion.218), channel_id=1, source_target_pairs={{0,2},{1,3},{4,0},{5,1},{8,4},{9,5},{12,8},{13,9},{14,12},{15,13},... | collective-permute-start | bytes 393224 | tf_op jit(solution)/shard_map/ppermute | solution.py:274
  875.0 14.2 %collective-permute-start.81 = (bf16[64,1024]{1,0:T(8,128)(2,1)S(1)}, bf16[64,1024]{1,0:T(8,128)(2,1)S(1)}, u32[]{:S(2)}, u32[]{:S(2)}) collective-permute-start(bf16[64,1024]{1,0:T(8,128)(2,1)S(1)} %fusion.186), channel_id=1, source_target_pairs={{0,2},{1,3},{4,0},{5,1},{8,4},{9,5},{12,8},{13,9},{14,12},{15,13},... | collective-permute-start | bytes 393224 | tf_op jit(solution)/shard_map/ppermute | solution.py:274
  908.8 18.5 %collective-permute-start.83 = (bf16[64,4096]{1,0:T(8,128)(2,1)S(1)}, bf16[64,4096]{1,0:T(8,128)(2,1)S(1)}, u32[]{:S(2)}, u32[]{:S(2)}) collective-permute-start(bf16[64,4096]{1,0:T(8,128)(2,1)S(1)} %fusion.146), channel_id=1, source_target_pairs={{0,4},{1,5},{4,8},{5,9},{8,12},{9,13},{12,14},{13,15},{14,10},{15,... | collective-permute-start | bytes 1572872 | tf_op jit(solution)/shard_map/ppermute | solution.py:274
  917.3 18.4 %collective-permute-start.52 = (bf16[64,3072]{1,0:T(8,128)(2,1)S(1)}, bf16[64,3072]{1,0:T(8,128)(2,1)S(1)}, u32[]{:S(2)}, u32[]{:S(2)}) collective-permute-start(bf16[64,3072]{1,0:T(8,128)(2,1)S(1)} %fusion.162), channel_id=1, source_target_pairs={{0,4},{1,5},{4,8},{5,9},{8,12},{9,13},{12,14},{13,15},{14,10},{15,... | collective-permute-start | bytes 1179656 | tf_op jit(solution)/shard_map/ppermute | solution.py:274
  920.9 18.2 %collective-permute-start.92 = (bf16[256,1024]{1,0:T(8,128)(2,1)S(1)}, bf16[256,1024]{1,0:T(8,128)(2,1)S(1)}, u32[]{:S(2)}, u32[]{:S(2)}) collective-permute-start(bf16[256,1024]{1,0:T(8,128)(2,1)S(1)} %fusion.130), channel_id=1, source_target_pairs={{0,2},{1,3},{4,0},{5,1},{8,4},{9,5},{12,8},{13,9},{14,12},{15,13},... | collective-permute-start | bytes 1572872 | tf_op jit(solution)/shard_map/ppermute | solution.py:274
  928.7 18.2 %collective-permute-start.84 = (bf16[64,4096]{1,0:T(8,128)(2,1)S(1)}, bf16[64,4096]{1,0:T(8,128)(2,1)S(1)}, u32[]{:S(2)}, u32[]{:S(2)}) collective-permute-start(bf16[64,4096]{1,0:T(8,128)(2,1)S(1)} %fusion.145), channel_id=1, source_target_pairs={{0,4},{1,5},{4,8},{5,9},{8,12},{9,13},{12,14},{13,15},{14,10},{15,... | collective-permute-start | bytes 1572872 | tf_op jit(solution)/shard_map/ppermute | solution.py:274
  937.0 18.4 %collective-permute-start.53 = (bf16[64,3072]{1,0:T(8,128)(2,1)S(1)}, bf16[64,3072]{1,0:T(8,128)(2,1)S(1)}, u32[]{:S(2)}, u32[]{:S(2)}) collective-permute-start(bf16[64,3072]{1,0:T(8,128)(2,1)S(1)} %fusion.160), channel_id=1, source_target_pairs={{0,4},{1,5},{4,8},{5,9},{8,12},{9,13},{12,14},{13,15},{14,10},{15,... | collective-permute-start | bytes 1179656 | tf_op jit(solution)/shard_map/ppermute | solution.py:274
  940.5 18.2 %collective-permute-start.93 = (bf16[256,1024]{1,0:T(8,128)(2,1)S(1)}, bf16[256,1024]{1,0:T(8,128)(2,1)S(1)}, u32[]{:S(2)}, u32[]{:S(2)}) collective-permute-start(bf16[256,1024]{1,0:T(8,128)(2,1)S(1)} %fusion.128), channel_id=1, source_target_pairs={{0,2},{1,3},{4,0},{5,1},{8,4},{9,5},{12,8},{13,9},{14,12},{15,13},... | collective-permute-start | bytes 1572872 | tf_op jit(solution)/shard_map/ppermute | solution.py:274
  948.3 18.2 %collective-permute-start.85 = (bf16[64,4096]{1,0:T(8,128)(2,1)S(1)}, bf16[64,4096]{1,0:T(8,128)(2,1)S(1)}, u32[]{:S(2)}, u32[]{:S(2)}) collective-permute-start(bf16[64,4096]{1,0:T(8,128)(2,1)S(1)} %fusion.143), channel_id=1, source_target_pairs={{0,4},{1,5},{4,8},{5,9},{8,12},{9,13},{12,14},{13,15},{14,10},{15,... | collective-permute-start | bytes 1572872 | tf_op jit(solution)/shard_map/ppermute | solution.py:274
  956.6 18.4 %collective-permute-start.54 = (bf16[64,3072]{1,0:T(8,128)(2,1)S(1)}, bf16[64,3072]{1,0:T(8,128)(2,1)S(1)}, u32[]{:S(2)}, u32[]{:S(2)}) collective-permute-start(bf16[64,3072]{1,0:T(8,128)(2,1)S(1)} %fusion.158), channel_id=1, source_target_pairs={{0,4},{1,5},{4,8},{5,9},{8,12},{9,13},{12,14},{13,15},{14,10},{15,... | collective-permute-start | bytes 1179656 | tf_op jit(solution)/shard_map/ppermute | solution.py:274
  960.2 18.2 %collective-permute-start.94 = (bf16[256,1024]{1,0:T(8,128)(2,1)S(1)}, bf16[256,1024]{1,0:T(8,128)(2,1)S(1)}, u32[]{:S(2)}, u32[]{:S(2)}) collective-permute-start(bf16[256,1024]{1,0:T(8,128)(2,1)S(1)} %fusion.126), channel_id=1, source_target_pairs={{0,2},{1,3},{4,0},{5,1},{8,4},{9,5},{12,8},{13,9},{14,12},{15,13},... | collective-permute-start | bytes 1572872 | tf_op jit(solution)/shard_map/ppermute | solution.py:274
  968.0 18.2 %collective-permute-start.86 = (bf16[64,4096]{1,0:T(8,128)(2,1)S(1)}, bf16[64,4096]{1,0:T(8,128)(2,1)S(1)}, u32[]{:S(2)}, u32[]{:S(2)}) collective-permute-start(bf16[64,4096]{1,0:T(8,128)(2,1)S(1)} %fusion.141), channel_id=1, source_target_pairs={{0,4},{1,5},{4,8},{5,9},{8,12},{9,13},{12,14},{13,15},{14,10},{15,... | collective-permute-start | bytes 1572872 | tf_op jit(solution)/shard_map/ppermute | solution.py:274
  976.3 18.4 %collective-permute-start.55 = (bf16[64,3072]{1,0:T(8,128)(2,1)S(1)}, bf16[64,3072]{1,0:T(8,128)(2,1)S(1)}, u32[]{:S(2)}, u32[]{:S(2)}) collective-permute-start(bf16[64,3072]{1,0:T(8,128)(2,1)S(1)} %fusion.156), channel_id=1, source_target_pairs={{0,4},{1,5},{4,8},{5,9},{8,12},{9,13},{12,14},{13,15},{14,10},{15,... | collective-permute-start | bytes 1179656 | tf_op jit(solution)/shard_map/ppermute | solution.py:274
  979.8 18.2 %collective-permute-start.95 = (bf16[256,1024]{1,0:T(8,128)(2,1)S(1)}, bf16[256,1024]{1,0:T(8,128)(2,1)S(1)}, u32[]{:S(2)}, u32[]{:S(2)}) collective-permute-start(bf16[256,1024]{1,0:T(8,128)(2,1)S(1)} %fusion.124), channel_id=1, source_target_pairs={{0,2},{1,3},{4,0},{5,1},{8,4},{9,5},{12,8},{13,9},{14,12},{15,13},... | collective-permute-start | bytes 1572872 | tf_op jit(solution)/shard_map/ppermute | solution.py:274
  987.7 18.2 %collective-permute-start.87 = (bf16[64,4096]{1,0:T(8,128)(2,1)S(1)}, bf16[64,4096]{1,0:T(8,128)(2,1)S(1)}, u32[]{:S(2)}, u32[]{:S(2)}) collective-permute-start(bf16[64,4096]{1,0:T(8,128)(2,1)S(1)} %fusion.139), channel_id=1, source_target_pairs={{0,4},{1,5},{4,8},{5,9},{8,12},{9,13},{12,14},{13,15},{14,10},{15,... | collective-permute-start | bytes 1572872 | tf_op jit(solution)/shard_map/ppermute | solution.py:274
  995.9 18.4 %collective-permute-start.56 = (bf16[64,3072]{1,0:T(8,128)(2,1)S(1)}, bf16[64,3072]{1,0:T(8,128)(2,1)S(1)}, u32[]{:S(2)}, u32[]{:S(2)}) collective-permute-start(bf16[64,3072]{1,0:T(8,128)(2,1)S(1)} %fusion.154), channel_id=1, source_target_pairs={{0,4},{1,5},{4,8},{5,9},{8,12},{9,13},{12,14},{13,15},{14,10},{15,... | collective-permute-start | bytes 1179656 | tf_op jit(solution)/shard_map/ppermute | solution.py:274
  999.5 18.2 %collective-permute-start.96 = (bf16[256,1024]{1,0:T(8,128)(2,1)S(1)}, bf16[256,1024]{1,0:T(8,128)(2,1)S(1)}, u32[]{:S(2)}, u32[]{:S(2)}) collective-permute-start(bf16[256,1024]{1,0:T(8,128)(2,1)S(1)} %fusion.122), channel_id=1, source_target_pairs={{0,2},{1,3},{4,0},{5,1},{8,4},{9,5},{12,8},{13,9},{14,12},{15,13},... | collective-permute-start | bytes 1572872 | tf_op jit(solution)/shard_map/ppermute | solution.py:274
  1007.3 18.2 %collective-permute-start.88 = (bf16[64,4096]{1,0:T(8,128)(2,1)S(1)}, bf16[64,4096]{1,0:T(8,128)(2,1)S(1)}, u32[]{:S(2)}, u32[]{:S(2)}) collective-permute-start(bf16[64,4096]{1,0:T(8,128)(2,1)S(1)} %fusion.137), channel_id=1, source_target_pairs={{0,4},{1,5},{4,8},{5,9},{8,12},{9,13},{12,14},{13,15},{14,10},{15,... | collective-permute-start | bytes 1572872 | tf_op jit(solution)/shard_map/ppermute | solution.py:274
  1015.6 18.4 %collective-permute-start.57 = (bf16[64,3072]{1,0:T(8,128)(2,1)S(1)}, bf16[64,3072]{1,0:T(8,128)(2,1)S(1)}, u32[]{:S(2)}, u32[]{:S(2)}) collective-permute-start(bf16[64,3072]{1,0:T(8,128)(2,1)S(1)} %fusion.152), channel_id=1, source_target_pairs={{0,4},{1,5},{4,8},{5,9},{8,12},{9,13},{12,14},{13,15},{14,10},{15,... | collective-permute-start | bytes 1179656 | tf_op jit(solution)/shard_map/ppermute | solution.py:274
  1019.2 17.0 %collective-permute-start.97 = (bf16[256,1024]{1,0:T(8,128)(2,1)S(1)}, bf16[256,1024]{1,0:T(8,128)(2,1)S(1)}, u32[]{:S(2)}, u32[]{:S(2)}) collective-permute-start(bf16[256,1024]{1,0:T(8,128)(2,1)S(1)} %fusion.120), channel_id=1, source_target_pairs={{0,2},{1,3},{4,0},{5,1},{8,4},{9,5},{12,8},{13,9},{14,12},{15,13},... | collective-permute-start | bytes 1572872 | tf_op jit(solution)/shard_map/ppermute | solution.py:274
  1027.0 15.5 %collective-permute-start.89 = (bf16[64,4096]{1,0:T(8,128)(2,1)S(1)}, bf16[64,4096]{1,0:T(8,128)(2,1)S(1)}, u32[]{:S(2)}, u32[]{:S(2)}) collective-permute-start(bf16[64,4096]{1,0:T(8,128)(2,1)S(1)} %fusion.135), channel_id=1, source_target_pairs={{0,4},{1,5},{4,8},{5,9},{8,12},{9,13},{12,14},{13,15},{14,10},{15,... | collective-permute-start | bytes 1572872 | tf_op jit(solution)/shard_map/ppermute | solution.py:274
  (209 other events, 2047.1 us)
Sparse Core Ops, SparseCore 0:
  10.8 48.4 all-gather.16
  62.0 43.3 all-gather.14
  108.1 41.5 all-gather.18
  151.9 60.7 all-gather.12
  215.2 87.1 all-gather.20
  305.0 81.6 all-gather.22

commit v2 on v1

v2 whole, which is shorter than its diff:
```python
import functools

import jax
import jax.numpy as jnp
import numpy as np
from jax import lax
from jax.experimental import pallas as pl
from jax.experimental.pallas import tpu as pltpu
from jax.sharding import PartitionSpec as P

D = 1024
HEADS = 16
HEAD = 64
FF = 4096
FRAMES = 5
BH = 8
BW = 4
CELLS = BH * BW
ROWS = 160
REL = 71
MEMBERS = 8
PAIR = 2 * HEAD
EPSILON = 1e-06
LOW = jnp.bfloat16
HIGH = jnp.float32
MIB = 1024 * 1024
SHORT = pl.CostEstimate(flops=1, bytes_accessed=1, transcendentals=0)


def dot(left, right):
    return lax.dot_general(left, right, (((1,), (0,)), ((), ())), preferred_element_type=HIGH)


def dot_right_t(left, right):
    return lax.dot_general(left, right, (((1,), (1,)), ((), ())), preferred_element_type=HIGH)


def dot_left_t(left, right):
    return lax.dot_general(left, right, (((0,), (0,)), ((), ())), preferred_element_type=HIGH)


def low(v):
    return v.astype(LOW)


def high(v):
    return v.astype(HIGH)


def layer_mod(inputs, offset, factor):
    average = jnp.mean(inputs, axis=-1, keepdims=True)
    centred = inputs - average
    spread = jnp.mean(centred * centred, axis=-1, keepdims=True)
    return centred * lax.rsqrt(spread + EPSILON) * (1.0 + factor) + offset


def swap(x, bits, sections=(0, 1)):
    count = lax.axis_size("dp")
    route = [(s * count + i, s * count + (i ^ bits)) for s in sections for i in range(count)]
    return lax.ppermute(x, ("section", "dp"), route)


def head_masks():
    lane = lax.broadcasted_iota(jnp.int32, (1, PAIR), 1)
    first = (lane < HEAD).astype(LOW)
    return first, 1 - first


def by_head(first, second):
    lane = lax.broadcasted_iota(jnp.int32, (1, PAIR), 1)
    return low(jnp.where(lane < HEAD, first, second))


def pairs_forward(pairs):
    masks = [mask * LOW(HEAD ** (-0.5)) for mask in head_masks()]
    heads = [(q * mask, k, v, bias) for q, k, v, biases in pairs for mask, bias in zip(masks, biases)]
    scores = [dot_right_t(q, k) + bias for q, k, _, bias in heads]
    highest = [jnp.max(x, axis=-1, keepdims=True) for x in scores]
    exponents = [jnp.exp(x - y) for x, y in zip(scores, highest)]
    totals = [jnp.sum(x, axis=-1, keepdims=True) for x in exponents]
    mixed = [dot(low(x), head[2]) * (1.0 / total) for x, head, total in zip(exponents, heads, totals)]
    norms = [x + jnp.log(y) for x, y in zip(highest, totals)]
    return [(by_head(*mixed[i : i + 2]), norms[i : i + 2]) for i in range(0, len(heads), 2)]


def pairs_backward(pairs):
    masks = head_masks()
    heads = [
        (q * mask, k, v, do * mask, bias, norm)
        for q, k, v, do, biases, norms in pairs
        for mask, bias, norm in zip(masks, biases, norms)
    ]
    scale = HEAD ** (-0.5)
    soft = [jnp.exp(dot_right_t(q * LOW(scale), k) + bias - norm) for q, k, _, _, bias, norm in heads]
    grads = [dot_right_t(do, v) for _, _, v, do, _, _ in heads]
    means = [jnp.sum(x * y, axis=-1, keepdims=True) for x, y in zip(soft, grads)]
    grads = [x * (y - z) for x, y, z in zip(soft, grads, means)]
    raw = [low(x * scale) for x in grads]
    dq = [dot(x, head[1]) for x, head in zip(raw, heads)]
    dk = [dot_left_t(head[0], x) for x, head in zip(raw, heads)]
    dv = [dot_left_t(head[3], low(x)) for x, head in zip(soft, heads)]
    return [
        (by_head(*dq[i : i + 2]), low((dk[i] + dk[i + 1]).T), low((dv[i] + dv[i + 1]).T), grads[i : i + 2])
        for i in range(0, len(heads), 2)
    ]


def add_over_steps(ref, index, value, axis):
    @pl.when(pl.program_id(axis) == 0)
    def _():
        ref[index] = value

    @pl.when(pl.program_id(axis) > 0)
    def _():
        ref[index] += value


def part_of(block, part):
    return block[:, part * PAIR : (part + 1) * PAIR]


def frames_pairs(joint_ref, bias_ref):
    for w in range(joint_ref.shape[1]):
        x = joint_ref[:, w].reshape(MEMBERS * CELLS, 3 * PAIR)
        yield part_of(x, 0), part_of(x, 1), part_of(x, 2), (bias_ref[0], bias_ref[1])


def frames_forward(joint_ref, bias_ref, o_ref, norm_ref):
    for w, (o, norms) in enumerate(pairs_forward(list(frames_pairs(joint_ref, bias_ref)))):
        o_ref[:, w] = o.reshape(MEMBERS, CELLS, PAIR)
        norm_ref[w] = jnp.concatenate(norms, 1)


def frames_backward(joint_ref, bias_ref, norm_ref, do_ref, grad_ref, dbias_ref):
    pairs = []
    for w, (q, k, v, biases) in enumerate(frames_pairs(joint_ref, bias_ref)):
        do = do_ref[:, w].reshape(MEMBERS * CELLS, PAIR)
        pairs.append((q, k, v, do, biases, (norm_ref[w, :, 0:1], norm_ref[w, :, 1:2])))
    sums = [0.0, 0.0]
    for w, (dq, dk, dv, dbias) in enumerate(pairs_backward(pairs)):
        for part, value in enumerate((dq, dk, dv)):
            grad_ref[:, w, :, part * PAIR : (part + 1) * PAIR] = value.reshape(MEMBERS, CELLS, PAIR)
        sums = [s + d for s, d in zip(sums, dbias)]
    for a in range(2):
        add_over_steps(dbias_ref, a, sums[a], 0)


def window_pairs(own_ref, other_ref, bias_ref):
    for h in range(own_ref.shape[0]):
        own, other = own_ref[h], other_ref[h]
        k, v = [jnp.concatenate([part_of(own, p), part_of(other, p)], 0) for p in (1, 2)]
        yield part_of(own, 0), k, v, (bias_ref[2 * h], bias_ref[2 * h + 1])


def window_forward(own_ref, other_ref, bias_ref, o_ref, norm_ref):
    made = pairs_forward(list(window_pairs(own_ref, other_ref, bias_ref)))
    for h, (o, _) in enumerate(made):
        o_ref[h] = o
    norm_ref[0, 0] = jnp.concatenate([norm for _, norms in made for norm in norms], 1)


def window_backward(own_ref, other_ref, bias_ref, norm_ref, do_ref, own_grad_ref, other_grad_ref, dbias_ref):
    norms = norm_ref[0, 0]
    pairs = []
    for h, (q, k, v, biases) in enumerate(window_pairs(own_ref, other_ref, bias_ref)):
        pairs.append((q, k, v, do_ref[h], biases, (norms[:, 2 * h : 2 * h + 1], norms[:, 2 * h + 1 : 2 * h + 2])))
    for h, (dq, dk, dv, dbias) in enumerate(pairs_backward(pairs)):
        own_grad_ref[h] = jnp.concatenate([dq, dk[:ROWS], dv[:ROWS]], 1)
        other_grad_ref[h] = jnp.concatenate([dk[ROWS:], dv[ROWS:]], 1)
        for a in range(2):
            add_over_steps(dbias_ref, 2 * h + a, dbias[a], 1)


def text_pairs(q_ref, k_ref, v_ref):
    for h in range(q_ref.shape[1] // PAIR):
        yield part_of(q_ref[...], h), part_of(k_ref[0], h), part_of(v_ref[0], h), (0.0, 0.0)


def text_forward(q_ref, k_ref, v_ref, o_ref, norm_ref):
    made = pairs_forward(list(text_pairs(q_ref, k_ref, v_ref)))
    o_ref[...] = jnp.concatenate([o for o, _ in made], 1)
    norm_ref[0, 0] = jnp.concatenate([norm for _, norms in made for norm in norms], 1)


def text_backward(q_ref, k_ref, v_ref, norm_ref, do_ref, dq_ref, dk_ref, dv_ref):
    norms = norm_ref[0, 0]
    pairs = []
    for h, (q, k, v, biases) in enumerate(text_pairs(q_ref, k_ref, v_ref)):
        heads = (norms[:, 2 * h : 2 * h + 1], norms[:, 2 * h + 1 : 2 * h + 2])
        pairs.append((q, k, v, part_of(do_ref[...], h), biases, heads))
    made = pairs_backward(pairs)
    dq_ref[...], dk_ref[0], dv_ref[0] = [jnp.concatenate([x[i] for x in made], 1) for i in range(3)]


def call(kernel, grid, in_specs, out_specs, out_shape, operands, limit=20):
    return pl.pallas_call(
        kernel,
        grid=grid,
        in_specs=in_specs,
        out_specs=out_specs,
        out_shape=out_shape,
        cost_estimate=SHORT,
        compiler_params=pltpu.CompilerParams(vmem_limit_bytes=limit * MIB),
    )(*operands)


def shaped(shape, dtype=LOW):
    return jax.ShapeDtypeStruct(shape, dtype)


GROUP = 4
GROUPS = HEADS // 2 // GROUP


def frames_specs(joint):
    steps = joint.shape[1] // FRAMES
    wide = pl.BlockSpec((MEMBERS, FRAMES, CELLS, 3 * PAIR), lambda i: (0, i, 0, 0))
    narrow = pl.BlockSpec((MEMBERS, FRAMES, CELLS, PAIR), lambda i: (0, i, 0, 0))
    size = MEMBERS * CELLS
    bias = pl.BlockSpec((2, size, size), lambda i: (0, 0, 0))
    norm = pl.BlockSpec((FRAMES, size, 2), lambda i: (i, 0, 0))
    return steps, wide, narrow, bias, norm


def attend_frames(joint, bias):
    steps, wide, narrow, bias_spec, norm = frames_specs(joint)
    size = MEMBERS * CELLS
    return call(
        frames_forward,
        (steps,),
        [wide, bias_spec],
        [narrow, norm],
        [shaped(joint.shape[:3] + (PAIR,)), shaped((steps * FRAMES, size, 2), HIGH)],
        (joint, bias),
    )


def attend_frames_back(joint, bias, norms, do):
    steps, wide, narrow, bias_spec, norm = frames_specs(joint)
    size = MEMBERS * CELLS
    return call(
        frames_backward,
        (steps,),
        [wide, bias_spec, norm, narrow],
        [wide, bias_spec],
        [shaped(joint.shape), shaped((2, size, size), HIGH)],
        (joint, bias, norms, do),
    )


def window_specs(width):
    return pl.BlockSpec((GROUP, ROWS, width), lambda g, w: (g, w, 0))


BIAS_SPEC = pl.BlockSpec((2 * GROUP, ROWS, 2 * ROWS), lambda g, w: (g, 0, 0))
NORM_SPEC = pl.BlockSpec((1, 1, ROWS, 2 * GROUP), lambda g, w: (g, w, 0, 0))


def attend_window(own, other, bias):
    micro = own.shape[1] // ROWS
    return call(
        window_forward,
        (GROUPS, micro),
        [window_specs(3 * PAIR), window_specs(3 * PAIR), BIAS_SPEC],
        [window_specs(PAIR), NORM_SPEC],
        [shaped(own.shape[:2] + (PAIR,)), shaped((GROUPS, micro, ROWS, 2 * GROUP), HIGH)],
        (own, other, bias),
    )


def attend_window_back(own, other, bias, norms, do):
    micro = own.shape[1] // ROWS
    return call(
        window_backward,
        (GROUPS, micro),
        [window_specs(3 * PAIR), window_specs(3 * PAIR), BIAS_SPEC, NORM_SPEC, window_specs(PAIR)],
        [window_specs(3 * PAIR), window_specs(2 * PAIR), BIAS_SPEC],
        [shaped(own.shape), shaped(own.shape[:2] + (2 * PAIR,)), shaped(bias.shape, HIGH)],
        (own, other, bias, norms, do),
    )


def text_specs(keys):
    rows = pl.BlockSpec((ROWS, GROUP * PAIR), lambda g, w: (w, g))
    k = pl.BlockSpec((1, keys, GROUP * PAIR), lambda g, w: (w, 0, g))
    v = pl.BlockSpec((1, keys, GROUP * PAIR), lambda g, w: (w, 0, GROUPS + g))
    return rows, k, v


def attend_text(asked, memory):
    micro, keys = memory.shape[:2]
    rows, k, v = text_specs(keys)
    return call(
        text_forward,
        (GROUPS, micro),
        [rows, k, v],
        [rows, NORM_SPEC],
        [shaped(asked.shape), shaped((GROUPS, micro, ROWS, 2 * GROUP), HIGH)],
        (asked, memory, memory),
    )


def attend_text_back(asked, memory, norms, do):
    micro, keys = memory.shape[:2]
    rows, k, v = text_specs(keys)
    return call(
        text_backward,
        (GROUPS, micro),
        [rows, k, v, NORM_SPEC, rows],
        [rows, k, k],
        [shaped(asked.shape), shaped((micro, keys, D)), shaped((micro, keys, D))],
        (asked, memory, memory, norms, do),
    )


PARTS = 16
ROWS_OF_PART = D // PARTS
SET = 4 * PAIR
STRIP = FF // 8
LARGE = 40


def block_spec(first):
    return pl.BlockSpec((PARTS, ROWS_OF_PART, SET), lambda j: (0, first + (j >> 1), j & 1))


def joined(ref):
    return ref[...].reshape(-1, ref.shape[-1])


def rows_spec(shape):
    return pl.BlockSpec(shape, lambda j: (0,) * len(shape))


def project_kernel(hidden_ref, w_ref, joint_ref, asked_ref):
    made = low(dot(hidden_ref[...], joined(w_ref)))
    joint_ref[0] = made[:, : 3 * PAIR]
    asked_ref[...] = made[:, 3 * PAIR :]


def project(hidden, packed):
    tokens = hidden.shape[0]
    return call(
        project_kernel,
        (MEMBERS,),
        [rows_spec((tokens, D)), block_spec(0)],
        [pl.BlockSpec((1, tokens, 3 * PAIR), lambda m: (m, 0, 0)), pl.BlockSpec((tokens, PAIR), lambda m: (0, m))],
        [shaped((MEMBERS, tokens, 3 * PAIR)), shaped((tokens, D))],
        (hidden, packed),
    )


def project_back_kernel(joint_ref, asked_ref, w_ref, out_ref):
    grad = jnp.concatenate([joint_ref[0], asked_ref[...]], 1)
    add_over_steps(out_ref, slice(None), dot_right_t(grad, joined(w_ref)), 0)


def project_back(joint_grad, asked_grad, packed):
    tokens = asked_grad.shape[0]
    return call(
        project_back_kernel,
        (MEMBERS,),
        [
            pl.BlockSpec((1, tokens, 3 * PAIR), lambda m: (m, 0, 0)),
            pl.BlockSpec((tokens, PAIR), lambda m: (0, m)),
            block_spec(0),
        ],
        rows_spec((tokens, D)),
        shaped((tokens, D), HIGH),
        (joint_grad, asked_grad, packed),
    )


def text_project_kernel(text_ref, w_ref, out_ref):
    out_ref[...] = low(dot(text_ref[...], joined(w_ref)))


def text_project(text, packed):
    return call(
        text_project_kernel,
        (2 * D // SET,),
        [rows_spec(text.shape), block_spec(6)],
        pl.BlockSpec((text.shape[0], SET), lambda j: (0, j)),
        shaped((text.shape[0], 2 * D)),
        (text, packed),
        LARGE,
    )


def merge_kernel(o_ref, text_ref, w_self_ref, w_cross_ref, out_ref):
    o = jnp.concatenate([o_ref[m] for m in range(MEMBERS)], 1)
    out_ref[...] = dot(o, joined(w_self_ref)) + dot(text_ref[...], joined(w_cross_ref))


def merge(o, text, packed):
    tokens = text.shape[0]
    return call(
        merge_kernel,
        (D // SET,),
        [rows_spec((MEMBERS, tokens, PAIR)), rows_spec((tokens, D)), block_spec(0), block_spec(1)],
        pl.BlockSpec((tokens, SET), lambda j: (0, j)),
        shaped((tokens, D), HIGH),
        (o, text, packed, packed),
        LARGE,
    )


def merge_back_kernel(grad_ref, w_self_ref, w_cross_ref, o_ref, text_ref):
    made = low(dot_right_t(grad_ref[...], joined(w_self_ref)))
    for m in range(o_ref.shape[0]):
        o_ref[m] = part_of(made, m)
    text_ref[...] = low(dot_right_t(grad_ref[...], joined(w_cross_ref)))


def merge_back(grad, packed):
    tokens = grad.shape[0]
    height = 2 * PAIR
    parts = height // ROWS_OF_PART
    return call(
        merge_back_kernel,
        (D // height,),
        [
            rows_spec((tokens, D)),
            pl.BlockSpec((parts, ROWS_OF_PART, D), lambda j: (j, 0, 0)),
            pl.BlockSpec((parts, ROWS_OF_PART, D), lambda j: (j, 1, 0)),
        ],
        [pl.BlockSpec((2, tokens, PAIR), lambda j: (j, 0, 0)), pl.BlockSpec((tokens, height), lambda j: (0, j))],
        [shaped((MEMBERS, tokens, PAIR)), shaped((tokens, D))],
        (grad, packed, packed),
        LARGE,
    )


def feed_kernel(s_ref, up_ref, down_ref, upper_ref, active_ref, feed_ref):
    upper = dot(s_ref[...], joined(up_ref))
    active = low(jax.nn.gelu(upper))
    upper_ref[...] = upper
    active_ref[...] = active
    add_over_steps(feed_ref, slice(None), dot(active, joined(down_ref)), 0)


def feed_specs(tokens):
    strip = pl.BlockSpec((tokens, STRIP), lambda j: (0, j))
    down = pl.BlockSpec((STRIP // (FF // PARTS), FF // PARTS, D), lambda j: (j, 2, 0))
    return rows_spec((tokens, D)), strip, block_spec(2), down


def feed_call(second, packed):
    tokens = second.shape[0]
    full, strip, up, down = feed_specs(tokens)
    return call(
        feed_kernel,
        (FF // STRIP,),
        [full, up, down],
        [strip, strip, full],
        [shaped((tokens, FF), HIGH), shaped((tokens, FF)), shaped((tokens, D), HIGH)],
        (second, packed, packed),
        LARGE,
    )


def feed_back_kernel(f_ref, upper_ref, up_ref, down_ref, upper_grad_ref, second_grad_ref):
    active_grad = dot_right_t(f_ref[...], joined(down_ref))
    upper_grad = low(jax.vjp(jax.nn.gelu, upper_ref[...])[1](active_grad)[0])
    upper_grad_ref[...] = upper_grad
    add_over_steps(second_grad_ref, slice(None), dot_right_t(upper_grad, joined(up_ref)), 0)


def feed_back_call(feed_grad, upper, packed):
    tokens = feed_grad.shape[0]
    full, strip, up, down = feed_specs(tokens)
    return call(
        feed_back_kernel,
        (FF // STRIP,),
        [full, strip, up, down],
        [strip, full],
        [shaped((tokens, FF)), shaped((tokens, D), HIGH)],
        (feed_grad, upper, packed, packed),
        LARGE,
    )


def pack_columns(x):
    rows = x.shape[0]
    return jnp.swapaxes(x.reshape(rows, -1, D), 0, 1).reshape(-1, D)


def unpack_columns(x, blocks):
    return jnp.swapaxes(x.reshape(blocks, -1, D), 0, 1).reshape(-1, blocks * D)


SPANS = ((FRAMES, FRAMES - 1), (2 * BH, 2 * FRAMES - 1 + 2 * BH - 1), (4 * BW, 2 * FRAMES - 1 + 4 * BH - 1 + 4 * BW - 1))
SPAN = sum(size for size, _ in SPANS)


def table_picks():
    picks = np.zeros((SPAN, SPAN, REL), np.float32)
    start = 0
    for size, middle in SPANS:
        for i in range(size):
            for j in range(size):
                picks[start + i, start + j, middle + i - j] = 1
        start += size
    return picks


def place_hot(frame, row, column):
    marks = []
    for (size, _), place in zip(SPANS, (frame, row, column)):
        marks.append(place[:, None] == jnp.arange(size)[None, :])
    return jnp.concatenate(marks, 1).astype(HIGH)


def places_of(member, within):
    cell = within & (CELLS - 1)
    return (
        within // CELLS + 0 * member,
        (member >> 2) * BH + cell // BW,
        (member & 3) * BW + (cell & (BW - 1)),
    )


def bias_of(table, hot_q, hot_k):
    exact = lax.Precision.HIGHEST
    blocks = jnp.einsum("hn,abn->hab", table, table_picks(), precision=exact)
    left = jnp.einsum("ia,hab->hib", hot_q, blocks, precision=exact)
    return jnp.einsum("hib,jb->hij", left, hot_k, precision=exact)


def bias_grad(grad, hot_q, hot_k):
    exact = lax.Precision.HIGHEST
    right = jnp.einsum("hij,jb->hib", grad, hot_k, precision=exact)
    blocks = jnp.einsum("ia,hib->hab", hot_q, right, precision=exact)
    return jnp.einsum("hab,abn->hn", blocks, table_picks(), precision=exact)


RING = [0, 2, 4, 6, 7, 5, 3, 1]
WAYS = (1, -1)


def together(*values):
    return lax.optimization_barrier(values)


def device_ring():
    device = lax.axis_index("dp")
    chip = device >> 1
    half = len(RING) // 2
    place = jnp.where((chip & 1) == 1, 2 * half - 1 - (chip >> 1), chip >> 1)
    spots = (place + jnp.arange(2 * half)) & (2 * half - 1)
    return jnp.where(spots < half, 2 * spots, 4 * half - 1 - 2 * spots), device & 1


def hop(x, way):
    count = lax.axis_size("dp")
    chips = len(RING)
    route = []
    for s in range(2):
        for i in range(chips):
            for c in range(2):
                source = s * count + RING[i] * 2 + c
                route.append((source, s * count + RING[(i + way) % chips] * 2 + c))
    return lax.ppermute(x, ("section", "dp"), route)


def ring_gather(own):
    chips = len(RING)
    half = own.shape[0] // 2
    chunks = [own[:half], own[half:]]
    held = []
    side = ()
    for step in range(chips):
        last = step + 1 == chips
        if not last:
            following = [hop(chunk, way) for chunk, way in zip(chunks, WAYS)]
        held.append([list(chunks), [swap(chunk, 1) for chunk in chunks]])
        if not last:
            side = yield side
            before = [x for pair in held[:-1] for x in pair[1]]
            tied = together(*following, *before, *side)
            chunks = list(tied[:2])
            for i, pair in enumerate(held[:-1]):
                pair[1] = list(tied[2 + 2 * i : 4 + 2 * i])
            side = tied[2 + len(before) :]
        if step == EARLY:
            made = assembled(held, 0, None)
        if step == EARLY + 1:
            made, *chunks = together(made, *chunks)
    return assembled(held, EARLY, made), side


EARLY = 5


def assembled(held, start, made):
    held = held[start:EARLY] if made is None else held[start:]
    chips = len(RING)
    spots, core = device_ring()
    order = jnp.concatenate([spots, jnp.broadcast_to(core, (1,))]).astype(jnp.int32)
    flat = [x for own, other in held for x in own + other]
    half = flat[0].shape[0]
    shape = (chips, 2, 2 * half, D)

    def kernel(order_ref, *refs):
        sources, (sink, scratch, arrive, leave) = refs[: len(flat)], refs[-4:]
        arriving, leaving = [], []
        for i, ref in enumerate(sources):
            step, which, way = start + i // 4, i // 2 % 2, i % 2
            spot = order_ref[-WAYS[way] * step % chips]
            place = order_ref[chips] if which == 0 else 1 - order_ref[chips]
            where = (spot, place, pl.ds(way * half, half))
            arriving.append(pltpu.make_async_copy(ref, scratch.at[i], arrive.at[i]))
            leaving.append(pltpu.make_async_copy(scratch.at[i], sink.at[where], leave.at[i]))
        for copy in arriving:
            copy.start()
        for copy, onward in zip(arriving, leaving):
            copy.wait()
            onward.start()
        for copy in leaving:
            copy.wait()

    operands = flat if made is None else flat + [made]
    anywhere = pl.BlockSpec(memory_space=pl.ANY)
    made = pl.pallas_call(
        kernel,
        grid_spec=pltpu.PrefetchScalarGridSpec(
            num_scalar_prefetch=1,
            grid=(),
            in_specs=[anywhere] * len(operands),
            out_specs=anywhere,
            scratch_shapes=[pltpu.VMEM((len(flat),) + flat[0].shape, LOW)]
            + [pltpu.SemaphoreType.DMA((len(flat),))] * 2,
        ),
        out_shape=shaped(shape),
        input_output_aliases={} if made is None else {1 + len(flat): 0},
        cost_estimate=SHORT,
        compiler_params=pltpu.CompilerParams(vmem_limit_bytes=58 * MIB),
    )(order, *operands)
    return made if start == 0 else made.reshape(PARTS, 2 * half, D)


def ring_sums(right, left):
    def term(step):
        return [jnp.concatenate([high(x[step]) for x in arrays], 0) for arrays in (right, left)]

    totals = term(0)
    side = ()
    for step in range(1, len(RING)):
        arrived = [hop(low(total), way) for total, way in zip(totals, WAYS)]
        side = yield side
        tied = together(*arrived, *side)
        side = tied[2:]
        totals = [high(x) + y for x, y in zip(tied, term(step))]
    return totals, side


def no_ring(result):
    side = ()
    for _ in RING[1:]:
        side = yield side
    return result, side


class Stages:
    def __init__(self, generator):
        self.generator = generator
        self.result = None
        next(generator)

    def step(self, *side):
        try:
            return self.generator.send(side)
        except StopIteration as stop:
            self.result, side = stop.value
            return side


def ring_order():
    spots, core = device_ring()
    back = jnp.concatenate([spots[:0:-1], spots[:1]])
    ahead = jnp.concatenate([spots[1:], spots[:1]])
    return jnp.stack([back, ahead, jnp.broadcast_to(core, spots.shape)]).astype(jnp.int32)


def call_ordered(kernel, steps, in_specs, out_specs, out_shape, scratch, order, operands):
    return pl.pallas_call(
        kernel,
        grid_spec=pltpu.PrefetchScalarGridSpec(
            num_scalar_prefetch=1, grid=(steps,), in_specs=in_specs, out_specs=out_specs, scratch_shapes=scratch
        ),
        out_shape=out_shape,
        cost_estimate=SHORT,
        compiler_params=pltpu.CompilerParams(vmem_limit_bytes=24 * MIB),
    )(order, *operands)


def grad_spec(block):
    return pl.BlockSpec((len(RING), HEAD, SET), lambda j, order: (0, block(j) >> 1, block(j) & 1))


def packed_grad_kernel(order_ref, h_ref, o_ref, t_ref, w_ref, j_ref, j2_ref, a_ref, a2_ref, b_ref, b2_ref, k_ref, k2_ref, v_ref, v2_ref, right_ref, left_ref, rows_ref, grad_ref):
    step = pl.program_id(0)
    chips = len(RING)
    tokens, words = a_ref.shape[0], k_ref.shape[0]

    def pick(source_ref, way):
        width = source_ref.shape[1]
        for j in range(chips):
            start = pl.multiple_of((2 * order_ref[way, j] + order_ref[2, 0]) * HEAD, HEAD)
            rows_ref[j * HEAD : (j + 1) * HEAD, :width] = source_ref[pl.ds(start, HEAD)]

    pl.when(step == 0)(lambda: pick(h_ref, 0))
    pl.when(step == MEMBERS)(lambda: pick(o_ref, 1))
    pl.when(step == MEMBERS + 2)(lambda: pick(t_ref, 1))
    pl.when(step == MEMBERS + 4)(lambda: pick(w_ref, 1))

    @pl.when(step < MEMBERS)
    def _():
        for i, (joint, asked) in enumerate(((j_ref, a_ref), (j2_ref, a2_ref))):
            grad_ref[i * tokens : (i + 1) * tokens, : 3 * PAIR] = joint[0]
            grad_ref[i * tokens : (i + 1) * tokens, 3 * PAIR :] = asked[...]
        right_ref[...] = low(dot(rows_ref[...], grad_ref[...])).reshape(chips, HEAD, SET)

    @pl.when((step >= MEMBERS) & (step < MEMBERS + 4))
    def _():
        grad_ref[:tokens] = b_ref[...]
        grad_ref[tokens:] = b2_ref[...]
        left_ref[...] = low(dot(rows_ref[...], grad_ref[...])).reshape(chips, HEAD, SET)

    def memory(first, second):
        grad_ref[:words] = first[...]
        grad_ref[words : 2 * words] = second[...]
        made = dot(rows_ref[:, : 2 * words], grad_ref[: 2 * words])
        left_ref[...] = low(made).reshape(chips, HEAD, SET)

    pl.when((step >= MEMBERS + 4) & (step < MEMBERS + 6))(lambda: memory(k_ref, k2_ref))
    pl.when(step >= MEMBERS + 6)(lambda: memory(v_ref, v2_ref))


def packed_grads(order, hidden, o, text, words, joint_grad, asked_grad, branch_grad, keys_grad, values_grad):
    tokens = asked_grad[0].shape[0]
    chips = len(RING)

    def full(x):
        return pl.BlockSpec(x.shape, lambda j, order: (0, 0))

    def strips(x, first, last):
        return pl.BlockSpec((x.shape[0], SET), lambda j, order: (0, jnp.clip(j - first, 0, last)))

    joint = pl.BlockSpec((1, tokens, 3 * PAIR), lambda j, order: (jnp.minimum(j, MEMBERS - 1), 0, 0))
    asked = pl.BlockSpec((tokens, PAIR), lambda j, order: (0, jnp.minimum(j, MEMBERS - 1)))
    branch = pl.BlockSpec((tokens, SET), lambda j, order: (0, jnp.maximum(j - MEMBERS, 0) & 1))
    keys = strips(keys_grad[0], MEMBERS + 4, 1)
    values = strips(values_grad[0], MEMBERS + 6, 1)
    return call_ordered(
        packed_grad_kernel,
        2 * MEMBERS,
        [full(hidden), full(o), full(text), full(words), joint, joint, asked, asked, branch, branch]
        + [keys, keys, values, values],
        [
            grad_spec(lambda j: jnp.minimum(j, MEMBERS - 1)),
            grad_spec(lambda j: jnp.maximum(j - MEMBERS, 0)),
        ],
        [shaped((chips, 4 * HEAD, D))] * 2,
        [pltpu.VMEM((chips * HEAD, 2 * tokens), LOW), pltpu.VMEM((2 * tokens, SET), LOW)],
        order,
        (hidden, o, text, words) + joint_grad + asked_grad + branch_grad + keys_grad + values_grad,
    )


def turn_kernel(*refs):
    count = len(refs) // 3
    unit = (
        lax.broadcasted_iota(jnp.int32, (PAIR, PAIR), 0) == lax.broadcasted_iota(jnp.int32, (PAIR, PAIR), 1)
    ).astype(LOW)
    for i in range(count):
        own, other, out = refs[2 * i], refs[2 * i + 1], refs[2 * count + i]
        rows = own.shape[-2]
        for j, ref in enumerate((own, other)):
            out[:, j * rows : (j + 1) * rows] = low(dot_right_t(unit, ref[...].reshape(rows, PAIR)))


def turned(*pairs):
    def spec(x):
        if x.ndim == 3:
            return pl.BlockSpec((1, x.shape[1], PAIR), lambda j: (j, 0, 0))
        return pl.BlockSpec((x.shape[0], PAIR), lambda j: (0, j))

    rows = [pair[0].shape[-2] for pair in pairs]
    return call(
        turn_kernel,
        (D // PAIR,),
        [spec(x) for pair in pairs for x in pair],
        [pl.BlockSpec((PAIR, 2 * n), lambda j: (j, 0)) for n in rows],
        [shaped((D, 2 * n)) for n in rows],
        tuple(x for pair in pairs for x in pair),
    )


def feed_grad_kernel(order_ref, s_ref, u_ref, u2_ref, a_ref, a2_ref, f_ref, f2_ref, right_ref, left_ref, rows_ref):
    chips = len(RING)

    @pl.when(pl.program_id(0) == 0)
    def _():
        for j in range(chips):
            start = pl.multiple_of((2 * order_ref[0, j] + order_ref[2, 0]) * HEAD, HEAD)
            rows_ref[j * HEAD : (j + 1) * HEAD] = s_ref[pl.ds(start, HEAD)]

    grad = jnp.concatenate([u_ref[...], u2_ref[...]], 0)
    right_ref[...] = low(dot(rows_ref[...], grad)).reshape(chips, HEAD, STRIP)
    left_ref[0] = low(dot_left_t(a_ref[...], f_ref[...]) + dot_left_t(a2_ref[...], f2_ref[...]))


def feed_grads(order, second, upper_grad, active, feed_grad):
    tokens = upper_grad[0].shape[0]
    chips = len(RING)
    rows = FF // (2 * chips)
    strip = pl.BlockSpec((tokens, STRIP), lambda j, order: (0, j))
    hidden = pl.BlockSpec((tokens, rows), lambda j, order: (0, 2 * order[1, j] + order[2, 0]))
    full = pl.BlockSpec((tokens, D), lambda j, order: (0, 0))
    return call_ordered(
        feed_grad_kernel,
        chips,
        [pl.BlockSpec((D, 2 * tokens), lambda j, order: (0, 0)), strip, strip, hidden, hidden, full, full],
        [grad_spec(lambda j: j), pl.BlockSpec((1, rows, D), lambda j, order: (j, 0, 0))],
        [shaped((chips, 4 * HEAD, D)), shaped((chips, rows, D))],
        [pltpu.VMEM((chips * HEAD, 2 * tokens), LOW)],
        order,
        (second,) + upper_grad + active + feed_grad,
    )


def per_device(
    block_input,
    conditioning,
    text_embed,
    text_keep,
    cotangent,
    self_input,
    self_output,
    cross_query,
    cross_memory,
    cross_output,
    up_weight,
    down_weight,
    modulation,
    modulation_bias,
    position_bias,
):
    section = lax.axis_index("section")
    device = lax.axis_index("dp")
    count = lax.axis_size("dp")
    member = device & (MEMBERS - 1)
    clip = device >> 3
    clips = count // MEMBERS
    micro = block_input.shape[0]
    tokens = micro * ROWS
    shard = D // count
    words = MEMBERS * text_embed.shape[1]
    members = [list(range(c * MEMBERS, (c + 1) * MEMBERS)) for c in range(clips)]

    def chosen(first, second):
        return jnp.where(section == 1, second, first)

    def slice_at(x, start, size, axis):
        starts = [0] * x.ndim
        starts[axis] = start
        sizes = list(x.shape)
        sizes[axis] = size
        return lax.dynamic_slice(x, starts, sizes, allow_negative_indices=False)

    def trade(x):
        return lax.all_to_all(x, "dp", 0, 0, tiled=True, axis_index_groups=members)

    def collect(x):
        return trade(jnp.broadcast_to(x, (MEMBERS,) + x.shape))

    ringed = count == 2 * len(RING)

    def parts_of(x):
        x = x.reshape(-1, min(shard, ROWS_OF_PART), x.shape[1] // D, D)
        return jnp.swapaxes(x, 1, 2).reshape(-1, D)

    def gathered(pieces):
        full = [lax.all_gather(x, "dp", axis=0, tiled=True) for x in pieces]
        full = [jnp.swapaxes(x.reshape(PARTS, -1, x.shape[1] // D, D), 1, 2) for x in full]
        return jnp.concatenate([x.reshape(PARTS, -1, D) for x in full], 1)

    grouped = [x[0].reshape(shard, -1, MEMBERS, PAIR) for x in (self_input, cross_query)]
    grouped = jnp.swapaxes(low(jnp.concatenate(grouped, 1)), 1, 2).reshape(shard, 4 * D)
    ring = Stages(ring_gather(parts_of(grouped)) if ringed else no_ring(gathered([grouped])))

    cond_low = low(jax.nn.silu(high(conditioning)))
    cond_rows = slice_at(cond_low, device * shard, shard, 2)
    sums = jnp.einsum("bck,kn->cbn", cond_rows, low(modulation[0]), preferred_element_type=HIGH)
    keep = slice_at(text_keep, clip, 1, 1).astype(LOW)
    text = text_embed * keep[:, :, None]
    sums, text = ring.step(sums, text)

    bit = clips // 2
    while bit:
        upper = (clip & bit) > 0
        halves = (sums[:bit], sums[bit:])
        sums = jnp.where(upper, halves[1], halves[0]) + swap(
            jnp.where(upper, halves[0], halves[1]), bit * MEMBERS
        )
        bit //= 2
    sums = sums[0]
    (sums,) = ring.step(sums)

    text_all = collect(text)
    sums = sums + swap(sums, 1)
    (sums,) = ring.step(sums)

    sums = sums + swap(sums, 2)
    sums, text_all = ring.step(sums, text_all)

    sums = sums + swap(sums, 4)
    (sums,) = ring.step(sums)

    mods = (sums + modulation_bias[0]).reshape(micro, 6, 1, D)
    shift1, scale1, gate1, shift2, scale2, gate2 = [mods[:, i] for i in range(6)]
    hidden = low(layer_mod(high(block_input), shift1, scale1)).reshape(tokens, D)
    mods, hidden = ring.step(mods, hidden)
    shift1, scale1, gate1, shift2, scale2, gate2 = [mods[:, i] for i in range(6)]

    spread = jnp.arange(MEMBERS * CELLS)
    hot0 = place_hot(*places_of(spread // CELLS, spread % CELLS))
    own_table = slice_at(position_bias[0], 2 * member, 2, 0)
    bias0 = bias_of(own_table, hot0, hot0)
    pieces = [low(x[0]) for x in (self_output, cross_output, up_weight, cross_memory, down_weight)]
    hidden, bias0, *pieces = ring.step(hidden, bias0, *pieces)
    packed = ring.result

    def of_frames(x):
        return x.reshape(MEMBERS, -1, CELLS, x.shape[-1])

    def of_tokens(x):
        return x.reshape(MEMBERS, -1, x.shape[-1])

    def branch_and_norm(inputs, mixture, mixture_text):
        branch = merge(mixture, mixture_text, outer).reshape(micro, ROWS, D)
        middle = inputs + gate1 * branch
        second = low(layer_mod(middle, shift2, scale2)).reshape(tokens, D)
        return branch, middle, second

    def feed_forward(kept):
        upper, active, feed = feed_call(kept["second"], outer)
        feed = feed.reshape(micro, ROWS, D)
        kept.update(upper=upper, active=active, feed=feed)
        return low(kept["middle"] + gate2 * feed)

    if ringed:
        ring = Stages(ring_gather(jnp.concatenate([parts_of(x) for x in pieces], 0)))
    else:
        ring = Stages(no_ring(gathered(pieces)))
    joint, asked = project(hidden, packed)
    joint, asked = ring.step(joint, asked)
    joint = [joint[:, i * ROWS : (i + 1) * ROWS] for i in range(micro)]
    joint[0], *joint[1:] = ring.step(trade(joint[0]), *joint[1:])
    mixture, norm = [None] * micro, [None] * micro
    for i in range(micro):
        joint[i] = of_frames(joint[i])
        mixture[i], norm[i] = attend_frames(joint[i], bias0)
        mixture[i] = trade(of_tokens(mixture[i]))
        if i + 1 < micro:
            joint[i + 1], norm[i] = ring.step(trade(joint[i + 1]), norm[i])
    norm[-1], *mixture = ring.step(norm[-1], *mixture)
    mixture = jnp.concatenate(mixture, 1)
    within = jnp.arange(ROWS)
    mine, partner = places_of(member, within), places_of(member ^ 1, within)
    hot_q1 = place_hot(*mine)
    hot_k1 = jnp.concatenate([hot_q1, place_hot(*partner)])
    bias1 = bias_of(position_bias[0], hot_q1, hot_k1)
    bias1, mixture = ring.step(bias1, mixture)
    for _ in range(4 - micro):
        ring.step()
    outer = ring.result
    text_all = jnp.swapaxes(text_all, 0, 1).reshape(micro * words, D)
    memory = text_project(text_all, outer).reshape(micro, words, 2 * D)
    mixture_text, text_norm = attend_text(asked, memory)
    branch, middle, second = branch_and_norm(high(block_input), mixture, mixture_text)
    first = dict(
        x=high(block_input),
        hidden=hidden,
        joint=joint,
        asked=asked,
        norm=norm,
        mixture=mixture,
        mixture_text=mixture_text,
        text_norm=text_norm,
        branch=branch,
        middle=middle,
        second=second,
    )
    first_result = feed_forward(first)

    def back_feed(kept, grad_result):
        gate2_grad = jnp.sum(grad_result * kept["feed"], 1)
        feed_grad = low(gate2 * grad_result).reshape(tokens, D)
        upper_grad, second_grad = feed_back_call(feed_grad, kept["upper"], outer)
        kept.update(feed_grad=feed_grad, upper_grad=upper_grad, second_grad=second_grad, gate2_grad=gate2_grad)

    def back_norm2(kept, grad_result):
        second_grad = kept["second_grad"].reshape(micro, ROWS, D)
        middle_norm, shift2_grad, scale2_grad = jax.vjp(layer_mod, kept["middle"], shift2, scale2)[1](second_grad)
        middle_grad = grad_result + middle_norm
        gate1_grad = jnp.sum(middle_grad * kept["branch"], 1)
        branch_grad = low(gate1 * middle_grad).reshape(tokens, D)
        kept.update(
            middle_grad=middle_grad,
            branch_grad=branch_grad,
            late=[gate1_grad, shift2_grad[:, 0], scale2_grad[:, 0], kept["gate2_grad"]],
        )
        return merge_back(branch_grad, outer)

    def back_norm1(kept):
        hidden_grad = project_back(kept["joint_grad"], kept["asked_grad"], packed)
        inputs_norm, shift1_grad, scale1_grad = jax.vjp(layer_mod, kept["x"], shift1, scale1)[1](
            hidden_grad.reshape(micro, ROWS, D)
        )
        kept["mods"] = jnp.concatenate([shift1_grad[:, 0], scale1_grad[:, 0]] + kept["late"], 1)
        return low(kept["middle_grad"] + inputs_norm)

    received = lax.ppermute(first_result, "section", [(0, 1)])
    received, bias1 = together(received, bias1)
    inputs = high(received)
    hidden = low(layer_mod(inputs, shift1, scale1)).reshape(tokens, D)
    joint, asked = project(hidden, packed)
    other = swap(joint, 1, (1,))
    mixture_text, text_norm = attend_text(asked, memory)
    mixture, norm = attend_window(joint, other, bias1)
    branch, middle, second = branch_and_norm(inputs, mixture, mixture_text)
    latter = dict(
        x=inputs, hidden=hidden, mixture=mixture, mixture_text=mixture_text, branch=branch, middle=middle, second=second
    )
    second_result = feed_forward(latter)
    grad_result = high(cotangent)
    back_feed(latter, grad_result)
    mixture_grad, text_grad = back_norm2(latter, grad_result)
    own, sent, dbias1 = attend_window_back(joint, other, bias1, norm, mixture_grad)
    arrived = swap(sent, 1, (1,))
    latter["asked_grad"], dkt1, dvt1 = attend_text_back(asked, memory, text_norm, text_grad)
    keys = low(high(own[:, :, PAIR:]) + high(arrived))
    latter["joint_grad"] = jnp.concatenate([own[:, :, :PAIR], keys], 2)
    second_grad = back_norm1(latter)
    returned = lax.ppermute(second_grad, "section", [(1, 0)])
    names = ("second", "active", "hidden", "mixture", "mixture_text")
    second_grad, dkt1, dvt1, *kept = together(second_grad, dkt1, dvt1, *[latter[name] for name in names])
    latter.update(zip(names, kept))

    def both(name):
        return chosen(first[name], latter[name])

    ready = [both(name) for name in names]
    apart = count != 2 * len(RING)
    order = None if apart else ring_order()

    def paired(x):
        return (x, x if apart else swap(x, 1))

    def summed(x):
        return high(lax.psum_scatter(x, "dp", scatter_dimension=0, tiled=True))

    second_all, active_all, hidden_all, mixture_all, text_all2 = ready
    columns = [paired(x) for x in (hidden_all, mixture_all, text_all2)] + [(text_all, text_all), paired(second_all)]
    columns = turned(*columns)
    returned, *flat = together(returned, *columns, *paired(active_all))
    columns, active2 = flat[:5], tuple(flat[5:])

    grad_result = high(returned)
    back_feed(first, grad_result)
    upper2, feed2 = paired(both("upper_grad")), paired(both("feed_grad"))
    mixture_grad, text_grad = back_norm2(first, grad_result)
    mixture_grad = of_frames(trade(mixture_grad))
    first["asked_grad"], dkt, dvt = attend_text_back(first["asked"], memory, first["text_norm"], text_grad)
    mixture_grad, dkt, dvt = together(mixture_grad, dkt, dvt)

    def frames_back(i):
        frames = mixture_grad[:, i * FRAMES : (i + 1) * FRAMES]
        grad, dbias = attend_frames_back(first["joint"][i], bias0, first["norm"][i], frames)
        return of_tokens(grad), dbias

    joint_grad, dbias0 = frames_back(0)
    feeds = () if apart else feed_grads(order, columns[4], upper2, active2, feed2)
    traded, *feeds = together(trade(joint_grad), *feeds)
    joint_grad = [traded]
    ring = Stages(no_ring(None) if apart else ring_sums(feeds[:1], feeds[1:]))
    asked2, branch2 = paired(both("asked_grad")), paired(both("branch_grad"))
    keys2, values2 = [paired(chosen(x, y).reshape(micro * words, D)) for x, y in ((dkt, dkt1), (dvt, dvt1))]
    for i in range(1, micro):
        grad, dbias = frames_back(i)
        dbias0 = dbias0 + dbias
        grad, dbias0 = ring.step(trade(grad), dbias0)
        joint_grad.append(grad)
    flat = ring.step(*asked2, *branch2, *keys2, *values2)
    asked2, branch2, keys2, values2 = [tuple(flat[2 * i : 2 * i + 2]) for i in range(4)]
    first["joint_grad"] = jnp.concatenate(joint_grad, 1)
    joint2 = paired(both("joint_grad"))
    if apart:
        joint_all = [jnp.swapaxes(joint2[0], 0, 1), asked2[0].reshape(tokens, MEMBERS, PAIR)]
        joint_all = jnp.concatenate(joint_all, 2).reshape(tokens, 4 * D)
        rights = (joint_all, branch2[0], branch2[0], keys2[0], values2[0], upper2[0], feed2[0])
        lefts = [x[:, :tokens] for x in columns[:3]] + [text_all.T] * 2 + [columns[4][:, :tokens], active2[0].T]
        grads = [summed(low(dot(x, y))) for x, y in zip(lefts, rights)]
    else:
        grads = packed_grads(order, *columns[:4], joint2, asked2, branch2, keys2, values2)
    first["joint_grad"], dbias0, dbias1, *grads = ring.step(first["joint_grad"], dbias0, dbias1, *grads)
    for _ in range(6 - micro):
        ring.step()
    feed_part = ring.result
    ring = Stages(no_ring(grads) if apart else ring_sums(grads[:1], grads[1:]))
    first_grad = back_norm1(first)
    (first_grad,) = ring.step(first_grad)

    table0 = lax.dynamic_update_slice(
        jnp.zeros((HEADS, REL), HIGH), bias_grad(dbias0, hot0, hot0), (2 * member, 0), allow_negative_indices=False
    )
    table = chosen(table0, bias_grad(dbias1, hot_q1, hot_k1))
    small = jnp.concatenate([both("mods").reshape(micro * 6 * D), table.reshape(HEADS * REL)])
    small = jnp.pad(small, (0, -small.shape[0] % 1024)).reshape(1, -1, 128)
    (small,) = ring.step(small)
    small = small + swap(small, 1)
    (small,) = ring.step(small)
    small = small + swap(small, 2)
    (small,) = ring.step(small)
    small = small + swap(small, 4)
    (small,) = ring.step(small)
    bit = 1
    while bit < clips:
        far = swap(small, bit * MEMBERS)
        upper = (clip & bit) > 0
        small = jnp.concatenate([jnp.where(upper, far, small), jnp.where(upper, small, far)])
        bit *= 2
    (small,) = ring.step(small)
    small = small.reshape(clips, -1)
    mods_all = small[:, : micro * 6 * D].reshape(clips, micro, 6 * D)
    table_sum = jnp.sum(small[:, micro * 6 * D : micro * 6 * D + HEADS * REL], 0).reshape(HEADS, REL)
    modul_shard = jnp.einsum("bck,cbn->kn", high(cond_rows), mods_all, precision=lax.Precision.HIGHEST)
    bias_sum = jnp.sum(mods_all, (0, 1))
    modul_shard, bias_sum, table_sum = ring.step(modul_shard, bias_sum, table_sum)

    if apart:
        grouped, out_shard, cross_shard, keys, values, up_shard, down_shard = ring.result
        memory_shard = jnp.concatenate([keys, values], 1)
    else:
        (grouped, outputs), (up_shard, down_shard) = ring.result, feed_part
        grouped, up_shard = [
            jnp.swapaxes(x.reshape(4, shard, D), 0, 1).reshape(shard, 4 * D) for x in (grouped, up_shard)
        ]
        out_shard, cross_shard = outputs[:shard], outputs[shard : 2 * shard]
        memory_shard = jnp.concatenate([outputs[2 * shard : 3 * shard], outputs[3 * shard :]], 1)
    grouped = jnp.swapaxes(grouped.reshape(shard, MEMBERS, 4, PAIR), 1, 2).reshape(shard, 4 * D)
    in_shard, query_shard = grouped[:, : 3 * D], grouped[:, 3 * D :]
    outputs = chosen(first_result, second_result)
    input_grads = chosen(first_grad, second_grad)
    return tuple(
        x[None]
        for x in (
            outputs,
            input_grads,
            in_shard,
            out_shard,
            query_shard,
            memory_shard,
            cross_shard,
            up_shard,
            down_shard,
            modul_shard,
            bias_sum,
            table_sum,
        )
    )


def solution(mesh):
    weights = P("section", "dp", None)
    return jax.shard_map(
        per_device,
        mesh=mesh,
        in_specs=(
            P(None, "dp", None),
            P(),
            P(None, "dp", None),
            P(),
            P(None, "dp", None),
        )
        + (weights,) * 8
        + (P("section", None), P("section", None, None)),
        out_specs=(P("section", None, "dp", None),) * 2
        + (weights,) * 8
        + (P("section", None), P("section", None, None)),
        check_vma=False,
    )
```

time: 1060 us -> 752 us (0.71)
  matrix products: 147 us -> 20.6 us
  Pallas kernels: 136 us -> 199 us
  waiting for transfers between devices: 322 us -> 260 us
  between operations: 57.4 us -> 4.37 us
  other arithmetic: 103 us -> 65 us
  starting transfers between devices: 156 us -> 118 us
  local copies, waits for them, and re-layouts: 108 us -> 72.6 us
  blocking collectives: 22.5 us -> 0 us
    dot_general x33 -> x1, matrix products: 131 us -> 2.7 us  [per_device(): jnp.einsum('bck,cbn->kn', high(cond_rows), mods_all, precision=lax.Precis...]
    all_gather x6 -> x0, waiting for transfers between devices: 84.2 us -> none  [gathered(): return lax.all_gather(low(x[0]), 'dp', axis=0, tiled=True)]
    ppermute x54, starting transfers between devices: 102 us -> 21.7 us  [swap(): return lax.ppermute(x, ('section', 'dp'), route)]
    pallas_call x8 -> x30, Pallas kernels: 136 us -> 199 us  [the longest x24 143 us: call(): pl.pallas_call(kernel, grid=grid, in_specs=in_specs, out_specs=out_specs,...]
    ppermute x42 -> x56, waiting for transfers between devices: 121 us -> 159 us  [hop(): return lax.ppermute(x, ('section', 'dp'), route)]
    convert_element_type x56 -> x37, other arithmetic: 62.6 us -> 28.2 us  [low(): return v.astype(LOW)]
    ppermute x54, waiting for transfers between devices: 86.5 us -> 53.2 us  [swap(): return lax.ppermute(x, ('section', 'dp'), route)]
    ppermute x42 -> x56, starting transfers between devices: 36.3 us -> 60.1 us  [hop(): return lax.ppermute(x, ('section', 'dp'), route)]
  transfers between devices with their start and end apart: 107 -> 120, of which waited for: 54 -> 54; matrix products, arithmetic and copies ran while one was open for 23% -> 11% of each run, Pallas kernels for 9% -> 12%
where the time goes in v2:
time: 752 us; the launch traced here: 740 us
  waiting for transfers between devices  260 us (35%)
  Pallas kernels  199 us (26%)
  starting transfers between devices  118 us (16%)
  local copies, waits for them, and re-layouts  72.6 us (10%)
  other arithmetic  65 us (9%)
  matrix products  20.6 us (3%)
    ppermute x56, waiting for transfers between devices, hop(): return lax.ppermute(x, ('section', 'dp'), route)  159 us
    pallas_call x24, Pallas kernels, call(): pl.pallas_call(kernel, grid=grid, in_specs=in_specs, out_specs=out_specs,...  143 us
    ppermute x56, starting transfers between devices, hop(): return lax.ppermute(x, ('section', 'dp'), route)  60.1 us
    unnamed x473, local copies, waits for them, and re-layouts  53.3 us
    ppermute x54, waiting for transfers between devices, swap(): return lax.ppermute(x, ('section', 'dp'), route)  53.2 us
    all_to_all x8, starting transfers between devices, trade(): return lax.all_to_all(x, 'dp', 0, 0, tiled=True, axis_index_groups=members)  31.8 us
    pallas_call x4, Pallas kernels, assembled(): pl.pallas_call(kernel, grid_spec=pltpu.PrefetchScalarGridSpec(num_scalar_...  29.1 us
    convert_element_type x37, other arithmetic, low(): return v.astype(LOW)  28.2 us
  transfers between devices with their start and end apart: 120, of which 54 were waited for; matrix products, arithmetic and copies ran while one was open for 11% of the time, Pallas kernels for 12%

profile of v2, /device:TPU:0, one launch (start us, length us, event | category | flops | bytes accessed | tf_op | source)
XLA Modules:
  0.0 739.6 jit_solution(831618642192468077)
XLA Ops:
  23.5 3.7 collective-permute-done.2.refs_8_
  32.9 3.5 all-to-all-start
  42.6 7.2 collective-permute-done.16
  53.7 7.1 collective-permute-done.21
  65.7 4.1 collective-permute-done.22.refs_4_
  69.8 4.2 collective-permute-done.23.refs_5_
  77.4 5.0 collective-permute-done.26.refs_8_
  89.4 5.7 shard_map.274.refs_12_
  98.1 3.5 shard_map.275
  101.6 3.4 copy-done.2
  105.0 4.8 shard_map.276
  111.3 3.7 all-to-all-start.1
  118.7 26.8 %collective-permute-done.36.refs_8_ = bf16[384,1024]{1,0:T(8,128)(2,1)S(1)} collective-permute-done((bf16[384,1024]{1,0:T(8,128)(2,1)}, bf16[384,1024]{1,0:T(8,128)(2,1)S(1)}, u32[]{:S(2)}, u32[]{:S(2)}) %collective-permute-start.36) | collective-permute-done | bytes 786464 | tf_op jit(solution)/shard_map/ppermute | solution.py:563
  146.4 3.9 all-to-all-start.2
  155.9 8.5 %all-to-all-done.2 = bf16[8,160,384]{2,1,0:T(8,128)(2,1)S(1)} async-done(((bf16[8,160,384]{2,1,0:T(8,128)(2,1)}), bf16[8,160,384]{2,1,0:T(8,128)(2,1)S(1)}, u32[]{:S(2)}, u32[]{:S(2)}) %all-to-all-start.2) | async-done | bytes 983072 | tf_op jit(solution)/shard_map/all_to_all | solution.py:873
  164.5 3.6 all-to-all-start.3
  168.7 12.7 %collective-permute-done.40.refs_12_ = bf16[384,1024]{1,0:T(8,128)(2,1)} collective-permute-done((bf16[384,1024]{1,0:T(8,128)(2,1)}, bf16[384,1024]{1,0:T(8,128)(2,1)}, u32[]{:S(2)}, u32[]{:S(2)}) %collective-permute-start.40) | collective-permute-done | bytes 786464 | tf_op jit(solution)/shard_map/ppermute | solution.py:563
  186.5 4.1 all-to-all-start.4
  193.7 11.1 %all-to-all-done.4 = bf16[8,160,128]{2,1,0:T(8,128)(2,1)} async-done(((bf16[8,160,128]{2,1,0:T(8,128)(2,1)}), bf16[8,160,128]{2,1,0:T(8,128)(2,1)}, u32[]{:S(2)}, u32[]{:S(2)}) %all-to-all-start.4) | async-done | bytes 327712 | tf_op jit(solution)/shard_map/all_to_all | solution.py:873
  207.5 3.8 fusion.88.bias_ref
  213.0 11.2 %collective-permute-done.48.refs_0_ = bf16[384,1024]{1,0:T(8,128)(2,1)S(1)} collective-permute-done((bf16[384,1024]{1,0:T(8,128)(2,1)}, bf16[384,1024]{1,0:T(8,128)(2,1)S(1)}, u32[]{:S(2)}, u32[]{:S(2)}) %collective-permute-start.48) | collective-permute-done | bytes 786464 | tf_op jit(solution)/shard_map/ppermute | solution.py:563
  227.0 15.6 %collective-permute-done.52.refs_4_ = bf16[384,1024]{1,0:T(8,128)(2,1)} collective-permute-done((bf16[384,1024]{1,0:T(8,128)(2,1)S(1)}, bf16[384,1024]{1,0:T(8,128)(2,1)}, u32[]{:S(2)}, u32[]{:S(2)}) %collective-permute-start.52) | collective-permute-done | bytes 786464 | tf_op jit(solution)/shard_map/ppermute | solution.py:563
  244.7 12.0 %shard_map.279.refs_12_ = bf16[8,2,768,1024]{3,2,1,0:T(8,128)(2,1)} custom-call(s32[9]{0:T(128)} %pad_add_fusion.order_ref, bf16[384,1024]{1,0:T(8,128)(2,1)} %copy-done.131, bf16[384,1024]{1,0:T(8,128)(2,1)} %pad_maximum_fusion.2.refs_1_, bf16[384,1024]{1,0:T(8,128)(2,1)} %copy-done.149, bf16[384,1024]{1,0:T(8,128)(2,1)} %copy-done.150, ...), custom_call_target="tpu_custom_call" | custom-call | flops 1 | bytes 1 | tf_op jit(solution)/shard_map/pallas_call | solution.py:624
  263.9 7.9 %shard_map.280 = bf16[8,2,768,1024]{3,2,1,0:T(8,128)(2,1)} custom-call(s32[9]{0:T(128)} %pad_add_fusion.order_ref, bf16[384,1024]{1,0:T(8,128)(2,1)} %copy-done.144, bf16[384,1024]{1,0:T(8,128)(2,1)} %copy-done.145, bf16[384,1024]{1,0:T(8,128)(2,1)} %copy-done.146, bf16[384,1024]{1,0:T(8,128)(2,1)} %copy-done.147, ...), custom_call_target="tpu_custom_call", output_to_operand_aliasing={{}: (13, {})} | custom-call | flops 1 | bytes 1 | tf_op jit(solution)/shard_map/pallas_call | solution.py:624
  271.8 3.7 shard_map.281
  278.3 3.7 shard_map.283
  283.8 13.9 %shard_map.284 = (f32[320,4096]{1,0:T(8,128)S(1)}, bf16[320,4096]{1,0:T(8,128)(2,1)S(1)}, f32[320,1024]{1,0:T(8,128)S(1)}) custom-call(bf16[320,1024]{1,0:T(8,128)(2,1)S(1)} %bitcast.323, bf16[16,768,1024]{2,1,0:T(8,128)(2,1)} %bitcast.348, bf16[16,768,1024]{2,1,0:T(8,128)(2,1)} %bitcast.349), custom_call_target="tpu_custom_call" | custom-call | flops 1 | bytes 1 | tf_op jit(solution)/shard_map/pallas_call | solution.py:196
  301.8 3.4 collective-permute-start.64
  305.3 14.3 %collective-permute-done.64 = bf16[2,160,1024]{2,1,0:T(8,128)(2,1)S(1)} collective-permute-done((bf16[2,160,1024]{2,1,0:T(8,128)(2,1)S(1)}, bf16[2,160,1024]{2,1,0:T(8,128)(2,1)S(1)}, u32[]{:S(2)}, u32[]{:S(2)}) %collective-permute-start.64) | collective-permute-done | bytes 655392 | tf_op jit(solution)/shard_map/ppermute | solution.py:1025
  320.5 4.8 shard_map.285
  329.0 4.7 shard_map.286
  333.8 3.6 shard_map.288
  338.3 12.9 %shard_map.289 = (f32[320,4096]{1,0:T(8,128)S(1)}, bf16[320,4096]{1,0:T(8,128)(2,1)S(1)}, f32[320,1024]{1,0:T(8,128)S(1)}) custom-call(bf16[320,1024]{1,0:T(8,128)(2,1)S(1)} %bitcast.324, bf16[16,768,1024]{2,1,0:T(8,128)(2,1)} %bitcast.352, bf16[16,768,1024]{2,1,0:T(8,128)(2,1)} %bitcast.353), custom_call_target="tpu_custom_call" | custom-call | flops 1 | bytes 1 | tf_op jit(solution)/shard_map/pallas_call | solution.py:196
  352.7 14.0 %shard_map.290 = (bf16[320,4096]{1,0:T(8,128)(2,1)S(1)}, f32[320,1024]{1,0:T(8,128)S(1)}) custom-call(bf16[320,1024]{1,0:T(8,128)(2,1)S(1)} %bitcast.322, f32[320,4096]{1,0:T(8,128)S(1)} %get-tuple-element.401.upper_ref, bf16[16,768,1024]{2,1,0:T(8,128)(2,1)} %bitcast.354, bf16[16,768,1024]{2,1,0:T(8,128)(2,1)} %bitcast.355), custom_call_target="tpu_custom_call" | custom-call | flops 1 | bytes 1 | tf_op jit(solution)/shard_map/pallas_call | solution.py:196
  369.8 4.5 shard_map.291
  375.1 10.6 %shard_map.292 = (bf16[8,320,384]{2,1,0:T(8,128)(2,1)S(1)}, bf16[8,320,256]{2,1,0:T(8,128)(2,1)}, f32[16,160,320]{2,1,0:T(8,128)S(1)}) custom-call(bf16[8,320,384]{2,1,0:T(8,128)(2,1)S(1)} %get-tuple-element.395.own_ref, bf16[8,320,384]{2,1,0:T(8,128)(2,1)S(1)} %collective-permute-done.65.other_ref, f32[16,160,320]{2,1,0:T(8,128)S(1)} %copy-done.5, ...), custom_call_target="tpu_custom_call" | custom-call | flops 1 | bytes 1 | tf_op jit(solution)/shard_map/pallas_call | solution.py:196
  394.0 4.8 shard_map.293
  402.5 3.4 copy-done.3
  405.9 6.2 shard_map.294
  424.8 5.6 shard_map.295
  433.7 9.8 %collective-permute-done.67 = bf16[2,160,1024]{2,1,0:T(8,128)(2,1)S(1)} collective-permute-done((bf16[2,160,1024]{2,1,0:T(8,128)(2,1)S(1)}, bf16[2,160,1024]{2,1,0:T(8,128)(2,1)S(1)}, u32[]{:S(2)}, u32[]{:S(2)}) %collective-permute-start.67) | collective-permute-done | bytes 655392 | tf_op jit(solution)/shard_map/ppermute | solution.py:1047
  443.7 14.8 %shard_map.296 = (bf16[320,4096]{1,0:T(8,128)(2,1)S(1)}, f32[320,1024]{1,0:T(8,128)S(1)}) custom-call(bf16[320,1024]{1,0:T(8,128)(2,1)S(1)} %bitcast.326, f32[320,4096]{1,0:T(8,128)S(1)} %bitcast.338, bf16[16,768,1024]{2,1,0:T(8,128)(2,1)} %bitcast.358, bf16[16,768,1024]{2,1,0:T(8,128)(2,1)} %bitcast.359), custom_call_target="tpu_custom_call" | custom-call | flops 1 | bytes 1 | tf_op jit(solution)/shard_map/pallas_call | solution.py:196
  461.6 4.4 shard_map.297
  467.8 4.6 all-to-all-start.5
  472.4 3.6 broadcast_select_fusion.u_ref
  476.4 4.9 shard_map.298
  491.0 4.2 all-to-all-start.6
  505.4 3.5 all-to-all-done.6
  509.0 4.2 all-to-all-start.7
  516.5 12.2 %shard_map.300 = (bf16[8,256,1024]{2,1,0:T(8,128)(2,1)S(1)}, bf16[8,256,1024]{2,1,0:T(8,128)(2,1)S(1)}) custom-call(s32[3,8]{1,0:T(4,128)S(1)} %add_add_fusion.4.order_ref, bf16[1024,640]{1,0:T(8,128)(2,1)S(1)} %copy-done.77, bf16[320,4096]{1,0:T(8,128)(2,1)} %broadcast_select_fusion.u_ref, bf16[320,4096]{1,0:T(8,128)(2,1)} %collective-permute-done.73.u2_ref, ...), custom_call_target="tpu_custom_call" | custom-call | flops 1 | bytes 1 | tf_op jit(solution)/shard_map/pallas_call | solution.py:686
  535.0 9.0 %collective-permute-done.75 = bf16[256,1024]{1,0:T(8,128)(2,1)} collective-permute-done((bf16[256,1024]{1,0:T(8,128)(2,1)}, bf16[256,1024]{1,0:T(8,128)(2,1)}, u32[]{:S(2)}, u32[]{:S(2)}) %collective-permute-start.75) | collective-permute-done | bytes 524320 | tf_op jit(solution)/shard_map/ppermute | solution.py:563
  555.8 8.4 %collective-permute-done.77 = bf16[256,1024]{1,0:T(8,128)(2,1)S(1)} collective-permute-done((bf16[256,1024]{1,0:T(8,128)(2,1)S(1)}, bf16[256,1024]{1,0:T(8,128)(2,1)S(1)}, u32[]{:S(2)}, u32[]{:S(2)}) %collective-permute-start.77) | collective-permute-done | bytes 524320 | tf_op jit(solution)/shard_map/ppermute | solution.py:563
  571.3 14.9 %shard_map.302 = (bf16[8,256,1024]{2,1,0:T(8,128)(2,1)S(1)}, bf16[8,256,1024]{2,1,0:T(8,128)(2,1)S(1)}) custom-call(s32[3,8]{1,0:T(4,128)S(1)} %add_add_fusion.4.order_ref, bf16[1024,640]{1,0:T(8,128)(2,1)S(1)} %copy-done.71, bf16[1024,640]{1,0:T(8,128)(2,1)S(1)} %copy-done.73, bf16[1024,640]{1,0:T(8,128)(2,1)S(1)} %copy-done.75, ...), custom_call_target="tpu_custom_call" | custom-call | flops 1 | bytes 1 | tf_op jit(solution)/shard_map/pallas_call | solution.py:686
  590.1 6.2 shard_map.303
  600.9 4.8 fusion.87
  618.5 6.5 collective-permute-done.104
  631.7 4.5 collective-permute-done.88
  647.4 3.2 collective-permute-done.107
  654.4 4.3 collective-permute-done.90
  664.5 5.4 collective-permute-done.108
  676.7 6.5 collective-permute-done.95
  690.1 3.5 collective-permute-done.110
  695.6 8.9 %collective-permute-done.98 = f32[1,112,128]{2,1,0:T(8,128)S(1)} collective-permute-done((f32[1,112,128]{2,1,0:T(8,128)S(1)}, f32[1,112,128]{2,1,0:T(8,128)S(1)}, u32[]{:S(2)}, u32[]{:S(2)}) %collective-permute-start.98) | collective-permute-done | bytes 57376 | tf_op jit(solution)/shard_map/ppermute | solution.py:60
  709.7 11.2 %collective-permute-done.101 = f32[1,112,128]{2,1,0:T(8,128)S(1)} collective-permute-done((f32[1,112,128]{2,1,0:T(8,128)S(1)}, f32[1,112,128]{2,1,0:T(8,128)S(1)}, u32[]{:S(2)}, u32[]{:S(2)}) %collective-permute-start.101) | collective-permute-done | bytes 57376 | tf_op jit(solution)/shard_map/ppermute | solution.py:60
  (873 shorter events, 280.4 us)
Async XLA Ops:
  7.5 15.9 %collective-permute-start.4 = (bf16[128,1024]{1,0:T(8,128)(2,1)S(1)}, bf16[128,1024]{1,0:T(8,128)(2,1)}, u32[]{:S(2)}, u32[]{:S(2)}) collective-permute-start(bf16[128,1024]{1,0:T(8,128)(2,1)S(1)} %bitcast.375), channel_id=1, source_target_pairs={{0,1},{1,0},{2,3},{3,2},{4,5},{5,4},{6,7},{7,6},{8,9},{9,8},{10,11... | collective-permute-start | bytes 786440 | tf_op jit(solution)/shard_map/ppermute | solution.py:60
  7.6 15.8 %collective-permute-start.5 = (bf16[128,1024]{1,0:T(8,128)(2,1)S(1)}, bf16[128,1024]{1,0:T(8,128)(2,1)}, u32[]{:S(2)}, u32[]{:S(2)}) collective-permute-start(bf16[128,1024]{1,0:T(8,128)(2,1)S(1)} %bitcast.378), channel_id=1, source_target_pairs={{0,1},{1,0},{2,3},{3,2},{4,5},{5,4},{6,7},{7,6},{8,9},{9,8},{10,11... | collective-permute-start | bytes 786440 | tf_op jit(solution)/shard_map/ppermute | solution.py:60
  20.7 17.5 %collective-permute-start.9 = (bf16[128,1024]{1,0:T(8,128)(2,1)}, bf16[128,1024]{1,0:T(8,128)(2,1)}, u32[]{:S(2)}, u32[]{:S(2)}) collective-permute-start(bf16[128,1024]{1,0:T(8,128)(2,1)} %collective-permute-done.refs_4_), channel_id=1, source_target_pairs={{0,1},{1,0},{2,3},{3,2},{4,5},{5,4},{6,7},{7,6},{8,9},{9,8},{10,11... | collective-permute-start | bytes 786440 | tf_op jit(solution)/shard_map/ppermute | solution.py:60
  32.9 17.6 %all-to-all-start = ((bf16[8,2,10,1024]{3,1,2,0:T(2,128)(2,1)}), bf16[8,2,10,1024]{3,1,2,0:T(2,128)(2,1)S(1)}, u32[]{:S(2)}, u32[]{:S(2)}) async-start(bf16[8,2,10,1024]{3,1,2,0:T(2,128)(2,1)} %broadcast_in_dim.44), calls=%async_computation | async-start | bytes 655360 | tf_op jit(solution)/shard_map/all_to_all | solution.py:873
  84.4 25.3 %collective-permute-start.30 = (bf16[384,1024]{1,0:T(8,128)(2,1)S(1)}, bf16[384,1024]{1,0:T(8,128)(2,1)}, u32[]{:S(2)}, u32[]{:S(2)}) collective-permute-start(bf16[384,1024]{1,0:T(8,128)(2,1)S(1)} %pad_maximum_fusion.1.refs_0_), channel_id=1, source_target_pairs={{0,4},{1,5},{4,8},{5,9},{8,12},{9,13},{12,14},{13,15},{14,10},{15,... | collective-permute-start | bytes 2359304 | tf_op jit(solution)/shard_map/ppermute | solution.py:563
  86.5 23.3 %collective-permute-start.31 = (bf16[384,1024]{1,0:T(8,128)(2,1)}, bf16[384,1024]{1,0:T(8,128)(2,1)}, u32[]{:S(2)}, u32[]{:S(2)}) collective-permute-start(bf16[384,1024]{1,0:T(8,128)(2,1)} %pad_maximum_fusion.2.refs_1_), channel_id=1, source_target_pairs={{0,2},{1,3},{4,0},{5,1},{8,4},{9,5},{12,8},{13,9},{14,12},{15,13},... | collective-permute-start | bytes 2359304 | tf_op jit(solution)/shard_map/ppermute | solution.py:563
  111.3 35.1 %all-to-all-start.1 = ((bf16[8,160,384]{2,1,0:T(8,128)(2,1)}), bf16[8,160,384]{2,1,0:T(8,128)(2,1)S(1)}, u32[]{:S(2)}, u32[]{:S(2)}) async-start(bf16[8,160,384]{2,1,0:T(8,128)(2,1)} %get-tuple-element.541), calls=%async_computation.1 | async-start | bytes 1966080 | tf_op jit(solution)/shard_map/all_to_all | solution.py:873
  115.6 29.9 %collective-permute-start.36 = (bf16[384,1024]{1,0:T(8,128)(2,1)}, bf16[384,1024]{1,0:T(8,128)(2,1)S(1)}, u32[]{:S(2)}, u32[]{:S(2)}) collective-permute-start(bf16[384,1024]{1,0:T(8,128)(2,1)} %collective-permute-done.30.refs_4_), channel_id=1, source_target_pairs={{0,4},{1,5},{4,8},{5,9},{8,12},{9,13},{12,14},{13,15},{14,10},{15,... | collective-permute-start | bytes 2359304 | tf_op jit(solution)/shard_map/ppermute | solution.py:563
  117.4 29.0 %collective-permute-start.37 = (bf16[384,1024]{1,0:T(8,128)(2,1)}, bf16[384,1024]{1,0:T(8,128)(2,1)}, u32[]{:S(2)}, u32[]{:S(2)}) collective-permute-start(bf16[384,1024]{1,0:T(8,128)(2,1)} %collective-permute-done.31.refs_5_), channel_id=1, source_target_pairs={{0,2},{1,3},{4,0},{5,1},{8,4},{9,5},{12,8},{13,9},{14,12},{15,13},... | collective-permute-start | bytes 2359304 | tf_op jit(solution)/shard_map/ppermute | solution.py:563
  146.4 18.1 %all-to-all-start.2 = ((bf16[8,160,384]{2,1,0:T(8,128)(2,1)}), bf16[8,160,384]{2,1,0:T(8,128)(2,1)S(1)}, u32[]{:S(2)}, u32[]{:S(2)}) async-start(bf16[8,160,384]{2,1,0:T(8,128)(2,1)} %get-tuple-element.335), calls=%async_computation.2 | async-start | bytes 1966080 | tf_op jit(solution)/shard_map/all_to_all | solution.py:873
  150.3 18.3 %collective-permute-start.42 = (bf16[384,1024]{1,0:T(8,128)(2,1)}, bf16[384,1024]{1,0:T(8,128)(2,1)}, u32[]{:S(2)}, u32[]{:S(2)}) collective-permute-start(bf16[384,1024]{1,0:T(8,128)(2,1)} %collective-permute-done.30.refs_4_), channel_id=1, source_target_pairs={{0,1},{1,0},{2,3},{3,2},{4,5},{5,4},{6,7},{7,6},{8,9},{9,8},{10,11... | collective-permute-start | bytes 2359304 | tf_op jit(solution)/shard_map/ppermute | solution.py:60
  150.7 18.0 %collective-permute-start.43 = (bf16[384,1024]{1,0:T(8,128)(2,1)}, bf16[384,1024]{1,0:T(8,128)(2,1)}, u32[]{:S(2)}, u32[]{:S(2)}) collective-permute-start(bf16[384,1024]{1,0:T(8,128)(2,1)} %collective-permute-done.31.refs_5_), channel_id=1, source_target_pairs={{0,1},{1,0},{2,3},{3,2},{4,5},{5,4},{6,7},{7,6},{8,9},{9,8},{10,11... | collective-permute-start | bytes 2359304 | tf_op jit(solution)/shard_map/ppermute | solution.py:60
  150.9 30.5 %collective-permute-start.40 = (bf16[384,1024]{1,0:T(8,128)(2,1)}, bf16[384,1024]{1,0:T(8,128)(2,1)}, u32[]{:S(2)}, u32[]{:S(2)}) collective-permute-start(bf16[384,1024]{1,0:T(8,128)(2,1)} %copy-done.151), channel_id=1, source_target_pairs={{0,4},{1,5},{4,8},{5,9},{8,12},{9,13},{12,14},{13,15},{14,10},{15,... | collective-permute-start | bytes 2359304 | tf_op jit(solution)/shard_map/ppermute | solution.py:563
  152.8 28.7 %collective-permute-start.41 = (bf16[384,1024]{1,0:T(8,128)(2,1)}, bf16[384,1024]{1,0:T(8,128)(2,1)}, u32[]{:S(2)}, u32[]{:S(2)}) collective-permute-start(bf16[384,1024]{1,0:T(8,128)(2,1)} %collective-permute-done.37.refs_9_), channel_id=1, source_target_pairs={{0,2},{1,3},{4,0},{5,1},{8,4},{9,5},{12,8},{13,9},{14,12},{15,13},... | collective-permute-start | bytes 2359304 | tf_op jit(solution)/shard_map/ppermute | solution.py:563
  164.5 22.0 %all-to-all-start.3 = ((bf16[8,160,128]{2,1,0:T(8,128)(2,1)}), bf16[8,160,128]{2,1,0:T(8,128)(2,1)S(1)}, u32[]{:S(2)}, u32[]{:S(2)}) async-start(bf16[8,160,128]{2,1,0:T(8,128)(2,1)} %bitcast.26), calls=%async_computation.3 | async-start | bytes 655360 | tf_op jit(solution)/shard_map/all_to_all | solution.py:873
  168.1 25.5 %collective-permute-start.46 = (bf16[384,1024]{1,0:T(8,128)(2,1)}, bf16[384,1024]{1,0:T(8,128)(2,1)}, u32[]{:S(2)}, u32[]{:S(2)}) collective-permute-start(bf16[384,1024]{1,0:T(8,128)(2,1)} %copy-done.151), channel_id=1, source_target_pairs={{0,1},{1,0},{2,3},{3,2},{4,5},{5,4},{6,7},{7,6},{8,9},{9,8},{10,11... | collective-permute-start | bytes 2359304 | tf_op jit(solution)/shard_map/ppermute | solution.py:60
  168.6 25.2 %collective-permute-start.47 = (bf16[384,1024]{1,0:T(8,128)(2,1)}, bf16[384,1024]{1,0:T(8,128)(2,1)}, u32[]{:S(2)}, u32[]{:S(2)}) collective-permute-start(bf16[384,1024]{1,0:T(8,128)(2,1)} %collective-permute-done.37.refs_9_), channel_id=1, source_target_pairs={{0,1},{1,0},{2,3},{3,2},{4,5},{5,4},{6,7},{7,6},{8,9},{9,8},{10,11... | collective-permute-start | bytes 2359304 | tf_op jit(solution)/shard_map/ppermute | solution.py:60
  181.4 23.5 %collective-permute-start.44 = (bf16[384,1024]{1,0:T(8,128)(2,1)}, bf16[384,1024]{1,0:T(8,128)(2,1)}, u32[]{:S(2)}, u32[]{:S(2)}) collective-permute-start(bf16[384,1024]{1,0:T(8,128)(2,1)} %collective-permute-done.40.refs_12_), channel_id=1, source_target_pairs={{0,4},{1,5},{4,8},{5,9},{8,12},{9,13},{12,14},{13,15},{14,10},{15,... | collective-permute-start | bytes 2359304 | tf_op jit(solution)/shard_map/ppermute | solution.py:563
  181.6 23.3 %collective-permute-start.45 = (bf16[384,1024]{1,0:T(8,128)(2,1)}, bf16[384,1024]{1,0:T(8,128)(2,1)}, u32[]{:S(2)}, u32[]{:S(2)}) collective-permute-start(bf16[384,1024]{1,0:T(8,128)(2,1)} %collective-permute-done.41.refs_13_), channel_id=1, source_target_pairs={{0,2},{1,3},{4,0},{5,1},{8,4},{9,5},{12,8},{13,9},{14,12},{15,13},... | collective-permute-start | bytes 2359304 | tf_op jit(solution)/shard_map/ppermute | solution.py:563
  186.5 18.4 %all-to-all-start.4 = ((bf16[8,160,128]{2,1,0:T(8,128)(2,1)}), bf16[8,160,128]{2,1,0:T(8,128)(2,1)}, u32[]{:S(2)}, u32[]{:S(2)}) async-start(bf16[8,160,128]{2,1,0:T(8,128)(2,1)} %bitcast.27), calls=%async_computation.4 | async-start | bytes 655360 | tf_op jit(solution)/shard_map/all_to_all | solution.py:873
  193.2 19.3 %collective-permute-start.50 = (bf16[384,1024]{1,0:T(8,128)(2,1)}, bf16[384,1024]{1,0:T(8,128)(2,1)}, u32[]{:S(2)}, u32[]{:S(2)}) collective-permute-start(bf16[384,1024]{1,0:T(8,128)(2,1)} %collective-permute-done.40.refs_12_), channel_id=1, source_target_pairs={{0,1},{1,0},{2,3},{3,2},{4,5},{5,4},{6,7},{7,6},{8,9},{9,8},{10,11... | collective-permute-start | bytes 2359304 | tf_op jit(solution)/shard_map/ppermute | solution.py:60
  193.6 19.4 %collective-permute-start.51 = (bf16[384,1024]{1,0:T(8,128)(2,1)}, bf16[384,1024]{1,0:T(8,128)(2,1)}, u32[]{:S(2)}, u32[]{:S(2)}) collective-permute-start(bf16[384,1024]{1,0:T(8,128)(2,1)} %collective-permute-done.41.refs_13_), channel_id=1, source_target_pairs={{0,1},{1,0},{2,3},{3,2},{4,5},{5,4},{6,7},{7,6},{8,9},{9,8},{10,11... | collective-permute-start | bytes 2359304 | tf_op jit(solution)/shard_map/ppermute | solution.py:60
  204.9 19.3 %collective-permute-start.48 = (bf16[384,1024]{1,0:T(8,128)(2,1)}, bf16[384,1024]{1,0:T(8,128)(2,1)S(1)}, u32[]{:S(2)}, u32[]{:S(2)}) collective-permute-start(bf16[384,1024]{1,0:T(8,128)(2,1)} %collective-permute-done.44.refs_16_), channel_id=1, source_target_pairs={{0,4},{1,5},{4,8},{5,9},{8,12},{9,13},{12,14},{13,15},{14,10},{15,... | collective-permute-start | bytes 2359304 | tf_op jit(solution)/shard_map/ppermute | solution.py:563
  205.7 18.8 %collective-permute-start.49 = (bf16[384,1024]{1,0:T(8,128)(2,1)}, bf16[384,1024]{1,0:T(8,128)(2,1)S(1)}, u32[]{:S(2)}, u32[]{:S(2)}) collective-permute-start(bf16[384,1024]{1,0:T(8,128)(2,1)} %collective-permute-done.45.refs_17_), channel_id=1, source_target_pairs={{0,2},{1,3},{4,0},{5,1},{8,4},{9,5},{12,8},{13,9},{14,12},{15,13},... | collective-permute-start | bytes 2359304 | tf_op jit(solution)/shard_map/ppermute | solution.py:563
  224.4 18.2 %collective-permute-start.52 = (bf16[384,1024]{1,0:T(8,128)(2,1)S(1)}, bf16[384,1024]{1,0:T(8,128)(2,1)}, u32[]{:S(2)}, u32[]{:S(2)}) collective-permute-start(bf16[384,1024]{1,0:T(8,128)(2,1)S(1)} %collective-permute-done.48.refs_0_), channel_id=1, source_target_pairs={{0,4},{1,5},{4,8},{5,9},{8,12},{9,13},{12,14},{13,15},{14,10},{15,... | collective-permute-start | bytes 2359304 | tf_op jit(solution)/shard_map/ppermute | solution.py:563
  224.8 17.9 %collective-permute-start.53 = (bf16[384,1024]{1,0:T(8,128)(2,1)S(1)}, bf16[384,1024]{1,0:T(8,128)(2,1)}, u32[]{:S(2)}, u32[]{:S(2)}) collective-permute-start(bf16[384,1024]{1,0:T(8,128)(2,1)S(1)} %collective-permute-done.49.refs_1_), channel_id=1, source_target_pairs={{0,2},{1,3},{4,0},{5,1},{8,4},{9,5},{12,8},{13,9},{14,12},{15,13},... | collective-permute-start | bytes 2359304 | tf_op jit(solution)/shard_map/ppermute | solution.py:563
  226.4 30.3 %collective-permute-start.58 = (bf16[384,1024]{1,0:T(8,128)(2,1)S(1)}, bf16[384,1024]{1,0:T(8,128)(2,1)S(1)}, u32[]{:S(2)}, u32[]{:S(2)}) collective-permute-start(bf16[384,1024]{1,0:T(8,128)(2,1)S(1)} %collective-permute-done.48.refs_0_), channel_id=1, source_target_pairs={{0,1},{1,0},{2,3},{3,2},{4,5},{5,4},{6,7},{7,6},{8,9},{9,8},{10,11... | collective-permute-start | bytes 2359304 | tf_op jit(solution)/shard_map/ppermute | solution.py:60
  226.5 30.8 %collective-permute-start.59 = (bf16[384,1024]{1,0:T(8,128)(2,1)S(1)}, bf16[384,1024]{1,0:T(8,128)(2,1)S(1)}, u32[]{:S(2)}, u32[]{:S(2)}) collective-permute-start(bf16[384,1024]{1,0:T(8,128)(2,1)S(1)} %collective-permute-done.49.refs_1_), channel_id=1, source_target_pairs={{0,1},{1,0},{2,3},{3,2},{4,5},{5,4},{6,7},{7,6},{8,9},{9,8},{10,11... | collective-permute-start | bytes 2359304 | tf_op jit(solution)/shard_map/ppermute | solution.py:60
  242.7 17.4 %collective-permute-start.56 = (bf16[384,1024]{1,0:T(8,128)(2,1)}, bf16[384,1024]{1,0:T(8,128)(2,1)}, u32[]{:S(2)}, u32[]{:S(2)}) collective-permute-start(bf16[384,1024]{1,0:T(8,128)(2,1)} %collective-permute-done.52.refs_4_), channel_id=1, source_target_pairs={{0,4},{1,5},{4,8},{5,9},{8,12},{9,13},{12,14},{13,15},{14,10},{15,... | collective-permute-start | bytes 2359304 | tf_op jit(solution)/shard_map/ppermute | solution.py:563
  243.2 17.0 %collective-permute-start.57 = (bf16[384,1024]{1,0:T(8,128)(2,1)}, bf16[384,1024]{1,0:T(8,128)(2,1)}, u32[]{:S(2)}, u32[]{:S(2)}) collective-permute-start(bf16[384,1024]{1,0:T(8,128)(2,1)} %collective-permute-done.53.refs_5_), channel_id=1, source_target_pairs={{0,2},{1,3},{4,0},{5,1},{8,4},{9,5},{12,8},{13,9},{14,12},{15,13},... | collective-permute-start | bytes 2359304 | tf_op jit(solution)/shard_map/ppermute | solution.py:563
  244.7 16.3 %collective-permute-start.60 = (bf16[384,1024]{1,0:T(8,128)(2,1)}, bf16[384,1024]{1,0:T(8,128)(2,1)}, u32[]{:S(2)}, u32[]{:S(2)}) collective-permute-start(bf16[384,1024]{1,0:T(8,128)(2,1)} %collective-permute-done.52.refs_4_), channel_id=1, source_target_pairs={{0,1},{1,0},{2,3},{3,2},{4,5},{5,4},{6,7},{7,6},{8,9},{9,8},{10,11... | collective-permute-start | bytes 2359304 | tf_op jit(solution)/shard_map/ppermute | solution.py:60
  301.8 17.7 %collective-permute-start.64 = (bf16[2,160,1024]{2,1,0:T(8,128)(2,1)S(1)}, bf16[2,160,1024]{2,1,0:T(8,128)(2,1)S(1)}, u32[]{:S(2)}, u32[]{:S(2)}) collective-permute-start(bf16[2,160,1024]{2,1,0:T(8,128)(2,1)S(1)} %get-tuple-element.563), channel_id=1, source_target_pairs={{0,16},{1,17},{2,18},{3,19},{4,20},{5,21},{6,22},{7,23},{8,24},{9,... | collective-permute-start | bytes 1966088 | tf_op jit(solution)/shard_map/ppermute | solution.py:1025
  416.1 27.3 %collective-permute-start.72 = (bf16[320,4096]{1,0:T(8,128)(2,1)S(1)}, bf16[320,4096]{1,0:T(8,128)(2,1)S(1)}, u32[]{:S(2)}, u32[]{:S(2)}) collective-permute-start(bf16[320,4096]{1,0:T(8,128)(2,1)S(1)} %broadcast_select_fusion.1.a_ref), channel_id=1, source_target_pairs={{0,1},{1,0},{2,3},{3,2},{4,5},{5,4},{6,7},{7,6},{8,9},{9,8},{10,11... | collective-permute-start | bytes 7864328 | tf_op jit(solution)/shard_map/ppermute | solution.py:60
  422.0 21.4 %collective-permute-start.67 = (bf16[2,160,1024]{2,1,0:T(8,128)(2,1)S(1)}, bf16[2,160,1024]{2,1,0:T(8,128)(2,1)S(1)}, u32[]{:S(2)}, u32[]{:S(2)}) collective-permute-start(bf16[2,160,1024]{2,1,0:T(8,128)(2,1)S(1)} %get-tuple-element.413), channel_id=1, source_target_pairs={{16,0},{17,1},{18,2},{19,3},{20,4},{21,5},{22,6},{23,7},{24,8},{25... | collective-permute-start | bytes 1966088 | tf_op jit(solution)/shard_map/ppermute | solution.py:1047
  467.8 15.9 %all-to-all-start.5 = ((bf16[8,320,128]{2,1,0:T(8,128)(2,1)}), bf16[8,320,128]{2,1,0:T(8,128)(2,1)}, u32[]{:S(2)}, u32[]{:S(2)}) async-start(bf16[8,320,128]{2,1,0:T(8,128)(2,1)} %copy-done.82), calls=%async_computation.5 | async-start | bytes 1310720 | tf_op jit(solution)/shard_map/all_to_all | solution.py:873
  476.0 38.8 %collective-permute-start.73 = (bf16[320,4096]{1,0:T(8,128)(2,1)}, bf16[320,4096]{1,0:T(8,128)(2,1)}, u32[]{:S(2)}, u32[]{:S(2)}) collective-permute-start(bf16[320,4096]{1,0:T(8,128)(2,1)} %broadcast_select_fusion.u_ref), channel_id=1, source_target_pairs={{0,1},{1,0},{2,3},{3,2},{4,5},{5,4},{6,7},{7,6},{8,9},{9,8},{10,11... | collective-permute-start | bytes 7864328 | tf_op jit(solution)/shard_map/ppermute | solution.py:60
  491.0 18.0 %all-to-all-start.6 = ((bf16[8,160,384]{2,1,0:T(8,128)(2,1)}), bf16[8,160,384]{2,1,0:T(8,128)(2,1)}, u32[]{:S(2)}, u32[]{:S(2)}) async-start(bf16[8,160,384]{2,1,0:T(8,128)(2,1)} %bitcast.344), calls=%async_computation.6 | async-start | bytes 1966080 | tf_op jit(solution)/shard_map/all_to_all | solution.py:873
  497.4 17.3 %collective-permute-start.74 = (bf16[320,1024]{1,0:T(8,128)(2,1)}, bf16[320,1024]{1,0:T(8,128)(2,1)}, u32[]{:S(2)}, u32[]{:S(2)}) collective-permute-start(bf16[320,1024]{1,0:T(8,128)(2,1)} %broadcast_select_fusion.6.f_ref), channel_id=1, source_target_pairs={{0,1},{1,0},{2,3},{3,2},{4,5},{5,4},{6,7},{7,6},{8,9},{9,8},{10,11... | collective-permute-start | bytes 1966088 | tf_op jit(solution)/shard_map/ppermute | solution.py:60
  509.0 26.0 %all-to-all-start.7 = ((bf16[8,160,384]{2,1,0:T(8,128)(2,1)}), bf16[8,160,384]{2,1,0:T(8,128)(2,1)}, u32[]{:S(2)}, u32[]{:S(2)}) async-start(bf16[8,160,384]{2,1,0:T(8,128)(2,1)} %bitcast.343), calls=%async_computation.7 | async-start | bytes 1966080 | tf_op jit(solution)/shard_map/all_to_all | solution.py:873
  514.4 39.3 %collective-permute-start.79 = (bf16[320,1024]{1,0:T(8,128)(2,1)}, bf16[320,1024]{1,0:T(8,128)(2,1)}, u32[]{:S(2)}, u32[]{:S(2)}) collective-permute-start(bf16[320,1024]{1,0:T(8,128)(2,1)} %broadcast_select_fusion.5.a_ref), channel_id=1, source_target_pairs={{0,1},{1,0},{2,3},{3,2},{4,5},{5,4},{6,7},{7,6},{8,9},{9,8},{10,11... | collective-permute-start | bytes 1966088 | tf_op jit(solution)/shard_map/ppermute | solution.py:60
  532.6 21.2 %collective-permute-start.80 = (bf16[320,1024]{1,0:T(8,128)(2,1)S(1)}, bf16[320,1024]{1,0:T(8,128)(2,1)}, u32[]{:S(2)}, u32[]{:S(2)}) collective-permute-start(bf16[320,1024]{1,0:T(8,128)(2,1)S(1)} %broadcast_select_fusion.4.b_ref), channel_id=1, source_target_pairs={{0,1},{1,0},{2,3},{3,2},{4,5},{5,4},{6,7},{7,6},{8,9},{9,8},{10,11... | collective-permute-start | bytes 1966088 | tf_op jit(solution)/shard_map/ppermute | solution.py:60
  548.3 23.0 %collective-permute-start.85 = (bf16[8,320,384]{2,1,0:T(8,128)(2,1)S(1)}, bf16[8,320,384]{2,1,0:T(8,128)(2,1)S(1)}, u32[]{:S(2)}, u32[]{:S(2)}) collective-permute-start(bf16[8,320,384]{2,1,0:T(8,128)(2,1)S(1)} %broadcast_select_fusion.2.j_ref), channel_id=1, source_target_pairs={{0,1},{1,0},{2,3},{3,2},{4,5},{5,4},{6,7},{7,6},{8,9},{9,8},{10,11... | collective-permute-start | bytes 5898248 | tf_op jit(solution)/shard_map/ppermute | solution.py:60
  567.6 18.7 %collective-permute-start.83 = (bf16[256,1024]{1,0:T(8,128)(2,1)S(1)}, bf16[256,1024]{1,0:T(8,128)(2,1)S(1)}, u32[]{:S(2)}, u32[]{:S(2)}) collective-permute-start(bf16[256,1024]{1,0:T(8,128)(2,1)S(1)} %fusion.50), channel_id=1, source_target_pairs={{0,4},{1,5},{4,8},{5,9},{8,12},{9,13},{12,14},{13,15},{14,10},{15,... | collective-permute-start | bytes 1572872 | tf_op jit(solution)/shard_map/ppermute | solution.py:563
  570.6 15.7 %collective-permute-start.84 = (bf16[256,1024]{1,0:T(8,128)(2,1)S(1)}, bf16[256,1024]{1,0:T(8,128)(2,1)S(1)}, u32[]{:S(2)}, u32[]{:S(2)}) collective-permute-start(bf16[256,1024]{1,0:T(8,128)(2,1)S(1)} %fusion.49), channel_id=1, source_target_pairs={{0,2},{1,3},{4,0},{5,1},{8,4},{9,5},{12,8},{13,9},{14,12},{15,13},... | collective-permute-start | bytes 1572872 | tf_op jit(solution)/shard_map/ppermute | solution.py:563
  587.1 26.3 %collective-permute-start.86 = (bf16[256,1024]{1,0:T(8,128)(2,1)}, bf16[256,1024]{1,0:T(8,128)(2,1)}, u32[]{:S(2)}, u32[]{:S(2)}) collective-permute-start(bf16[256,1024]{1,0:T(8,128)(2,1)} %slice_bitcast_fusion.2), channel_id=1, source_target_pairs={{0,4},{1,5},{4,8},{5,9},{8,12},{9,13},{12,14},{13,15},{14,10},{15,... | collective-permute-start | bytes 1572872 | tf_op jit(solution)/shard_map/ppermute | solution.py:563
  590.1 23.3 %collective-permute-start.87 = (bf16[256,1024]{1,0:T(8,128)(2,1)}, bf16[256,1024]{1,0:T(8,128)(2,1)}, u32[]{:S(2)}, u32[]{:S(2)}) collective-permute-start(bf16[256,1024]{1,0:T(8,128)(2,1)} %slice_bitcast_fusion.1), channel_id=1, source_target_pairs={{0,2},{1,3},{4,0},{5,1},{8,4},{9,5},{12,8},{13,9},{14,12},{15,13},... | collective-permute-start | bytes 1572872 | tf_op jit(solution)/shard_map/ppermute | solution.py:563
  615.0 21.2 %collective-permute-start.88 = (bf16[256,1024]{1,0:T(8,128)(2,1)S(1)}, bf16[256,1024]{1,0:T(8,128)(2,1)S(1)}, u32[]{:S(2)}, u32[]{:S(2)}) collective-permute-start(bf16[256,1024]{1,0:T(8,128)(2,1)S(1)} %fusion.48), channel_id=1, source_target_pairs={{0,4},{1,5},{4,8},{5,9},{8,12},{9,13},{12,14},{13,15},{14,10},{15,... | collective-permute-start | bytes 1572872 | tf_op jit(solution)/shard_map/ppermute | solution.py:563
  618.4 21.0 %collective-permute-start.89 = (bf16[256,1024]{1,0:T(8,128)(2,1)S(1)}, bf16[256,1024]{1,0:T(8,128)(2,1)S(1)}, u32[]{:S(2)}, u32[]{:S(2)}) collective-permute-start(bf16[256,1024]{1,0:T(8,128)(2,1)S(1)} %fusion.47), channel_id=1, source_target_pairs={{0,2},{1,3},{4,0},{5,1},{8,4},{9,5},{12,8},{13,9},{14,12},{15,13},... | collective-permute-start | bytes 1572872 | tf_op jit(solution)/shard_map/ppermute | solution.py:563
  629.4 18.1 %collective-permute-start.106 = (bf16[256,1024]{1,0:T(8,128)(2,1)S(1)}, bf16[256,1024]{1,0:T(8,128)(2,1)S(1)}, u32[]{:S(2)}, u32[]{:S(2)}) collective-permute-start(bf16[256,1024]{1,0:T(8,128)(2,1)S(1)} %fusion.34), channel_id=1, source_target_pairs={{0,4},{1,5},{4,8},{5,9},{8,12},{9,13},{12,14},{13,15},{14,10},{15,... | collective-permute-start | bytes 1572872 | tf_op jit(solution)/shard_map/ppermute | solution.py:563
  630.7 20.0 %collective-permute-start.107 = (bf16[256,1024]{1,0:T(8,128)(2,1)S(1)}, bf16[256,1024]{1,0:T(8,128)(2,1)S(1)}, u32[]{:S(2)}, u32[]{:S(2)}) collective-permute-start(bf16[256,1024]{1,0:T(8,128)(2,1)S(1)} %fusion.33), channel_id=1, source_target_pairs={{0,2},{1,3},{4,0},{5,1},{8,4},{9,5},{12,8},{13,9},{14,12},{15,13},... | collective-permute-start | bytes 1572872 | tf_op jit(solution)/shard_map/ppermute | solution.py:563
  640.7 18.0 %collective-permute-start.90 = (bf16[256,1024]{1,0:T(8,128)(2,1)S(1)}, bf16[256,1024]{1,0:T(8,128)(2,1)S(1)}, u32[]{:S(2)}, u32[]{:S(2)}) collective-permute-start(bf16[256,1024]{1,0:T(8,128)(2,1)S(1)} %fusion.46), channel_id=1, source_target_pairs={{0,4},{1,5},{4,8},{5,9},{8,12},{9,13},{12,14},{13,15},{14,10},{15,... | collective-permute-start | bytes 1572872 | tf_op jit(solution)/shard_map/ppermute | solution.py:563
  643.0 18.9 %collective-permute-start.91 = (bf16[256,1024]{1,0:T(8,128)(2,1)S(1)}, bf16[256,1024]{1,0:T(8,128)(2,1)S(1)}, u32[]{:S(2)}, u32[]{:S(2)}) collective-permute-start(bf16[256,1024]{1,0:T(8,128)(2,1)S(1)} %fusion.45), channel_id=1, source_target_pairs={{0,2},{1,3},{4,0},{5,1},{8,4},{9,5},{12,8},{13,9},{14,12},{15,13},... | collective-permute-start | bytes 1572872 | tf_op jit(solution)/shard_map/ppermute | solution.py:563
  652.0 17.9 %collective-permute-start.108 = (bf16[256,1024]{1,0:T(8,128)(2,1)S(1)}, bf16[256,1024]{1,0:T(8,128)(2,1)S(1)}, u32[]{:S(2)}, u32[]{:S(2)}) collective-permute-start(bf16[256,1024]{1,0:T(8,128)(2,1)S(1)} %fusion.32), channel_id=1, source_target_pairs={{0,4},{1,5},{4,8},{5,9},{8,12},{9,13},{12,14},{13,15},{14,10},{15,... | collective-permute-start | bytes 1572872 | tf_op jit(solution)/shard_map/ppermute | solution.py:563
  653.3 19.8 %collective-permute-start.109 = (bf16[256,1024]{1,0:T(8,128)(2,1)S(1)}, bf16[256,1024]{1,0:T(8,128)(2,1)S(1)}, u32[]{:S(2)}, u32[]{:S(2)}) collective-permute-start(bf16[256,1024]{1,0:T(8,128)(2,1)S(1)} %fusion.31), channel_id=1, source_target_pairs={{0,2},{1,3},{4,0},{5,1},{8,4},{9,5},{12,8},{13,9},{14,12},{15,13},... | collective-permute-start | bytes 1572872 | tf_op jit(solution)/shard_map/ppermute | solution.py:563
  662.1 21.1 %collective-permute-start.93 = (bf16[256,1024]{1,0:T(8,128)(2,1)S(1)}, bf16[256,1024]{1,0:T(8,128)(2,1)S(1)}, u32[]{:S(2)}, u32[]{:S(2)}) collective-permute-start(bf16[256,1024]{1,0:T(8,128)(2,1)S(1)} %fusion.44), channel_id=1, source_target_pairs={{0,4},{1,5},{4,8},{5,9},{8,12},{9,13},{12,14},{13,15},{14,10},{15,... | collective-permute-start | bytes 1572872 | tf_op jit(solution)/shard_map/ppermute | solution.py:563
  663.4 21.0 %collective-permute-start.94 = (bf16[256,1024]{1,0:T(8,128)(2,1)S(1)}, bf16[256,1024]{1,0:T(8,128)(2,1)S(1)}, u32[]{:S(2)}, u32[]{:S(2)}) collective-permute-start(bf16[256,1024]{1,0:T(8,128)(2,1)S(1)} %fusion.43), channel_id=1, source_target_pairs={{0,2},{1,3},{4,0},{5,1},{8,4},{9,5},{12,8},{13,9},{14,12},{15,13},... | collective-permute-start | bytes 1572872 | tf_op jit(solution)/shard_map/ppermute | solution.py:563
  664.4 18.7 %collective-permute-start.95 = (f32[1,112,128]{2,1,0:T(8,128)S(1)}, f32[1,112,128]{2,1,0:T(8,128)S(1)}, u32[]{:S(2)}, u32[]{:S(2)}) collective-permute-start(f32[1,112,128]{2,1,0:T(8,128)S(1)} %add.447), channel_id=1, source_target_pairs={{0,2},{1,3},{2,0},{3,1},{4,6},{5,7},{6,4},{7,5},{8,10},{9,11},{10,... | collective-permute-start | bytes 172040 | tf_op jit(solution)/shard_map/ppermute | solution.py:60
  674.3 19.3 %collective-permute-start.110 = (bf16[256,1024]{1,0:T(8,128)(2,1)S(1)}, bf16[256,1024]{1,0:T(8,128)(2,1)S(1)}, u32[]{:S(2)}, u32[]{:S(2)}) collective-permute-start(bf16[256,1024]{1,0:T(8,128)(2,1)S(1)} %fusion.30), channel_id=1, source_target_pairs={{0,4},{1,5},{4,8},{5,9},{8,12},{9,13},{12,14},{13,15},{14,10},{15,... | collective-permute-start | bytes 1572872 | tf_op jit(solution)/shard_map/ppermute | solution.py:563
  675.6 20.0 %collective-permute-start.111 = (bf16[256,1024]{1,0:T(8,128)(2,1)S(1)}, bf16[256,1024]{1,0:T(8,128)(2,1)S(1)}, u32[]{:S(2)}, u32[]{:S(2)}) collective-permute-start(bf16[256,1024]{1,0:T(8,128)(2,1)S(1)} %fusion.29), channel_id=1, source_target_pairs={{0,2},{1,3},{4,0},{5,1},{8,4},{9,5},{12,8},{13,9},{14,12},{15,13},... | collective-permute-start | bytes 1572872 | tf_op jit(solution)/shard_map/ppermute | solution.py:563
  684.6 20.0 %collective-permute-start.96 = (bf16[256,1024]{1,0:T(8,128)(2,1)S(1)}, bf16[256,1024]{1,0:T(8,128)(2,1)S(1)}, u32[]{:S(2)}, u32[]{:S(2)}) collective-permute-start(bf16[256,1024]{1,0:T(8,128)(2,1)S(1)} %fusion.42), channel_id=1, source_target_pairs={{0,4},{1,5},{4,8},{5,9},{8,12},{9,13},{12,14},{13,15},{14,10},{15,... | collective-permute-start | bytes 1572872 | tf_op jit(solution)/shard_map/ppermute | solution.py:563
  685.9 18.7 %collective-permute-start.97 = (bf16[256,1024]{1,0:T(8,128)(2,1)S(1)}, bf16[256,1024]{1,0:T(8,128)(2,1)S(1)}, u32[]{:S(2)}, u32[]{:S(2)}) collective-permute-start(bf16[256,1024]{1,0:T(8,128)(2,1)S(1)} %fusion.41), channel_id=1, source_target_pairs={{0,2},{1,3},{4,0},{5,1},{8,4},{9,5},{12,8},{13,9},{14,12},{15,13},... | collective-permute-start | bytes 1572872 | tf_op jit(solution)/shard_map/ppermute | solution.py:563
  688.1 16.4 %collective-permute-start.98 = (f32[1,112,128]{2,1,0:T(8,128)S(1)}, f32[1,112,128]{2,1,0:T(8,128)S(1)}, u32[]{:S(2)}, u32[]{:S(2)}) collective-permute-start(f32[1,112,128]{2,1,0:T(8,128)S(1)} %add.450), channel_id=1, source_target_pairs={{0,4},{1,5},{2,6},{3,7},{4,0},{5,1},{6,2},{7,3},{8,12},{9,13},{10,... | collective-permute-start | bytes 172040 | tf_op jit(solution)/shard_map/ppermute | solution.py:60
  704.8 16.3 %collective-permute-start.99 = (bf16[256,1024]{1,0:T(8,128)(2,1)S(1)}, bf16[256,1024]{1,0:T(8,128)(2,1)S(1)}, u32[]{:S(2)}, u32[]{:S(2)}) collective-permute-start(bf16[256,1024]{1,0:T(8,128)(2,1)S(1)} %fusion.40), channel_id=1, source_target_pairs={{0,4},{1,5},{4,8},{5,9},{8,12},{9,13},{12,14},{13,15},{14,10},{15,... | collective-permute-start | bytes 1572872 | tf_op jit(solution)/shard_map/ppermute | solution.py:563
  705.2 15.8 %collective-permute-start.100 = (bf16[256,1024]{1,0:T(8,128)(2,1)S(1)}, bf16[256,1024]{1,0:T(8,128)(2,1)S(1)}, u32[]{:S(2)}, u32[]{:S(2)}) collective-permute-start(bf16[256,1024]{1,0:T(8,128)(2,1)S(1)} %fusion.39), channel_id=1, source_target_pairs={{0,2},{1,3},{4,0},{5,1},{8,4},{9,5},{12,8},{13,9},{14,12},{15,13},... | collective-permute-start | bytes 1572872 | tf_op jit(solution)/shard_map/ppermute | solution.py:563
  (281 other events, 2846.2 us)

commit v3 on v2

--- a/solution.py
+++ b/solution.py
@@ -316,7 +316,7 @@
 PARTS = 16
 ROWS_OF_PART = D // PARTS
 SET = 4 * PAIR
-STRIP = FF // 8
+STRIP = D
 LARGE = 40
 
 
@@ -328,30 +328,49 @@
     return ref[...].reshape(-1, ref.shape[-1])
 
 
+def wide_spec(first):
+    return pl.BlockSpec((PARTS, ROWS_OF_PART, D), lambda j: (0, first + j, 0))
+
+
 def rows_spec(shape):
     return pl.BlockSpec(shape, lambda j: (0,) * len(shape))
 
 
+SETS = D // SET
+
+
 def project_kernel(hidden_ref, w_ref, joint_ref, asked_ref):
     made = low(dot(hidden_ref[...], joined(w_ref)))
-    joint_ref[0] = made[:, : 3 * PAIR]
-    asked_ref[...] = made[:, 3 * PAIR :]
+    for i in range(SETS):
+        joint_ref[i] = made[:, i * SET : i * SET + 3 * PAIR]
+        asked_ref[:, i * PAIR : (i + 1) * PAIR] = made[:, i * SET + 3 * PAIR : (i + 1) * SET]
+
+
+def project_specs(tokens):
+    joint = pl.BlockSpec((SETS, tokens, 3 * PAIR), lambda m: (m, 0, 0))
+    asked = pl.BlockSpec((tokens, SETS * PAIR), lambda m: (0, m))
+    return joint, asked
 
 
 def project(hidden, packed):
     tokens = hidden.shape[0]
     return call(
         project_kernel,
-        (MEMBERS,),
-        [rows_spec((tokens, D)), block_spec(0)],
-        [pl.BlockSpec((1, tokens, 3 * PAIR), lambda m: (m, 0, 0)), pl.BlockSpec((tokens, PAIR), lambda m: (0, m))],
+        (MEMBERS // SETS,),
+        [rows_spec((tokens, D)), wide_spec(0)],
+        list(project_specs(tokens)),
         [shaped((MEMBERS, tokens, 3 * PAIR)), shaped((tokens, D))],
         (hidden, packed),
     )
 
 
+def joint_columns(joint_ref, asked_ref):
+    pieces = [x for i in range(SETS) for x in (joint_ref[i], part_of(asked_ref[...], i))]
+    return jnp.concatenate(pieces, 1)
+
+
 def project_back_kernel(joint_ref, asked_ref, w_ref, out_ref):
-    grad = jnp.concatenate([joint_ref[0], asked_ref[...]], 1)
+    grad = joint_columns(joint_ref, asked_ref)
     add_over_steps(out_ref, slice(None), dot_right_t(grad, joined(w_ref)), 0)
 
 
@@ -359,12 +378,8 @@
     tokens = asked_grad.shape[0]
     return call(
         project_back_kernel,
-        (MEMBERS,),
-        [
-            pl.BlockSpec((1, tokens, 3 * PAIR), lambda m: (m, 0, 0)),
-            pl.BlockSpec((tokens, PAIR), lambda m: (0, m)),
-            block_spec(0),
-        ],
+        (MEMBERS // SETS,),
+        [*project_specs(tokens), wide_spec(0)],
         rows_spec((tokens, D)),
         shaped((tokens, D), HIGH),
         (joint_grad, asked_grad, packed),
@@ -431,18 +446,25 @@
     )
 
 
+def slices(count):
+    width = STRIP // count
+    return [slice(i * width, (i + 1) * width) for i in range(count)]
+
+
 def feed_kernel(s_ref, up_ref, down_ref, upper_ref, active_ref, feed_ref):
-    upper = dot(s_ref[...], joined(up_ref))
-    active = low(jax.nn.gelu(upper))
-    upper_ref[...] = upper
-    active_ref[...] = active
-    add_over_steps(feed_ref, slice(None), dot(active, joined(down_ref)), 0)
+    up, down = joined(up_ref), joined(down_ref)
+    uppers = [dot(s_ref[...], up[:, at]) for at in slices(4)]
+    actives = [low(jax.nn.gelu(x)) for x in uppers]
+    for at, upper, active in zip(slices(4), uppers, actives):
+        upper_ref[:, at] = low(upper)
+        active_ref[:, at] = active
+    add_over_steps(feed_ref, slice(None), sum(dot(x, down[at]) for at, x in zip(slices(4), actives)), 0)
 
 
 def feed_specs(tokens):
     strip = pl.BlockSpec((tokens, STRIP), lambda j: (0, j))
     down = pl.BlockSpec((STRIP // (FF // PARTS), FF // PARTS, D), lambda j: (j, 2, 0))
-    return rows_spec((tokens, D)), strip, block_spec(2), down
+    return rows_spec((tokens, D)), strip, wide_spec(2), down
 
 
 def feed_call(second, packed):
@@ -453,17 +475,19 @@
         (FF // STRIP,),
         [full, up, down],
         [strip, strip, full],
-        [shaped((tokens, FF), HIGH), shaped((tokens, FF)), shaped((tokens, D), HIGH)],
+        [shaped((tokens, FF)), shaped((tokens, FF)), shaped((tokens, D), HIGH)],
         (second, packed, packed),
         LARGE,
     )
 
 
 def feed_back_kernel(f_ref, upper_ref, up_ref, down_ref, upper_grad_ref, second_grad_ref):
-    active_grad = dot_right_t(f_ref[...], joined(down_ref))
-    upper_grad = low(jax.vjp(jax.nn.gelu, upper_ref[...])[1](active_grad)[0])
-    upper_grad_ref[...] = upper_grad
-    add_over_steps(second_grad_ref, slice(None), dot_right_t(upper_grad, joined(up_ref)), 0)
+    up, down = joined(up_ref), joined(down_ref)
+    grads = [dot_right_t(f_ref[...], down[at]) for at in slices(4)]
+    grads = [low(jax.vjp(jax.nn.gelu, high(upper_ref[:, at]))[1](x)[0]) for at, x in zip(slices(4), grads)]
+    for at, x in zip(slices(4), grads):
+        upper_grad_ref[:, at] = x
+    add_over_steps(second_grad_ref, slice(None), sum(dot_right_t(x, up[:, at]) for at, x in zip(slices(4), grads)), 0)
 
 
 def feed_back_call(feed_grad, upper, packed):
@@ -589,7 +613,7 @@
     return assembled(held, EARLY, made), side
 
 
-EARLY = 5
+EARLY = 4
 
 
 def assembled(held, start, made):
@@ -807,7 +831,7 @@
             rows_ref[j * HEAD : (j + 1) * HEAD] = s_ref[pl.ds(start, HEAD)]
 
     grad = jnp.concatenate([u_ref[...], u2_ref[...]], 0)
-    right_ref[...] = low(dot(rows_ref[...], grad)).reshape(chips, HEAD, STRIP)
+    right_ref[...] = low(dot(rows_ref[...], grad)).reshape(chips, HEAD, SET)
     left_ref[0] = low(dot_left_t(a_ref[...], f_ref[...]) + dot_left_t(a2_ref[...], f2_ref[...]))
 
 
@@ -815,7 +839,7 @@
     tokens = upper_grad[0].shape[0]
     chips = len(RING)
     rows = FF // (2 * chips)
-    strip = pl.BlockSpec((tokens, STRIP), lambda j, order: (0, j))
+    strip = pl.BlockSpec((tokens, SET), lambda j, order: (0, j))
     hidden = pl.BlockSpec((tokens, rows), lambda j, order: (0, 2 * order[1, j] + order[2, 0]))
     full = pl.BlockSpec((tokens, D), lambda j, order: (0, 0))
     return call_ordered(
@@ -1138,16 +1162,21 @@
     table_sum = jnp.sum(small[:, micro * 6 * D : micro * 6 * D + HEADS * REL], 0).reshape(HEADS, REL)
     modul_shard = jnp.einsum("bck,cbn->kn", high(cond_rows), mods_all, precision=lax.Precision.HIGHEST)
     bias_sum = jnp.sum(mods_all, (0, 1))
-    modul_shard, bias_sum, table_sum = ring.step(modul_shard, bias_sum, table_sum)
+    if apart:
+        up_shard = down_shard = bias_sum
+    else:
+        up_shard, down_shard = feed_part
+        up_shard = jnp.swapaxes(up_shard.reshape(4, shard, D), 0, 1).reshape(shard, 4 * D)
+    modul_shard, bias_sum, table_sum, up_shard, down_shard = ring.step(
+        modul_shard, bias_sum, table_sum, up_shard, down_shard
+    )
 
     if apart:
         grouped, out_shard, cross_shard, keys, values, up_shard, down_shard = ring.result
         memory_shard = jnp.concatenate([keys, values], 1)
     else:
-        (grouped, outputs), (up_shard, down_shard) = ring.result, feed_part
-        grouped, up_shard = [
-            jnp.swapaxes(x.reshape(4, shard, D), 0, 1).reshape(shard, 4 * D) for x in (grouped, up_shard)
-        ]
+        grouped, outputs = ring.result
+        grouped = jnp.swapaxes(grouped.reshape(4, shard, D), 0, 1).reshape(shard, 4 * D)
         out_shard, cross_shard = outputs[:shard], outputs[shard : 2 * shard]
         memory_shard = jnp.concatenate([outputs[2 * shard : 3 * shard], outputs[3 * shard :]], 1)
     grouped = jnp.swapaxes(grouped.reshape(shard, MEMBERS, 4, PAIR), 1, 2).reshape(shard, 4 * D)

time: 752 us -> 738 us (0.981)
  Pallas kernels: 199 us -> 184 us
  starting transfers between devices: 118 us -> 129 us
  waiting for transfers between devices: 260 us -> 252 us
    pallas_call x24, Pallas kernels: 143 us -> 129 us  [call(): pl.pallas_call(kernel, grid=grid, in_specs=in_specs, out_specs=out_specs,...]
    ppermute x56, starting transfers between devices: 60.1 us -> 72.4 us  [hop(): return lax.ppermute(x, ('section', 'dp'), route)]
    unnamed x473 -> x471, local copies, waits for them, and re-layouts: 53.3 us -> 54.4 us
  transfers between devices with their start and end apart: 120 -> 120, of which waited for: 54 -> 59; matrix products, arithmetic and copies ran while one was open for 11% -> 11% of each run, Pallas kernels for 12% -> 11%
where the time goes in v3:
time: 738 us; the launch traced here: 727 us
  waiting for transfers between devices  252 us (34%)
  Pallas kernels  184 us (25%)
  starting transfers between devices  129 us (17%)
  local copies, waits for them, and re-layouts  73.2 us (10%)
  other arithmetic  62.9 us (9%)
  matrix products  21.1 us (3%)
    ppermute x56, waiting for transfers between devices, hop(): return lax.ppermute(x, ('section', 'dp'), route)  158 us
    pallas_call x24, Pallas kernels, call(): pl.pallas_call(kernel, grid=grid, in_specs=in_specs, out_specs=out_specs,...  129 us
    ppermute x56, starting transfers between devices, hop(): return lax.ppermute(x, ('section', 'dp'), route)  72.4 us
    unnamed x471, local copies, waits for them, and re-layouts  54.4 us
    ppermute x54, waiting for transfers between devices, swap(): return lax.ppermute(x, ('section', 'dp'), route)  49.3 us
    all_to_all x8, starting transfers between devices, trade(): return lax.all_to_all(x, 'dp', 0, 0, tiled=True, axis_index_groups=members)  31.2 us
    pallas_call x4, Pallas kernels, assembled(): pl.pallas_call(kernel, grid_spec=pltpu.PrefetchScalarGridSpec(num_scalar_...  28.6 us
    pallas_call x2, Pallas kernels, call_ordered(): pl.pallas_call(kernel, grid_spec=pltpu.PrefetchScalarGridSpec(num_scalar_...  27.1 us
  transfers between devices with their start and end apart: 120, of which 59 were waited for; matrix products, arithmetic and copies ran while one was open for 11% of the time, Pallas kernels for 11%

profile of v3, /device:TPU:0, one launch (start us, length us, event | category | flops | bytes accessed | tf_op | source)
XLA Modules:
  0.0 727.0 jit_solution(8957042211074543161)
XLA Ops:
  22.7 3.4 all-to-all-start
  28.7 9.8 %collective-permute-done.3.refs_9_ = bf16[128,1024]{1,0:T(8,128)(2,1)S(1)} collective-permute-done((bf16[128,1024]{1,0:T(8,128)(2,1)}, bf16[128,1024]{1,0:T(8,128)(2,1)S(1)}, u32[]{:S(2)}, u32[]{:S(2)}) %collective-permute-start.3) | collective-permute-done | bytes 262176 | tf_op jit(solution)/shard_map/ppermute | solution.py:587
  42.9 3.8 collective-permute-done.7.refs_12_
  50.5 4.4 collective-permute-done.16
  58.4 6.6 collective-permute-done.21
  68.6 4.5 shard_map.274.refs_16_
  78.9 6.2 collective-permute-done.26.refs_12_
  93.7 4.5 shard_map.275
  98.2 3.4 copy-done.2
  101.6 4.1 shard_map.276
  108.0 3.7 all-to-all-start.1
  112.3 13.2 %collective-permute-start.36 = (bf16[384,1024]{1,0:T(8,128)(2,1)}, bf16[384,1024]{1,0:T(8,128)(2,1)S(1)}, u32[]{:S(2)}, u32[]{:S(2)}) collective-permute-start(bf16[384,1024]{1,0:T(8,128)(2,1)} %collective-permute-done.30.refs_4_), channel_id=1, source_target_pairs={{0,4},{1,5},{4,8},{5,9},{8,12},{9,13},{12,14},{13,15},{14,10},{15,... | collective-permute-start | bytes 2359304 | tf_op jit(solution)/shard_map/ppermute | solution.py:587
  125.7 17.9 %collective-permute-done.36.refs_8_ = bf16[384,1024]{1,0:T(8,128)(2,1)S(1)} collective-permute-done((bf16[384,1024]{1,0:T(8,128)(2,1)}, bf16[384,1024]{1,0:T(8,128)(2,1)S(1)}, u32[]{:S(2)}, u32[]{:S(2)}) %collective-permute-start.36) | collective-permute-done | bytes 786464 | tf_op jit(solution)/shard_map/ppermute | solution.py:587
  145.1 3.6 all-to-all-start.2
  154.3 8.5 %all-to-all-done.2 = bf16[8,160,384]{2,1,0:T(8,128)(2,1)S(1)} async-done(((bf16[8,160,384]{2,1,0:T(8,128)(2,1)}), bf16[8,160,384]{2,1,0:T(8,128)(2,1)S(1)}, u32[]{:S(2)}, u32[]{:S(2)}) %all-to-all-start.2) | async-done | bytes 983072 | tf_op jit(solution)/shard_map/all_to_all | solution.py:897
  162.9 3.6 all-to-all-start.3
  167.1 12.7 %collective-permute-done.40.refs_12_ = bf16[384,1024]{1,0:T(8,128)(2,1)} collective-permute-done((bf16[384,1024]{1,0:T(8,128)(2,1)}, bf16[384,1024]{1,0:T(8,128)(2,1)}, u32[]{:S(2)}, u32[]{:S(2)}) %collective-permute-start.40) | collective-permute-done | bytes 786464 | tf_op jit(solution)/shard_map/ppermute | solution.py:587
  184.9 4.1 all-to-all-start.4
  192.2 11.1 %all-to-all-done.4 = bf16[8,160,128]{2,1,0:T(8,128)(2,1)} async-done(((bf16[8,160,128]{2,1,0:T(8,128)(2,1)}), bf16[8,160,128]{2,1,0:T(8,128)(2,1)}, u32[]{:S(2)}, u32[]{:S(2)}) %all-to-all-start.4) | async-done | bytes 327712 | tf_op jit(solution)/shard_map/all_to_all | solution.py:897
  205.9 3.8 fusion.87.bias_ref
  211.3 11.3 %collective-permute-done.48.refs_4_ = bf16[384,1024]{1,0:T(8,128)(2,1)S(1)} collective-permute-done((bf16[384,1024]{1,0:T(8,128)(2,1)}, bf16[384,1024]{1,0:T(8,128)(2,1)S(1)}, u32[]{:S(2)}, u32[]{:S(2)}) %collective-permute-start.48) | collective-permute-done | bytes 786464 | tf_op jit(solution)/shard_map/ppermute | solution.py:587
  224.8 9.8 %shard_map.279.refs_16_ = bf16[8,2,768,1024]{3,2,1,0:T(8,128)(2,1)} custom-call(s32[9]{0:T(128)} %pad_add_fusion.order_ref, bf16[384,1024]{1,0:T(8,128)(2,1)} %copy-done.132, bf16[384,1024]{1,0:T(8,128)(2,1)} %copy-done.134, bf16[384,1024]{1,0:T(8,128)(2,1)} %copy-done.153, bf16[384,1024]{1,0:T(8,128)(2,1)} %copy-done.154, ...), custom_call_target="tpu_custom_call" | custom-call | flops 1 | bytes 1 | tf_op jit(solution)/shard_map/pallas_call | solution.py:648
  235.3 5.7 collective-permute-done.52.refs_8_
  244.2 14.5 %collective-permute-done.56.refs_12_ = bf16[384,1024]{1,0:T(8,128)(2,1)} collective-permute-done((bf16[384,1024]{1,0:T(8,128)(2,1)}, bf16[384,1024]{1,0:T(8,128)(2,1)}, u32[]{:S(2)}, u32[]{:S(2)}) %collective-permute-start.56) | collective-permute-done | bytes 786464 | tf_op jit(solution)/shard_map/ppermute | solution.py:587
  262.7 9.8 %shard_map.280 = bf16[8,2,768,1024]{3,2,1,0:T(8,128)(2,1)} custom-call(s32[9]{0:T(128)} %pad_add_fusion.order_ref, bf16[384,1024]{1,0:T(8,128)(2,1)} %collective-permute-done.44.refs_0_, bf16[384,1024]{1,0:T(8,128)(2,1)} %collective-permute-done.45.refs_1_, bf16[384,1024]{1,0:T(8,128)(2,1)} %copy-done.147, ...), custom_call_target="tpu_custom_call", output_to_operand_aliasing={{}: (17, {})} | custom-call | flops 1 | bytes 1 | tf_op jit(solution)/shard_map/pallas_call | solution.py:648
  272.5 3.7 shard_map.281
  279.0 3.7 shard_map.283
  284.5 11.5 %shard_map.284 = (bf16[320,4096]{1,0:T(8,128)(2,1)S(1)}, bf16[320,4096]{1,0:T(8,128)(2,1)S(1)}, f32[320,1024]{1,0:T(8,128)S(1)}) custom-call(bf16[320,1024]{1,0:T(8,128)(2,1)S(1)} %bitcast.325, bf16[16,768,1024]{2,1,0:T(8,128)(2,1)} %bitcast.348, bf16[16,768,1024]{2,1,0:T(8,128)(2,1)} %bitcast.349), custom_call_target="tpu_custom_call" | custom-call | flops 1 | bytes 1 | tf_op jit(solution)/shard_map/pallas_call | solution.py:196
  299.5 3.4 collective-permute-start.64
  303.0 14.2 %collective-permute-done.64 = bf16[2,160,1024]{2,1,0:T(8,128)(2,1)S(1)} collective-permute-done((bf16[2,160,1024]{2,1,0:T(8,128)(2,1)S(1)}, bf16[2,160,1024]{2,1,0:T(8,128)(2,1)S(1)}, u32[]{:S(2)}, u32[]{:S(2)}) %collective-permute-start.64) | collective-permute-done | bytes 655392 | tf_op jit(solution)/shard_map/ppermute | solution.py:1049
  318.1 4.1 shard_map.285
  326.2 4.7 shard_map.286
  330.9 3.6 shard_map.288
  335.4 10.6 %shard_map.289 = (bf16[320,4096]{1,0:T(8,128)(2,1)S(1)}, bf16[320,4096]{1,0:T(8,128)(2,1)S(1)}, f32[320,1024]{1,0:T(8,128)S(1)}) custom-call(bf16[320,1024]{1,0:T(8,128)(2,1)S(1)} %bitcast.326, bf16[16,768,1024]{2,1,0:T(8,128)(2,1)} %bitcast.352, bf16[16,768,1024]{2,1,0:T(8,128)(2,1)} %bitcast.353), custom_call_target="tpu_custom_call" | custom-call | flops 1 | bytes 1 | tf_op jit(solution)/shard_map/pallas_call | solution.py:196
  347.4 12.1 %shard_map.290 = (bf16[320,4096]{1,0:T(8,128)(2,1)S(1)}, f32[320,1024]{1,0:T(8,128)S(1)}) custom-call(bf16[320,1024]{1,0:T(8,128)(2,1)S(1)} %bitcast.324, bf16[320,4096]{1,0:T(8,128)(2,1)S(1)} %get-tuple-element.379.upper_ref, bf16[16,768,1024]{2,1,0:T(8,128)(2,1)} %bitcast.354, bf16[16,768,1024]{2,1,0:T(8,128)(2,1)} %bitcast.355), custom_call_target="tpu_custom_call" | custom-call | flops 1 | bytes 1 | tf_op jit(solution)/shard_map/pallas_call | solution.py:196
  362.7 4.4 shard_map.291
  368.0 10.6 %shard_map.292 = (bf16[8,320,384]{2,1,0:T(8,128)(2,1)S(1)}, bf16[8,320,256]{2,1,0:T(8,128)(2,1)}, f32[16,160,320]{2,1,0:T(8,128)S(1)}) custom-call(bf16[8,320,384]{2,1,0:T(8,128)(2,1)S(1)} %get-tuple-element.373.own_ref, bf16[8,320,384]{2,1,0:T(8,128)(2,1)S(1)} %collective-permute-done.65.other_ref, f32[16,160,320]{2,1,0:T(8,128)S(1)} %copy-done.4, ...), custom_call_target="tpu_custom_call" | custom-call | flops 1 | bytes 1 | tf_op jit(solution)/shard_map/pallas_call | solution.py:196
  386.8 4.8 shard_map.293
  395.3 3.4 copy-done.3
  398.7 4.7 shard_map.294
  416.9 5.7 shard_map.295
  427.8 7.5 %collective-permute-done.67 = bf16[2,160,1024]{2,1,0:T(8,128)(2,1)S(1)} collective-permute-done((bf16[2,160,1024]{2,1,0:T(8,128)(2,1)S(1)}, bf16[2,160,1024]{2,1,0:T(8,128)(2,1)S(1)}, u32[]{:S(2)}, u32[]{:S(2)}) %collective-permute-start.67) | collective-permute-done | bytes 655392 | tf_op jit(solution)/shard_map/ppermute | solution.py:1071
  437.0 12.0 %shard_map.296 = (bf16[320,4096]{1,0:T(8,128)(2,1)S(1)}, f32[320,1024]{1,0:T(8,128)S(1)}) custom-call(bf16[320,1024]{1,0:T(8,128)(2,1)S(1)} %bitcast.328, bf16[320,4096]{1,0:T(8,128)(2,1)S(1)} %copy-done.44, bf16[16,768,1024]{2,1,0:T(8,128)(2,1)} %bitcast.358, bf16[16,768,1024]{2,1,0:T(8,128)(2,1)} %bitcast.359), custom_call_target="tpu_custom_call" | custom-call | flops 1 | bytes 1 | tf_op jit(solution)/shard_map/pallas_call | solution.py:196
  452.1 4.4 shard_map.297
  458.2 4.4 all-to-all-start.5
  462.7 3.7 broadcast_select_fusion.u_ref
  466.8 4.9 shard_map.298
  481.3 4.2 all-to-all-start.6
  495.8 3.5 all-to-all-done.6
  499.3 4.2 all-to-all-start.7
  506.8 12.2 %shard_map.300 = (bf16[8,256,1024]{2,1,0:T(8,128)(2,1)S(1)}, bf16[8,256,1024]{2,1,0:T(8,128)(2,1)S(1)}) custom-call(s32[3,8]{1,0:T(4,128)S(1)} %add_add_fusion.4.order_ref, bf16[1024,640]{1,0:T(8,128)(2,1)S(1)} %copy-done.77, bf16[320,4096]{1,0:T(8,128)(2,1)} %broadcast_select_fusion.u_ref, bf16[320,4096]{1,0:T(8,128)(2,1)} %collective-permute-done.73.u2_ref, ...), custom_call_target="tpu_custom_call" | custom-call | flops 1 | bytes 1 | tf_op jit(solution)/shard_map/pallas_call | solution.py:710
  525.3 9.0 %collective-permute-done.75 = bf16[256,1024]{1,0:T(8,128)(2,1)} collective-permute-done((bf16[256,1024]{1,0:T(8,128)(2,1)}, bf16[256,1024]{1,0:T(8,128)(2,1)}, u32[]{:S(2)}, u32[]{:S(2)}) %collective-permute-start.75) | collective-permute-done | bytes 524320 | tf_op jit(solution)/shard_map/ppermute | solution.py:587
  546.2 8.4 %collective-permute-done.77 = bf16[256,1024]{1,0:T(8,128)(2,1)S(1)} collective-permute-done((bf16[256,1024]{1,0:T(8,128)(2,1)S(1)}, bf16[256,1024]{1,0:T(8,128)(2,1)S(1)}, u32[]{:S(2)}, u32[]{:S(2)}) %collective-permute-start.77) | collective-permute-done | bytes 524320 | tf_op jit(solution)/shard_map/ppermute | solution.py:587
  561.4 14.9 %shard_map.302 = (bf16[8,256,1024]{2,1,0:T(8,128)(2,1)S(1)}, bf16[8,256,1024]{2,1,0:T(8,128)(2,1)S(1)}) custom-call(s32[3,8]{1,0:T(4,128)S(1)} %add_add_fusion.4.order_ref, bf16[1024,640]{1,0:T(8,128)(2,1)S(1)} %copy-done.71, bf16[1024,640]{1,0:T(8,128)(2,1)S(1)} %copy-done.73, bf16[1024,640]{1,0:T(8,128)(2,1)S(1)} %copy-done.75, ...), custom_call_target="tpu_custom_call" | custom-call | flops 1 | bytes 1 | tf_op jit(solution)/shard_map/pallas_call | solution.py:710
  580.3 4.7 shard_map.303
  589.6 4.8 fusion.86
  607.2 6.5 collective-permute-done.104
  620.4 4.5 collective-permute-done.88
  643.0 4.3 collective-permute-done.90
  653.2 5.4 collective-permute-done.108
  665.3 6.5 collective-permute-done.95
  678.7 3.5 collective-permute-done.110
  684.3 8.9 %collective-permute-done.98 = f32[1,112,128]{2,1,0:T(8,128)S(1)} collective-permute-done((f32[1,112,128]{2,1,0:T(8,128)S(1)}, f32[1,112,128]{2,1,0:T(8,128)S(1)}, u32[]{:S(2)}, u32[]{:S(2)}) %collective-permute-start.98) | collective-permute-done | bytes 57376 | tf_op jit(solution)/shard_map/ppermute | solution.py:60
  698.4 10.7 %collective-permute-done.101 = f32[1,112,128]{2,1,0:T(8,128)S(1)} collective-permute-done((f32[1,112,128]{2,1,0:T(8,128)S(1)}, f32[1,112,128]{2,1,0:T(8,128)S(1)}, u32[]{:S(2)}, u32[]{:S(2)}) %collective-permute-start.101) | collective-permute-done | bytes 57376 | tf_op jit(solution)/shard_map/ppermute | solution.py:60
  (869 shorter events, 280.3 us)
Async XLA Ops:
  7.5 20.7 %collective-permute-start.4 = (bf16[128,1024]{1,0:T(8,128)(2,1)S(1)}, bf16[128,1024]{1,0:T(8,128)(2,1)}, u32[]{:S(2)}, u32[]{:S(2)}) collective-permute-start(bf16[128,1024]{1,0:T(8,128)(2,1)S(1)} %bitcast.375), channel_id=1, source_target_pairs={{0,1},{1,0},{2,3},{3,2},{4,5},{5,4},{6,7},{7,6},{8,9},{9,8},{10,11... | collective-permute-start | bytes 786440 | tf_op jit(solution)/shard_map/ppermute | solution.py:60
  8.3 20.0 %collective-permute-start.5 = (bf16[128,1024]{1,0:T(8,128)(2,1)}, bf16[128,1024]{1,0:T(8,128)(2,1)}, u32[]{:S(2)}, u32[]{:S(2)}) collective-permute-start(bf16[128,1024]{1,0:T(8,128)(2,1)} %bitcast.3.refs_1_), channel_id=1, source_target_pairs={{0,1},{1,0},{2,3},{3,2},{4,5},{5,4},{6,7},{7,6},{8,9},{9,8},{10,11... | collective-permute-start | bytes 786440 | tf_op jit(solution)/shard_map/ppermute | solution.py:60
  21.8 20.6 %collective-permute-start.9 = (bf16[128,1024]{1,0:T(8,128)(2,1)}, bf16[128,1024]{1,0:T(8,128)(2,1)S(1)}, u32[]{:S(2)}, u32[]{:S(2)}) collective-permute-start(bf16[128,1024]{1,0:T(8,128)(2,1)} %collective-permute-done.refs_4_), channel_id=1, source_target_pairs={{0,1},{1,0},{2,3},{3,2},{4,5},{5,4},{6,7},{7,6},{8,9},{9,8},{10,11... | collective-permute-start | bytes 786440 | tf_op jit(solution)/shard_map/ppermute | solution.py:60
  22.7 32.8 %all-to-all-start = ((bf16[8,2,10,1024]{3,1,2,0:T(2,128)(2,1)}), bf16[8,2,10,1024]{3,1,2,0:T(2,128)(2,1)S(1)}, u32[]{:S(2)}, u32[]{:S(2)}) async-start(bf16[8,2,10,1024]{3,1,2,0:T(2,128)(2,1)} %broadcast_in_dim.46), calls=%async_computation | async-start | bytes 655360 | tf_op jit(solution)/shard_map/all_to_all | solution.py:897
  87.2 18.5 %collective-permute-start.30 = (bf16[384,1024]{1,0:T(8,128)(2,1)S(1)}, bf16[384,1024]{1,0:T(8,128)(2,1)}, u32[]{:S(2)}, u32[]{:S(2)}) collective-permute-start(bf16[384,1024]{1,0:T(8,128)(2,1)S(1)} %pad_maximum_fusion.1.refs_0_), channel_id=1, source_target_pairs={{0,4},{1,5},{4,8},{5,9},{8,12},{9,13},{12,14},{13,15},{14,10},{15,... | collective-permute-start | bytes 2359304 | tf_op jit(solution)/shard_map/ppermute | solution.py:587
  88.4 18.1 %collective-permute-start.31 = (bf16[384,1024]{1,0:T(8,128)(2,1)S(1)}, bf16[384,1024]{1,0:T(8,128)(2,1)S(1)}, u32[]{:S(2)}, u32[]{:S(2)}) collective-permute-start(bf16[384,1024]{1,0:T(8,128)(2,1)S(1)} %pad_maximum_fusion.2.refs_1_), channel_id=1, source_target_pairs={{0,2},{1,3},{4,0},{5,1},{8,4},{9,5},{12,8},{13,9},{14,12},{15,13},... | collective-permute-start | bytes 2359304 | tf_op jit(solution)/shard_map/ppermute | solution.py:587
  108.0 37.2 %all-to-all-start.1 = ((bf16[8,160,384]{2,1,0:T(8,128)(2,1)}), bf16[8,160,384]{2,1,0:T(8,128)(2,1)S(1)}, u32[]{:S(2)}, u32[]{:S(2)}) async-start(bf16[8,160,384]{2,1,0:T(8,128)(2,1)} %get-tuple-element.521), calls=%async_computation.1 | async-start | bytes 1966080 | tf_op jit(solution)/shard_map/all_to_all | solution.py:897
  112.3 31.4 %collective-permute-start.36 = (bf16[384,1024]{1,0:T(8,128)(2,1)}, bf16[384,1024]{1,0:T(8,128)(2,1)S(1)}, u32[]{:S(2)}, u32[]{:S(2)}) collective-permute-start(bf16[384,1024]{1,0:T(8,128)(2,1)} %collective-permute-done.30.refs_4_), channel_id=1, source_target_pairs={{0,4},{1,5},{4,8},{5,9},{8,12},{9,13},{12,14},{13,15},{14,10},{15,... | collective-permute-start | bytes 2359304 | tf_op jit(solution)/shard_map/ppermute | solution.py:587
  125.5 19.6 %collective-permute-start.37 = (bf16[384,1024]{1,0:T(8,128)(2,1)}, bf16[384,1024]{1,0:T(8,128)(2,1)}, u32[]{:S(2)}, u32[]{:S(2)}) collective-permute-start(bf16[384,1024]{1,0:T(8,128)(2,1)} %copy-done.152), channel_id=1, source_target_pairs={{0,2},{1,3},{4,0},{5,1},{8,4},{9,5},{12,8},{13,9},{14,12},{15,13},... | collective-permute-start | bytes 2359304 | tf_op jit(solution)/shard_map/ppermute | solution.py:587
  145.1 17.7 %all-to-all-start.2 = ((bf16[8,160,384]{2,1,0:T(8,128)(2,1)}), bf16[8,160,384]{2,1,0:T(8,128)(2,1)S(1)}, u32[]{:S(2)}, u32[]{:S(2)}) async-start(bf16[8,160,384]{2,1,0:T(8,128)(2,1)} %get-tuple-element.319), calls=%async_computation.2 | async-start | bytes 1966080 | tf_op jit(solution)/shard_map/all_to_all | solution.py:897
  148.7 18.3 %collective-permute-start.42 = (bf16[384,1024]{1,0:T(8,128)(2,1)}, bf16[384,1024]{1,0:T(8,128)(2,1)}, u32[]{:S(2)}, u32[]{:S(2)}) collective-permute-start(bf16[384,1024]{1,0:T(8,128)(2,1)} %collective-permute-done.30.refs_4_), channel_id=1, source_target_pairs={{0,1},{1,0},{2,3},{3,2},{4,5},{5,4},{6,7},{7,6},{8,9},{9,8},{10,11... | collective-permute-start | bytes 2359304 | tf_op jit(solution)/shard_map/ppermute | solution.py:60
  149.1 18.0 %collective-permute-start.43 = (bf16[384,1024]{1,0:T(8,128)(2,1)}, bf16[384,1024]{1,0:T(8,128)(2,1)}, u32[]{:S(2)}, u32[]{:S(2)}) collective-permute-start(bf16[384,1024]{1,0:T(8,128)(2,1)} %copy-done.152), channel_id=1, source_target_pairs={{0,1},{1,0},{2,3},{3,2},{4,5},{5,4},{6,7},{7,6},{8,9},{9,8},{10,11... | collective-permute-start | bytes 2359304 | tf_op jit(solution)/shard_map/ppermute | solution.py:60
  149.3 30.5 %collective-permute-start.40 = (bf16[384,1024]{1,0:T(8,128)(2,1)}, bf16[384,1024]{1,0:T(8,128)(2,1)}, u32[]{:S(2)}, u32[]{:S(2)}) collective-permute-start(bf16[384,1024]{1,0:T(8,128)(2,1)} %copy-done.155), channel_id=1, source_target_pairs={{0,4},{1,5},{4,8},{5,9},{8,12},{9,13},{12,14},{13,15},{14,10},{15,... | collective-permute-start | bytes 2359304 | tf_op jit(solution)/shard_map/ppermute | solution.py:587
  151.2 28.7 %collective-permute-start.41 = (bf16[384,1024]{1,0:T(8,128)(2,1)}, bf16[384,1024]{1,0:T(8,128)(2,1)}, u32[]{:S(2)}, u32[]{:S(2)}) collective-permute-start(bf16[384,1024]{1,0:T(8,128)(2,1)} %collective-permute-done.37.refs_9_), channel_id=1, source_target_pairs={{0,2},{1,3},{4,0},{5,1},{8,4},{9,5},{12,8},{13,9},{14,12},{15,13},... | collective-permute-start | bytes 2359304 | tf_op jit(solution)/shard_map/ppermute | solution.py:587
  162.9 22.0 %all-to-all-start.3 = ((bf16[8,160,128]{2,1,0:T(8,128)(2,1)}), bf16[8,160,128]{2,1,0:T(8,128)(2,1)S(1)}, u32[]{:S(2)}, u32[]{:S(2)}) async-start(bf16[8,160,128]{2,1,0:T(8,128)(2,1)} %bitcast.26), calls=%async_computation.3 | async-start | bytes 655360 | tf_op jit(solution)/shard_map/all_to_all | solution.py:897
  166.5 25.5 %collective-permute-start.46 = (bf16[384,1024]{1,0:T(8,128)(2,1)}, bf16[384,1024]{1,0:T(8,128)(2,1)}, u32[]{:S(2)}, u32[]{:S(2)}) collective-permute-start(bf16[384,1024]{1,0:T(8,128)(2,1)} %copy-done.155), channel_id=1, source_target_pairs={{0,1},{1,0},{2,3},{3,2},{4,5},{5,4},{6,7},{7,6},{8,9},{9,8},{10,11... | collective-permute-start | bytes 2359304 | tf_op jit(solution)/shard_map/ppermute | solution.py:60
  167.0 25.2 %collective-permute-start.47 = (bf16[384,1024]{1,0:T(8,128)(2,1)}, bf16[384,1024]{1,0:T(8,128)(2,1)}, u32[]{:S(2)}, u32[]{:S(2)}) collective-permute-start(bf16[384,1024]{1,0:T(8,128)(2,1)} %collective-permute-done.37.refs_9_), channel_id=1, source_target_pairs={{0,1},{1,0},{2,3},{3,2},{4,5},{5,4},{6,7},{7,6},{8,9},{9,8},{10,11... | collective-permute-start | bytes 2359304 | tf_op jit(solution)/shard_map/ppermute | solution.py:60
  179.8 23.5 %collective-permute-start.44 = (bf16[384,1024]{1,0:T(8,128)(2,1)}, bf16[384,1024]{1,0:T(8,128)(2,1)}, u32[]{:S(2)}, u32[]{:S(2)}) collective-permute-start(bf16[384,1024]{1,0:T(8,128)(2,1)} %collective-permute-done.40.refs_12_), channel_id=1, source_target_pairs={{0,4},{1,5},{4,8},{5,9},{8,12},{9,13},{12,14},{13,15},{14,10},{15,... | collective-permute-start | bytes 2359304 | tf_op jit(solution)/shard_map/ppermute | solution.py:587
  180.0 23.3 %collective-permute-start.45 = (bf16[384,1024]{1,0:T(8,128)(2,1)}, bf16[384,1024]{1,0:T(8,128)(2,1)}, u32[]{:S(2)}, u32[]{:S(2)}) collective-permute-start(bf16[384,1024]{1,0:T(8,128)(2,1)} %collective-permute-done.41.refs_13_), channel_id=1, source_target_pairs={{0,2},{1,3},{4,0},{5,1},{8,4},{9,5},{12,8},{13,9},{14,12},{15,13},... | collective-permute-start | bytes 2359304 | tf_op jit(solution)/shard_map/ppermute | solution.py:587
  184.9 18.4 %all-to-all-start.4 = ((bf16[8,160,128]{2,1,0:T(8,128)(2,1)}), bf16[8,160,128]{2,1,0:T(8,128)(2,1)}, u32[]{:S(2)}, u32[]{:S(2)}) async-start(bf16[8,160,128]{2,1,0:T(8,128)(2,1)} %bitcast.27), calls=%async_computation.4 | async-start | bytes 655360 | tf_op jit(solution)/shard_map/all_to_all | solution.py:897
  191.6 19.2 %collective-permute-start.50 = (bf16[384,1024]{1,0:T(8,128)(2,1)}, bf16[384,1024]{1,0:T(8,128)(2,1)}, u32[]{:S(2)}, u32[]{:S(2)}) collective-permute-start(bf16[384,1024]{1,0:T(8,128)(2,1)} %collective-permute-done.40.refs_12_), channel_id=1, source_target_pairs={{0,1},{1,0},{2,3},{3,2},{4,5},{5,4},{6,7},{7,6},{8,9},{9,8},{10,11... | collective-permute-start | bytes 2359304 | tf_op jit(solution)/shard_map/ppermute | solution.py:60
  192.0 19.3 %collective-permute-start.51 = (bf16[384,1024]{1,0:T(8,128)(2,1)}, bf16[384,1024]{1,0:T(8,128)(2,1)}, u32[]{:S(2)}, u32[]{:S(2)}) collective-permute-start(bf16[384,1024]{1,0:T(8,128)(2,1)} %collective-permute-done.41.refs_13_), channel_id=1, source_target_pairs={{0,1},{1,0},{2,3},{3,2},{4,5},{5,4},{6,7},{7,6},{8,9},{9,8},{10,11... | collective-permute-start | bytes 2359304 | tf_op jit(solution)/shard_map/ppermute | solution.py:60
  203.3 19.3 %collective-permute-start.48 = (bf16[384,1024]{1,0:T(8,128)(2,1)}, bf16[384,1024]{1,0:T(8,128)(2,1)S(1)}, u32[]{:S(2)}, u32[]{:S(2)}) collective-permute-start(bf16[384,1024]{1,0:T(8,128)(2,1)} %collective-permute-done.44.refs_0_), channel_id=1, source_target_pairs={{0,4},{1,5},{4,8},{5,9},{8,12},{9,13},{12,14},{13,15},{14,10},{15,... | collective-permute-start | bytes 2359304 | tf_op jit(solution)/shard_map/ppermute | solution.py:587
  204.1 18.8 %collective-permute-start.49 = (bf16[384,1024]{1,0:T(8,128)(2,1)}, bf16[384,1024]{1,0:T(8,128)(2,1)S(1)}, u32[]{:S(2)}, u32[]{:S(2)}) collective-permute-start(bf16[384,1024]{1,0:T(8,128)(2,1)} %collective-permute-done.45.refs_1_), channel_id=1, source_target_pairs={{0,2},{1,3},{4,0},{5,1},{8,4},{9,5},{12,8},{13,9},{14,12},{15,13},... | collective-permute-start | bytes 2359304 | tf_op jit(solution)/shard_map/ppermute | solution.py:587
  209.6 25.0 %collective-permute-start.54 = (bf16[384,1024]{1,0:T(8,128)(2,1)}, bf16[384,1024]{1,0:T(8,128)(2,1)S(1)}, u32[]{:S(2)}, u32[]{:S(2)}) collective-permute-start(bf16[384,1024]{1,0:T(8,128)(2,1)} %collective-permute-done.44.refs_0_), channel_id=1, source_target_pairs={{0,1},{1,0},{2,3},{3,2},{4,5},{5,4},{6,7},{7,6},{8,9},{9,8},{10,11... | collective-permute-start | bytes 2359304 | tf_op jit(solution)/shard_map/ppermute | solution.py:60
  210.8 24.6 %collective-permute-start.55 = (bf16[384,1024]{1,0:T(8,128)(2,1)}, bf16[384,1024]{1,0:T(8,128)(2,1)S(1)}, u32[]{:S(2)}, u32[]{:S(2)}) collective-permute-start(bf16[384,1024]{1,0:T(8,128)(2,1)} %collective-permute-done.45.refs_1_), channel_id=1, source_target_pairs={{0,1},{1,0},{2,3},{3,2},{4,5},{5,4},{6,7},{7,6},{8,9},{9,8},{10,11... | collective-permute-start | bytes 2359304 | tf_op jit(solution)/shard_map/ppermute | solution.py:60
  222.8 18.2 %collective-permute-start.52 = (bf16[384,1024]{1,0:T(8,128)(2,1)S(1)}, bf16[384,1024]{1,0:T(8,128)(2,1)}, u32[]{:S(2)}, u32[]{:S(2)}) collective-permute-start(bf16[384,1024]{1,0:T(8,128)(2,1)S(1)} %collective-permute-done.48.refs_4_), channel_id=1, source_target_pairs={{0,4},{1,5},{4,8},{5,9},{8,12},{9,13},{12,14},{13,15},{14,10},{15,... | collective-permute-start | bytes 2359304 | tf_op jit(solution)/shard_map/ppermute | solution.py:587
  223.9 17.7 %collective-permute-start.53 = (bf16[384,1024]{1,0:T(8,128)(2,1)S(1)}, bf16[384,1024]{1,0:T(8,128)(2,1)}, u32[]{:S(2)}, u32[]{:S(2)}) collective-permute-start(bf16[384,1024]{1,0:T(8,128)(2,1)S(1)} %collective-permute-done.49.refs_5_), channel_id=1, source_target_pairs={{0,2},{1,3},{4,0},{5,1},{8,4},{9,5},{12,8},{13,9},{14,12},{15,13},... | collective-permute-start | bytes 2359304 | tf_op jit(solution)/shard_map/ppermute | solution.py:587
  224.8 18.8 %collective-permute-start.58 = (bf16[384,1024]{1,0:T(8,128)(2,1)S(1)}, bf16[384,1024]{1,0:T(8,128)(2,1)S(1)}, u32[]{:S(2)}, u32[]{:S(2)}) collective-permute-start(bf16[384,1024]{1,0:T(8,128)(2,1)S(1)} %collective-permute-done.48.refs_4_), channel_id=1, source_target_pairs={{0,1},{1,0},{2,3},{3,2},{4,5},{5,4},{6,7},{7,6},{8,9},{9,8},{10,11... | collective-permute-start | bytes 2359304 | tf_op jit(solution)/shard_map/ppermute | solution.py:60
  241.6 17.0 %collective-permute-start.56 = (bf16[384,1024]{1,0:T(8,128)(2,1)}, bf16[384,1024]{1,0:T(8,128)(2,1)}, u32[]{:S(2)}, u32[]{:S(2)}) collective-permute-start(bf16[384,1024]{1,0:T(8,128)(2,1)} %collective-permute-done.52.refs_8_), channel_id=1, source_target_pairs={{0,4},{1,5},{4,8},{5,9},{8,12},{9,13},{12,14},{13,15},{14,10},{15,... | collective-permute-start | bytes 2359304 | tf_op jit(solution)/shard_map/ppermute | solution.py:587
  242.4 16.5 %collective-permute-start.57 = (bf16[384,1024]{1,0:T(8,128)(2,1)}, bf16[384,1024]{1,0:T(8,128)(2,1)}, u32[]{:S(2)}, u32[]{:S(2)}) collective-permute-start(bf16[384,1024]{1,0:T(8,128)(2,1)} %collective-permute-done.53.refs_9_), channel_id=1, source_target_pairs={{0,2},{1,3},{4,0},{5,1},{8,4},{9,5},{12,8},{13,9},{14,12},{15,13},... | collective-permute-start | bytes 2359304 | tf_op jit(solution)/shard_map/ppermute | solution.py:587
  243.7 16.2 %collective-permute-start.60 = (bf16[384,1024]{1,0:T(8,128)(2,1)}, bf16[384,1024]{1,0:T(8,128)(2,1)}, u32[]{:S(2)}, u32[]{:S(2)}) collective-permute-start(bf16[384,1024]{1,0:T(8,128)(2,1)} %collective-permute-done.52.refs_8_), channel_id=1, source_target_pairs={{0,1},{1,0},{2,3},{3,2},{4,5},{5,4},{6,7},{7,6},{8,9},{9,8},{10,11... | collective-permute-start | bytes 2359304 | tf_op jit(solution)/shard_map/ppermute | solution.py:60
  243.7 16.2 %collective-permute-start.61 = (bf16[384,1024]{1,0:T(8,128)(2,1)}, bf16[384,1024]{1,0:T(8,128)(2,1)S(1)}, u32[]{:S(2)}, u32[]{:S(2)}) collective-permute-start(bf16[384,1024]{1,0:T(8,128)(2,1)} %collective-permute-done.53.refs_9_), channel_id=1, source_target_pairs={{0,1},{1,0},{2,3},{3,2},{4,5},{5,4},{6,7},{7,6},{8,9},{9,8},{10,11... | collective-permute-start | bytes 2359304 | tf_op jit(solution)/shard_map/ppermute | solution.py:60
  299.5 17.6 %collective-permute-start.64 = (bf16[2,160,1024]{2,1,0:T(8,128)(2,1)S(1)}, bf16[2,160,1024]{2,1,0:T(8,128)(2,1)S(1)}, u32[]{:S(2)}, u32[]{:S(2)}) collective-permute-start(bf16[2,160,1024]{2,1,0:T(8,128)(2,1)S(1)} %get-tuple-element.543), channel_id=1, source_target_pairs={{0,16},{1,17},{2,18},{3,19},{4,20},{5,21},{6,22},{7,23},{8,24},{9,... | collective-permute-start | bytes 1966088 | tf_op jit(solution)/shard_map/ppermute | solution.py:1049
  408.2 27.1 %collective-permute-start.72 = (bf16[320,4096]{1,0:T(8,128)(2,1)S(1)}, bf16[320,4096]{1,0:T(8,128)(2,1)S(1)}, u32[]{:S(2)}, u32[]{:S(2)}) collective-permute-start(bf16[320,4096]{1,0:T(8,128)(2,1)S(1)} %broadcast_select_fusion.1.a_ref), channel_id=1, source_target_pairs={{0,1},{1,0},{2,3},{3,2},{4,5},{5,4},{6,7},{7,6},{8,9},{9,8},{10,11... | collective-permute-start | bytes 7864328 | tf_op jit(solution)/shard_map/ppermute | solution.py:60
  414.1 21.2 %collective-permute-start.67 = (bf16[2,160,1024]{2,1,0:T(8,128)(2,1)S(1)}, bf16[2,160,1024]{2,1,0:T(8,128)(2,1)S(1)}, u32[]{:S(2)}, u32[]{:S(2)}) collective-permute-start(bf16[2,160,1024]{2,1,0:T(8,128)(2,1)S(1)} %get-tuple-element.391), channel_id=1, source_target_pairs={{16,0},{17,1},{18,2},{19,3},{20,4},{21,5},{22,6},{23,7},{24,8},{25... | collective-permute-start | bytes 1966088 | tf_op jit(solution)/shard_map/ppermute | solution.py:1071
  458.2 15.8 %all-to-all-start.5 = ((bf16[8,320,128]{2,1,0:T(8,128)(2,1)}), bf16[8,320,128]{2,1,0:T(8,128)(2,1)}, u32[]{:S(2)}, u32[]{:S(2)}) async-start(bf16[8,320,128]{2,1,0:T(8,128)(2,1)} %copy-done.82), calls=%async_computation.5 | async-start | bytes 1310720 | tf_op jit(solution)/shard_map/all_to_all | solution.py:897
  466.4 38.7 %collective-permute-start.73 = (bf16[320,4096]{1,0:T(8,128)(2,1)}, bf16[320,4096]{1,0:T(8,128)(2,1)}, u32[]{:S(2)}, u32[]{:S(2)}) collective-permute-start(bf16[320,4096]{1,0:T(8,128)(2,1)} %broadcast_select_fusion.u_ref), channel_id=1, source_target_pairs={{0,1},{1,0},{2,3},{3,2},{4,5},{5,4},{6,7},{7,6},{8,9},{9,8},{10,11... | collective-permute-start | bytes 7864328 | tf_op jit(solution)/shard_map/ppermute | solution.py:60
  481.3 18.0 %all-to-all-start.6 = ((bf16[8,160,384]{2,1,0:T(8,128)(2,1)}), bf16[8,160,384]{2,1,0:T(8,128)(2,1)}, u32[]{:S(2)}, u32[]{:S(2)}) async-start(bf16[8,160,384]{2,1,0:T(8,128)(2,1)} %bitcast.344), calls=%async_computation.6 | async-start | bytes 1966080 | tf_op jit(solution)/shard_map/all_to_all | solution.py:897
  487.8 17.3 %collective-permute-start.74 = (bf16[320,1024]{1,0:T(8,128)(2,1)}, bf16[320,1024]{1,0:T(8,128)(2,1)}, u32[]{:S(2)}, u32[]{:S(2)}) collective-permute-start(bf16[320,1024]{1,0:T(8,128)(2,1)} %broadcast_select_fusion.6.f_ref), channel_id=1, source_target_pairs={{0,1},{1,0},{2,3},{3,2},{4,5},{5,4},{6,7},{7,6},{8,9},{9,8},{10,11... | collective-permute-start | bytes 1966088 | tf_op jit(solution)/shard_map/ppermute | solution.py:60
  499.3 26.0 %all-to-all-start.7 = ((bf16[8,160,384]{2,1,0:T(8,128)(2,1)}), bf16[8,160,384]{2,1,0:T(8,128)(2,1)}, u32[]{:S(2)}, u32[]{:S(2)}) async-start(bf16[8,160,384]{2,1,0:T(8,128)(2,1)} %bitcast.343), calls=%async_computation.7 | async-start | bytes 1966080 | tf_op jit(solution)/shard_map/all_to_all | solution.py:897
  504.7 39.3 %collective-permute-start.79 = (bf16[320,1024]{1,0:T(8,128)(2,1)}, bf16[320,1024]{1,0:T(8,128)(2,1)}, u32[]{:S(2)}, u32[]{:S(2)}) collective-permute-start(bf16[320,1024]{1,0:T(8,128)(2,1)} %broadcast_select_fusion.5.a_ref), channel_id=1, source_target_pairs={{0,1},{1,0},{2,3},{3,2},{4,5},{5,4},{6,7},{7,6},{8,9},{9,8},{10,11... | collective-permute-start | bytes 1966088 | tf_op jit(solution)/shard_map/ppermute | solution.py:60
  522.9 21.2 %collective-permute-start.80 = (bf16[320,1024]{1,0:T(8,128)(2,1)S(1)}, bf16[320,1024]{1,0:T(8,128)(2,1)}, u32[]{:S(2)}, u32[]{:S(2)}) collective-permute-start(bf16[320,1024]{1,0:T(8,128)(2,1)S(1)} %broadcast_select_fusion.4.b_ref), channel_id=1, source_target_pairs={{0,1},{1,0},{2,3},{3,2},{4,5},{5,4},{6,7},{7,6},{8,9},{9,8},{10,11... | collective-permute-start | bytes 1966088 | tf_op jit(solution)/shard_map/ppermute | solution.py:60
  538.6 22.8 %collective-permute-start.85 = (bf16[8,320,384]{2,1,0:T(8,128)(2,1)S(1)}, bf16[8,320,384]{2,1,0:T(8,128)(2,1)S(1)}, u32[]{:S(2)}, u32[]{:S(2)}) collective-permute-start(bf16[8,320,384]{2,1,0:T(8,128)(2,1)S(1)} %broadcast_select_fusion.2.j_ref), channel_id=1, source_target_pairs={{0,1},{1,0},{2,3},{3,2},{4,5},{5,4},{6,7},{7,6},{8,9},{9,8},{10,11... | collective-permute-start | bytes 5898248 | tf_op jit(solution)/shard_map/ppermute | solution.py:60
  557.5 18.9 %collective-permute-start.83 = (bf16[256,1024]{1,0:T(8,128)(2,1)S(1)}, bf16[256,1024]{1,0:T(8,128)(2,1)S(1)}, u32[]{:S(2)}, u32[]{:S(2)}) collective-permute-start(bf16[256,1024]{1,0:T(8,128)(2,1)S(1)} %fusion.49), channel_id=1, source_target_pairs={{0,4},{1,5},{4,8},{5,9},{8,12},{9,13},{12,14},{13,15},{14,10},{15,... | collective-permute-start | bytes 1572872 | tf_op jit(solution)/shard_map/ppermute | solution.py:587
  560.5 15.9 %collective-permute-start.84 = (bf16[256,1024]{1,0:T(8,128)(2,1)S(1)}, bf16[256,1024]{1,0:T(8,128)(2,1)S(1)}, u32[]{:S(2)}, u32[]{:S(2)}) collective-permute-start(bf16[256,1024]{1,0:T(8,128)(2,1)S(1)} %fusion.48), channel_id=1, source_target_pairs={{0,2},{1,3},{4,0},{5,1},{8,4},{9,5},{12,8},{13,9},{14,12},{15,13},... | collective-permute-start | bytes 1572872 | tf_op jit(solution)/shard_map/ppermute | solution.py:587
  577.2 24.8 %collective-permute-start.86 = (bf16[256,1024]{1,0:T(8,128)(2,1)}, bf16[256,1024]{1,0:T(8,128)(2,1)}, u32[]{:S(2)}, u32[]{:S(2)}) collective-permute-start(bf16[256,1024]{1,0:T(8,128)(2,1)} %slice_bitcast_fusion.2), channel_id=1, source_target_pairs={{0,4},{1,5},{4,8},{5,9},{8,12},{9,13},{12,14},{13,15},{14,10},{15,... | collective-permute-start | bytes 1572872 | tf_op jit(solution)/shard_map/ppermute | solution.py:587
  580.2 21.8 %collective-permute-start.87 = (bf16[256,1024]{1,0:T(8,128)(2,1)}, bf16[256,1024]{1,0:T(8,128)(2,1)}, u32[]{:S(2)}, u32[]{:S(2)}) collective-permute-start(bf16[256,1024]{1,0:T(8,128)(2,1)} %slice_bitcast_fusion.1), channel_id=1, source_target_pairs={{0,2},{1,3},{4,0},{5,1},{8,4},{9,5},{12,8},{13,9},{14,12},{15,13},... | collective-permute-start | bytes 1572872 | tf_op jit(solution)/shard_map/ppermute | solution.py:587
  603.6 21.2 %collective-permute-start.88 = (bf16[256,1024]{1,0:T(8,128)(2,1)S(1)}, bf16[256,1024]{1,0:T(8,128)(2,1)S(1)}, u32[]{:S(2)}, u32[]{:S(2)}) collective-permute-start(bf16[256,1024]{1,0:T(8,128)(2,1)S(1)} %fusion.47), channel_id=1, source_target_pairs={{0,4},{1,5},{4,8},{5,9},{8,12},{9,13},{12,14},{13,15},{14,10},{15,... | collective-permute-start | bytes 1572872 | tf_op jit(solution)/shard_map/ppermute | solution.py:587
  607.1 21.0 %collective-permute-start.89 = (bf16[256,1024]{1,0:T(8,128)(2,1)S(1)}, bf16[256,1024]{1,0:T(8,128)(2,1)S(1)}, u32[]{:S(2)}, u32[]{:S(2)}) collective-permute-start(bf16[256,1024]{1,0:T(8,128)(2,1)S(1)} %fusion.46), channel_id=1, source_target_pairs={{0,2},{1,3},{4,0},{5,1},{8,4},{9,5},{12,8},{13,9},{14,12},{15,13},... | collective-permute-start | bytes 1572872 | tf_op jit(solution)/shard_map/ppermute | solution.py:587
  618.1 18.0 %collective-permute-start.106 = (bf16[256,1024]{1,0:T(8,128)(2,1)S(1)}, bf16[256,1024]{1,0:T(8,128)(2,1)S(1)}, u32[]{:S(2)}, u32[]{:S(2)}) collective-permute-start(bf16[256,1024]{1,0:T(8,128)(2,1)S(1)} %fusion.33), channel_id=1, source_target_pairs={{0,4},{1,5},{4,8},{5,9},{8,12},{9,13},{12,14},{13,15},{14,10},{15,... | collective-permute-start | bytes 1572872 | tf_op jit(solution)/shard_map/ppermute | solution.py:587
  619.3 20.0 %collective-permute-start.107 = (bf16[256,1024]{1,0:T(8,128)(2,1)S(1)}, bf16[256,1024]{1,0:T(8,128)(2,1)S(1)}, u32[]{:S(2)}, u32[]{:S(2)}) collective-permute-start(bf16[256,1024]{1,0:T(8,128)(2,1)S(1)} %fusion.32), channel_id=1, source_target_pairs={{0,2},{1,3},{4,0},{5,1},{8,4},{9,5},{12,8},{13,9},{14,12},{15,13},... | collective-permute-start | bytes 1572872 | tf_op jit(solution)/shard_map/ppermute | solution.py:587
  629.4 18.0 %collective-permute-start.90 = (bf16[256,1024]{1,0:T(8,128)(2,1)S(1)}, bf16[256,1024]{1,0:T(8,128)(2,1)S(1)}, u32[]{:S(2)}, u32[]{:S(2)}) collective-permute-start(bf16[256,1024]{1,0:T(8,128)(2,1)S(1)} %fusion.45), channel_id=1, source_target_pairs={{0,4},{1,5},{4,8},{5,9},{8,12},{9,13},{12,14},{13,15},{14,10},{15,... | collective-permute-start | bytes 1572872 | tf_op jit(solution)/shard_map/ppermute | solution.py:587
  631.8 18.8 %collective-permute-start.91 = (bf16[256,1024]{1,0:T(8,128)(2,1)S(1)}, bf16[256,1024]{1,0:T(8,128)(2,1)S(1)}, u32[]{:S(2)}, u32[]{:S(2)}) collective-permute-start(bf16[256,1024]{1,0:T(8,128)(2,1)S(1)} %fusion.44), channel_id=1, source_target_pairs={{0,2},{1,3},{4,0},{5,1},{8,4},{9,5},{12,8},{13,9},{14,12},{15,13},... | collective-permute-start | bytes 1572872 | tf_op jit(solution)/shard_map/ppermute | solution.py:587
  640.7 17.9 %collective-permute-start.108 = (bf16[256,1024]{1,0:T(8,128)(2,1)S(1)}, bf16[256,1024]{1,0:T(8,128)(2,1)S(1)}, u32[]{:S(2)}, u32[]{:S(2)}) collective-permute-start(bf16[256,1024]{1,0:T(8,128)(2,1)S(1)} %fusion.31), channel_id=1, source_target_pairs={{0,4},{1,5},{4,8},{5,9},{8,12},{9,13},{12,14},{13,15},{14,10},{15,... | collective-permute-start | bytes 1572872 | tf_op jit(solution)/shard_map/ppermute | solution.py:587
  641.9 19.9 %collective-permute-start.109 = (bf16[256,1024]{1,0:T(8,128)(2,1)S(1)}, bf16[256,1024]{1,0:T(8,128)(2,1)S(1)}, u32[]{:S(2)}, u32[]{:S(2)}) collective-permute-start(bf16[256,1024]{1,0:T(8,128)(2,1)S(1)} %fusion.30), channel_id=1, source_target_pairs={{0,2},{1,3},{4,0},{5,1},{8,4},{9,5},{12,8},{13,9},{14,12},{15,13},... | collective-permute-start | bytes 1572872 | tf_op jit(solution)/shard_map/ppermute | solution.py:587
  650.8 21.1 %collective-permute-start.93 = (bf16[256,1024]{1,0:T(8,128)(2,1)S(1)}, bf16[256,1024]{1,0:T(8,128)(2,1)S(1)}, u32[]{:S(2)}, u32[]{:S(2)}) collective-permute-start(bf16[256,1024]{1,0:T(8,128)(2,1)S(1)} %fusion.43), channel_id=1, source_target_pairs={{0,4},{1,5},{4,8},{5,9},{8,12},{9,13},{12,14},{13,15},{14,10},{15,... | collective-permute-start | bytes 1572872 | tf_op jit(solution)/shard_map/ppermute | solution.py:587
  652.1 21.0 %collective-permute-start.94 = (bf16[256,1024]{1,0:T(8,128)(2,1)S(1)}, bf16[256,1024]{1,0:T(8,128)(2,1)S(1)}, u32[]{:S(2)}, u32[]{:S(2)}) collective-permute-start(bf16[256,1024]{1,0:T(8,128)(2,1)S(1)} %fusion.42), channel_id=1, source_target_pairs={{0,2},{1,3},{4,0},{5,1},{8,4},{9,5},{12,8},{13,9},{14,12},{15,13},... | collective-permute-start | bytes 1572872 | tf_op jit(solution)/shard_map/ppermute | solution.py:587
  653.1 18.7 %collective-permute-start.95 = (f32[1,112,128]{2,1,0:T(8,128)S(1)}, f32[1,112,128]{2,1,0:T(8,128)S(1)}, u32[]{:S(2)}, u32[]{:S(2)}) collective-permute-start(f32[1,112,128]{2,1,0:T(8,128)S(1)} %add.447), channel_id=1, source_target_pairs={{0,2},{1,3},{2,0},{3,1},{4,6},{5,7},{6,4},{7,5},{8,10},{9,11},{10,... | collective-permute-start | bytes 172040 | tf_op jit(solution)/shard_map/ppermute | solution.py:60
  663.0 19.3 %collective-permute-start.110 = (bf16[256,1024]{1,0:T(8,128)(2,1)S(1)}, bf16[256,1024]{1,0:T(8,128)(2,1)S(1)}, u32[]{:S(2)}, u32[]{:S(2)}) collective-permute-start(bf16[256,1024]{1,0:T(8,128)(2,1)S(1)} %fusion.29), channel_id=1, source_target_pairs={{0,4},{1,5},{4,8},{5,9},{8,12},{9,13},{12,14},{13,15},{14,10},{15,... | collective-permute-start | bytes 1572872 | tf_op jit(solution)/shard_map/ppermute | solution.py:587
  664.3 20.0 %collective-permute-start.111 = (bf16[256,1024]{1,0:T(8,128)(2,1)S(1)}, bf16[256,1024]{1,0:T(8,128)(2,1)S(1)}, u32[]{:S(2)}, u32[]{:S(2)}) collective-permute-start(bf16[256,1024]{1,0:T(8,128)(2,1)S(1)} %fusion.28), channel_id=1, source_target_pairs={{0,2},{1,3},{4,0},{5,1},{8,4},{9,5},{12,8},{13,9},{14,12},{15,13},... | collective-permute-start | bytes 1572872 | tf_op jit(solution)/shard_map/ppermute | solution.py:587
  673.3 19.9 %collective-permute-start.96 = (bf16[256,1024]{1,0:T(8,128)(2,1)S(1)}, bf16[256,1024]{1,0:T(8,128)(2,1)S(1)}, u32[]{:S(2)}, u32[]{:S(2)}) collective-permute-start(bf16[256,1024]{1,0:T(8,128)(2,1)S(1)} %fusion.41), channel_id=1, source_target_pairs={{0,4},{1,5},{4,8},{5,9},{8,12},{9,13},{12,14},{13,15},{14,10},{15,... | collective-permute-start | bytes 1572872 | tf_op jit(solution)/shard_map/ppermute | solution.py:587
  674.5 18.7 %collective-permute-start.97 = (bf16[256,1024]{1,0:T(8,128)(2,1)S(1)}, bf16[256,1024]{1,0:T(8,128)(2,1)S(1)}, u32[]{:S(2)}, u32[]{:S(2)}) collective-permute-start(bf16[256,1024]{1,0:T(8,128)(2,1)S(1)} %fusion.40), channel_id=1, source_target_pairs={{0,2},{1,3},{4,0},{5,1},{8,4},{9,5},{12,8},{13,9},{14,12},{15,13},... | collective-permute-start | bytes 1572872 | tf_op jit(solution)/shard_map/ppermute | solution.py:587
  676.8 16.4 %collective-permute-start.98 = (f32[1,112,128]{2,1,0:T(8,128)S(1)}, f32[1,112,128]{2,1,0:T(8,128)S(1)}, u32[]{:S(2)}, u32[]{:S(2)}) collective-permute-start(f32[1,112,128]{2,1,0:T(8,128)S(1)} %add.450), channel_id=1, source_target_pairs={{0,4},{1,5},{2,6},{3,7},{4,0},{5,1},{6,2},{7,3},{8,12},{9,13},{10,... | collective-permute-start | bytes 172040 | tf_op jit(solution)/shard_map/ppermute | solution.py:60
  (280 other events, 2684.8 us)

commit v4 on v3

--- a/solution.py
+++ b/solution.py
@@ -394,11 +394,10 @@
     return call(
         text_project_kernel,
         (2 * D // SET,),
-        [rows_spec(text.shape), block_spec(6)],
+        [rows_spec(text.shape), block_spec(4)],
         pl.BlockSpec((text.shape[0], SET), lambda j: (0, j)),
         shaped((text.shape[0], 2 * D)),
         (text, packed),
-        LARGE,
     )
 
 
@@ -412,7 +411,7 @@
     return call(
         merge_kernel,
         (D // SET,),
-        [rows_spec((MEMBERS, tokens, PAIR)), rows_spec((tokens, D)), block_spec(0), block_spec(1)],
+        [rows_spec((MEMBERS, tokens, PAIR)), rows_spec((tokens, D)), block_spec(8), block_spec(9)],
         pl.BlockSpec((tokens, SET), lambda j: (0, j)),
         shaped((tokens, D), HIGH),
         (o, text, packed, packed),
@@ -436,8 +435,8 @@
         (D // height,),
         [
             rows_spec((tokens, D)),
-            pl.BlockSpec((parts, ROWS_OF_PART, D), lambda j: (j, 0, 0)),
-            pl.BlockSpec((parts, ROWS_OF_PART, D), lambda j: (j, 1, 0)),
+            pl.BlockSpec((parts, ROWS_OF_PART, D), lambda j: (j, 8, 0)),
+            pl.BlockSpec((parts, ROWS_OF_PART, D), lambda j: (j, 9, 0)),
         ],
         [pl.BlockSpec((2, tokens, PAIR), lambda j: (j, 0, 0)), pl.BlockSpec((tokens, height), lambda j: (0, j))],
         [shaped((MEMBERS, tokens, PAIR)), shaped((tokens, D))],
@@ -463,8 +462,8 @@
 
 def feed_specs(tokens):
     strip = pl.BlockSpec((tokens, STRIP), lambda j: (0, j))
-    down = pl.BlockSpec((STRIP // (FF // PARTS), FF // PARTS, D), lambda j: (j, 2, 0))
-    return rows_spec((tokens, D)), strip, wide_spec(2), down
+    down = pl.BlockSpec((STRIP // (FF // PARTS), FF // PARTS, D), lambda j: (j, 0, 0))
+    return rows_spec((tokens, D)), strip, wide_spec(4), down
 
 
 def feed_call(second, packed):
@@ -587,7 +586,7 @@
     return lax.ppermute(x, ("section", "dp"), route)
 
 
-def ring_gather(own):
+def ring_gather(own, early):
     chips = len(RING)
     half = own.shape[0] // 2
     chunks = [own[:half], own[half:]]
@@ -606,19 +605,16 @@
             for i, pair in enumerate(held[:-1]):
                 pair[1] = list(tied[2 + 2 * i : 4 + 2 * i])
             side = tied[2 + len(before) :]
-        if step == EARLY:
-            made = assembled(held, 0, None)
-        if step == EARLY + 1:
+        if step == early:
+            made = assembled(held, 0, early, None)
+        if step == early + 1:
             made, *chunks = together(made, *chunks)
-    return assembled(held, EARLY, made), side
-
-
-EARLY = 4
-
-
-def assembled(held, start, made):
-    held = held[start:EARLY] if made is None else held[start:]
+    return assembled(held, early, chips, made), side
+
+
+def assembled(held, start, end, made):
     chips = len(RING)
+    held = held[start:end]
     spots, core = device_ring()
     order = jnp.concatenate([spots, jnp.broadcast_to(core, (1,))]).astype(jnp.int32)
     flat = [x for own, other in held for x in own + other]
@@ -912,7 +908,11 @@
 
     grouped = [x[0].reshape(shard, -1, MEMBERS, PAIR) for x in (self_input, cross_query)]
     grouped = jnp.swapaxes(low(jnp.concatenate(grouped, 1)), 1, 2).reshape(shard, 4 * D)
-    ring = Stages(ring_gather(parts_of(grouped)) if ringed else no_ring(gathered([grouped])))
+    pieces = [grouped, low(cross_memory[0])]
+    if ringed:
+        ring = Stages(ring_gather(jnp.concatenate([parts_of(x) for x in pieces], 0), 4))
+    else:
+        ring = Stages(no_ring(gathered(pieces)))
 
     cond_low = low(jax.nn.silu(high(conditioning)))
     cond_rows = slice_at(cond_low, device * shard, shard, 2)
@@ -932,12 +932,11 @@
     sums = sums[0]
     (sums,) = ring.step(sums)
 
-    text_all = collect(text)
     sums = sums + swap(sums, 1)
     (sums,) = ring.step(sums)
 
     sums = sums + swap(sums, 2)
-    sums, text_all = ring.step(sums, text_all)
+    (sums,) = ring.step(sums)
 
     sums = sums + swap(sums, 4)
     (sums,) = ring.step(sums)
@@ -952,7 +951,7 @@
     hot0 = place_hot(*places_of(spread // CELLS, spread % CELLS))
     own_table = slice_at(position_bias[0], 2 * member, 2, 0)
     bias0 = bias_of(own_table, hot0, hot0)
-    pieces = [low(x[0]) for x in (self_output, cross_output, up_weight, cross_memory, down_weight)]
+    pieces = [low(x[0]) for x in (down_weight, up_weight, self_output, cross_output)]
     hidden, bias0, *pieces = ring.step(hidden, bias0, *pieces)
     packed = ring.result
 
@@ -975,7 +974,7 @@
         return low(kept["middle"] + gate2 * feed)
 
     if ringed:
-        ring = Stages(ring_gather(jnp.concatenate([parts_of(x) for x in pieces], 0)))
+        ring = Stages(ring_gather(jnp.concatenate([parts_of(x) for x in pieces], 0), 5))
     else:
         ring = Stages(no_ring(gathered(pieces)))
     joint, asked = project(hidden, packed)
@@ -996,13 +995,15 @@
     hot_q1 = place_hot(*mine)
     hot_k1 = jnp.concatenate([hot_q1, place_hot(*partner)])
     bias1 = bias_of(position_bias[0], hot_q1, hot_k1)
-    bias1, mixture = ring.step(bias1, mixture)
-    for _ in range(4 - micro):
+    text_all = collect(text)
+    bias1, mixture, text_all = ring.step(bias1, mixture, text_all)
+    text_all = jnp.swapaxes(text_all, 0, 1).reshape(micro * words, D)
+    memory = text_project(text_all, packed).reshape(micro, words, 2 * D)
+    mixture_text, text_norm = attend_text(asked, memory)
+    text_all, memory, mixture_text, text_norm = ring.step(text_all, memory, mixture_text, text_norm)
+    for _ in range(3 - micro):
         ring.step()
     outer = ring.result
-    text_all = jnp.swapaxes(text_all, 0, 1).reshape(micro * words, D)
-    memory = text_project(text_all, outer).reshape(micro, words, 2 * D)
-    mixture_text, text_norm = attend_text(asked, memory)
     branch, middle, second = branch_and_norm(high(block_input), mixture, mixture_text)
     first = dict(
         x=high(block_input),
@@ -1047,7 +1048,8 @@
         return low(kept["middle_grad"] + inputs_norm)
 
     received = lax.ppermute(first_result, "section", [(0, 1)])
-    received, bias1 = together(received, bias1)
+    first["joint"], first["norm"] = jnp.concatenate(first["joint"], 1), jnp.concatenate(first["norm"], 0)
+    received, bias1, first["joint"], first["norm"] = together(received, bias1, first["joint"], first["norm"])
     inputs = high(received)
     hidden = low(layer_mod(inputs, shift1, scale1)).reshape(tokens, D)
     joint, asked = project(hidden, packed)
@@ -1098,29 +1100,19 @@
     mixture_grad, text_grad = back_norm2(first, grad_result)
     mixture_grad = of_frames(trade(mixture_grad))
     first["asked_grad"], dkt, dvt = attend_text_back(first["asked"], memory, first["text_norm"], text_grad)
-    mixture_grad, dkt, dvt = together(mixture_grad, dkt, dvt)
-
-    def frames_back(i):
-        frames = mixture_grad[:, i * FRAMES : (i + 1) * FRAMES]
-        grad, dbias = attend_frames_back(first["joint"][i], bias0, first["norm"][i], frames)
-        return of_tokens(grad), dbias
-
-    joint_grad, dbias0 = frames_back(0)
+    mixture_grad, dkt, dvt, *flat = together(mixture_grad, dkt, dvt, *upper2, *feed2)
+    upper2, feed2 = tuple(flat[:2]), tuple(flat[2:])
+
+    joint_grad, dbias0 = attend_frames_back(
+        first["joint"], bias0, first["norm"], mixture_grad
+    )
     feeds = () if apart else feed_grads(order, columns[4], upper2, active2, feed2)
-    traded, *feeds = together(trade(joint_grad), *feeds)
-    joint_grad = [traded]
+    first["joint_grad"], *feeds = together(trade(of_tokens(joint_grad)), *feeds)
     ring = Stages(no_ring(None) if apart else ring_sums(feeds[:1], feeds[1:]))
-    asked2, branch2 = paired(both("asked_grad")), paired(both("branch_grad"))
-    keys2, values2 = [paired(chosen(x, y).reshape(micro * words, D)) for x, y in ((dkt, dkt1), (dvt, dvt1))]
-    for i in range(1, micro):
-        grad, dbias = frames_back(i)
-        dbias0 = dbias0 + dbias
-        grad, dbias0 = ring.step(trade(grad), dbias0)
-        joint_grad.append(grad)
-    flat = ring.step(*asked2, *branch2, *keys2, *values2)
-    asked2, branch2, keys2, values2 = [tuple(flat[2 * i : 2 * i + 2]) for i in range(4)]
-    first["joint_grad"] = jnp.concatenate(joint_grad, 1)
-    joint2 = paired(both("joint_grad"))
+    items = [paired(both(x)) for x in ("asked_grad", "branch_grad", "joint_grad")]
+    items += [paired(chosen(x, y).reshape(micro * words, D)) for x, y in ((dkt, dkt1), (dvt, dvt1))]
+    flat = ring.step(*[x for pair in items for x in pair])
+    asked2, branch2, joint2, keys2, values2 = [tuple(flat[2 * i : 2 * i + 2]) for i in range(5)]
     if apart:
         joint_all = [jnp.swapaxes(joint2[0], 0, 1), asked2[0].reshape(tokens, MEMBERS, PAIR)]
         joint_all = jnp.concatenate(joint_all, 2).reshape(tokens, 4 * D)
@@ -1130,7 +1122,7 @@
     else:
         grads = packed_grads(order, *columns[:4], joint2, asked2, branch2, keys2, values2)
     first["joint_grad"], dbias0, dbias1, *grads = ring.step(first["joint_grad"], dbias0, dbias1, *grads)
-    for _ in range(6 - micro):
+    for _ in range(5):
         ring.step()
     feed_part = ring.result
     ring = Stages(no_ring(grads) if apart else ring_sums(grads[:1], grads[1:]))

time: 738 us -> 733 us (level)
  local copies, waits for them, and re-layouts: 73.2 us -> 93.2 us
  waiting for transfers between devices: 252 us -> 232 us
  starting transfers between devices: 129 us -> 115 us
  other arithmetic: 62.9 us -> 72.5 us
    unnamed x471 -> x424, local copies, waits for them, and re-layouts: 54.4 us -> 73 us
    ppermute x56, starting transfers between devices: 72.4 us -> 61.6 us  [hop(): return lax.ppermute(x, ('section', 'dp'), route)]
    ppermute x56, waiting for transfers between devices: 158 us -> 149 us  [hop(): return lax.ppermute(x, ('section', 'dp'), route)]
    all_to_all x8 -> x7, waiting for transfers between devices: 23.2 us -> 18.2 us  [trade(): return lax.all_to_all(x, 'dp', 0, 0, tiled=True, axis_index_groups=members)]
    all_to_all x8 -> x7, starting transfers between devices: 31.2 us -> 26.4 us  [trade(): return lax.all_to_all(x, 'dp', 0, 0, tiled=True, axis_index_groups=members)]
    pallas_call x24 -> x23, Pallas kernels: 129 us -> 126 us  [call(): pl.pallas_call(kernel, grid=grid, in_specs=in_specs, out_specs=out_specs,...]
  transfers between devices with their start and end apart: 120 -> 119, of which waited for: 59 -> 55; matrix products, arithmetic and copies ran while one was open for 11% -> 11% of each run, Pallas kernels for 11% -> 12%
where the time goes in v4:
time: 733 us; the launch traced here: 721 us
  waiting for transfers between devices  232 us (32%)
  Pallas kernels  181 us (25%)
  starting transfers between devices  115 us (16%)
  local copies, waits for them, and re-layouts  93.2 us (13%)
  other arithmetic  72.5 us (10%)
  matrix products  23.1 us (3%)
    ppermute x56, waiting for transfers between devices, hop(): return lax.ppermute(x, ('section', 'dp'), route)  149 us
    pallas_call x23, Pallas kernels, call(): pl.pallas_call(kernel, grid=grid, in_specs=in_specs, out_specs=out_specs,...  126 us
    unnamed x424, local copies, waits for them, and re-layouts  73 us
    ppermute x56, starting transfers between devices, hop(): return lax.ppermute(x, ('section', 'dp'), route)  61.6 us
    ppermute x54, waiting for transfers between devices, swap(): return lax.ppermute(x, ('section', 'dp'), route)  50.3 us
    pallas_call x4, Pallas kernels, assembled(): pl.pallas_call(kernel, grid_spec=pltpu.PrefetchScalarGridSpec(num_scalar_...  29.7 us
    convert_element_type x37, other arithmetic, low(): return v.astype(LOW)  27.4 us
    all_to_all x7, starting transfers between devices, trade(): return lax.all_to_all(x, 'dp', 0, 0, tiled=True, axis_index_groups=members)  26.4 us
  transfers between devices with their start and end apart: 119, of which 55 were waited for; matrix products, arithmetic and copies ran while one was open for 11% of the time, Pallas kernels for 12%

profile of v4, /device:TPU:0, one launch (start us, length us, event | category | flops | bytes accessed | tf_op | source)
XLA Modules:
  0.0 721.2 jit_solution(5267526742340990076)
XLA Ops:
  4.1 3.1 collective-permute-start
  25.3 7.3 %collective-permute-done.2.refs_8_ = bf16[192,1024]{1,0:T(8,128)(2,1)} collective-permute-done((bf16[192,1024]{1,0:T(8,128)(2,1)S(1)}, bf16[192,1024]{1,0:T(8,128)(2,1)}, u32[]{:S(2)}, u32[]{:S(2)}) %collective-permute-start.2) | collective-permute-done | bytes 393248 | tf_op jit(solution)/shard_map/ppermute | solution.py:586
  40.1 5.0 collective-permute-done.7.refs_12_
  49.9 5.0 collective-permute-done.16
  61.4 7.2 %collective-permute-done.21 = f32[2,6144]{1,0:T(2,128)S(1)} collective-permute-done((f32[2,6144]{1,0:T(2,128)S(1)}, f32[2,6144]{1,0:T(2,128)S(1)}, u32[]{:S(2)}, u32[]{:S(2)}) %collective-permute-start.21) | collective-permute-done | bytes 49184 | tf_op jit(solution)/shard_map/ppermute | solution.py:60
  73.7 6.2 shard_map.274.refs_16_
  84.6 8.5 %collective-permute-done.26.refs_12_ = bf16[192,1024]{1,0:T(8,128)(2,1)S(1)} collective-permute-done((bf16[192,1024]{1,0:T(8,128)(2,1)}, bf16[192,1024]{1,0:T(8,128)(2,1)S(1)}, u32[]{:S(2)}, u32[]{:S(2)}) %collective-permute-start.26) | collective-permute-done | bytes 393248 | tf_op jit(solution)/shard_map/ppermute | solution.py:586
  101.9 6.2 shard_map.275
  108.1 4.6 copy-done.2
  112.7 4.1 shard_map.276
  118.7 3.7 all-to-all-start
  125.5 24.6 %collective-permute-done.36.refs_8_ = bf16[320,1024]{1,0:T(8,128)(2,1)S(1)} collective-permute-done((bf16[320,1024]{1,0:T(8,128)(2,1)}, bf16[320,1024]{1,0:T(8,128)(2,1)S(1)}, u32[]{:S(2)}, u32[]{:S(2)}) %collective-permute-start.36) | collective-permute-done | bytes 655392 | tf_op jit(solution)/shard_map/ppermute | solution.py:586
  151.0 3.6 all-to-all-start.1
  160.7 8.0 %all-to-all-done.1 = bf16[8,160,384]{2,1,0:T(8,128)(2,1)S(1)} async-done(((bf16[8,160,384]{2,1,0:T(8,128)(2,1)}), bf16[8,160,384]{2,1,0:T(8,128)(2,1)S(1)}, u32[]{:S(2)}, u32[]{:S(2)}) %all-to-all-start.1) | async-done | bytes 983072 | tf_op jit(solution)/shard_map/all_to_all | solution.py:893
  168.7 3.4 all-to-all-start.2
  172.8 10.0 %collective-permute-done.40.refs_12_ = bf16[320,1024]{1,0:T(8,128)(2,1)} collective-permute-done((bf16[320,1024]{1,0:T(8,128)(2,1)}, bf16[320,1024]{1,0:T(8,128)(2,1)}, u32[]{:S(2)}, u32[]{:S(2)}) %collective-permute-start.40) | collective-permute-done | bytes 655392 | tf_op jit(solution)/shard_map/ppermute | solution.py:586
  187.9 3.6 all-to-all-start.3
  191.5 3.7 convolution_bitcast_fusion.4
  196.2 7.2 %all-to-all-done.3 = bf16[8,160,128]{2,1,0:T(8,128)(2,1)S(1)} async-done(((bf16[8,160,128]{2,1,0:T(8,128)(2,1)}), bf16[8,160,128]{2,1,0:T(8,128)(2,1)S(1)}, u32[]{:S(2)}, u32[]{:S(2)}) %all-to-all-start.3) | async-done | bytes 327712 | tf_op jit(solution)/shard_map/all_to_all | solution.py:893
  204.3 3.4 all-to-all-start.4
  210.3 3.7 fusion.87.bias_ref
  215.4 13.1 %collective-permute-done.48.refs_0_ = bf16[320,1024]{1,0:T(8,128)(2,1)} collective-permute-done((bf16[320,1024]{1,0:T(8,128)(2,1)}, bf16[320,1024]{1,0:T(8,128)(2,1)}, u32[]{:S(2)}, u32[]{:S(2)}) %collective-permute-start.48) | collective-permute-done | bytes 655392 | tf_op jit(solution)/shard_map/ppermute | solution.py:586
  230.9 4.6 copy-done.3
  240.7 4.5 collective-permute-done.52.refs_4_
  247.5 10.4 %shard_map.281.refs_12_ = bf16[8,2,640,1024]{3,2,1,0:T(8,128)(2,1)} custom-call(s32[9]{0:T(128)} %pad_add_fusion.order_ref, bf16[320,1024]{1,0:T(8,128)(2,1)} %copy-done.127, bf16[320,1024]{1,0:T(8,128)(2,1)} %copy-done.126, bf16[320,1024]{1,0:T(8,128)(2,1)} %copy-done.134, bf16[320,1024]{1,0:T(8,128)(2,1)} %copy-done.135, bf16[320,1024]{1,0:T(8,128)(2,1)} %copy-done.132, ...), custom_call_target="tpu_custom_call" | custom-call | flops 1 | bytes 1 | tf_op jit(solution)/shard_map/pallas_call | solution.py:644
  265.8 6.9 shard_map.282
  272.7 3.4 shard_map.283
  277.1 10.6 %shard_map.284 = (bf16[320,4096]{1,0:T(8,128)(2,1)S(1)}, bf16[320,4096]{1,0:T(8,128)(2,1)S(1)}, f32[320,1024]{1,0:T(8,128)S(1)}) custom-call(bf16[320,1024]{1,0:T(8,128)(2,1)S(1)} %bitcast.327, bf16[16,640,1024]{2,1,0:T(8,128)(2,1)} %bitcast.347, bf16[16,640,1024]{2,1,0:T(8,128)(2,1)} %bitcast.348), custom_call_target="tpu_custom_call" | custom-call | flops 1 | bytes 1 | tf_op jit(solution)/shard_map/pallas_call | solution.py:196
  291.6 4.2 collective-permute-start.64
  301.2 8.4 %collective-permute-done.64 = bf16[2,160,1024]{2,1,0:T(8,128)(2,1)} collective-permute-done((bf16[2,160,1024]{2,1,0:T(8,128)(2,1)}, bf16[2,160,1024]{2,1,0:T(8,128)(2,1)}, u32[]{:S(2)}, u32[]{:S(2)}) %collective-permute-start.64) | collective-permute-done | bytes 655392 | tf_op jit(solution)/shard_map/ppermute | solution.py:1050
  313.7 4.8 copy-done.4
  318.5 4.1 shard_map.285
  327.1 4.7 shard_map.286
  331.8 3.6 shard_map.288
  337.4 10.6 %shard_map.289 = (bf16[320,4096]{1,0:T(8,128)(2,1)S(1)}, bf16[320,4096]{1,0:T(8,128)(2,1)S(1)}, f32[320,1024]{1,0:T(8,128)S(1)}) custom-call(bf16[320,1024]{1,0:T(8,128)(2,1)S(1)} %bitcast.328, bf16[16,640,1024]{2,1,0:T(8,128)(2,1)} %bitcast.351, bf16[16,640,1024]{2,1,0:T(8,128)(2,1)} %bitcast.352), custom_call_target="tpu_custom_call" | custom-call | flops 1 | bytes 1 | tf_op jit(solution)/shard_map/pallas_call | solution.py:196
  350.6 11.7 %shard_map.290 = (bf16[320,4096]{1,0:T(8,128)(2,1)S(1)}, f32[320,1024]{1,0:T(8,128)S(1)}) custom-call(bf16[320,1024]{1,0:T(8,128)(2,1)S(1)} %bitcast.325, bf16[320,4096]{1,0:T(8,128)(2,1)S(1)} %get-tuple-element.402.upper_ref, bf16[16,640,1024]{2,1,0:T(8,128)(2,1)} %bitcast.353, bf16[16,640,1024]{2,1,0:T(8,128)(2,1)} %bitcast.354), custom_call_target="tpu_custom_call" | custom-call | flops 1 | bytes 1 | tf_op jit(solution)/shard_map/pallas_call | solution.py:196
  365.4 4.4 shard_map.291
  370.7 10.5 %shard_map.292 = (bf16[8,320,384]{2,1,0:T(8,128)(2,1)S(1)}, bf16[8,320,256]{2,1,0:T(8,128)(2,1)}, f32[16,160,320]{2,1,0:T(8,128)S(1)}) custom-call(bf16[8,320,384]{2,1,0:T(8,128)(2,1)S(1)} %get-tuple-element.395.own_ref, bf16[8,320,384]{2,1,0:T(8,128)(2,1)S(1)} %collective-permute-done.65.other_ref, f32[16,160,320]{2,1,0:T(8,128)S(1)} %copy-done.6, ...), custom_call_target="tpu_custom_call" | custom-call | flops 1 | bytes 1 | tf_op jit(solution)/shard_map/pallas_call | solution.py:196
  389.4 4.8 shard_map.293
  397.9 4.6 copy-done.5
  402.5 4.7 shard_map.294
  423.2 5.7 shard_map.295
  434.1 7.1 collective-permute-done.67
  442.8 11.9 %shard_map.296 = (bf16[320,4096]{1,0:T(8,128)(2,1)S(1)}, f32[320,1024]{1,0:T(8,128)S(1)}) custom-call(bf16[320,1024]{1,0:T(8,128)(2,1)S(1)} %bitcast.326, bf16[320,4096]{1,0:T(8,128)(2,1)S(1)} %copy-done.46, bf16[16,640,1024]{2,1,0:T(8,128)(2,1)} %bitcast.357, bf16[16,640,1024]{2,1,0:T(8,128)(2,1)} %bitcast.358), custom_call_target="tpu_custom_call" | custom-call | flops 1 | bytes 1 | tf_op jit(solution)/shard_map/pallas_call | solution.py:196
  458.7 4.4 shard_map.297
  464.9 4.7 all-to-all-start.5
  473.7 4.8 shard_map.298
  483.8 6.2 shard_map.299
  492.1 4.0 all-to-all-start.6
  501.3 12.2 %shard_map.300 = (bf16[8,256,1024]{2,1,0:T(8,128)(2,1)S(1)}, bf16[8,256,1024]{2,1,0:T(8,128)(2,1)S(1)}) custom-call(s32[3,8]{1,0:T(4,128)S(1)} %add_add_fusion.4.order_ref, bf16[1024,640]{1,0:T(8,128)(2,1)S(1)} %copy-done.80, bf16[320,4096]{1,0:T(8,128)(2,1)} %broadcast_select_fusion.u_ref, bf16[320,4096]{1,0:T(8,128)(2,1)} %collective-permute-done.73.u2_ref, ...), custom_call_target="tpu_custom_call" | custom-call | flops 1 | bytes 1 | tf_op jit(solution)/shard_map/pallas_call | solution.py:706
  531.9 7.9 %collective-permute-done.75 = bf16[256,1024]{1,0:T(8,128)(2,1)S(1)} collective-permute-done((bf16[256,1024]{1,0:T(8,128)(2,1)S(1)}, bf16[256,1024]{1,0:T(8,128)(2,1)S(1)}, u32[]{:S(2)}, u32[]{:S(2)}) %collective-permute-start.75) | collective-permute-done | bytes 524320 | tf_op jit(solution)/shard_map/ppermute | solution.py:586
  546.8 13.0 %shard_map.301 = (bf16[8,256,1024]{2,1,0:T(8,128)(2,1)S(1)}, bf16[8,256,1024]{2,1,0:T(8,128)(2,1)S(1)}) custom-call(s32[3,8]{1,0:T(4,128)S(1)} %add_add_fusion.4.order_ref, bf16[1024,640]{1,0:T(8,128)(2,1)S(1)} %copy-done.74, bf16[1024,640]{1,0:T(8,128)(2,1)S(1)} %copy-done.76, bf16[1024,640]{1,0:T(8,128)(2,1)S(1)} %copy-done.78, ...), custom_call_target="tpu_custom_call" | custom-call | flops 1 | bytes 1 | tf_op jit(solution)/shard_map/pallas_call | solution.py:706
  564.5 4.7 shard_map.302
  573.2 4.8 fusion.86
  590.7 6.5 collective-permute-done.102
  603.7 4.8 collective-permute-done.86
  615.0 4.7 collective-permute-done.104
  624.2 6.7 collective-permute-done.88
  637.8 4.4 collective-permute-done.106
  646.7 8.8 %collective-permute-done.93 = f32[1,112,128]{2,1,0:T(8,128)S(1)} collective-permute-done((f32[1,112,128]{2,1,0:T(8,128)S(1)}, f32[1,112,128]{2,1,0:T(8,128)S(1)}, u32[]{:S(2)}, u32[]{:S(2)}) %collective-permute-start.93) | collective-permute-done | bytes 57376 | tf_op jit(solution)/shard_map/ppermute | solution.py:60
  660.7 5.2 collective-permute-done.108
  669.6 9.4 %collective-permute-done.96 = f32[1,112,128]{2,1,0:T(8,128)S(1)} collective-permute-done((f32[1,112,128]{2,1,0:T(8,128)S(1)}, f32[1,112,128]{2,1,0:T(8,128)S(1)}, u32[]{:S(2)}, u32[]{:S(2)}) %collective-permute-start.96) | collective-permute-done | bytes 57376 | tf_op jit(solution)/shard_map/ppermute | solution.py:60
  684.1 4.2 collective-permute-done.110
  690.5 9.5 %collective-permute-done.99 = f32[1,112,128]{2,1,0:T(8,128)S(1)} collective-permute-done((f32[1,112,128]{2,1,0:T(8,128)S(1)}, f32[1,112,128]{2,1,0:T(8,128)S(1)}, u32[]{:S(2)}, u32[]{:S(2)}) %collective-permute-start.99) | collective-permute-done | bytes 57376 | tf_op jit(solution)/shard_map/ppermute | solution.py:60
  (818 shorter events, 295.1 us)
Async XLA Ops:
  7.2 18.0 %collective-permute-start.4 = (bf16[192,1024]{1,0:T(8,128)(2,1)S(1)}, bf16[192,1024]{1,0:T(8,128)(2,1)}, u32[]{:S(2)}, u32[]{:S(2)}) collective-permute-start(bf16[192,1024]{1,0:T(8,128)(2,1)S(1)} %bitcast.375), channel_id=1, source_target_pairs={{0,1},{1,0},{2,3},{3,2},{4,5},{5,4},{6,7},{7,6},{8,9},{9,8},{10,11... | collective-permute-start | bytes 1179656 | tf_op jit(solution)/shard_map/ppermute | solution.py:60
  8.0 17.3 %collective-permute-start.5 = (bf16[192,1024]{1,0:T(8,128)(2,1)S(1)}, bf16[192,1024]{1,0:T(8,128)(2,1)}, u32[]{:S(2)}, u32[]{:S(2)}) collective-permute-start(bf16[192,1024]{1,0:T(8,128)(2,1)S(1)} %pad_maximum_fusion.6.refs_1_), channel_id=1, source_target_pairs={{0,1},{1,0},{2,3},{3,2},{4,5},{5,4},{6,7},{7,6},{8,9},{9,8},{10,11... | collective-permute-start | bytes 1179656 | tf_op jit(solution)/shard_map/ppermute | solution.py:60
  23.5 16.2 %collective-permute-start.9 = (bf16[192,1024]{1,0:T(8,128)(2,1)S(1)}, bf16[192,1024]{1,0:T(8,128)(2,1)S(1)}, u32[]{:S(2)}, u32[]{:S(2)}) collective-permute-start(bf16[192,1024]{1,0:T(8,128)(2,1)S(1)} %collective-permute-done.refs_4_), channel_id=1, source_target_pairs={{0,1},{1,0},{2,3},{3,2},{4,5},{5,4},{6,7},{7,6},{8,9},{9,8},{10,11... | collective-permute-start | bytes 1179656 | tf_op jit(solution)/shard_map/ppermute | solution.py:60
  38.9 16.8 %collective-permute-start.14 = (bf16[192,1024]{1,0:T(8,128)(2,1)}, bf16[192,1024]{1,0:T(8,128)(2,1)S(1)}, u32[]{:S(2)}, u32[]{:S(2)}) collective-permute-start(bf16[192,1024]{1,0:T(8,128)(2,1)} %collective-permute-done.2.refs_8_), channel_id=1, source_target_pairs={{0,1},{1,0},{2,3},{3,2},{4,5},{5,4},{6,7},{7,6},{8,9},{9,8},{10,11... | collective-permute-start | bytes 1179656 | tf_op jit(solution)/shard_map/ppermute | solution.py:60
  39.7 16.6 %collective-permute-start.15 = (bf16[192,1024]{1,0:T(8,128)(2,1)}, bf16[192,1024]{1,0:T(8,128)(2,1)}, u32[]{:S(2)}, u32[]{:S(2)}) collective-permute-start(bf16[192,1024]{1,0:T(8,128)(2,1)} %collective-permute-done.3.refs_9_), channel_id=1, source_target_pairs={{0,1},{1,0},{2,3},{3,2},{4,5},{5,4},{6,7},{7,6},{8,9},{9,8},{10,11... | collective-permute-start | bytes 1179656 | tf_op jit(solution)/shard_map/ppermute | solution.py:60
  69.5 15.1 %collective-permute-start.28 = (bf16[192,1024]{1,0:T(8,128)(2,1)}, bf16[192,1024]{1,0:T(8,128)(2,1)}, u32[]{:S(2)}, u32[]{:S(2)}) collective-permute-start(bf16[192,1024]{1,0:T(8,128)(2,1)} %collective-permute-done.17.refs_4_), channel_id=1, source_target_pairs={{0,1},{1,0},{2,3},{3,2},{4,5},{5,4},{6,7},{7,6},{8,9},{9,8},{10,11... | collective-permute-start | bytes 1179656 | tf_op jit(solution)/shard_map/ppermute | solution.py:60
  95.8 21.0 %collective-permute-start.30 = (bf16[320,1024]{1,0:T(8,128)(2,1)S(1)}, bf16[320,1024]{1,0:T(8,128)(2,1)S(1)}, u32[]{:S(2)}, u32[]{:S(2)}) collective-permute-start(bf16[320,1024]{1,0:T(8,128)(2,1)S(1)} %get-tuple-element.553.refs_0_), channel_id=1, source_target_pairs={{0,4},{1,5},{4,8},{5,9},{8,12},{9,13},{12,14},{13,15},{14,10},{15,... | collective-permute-start | bytes 1966088 | tf_op jit(solution)/shard_map/ppermute | solution.py:586
  96.2 20.6 %collective-permute-start.31 = (bf16[320,1024]{1,0:T(8,128)(2,1)S(1)}, bf16[320,1024]{1,0:T(8,128)(2,1)S(1)}, u32[]{:S(2)}, u32[]{:S(2)}) collective-permute-start(bf16[320,1024]{1,0:T(8,128)(2,1)S(1)} %get-tuple-element.552.refs_1_), channel_id=1, source_target_pairs={{0,2},{1,3},{4,0},{5,1},{8,4},{9,5},{12,8},{13,9},{14,12},{15,13},... | collective-permute-start | bytes 1966088 | tf_op jit(solution)/shard_map/ppermute | solution.py:586
  118.7 32.3 %all-to-all-start = ((bf16[8,160,384]{2,1,0:T(8,128)(2,1)}), bf16[8,160,384]{2,1,0:T(8,128)(2,1)S(1)}, u32[]{:S(2)}, u32[]{:S(2)}) async-start(bf16[8,160,384]{2,1,0:T(8,128)(2,1)} %get-tuple-element.547), calls=%async_computation | async-start | bytes 1966080 | tf_op jit(solution)/shard_map/all_to_all | solution.py:893
  123.0 27.1 %collective-permute-start.36 = (bf16[320,1024]{1,0:T(8,128)(2,1)}, bf16[320,1024]{1,0:T(8,128)(2,1)S(1)}, u32[]{:S(2)}, u32[]{:S(2)}) collective-permute-start(bf16[320,1024]{1,0:T(8,128)(2,1)} %copy-done.132), channel_id=1, source_target_pairs={{0,4},{1,5},{4,8},{5,9},{8,12},{9,13},{12,14},{13,15},{14,10},{15,... | collective-permute-start | bytes 1966088 | tf_op jit(solution)/shard_map/ppermute | solution.py:586
  124.9 26.1 %collective-permute-start.37 = (bf16[320,1024]{1,0:T(8,128)(2,1)}, bf16[320,1024]{1,0:T(8,128)(2,1)}, u32[]{:S(2)}, u32[]{:S(2)}) collective-permute-start(bf16[320,1024]{1,0:T(8,128)(2,1)} %copy-done.133), channel_id=1, source_target_pairs={{0,2},{1,3},{4,0},{5,1},{8,4},{9,5},{12,8},{13,9},{14,12},{15,13},... | collective-permute-start | bytes 1966088 | tf_op jit(solution)/shard_map/ppermute | solution.py:586
  151.0 17.7 %all-to-all-start.1 = ((bf16[8,160,384]{2,1,0:T(8,128)(2,1)}), bf16[8,160,384]{2,1,0:T(8,128)(2,1)S(1)}, u32[]{:S(2)}, u32[]{:S(2)}) async-start(bf16[8,160,384]{2,1,0:T(8,128)(2,1)} %get-tuple-element.330), calls=%async_computation.1 | async-start | bytes 1966080 | tf_op jit(solution)/shard_map/all_to_all | solution.py:893
  154.6 18.1 %collective-permute-start.42 = (bf16[320,1024]{1,0:T(8,128)(2,1)}, bf16[320,1024]{1,0:T(8,128)(2,1)}, u32[]{:S(2)}, u32[]{:S(2)}) collective-permute-start(bf16[320,1024]{1,0:T(8,128)(2,1)} %copy-done.132), channel_id=1, source_target_pairs={{0,1},{1,0},{2,3},{3,2},{4,5},{5,4},{6,7},{7,6},{8,9},{9,8},{10,11... | collective-permute-start | bytes 1966088 | tf_op jit(solution)/shard_map/ppermute | solution.py:60
  155.0 17.8 %collective-permute-start.43 = (bf16[320,1024]{1,0:T(8,128)(2,1)}, bf16[320,1024]{1,0:T(8,128)(2,1)}, u32[]{:S(2)}, u32[]{:S(2)}) collective-permute-start(bf16[320,1024]{1,0:T(8,128)(2,1)} %copy-done.133), channel_id=1, source_target_pairs={{0,1},{1,0},{2,3},{3,2},{4,5},{5,4},{6,7},{7,6},{8,9},{9,8},{10,11... | collective-permute-start | bytes 1966088 | tf_op jit(solution)/shard_map/ppermute | solution.py:60
  155.2 27.7 %collective-permute-start.40 = (bf16[320,1024]{1,0:T(8,128)(2,1)}, bf16[320,1024]{1,0:T(8,128)(2,1)}, u32[]{:S(2)}, u32[]{:S(2)}) collective-permute-start(bf16[320,1024]{1,0:T(8,128)(2,1)} %copy-done.136), channel_id=1, source_target_pairs={{0,4},{1,5},{4,8},{5,9},{8,12},{9,13},{12,14},{13,15},{14,10},{15,... | collective-permute-start | bytes 1966088 | tf_op jit(solution)/shard_map/ppermute | solution.py:586
  157.1 25.8 %collective-permute-start.41 = (bf16[320,1024]{1,0:T(8,128)(2,1)}, bf16[320,1024]{1,0:T(8,128)(2,1)}, u32[]{:S(2)}, u32[]{:S(2)}) collective-permute-start(bf16[320,1024]{1,0:T(8,128)(2,1)} %collective-permute-done.37.refs_9_), channel_id=1, source_target_pairs={{0,2},{1,3},{4,0},{5,1},{8,4},{9,5},{12,8},{13,9},{14,12},{15,13},... | collective-permute-start | bytes 1966088 | tf_op jit(solution)/shard_map/ppermute | solution.py:586
  168.7 19.2 %all-to-all-start.2 = ((bf16[8,160,128]{2,1,0:T(8,128)(2,1)}), bf16[8,160,128]{2,1,0:T(8,128)(2,1)S(1)}, u32[]{:S(2)}, u32[]{:S(2)}) async-start(bf16[8,160,128]{2,1,0:T(8,128)(2,1)} %bitcast.26), calls=%async_computation.2 | async-start | bytes 655360 | tf_op jit(solution)/shard_map/all_to_all | solution.py:893
  172.2 35.5 %collective-permute-start.46 = (bf16[320,1024]{1,0:T(8,128)(2,1)}, bf16[320,1024]{1,0:T(8,128)(2,1)}, u32[]{:S(2)}, u32[]{:S(2)}) collective-permute-start(bf16[320,1024]{1,0:T(8,128)(2,1)} %copy-done.136), channel_id=1, source_target_pairs={{0,1},{1,0},{2,3},{3,2},{4,5},{5,4},{6,7},{7,6},{8,9},{9,8},{10,11... | collective-permute-start | bytes 1966088 | tf_op jit(solution)/shard_map/ppermute | solution.py:60
  172.7 35.4 %collective-permute-start.47 = (bf16[320,1024]{1,0:T(8,128)(2,1)}, bf16[320,1024]{1,0:T(8,128)(2,1)}, u32[]{:S(2)}, u32[]{:S(2)}) collective-permute-start(bf16[320,1024]{1,0:T(8,128)(2,1)} %collective-permute-done.37.refs_9_), channel_id=1, source_target_pairs={{0,1},{1,0},{2,3},{3,2},{4,5},{5,4},{6,7},{7,6},{8,9},{9,8},{10,11... | collective-permute-start | bytes 1966088 | tf_op jit(solution)/shard_map/ppermute | solution.py:60
  182.8 25.3 %collective-permute-start.44 = (bf16[320,1024]{1,0:T(8,128)(2,1)}, bf16[320,1024]{1,0:T(8,128)(2,1)}, u32[]{:S(2)}, u32[]{:S(2)}) collective-permute-start(bf16[320,1024]{1,0:T(8,128)(2,1)} %collective-permute-done.40.refs_12_), channel_id=1, source_target_pairs={{0,4},{1,5},{4,8},{5,9},{8,12},{9,13},{12,14},{13,15},{14,10},{15,... | collective-permute-start | bytes 1966088 | tf_op jit(solution)/shard_map/ppermute | solution.py:586
  183.0 25.2 %collective-permute-start.45 = (bf16[320,1024]{1,0:T(8,128)(2,1)}, bf16[320,1024]{1,0:T(8,128)(2,1)}, u32[]{:S(2)}, u32[]{:S(2)}) collective-permute-start(bf16[320,1024]{1,0:T(8,128)(2,1)} %collective-permute-done.41.refs_13_), channel_id=1, source_target_pairs={{0,2},{1,3},{4,0},{5,1},{8,4},{9,5},{12,8},{13,9},{14,12},{15,13},... | collective-permute-start | bytes 1966088 | tf_op jit(solution)/shard_map/ppermute | solution.py:586
  187.9 15.5 %all-to-all-start.3 = ((bf16[8,160,128]{2,1,0:T(8,128)(2,1)}), bf16[8,160,128]{2,1,0:T(8,128)(2,1)S(1)}, u32[]{:S(2)}, u32[]{:S(2)}) async-start(bf16[8,160,128]{2,1,0:T(8,128)(2,1)} %bitcast.27), calls=%async_computation.3 | async-start | bytes 655360 | tf_op jit(solution)/shard_map/all_to_all | solution.py:893
  195.7 19.2 %collective-permute-start.50 = (bf16[320,1024]{1,0:T(8,128)(2,1)}, bf16[320,1024]{1,0:T(8,128)(2,1)}, u32[]{:S(2)}, u32[]{:S(2)}) collective-permute-start(bf16[320,1024]{1,0:T(8,128)(2,1)} %collective-permute-done.40.refs_12_), channel_id=1, source_target_pairs={{0,1},{1,0},{2,3},{3,2},{4,5},{5,4},{6,7},{7,6},{8,9},{9,8},{10,11... | collective-permute-start | bytes 1966088 | tf_op jit(solution)/shard_map/ppermute | solution.py:60
  208.2 20.4 %collective-permute-start.48 = (bf16[320,1024]{1,0:T(8,128)(2,1)}, bf16[320,1024]{1,0:T(8,128)(2,1)}, u32[]{:S(2)}, u32[]{:S(2)}) collective-permute-start(bf16[320,1024]{1,0:T(8,128)(2,1)} %collective-permute-done.44.refs_16_), channel_id=1, source_target_pairs={{0,4},{1,5},{4,8},{5,9},{8,12},{9,13},{12,14},{13,15},{14,10},{15,... | collective-permute-start | bytes 1966088 | tf_op jit(solution)/shard_map/ppermute | solution.py:586
  209.9 18.7 %collective-permute-start.49 = (bf16[320,1024]{1,0:T(8,128)(2,1)}, bf16[320,1024]{1,0:T(8,128)(2,1)}, u32[]{:S(2)}, u32[]{:S(2)}) collective-permute-start(bf16[320,1024]{1,0:T(8,128)(2,1)} %collective-permute-done.45.refs_17_), channel_id=1, source_target_pairs={{0,2},{1,3},{4,0},{5,1},{8,4},{9,5},{12,8},{13,9},{14,12},{15,13},... | collective-permute-start | bytes 1966088 | tf_op jit(solution)/shard_map/ppermute | solution.py:586
  214.0 26.1 %collective-permute-start.54 = (bf16[320,1024]{1,0:T(8,128)(2,1)}, bf16[320,1024]{1,0:T(8,128)(2,1)}, u32[]{:S(2)}, u32[]{:S(2)}) collective-permute-start(bf16[320,1024]{1,0:T(8,128)(2,1)} %collective-permute-done.44.refs_16_), channel_id=1, source_target_pairs={{0,1},{1,0},{2,3},{3,2},{4,5},{5,4},{6,7},{7,6},{8,9},{9,8},{10,11... | collective-permute-start | bytes 1966088 | tf_op jit(solution)/shard_map/ppermute | solution.py:60
  214.9 25.7 %collective-permute-start.55 = (bf16[320,1024]{1,0:T(8,128)(2,1)}, bf16[320,1024]{1,0:T(8,128)(2,1)}, u32[]{:S(2)}, u32[]{:S(2)}) collective-permute-start(bf16[320,1024]{1,0:T(8,128)(2,1)} %collective-permute-done.45.refs_17_), channel_id=1, source_target_pairs={{0,1},{1,0},{2,3},{3,2},{4,5},{5,4},{6,7},{7,6},{8,9},{9,8},{10,11... | collective-permute-start | bytes 1966088 | tf_op jit(solution)/shard_map/ppermute | solution.py:60
  228.6 16.6 %collective-permute-start.52 = (bf16[320,1024]{1,0:T(8,128)(2,1)}, bf16[320,1024]{1,0:T(8,128)(2,1)}, u32[]{:S(2)}, u32[]{:S(2)}) collective-permute-start(bf16[320,1024]{1,0:T(8,128)(2,1)} %collective-permute-done.48.refs_0_), channel_id=1, source_target_pairs={{0,4},{1,5},{4,8},{5,9},{8,12},{9,13},{12,14},{13,15},{14,10},{15,... | collective-permute-start | bytes 1966088 | tf_op jit(solution)/shard_map/ppermute | solution.py:586
  228.9 16.6 %collective-permute-start.53 = (bf16[320,1024]{1,0:T(8,128)(2,1)}, bf16[320,1024]{1,0:T(8,128)(2,1)}, u32[]{:S(2)}, u32[]{:S(2)}) collective-permute-start(bf16[320,1024]{1,0:T(8,128)(2,1)} %collective-permute-done.49.refs_1_), channel_id=1, source_target_pairs={{0,2},{1,3},{4,0},{5,1},{8,4},{9,5},{12,8},{13,9},{14,12},{15,13},... | collective-permute-start | bytes 1966088 | tf_op jit(solution)/shard_map/ppermute | solution.py:586
  230.9 27.1 %collective-permute-start.58 = (bf16[320,1024]{1,0:T(8,128)(2,1)}, bf16[320,1024]{1,0:T(8,128)(2,1)S(1)}, u32[]{:S(2)}, u32[]{:S(2)}) collective-permute-start(bf16[320,1024]{1,0:T(8,128)(2,1)} %collective-permute-done.48.refs_0_), channel_id=1, source_target_pairs={{0,1},{1,0},{2,3},{3,2},{4,5},{5,4},{6,7},{7,6},{8,9},{9,8},{10,11... | collective-permute-start | bytes 1966088 | tf_op jit(solution)/shard_map/ppermute | solution.py:60
  240.1 18.4 %collective-permute-start.59 = (bf16[320,1024]{1,0:T(8,128)(2,1)}, bf16[320,1024]{1,0:T(8,128)(2,1)S(1)}, u32[]{:S(2)}, u32[]{:S(2)}) collective-permute-start(bf16[320,1024]{1,0:T(8,128)(2,1)} %collective-permute-done.49.refs_1_), channel_id=1, source_target_pairs={{0,1},{1,0},{2,3},{3,2},{4,5},{5,4},{6,7},{7,6},{8,9},{9,8},{10,11... | collective-permute-start | bytes 1966088 | tf_op jit(solution)/shard_map/ppermute | solution.py:60
  245.5 15.5 %collective-permute-start.56 = (bf16[320,1024]{1,0:T(8,128)(2,1)}, bf16[320,1024]{1,0:T(8,128)(2,1)S(1)}, u32[]{:S(2)}, u32[]{:S(2)}) collective-permute-start(bf16[320,1024]{1,0:T(8,128)(2,1)} %collective-permute-done.52.refs_4_), channel_id=1, source_target_pairs={{0,4},{1,5},{4,8},{5,9},{8,12},{9,13},{12,14},{13,15},{14,10},{15,... | collective-permute-start | bytes 1966088 | tf_op jit(solution)/shard_map/ppermute | solution.py:586
  246.8 15.1 %collective-permute-start.57 = (bf16[320,1024]{1,0:T(8,128)(2,1)}, bf16[320,1024]{1,0:T(8,128)(2,1)}, u32[]{:S(2)}, u32[]{:S(2)}) collective-permute-start(bf16[320,1024]{1,0:T(8,128)(2,1)} %collective-permute-done.53.refs_5_), channel_id=1, source_target_pairs={{0,2},{1,3},{4,0},{5,1},{8,4},{9,5},{12,8},{13,9},{14,12},{15,13},... | collective-permute-start | bytes 1966088 | tf_op jit(solution)/shard_map/ppermute | solution.py:586
  291.6 18.0 %collective-permute-start.64 = (bf16[2,160,1024]{2,1,0:T(8,128)(2,1)}, bf16[2,160,1024]{2,1,0:T(8,128)(2,1)}, u32[]{:S(2)}, u32[]{:S(2)}) collective-permute-start(bf16[2,160,1024]{2,1,0:T(8,128)(2,1)} %get-tuple-element.567), channel_id=1, source_target_pairs={{0,16},{1,17},{2,18},{3,19},{4,20},{5,21},{6,22},{7,23},{8,24},{9,... | collective-permute-start | bytes 1966088 | tf_op jit(solution)/shard_map/ppermute | solution.py:1050
  414.5 26.6 %collective-permute-start.72 = (bf16[320,4096]{1,0:T(8,128)(2,1)S(1)}, bf16[320,4096]{1,0:T(8,128)(2,1)S(1)}, u32[]{:S(2)}, u32[]{:S(2)}) collective-permute-start(bf16[320,4096]{1,0:T(8,128)(2,1)S(1)} %broadcast_select_fusion.1.a_ref), channel_id=1, source_target_pairs={{0,1},{1,0},{2,3},{3,2},{4,5},{5,4},{6,7},{7,6},{8,9},{9,8},{10,11... | collective-permute-start | bytes 7864328 | tf_op jit(solution)/shard_map/ppermute | solution.py:60
  420.4 20.7 %collective-permute-start.67 = (bf16[2,160,1024]{2,1,0:T(8,128)(2,1)S(1)}, bf16[2,160,1024]{2,1,0:T(8,128)(2,1)S(1)}, u32[]{:S(2)}, u32[]{:S(2)}) collective-permute-start(bf16[2,160,1024]{2,1,0:T(8,128)(2,1)S(1)} %get-tuple-element.414), channel_id=1, source_target_pairs={{16,0},{17,1},{18,2},{19,3},{20,4},{21,5},{22,6},{23,7},{24,8},{25... | collective-permute-start | bytes 1966088 | tf_op jit(solution)/shard_map/ppermute | solution.py:1073
  456.5 24.4 %collective-permute-start.73 = (bf16[320,4096]{1,0:T(8,128)(2,1)}, bf16[320,4096]{1,0:T(8,128)(2,1)}, u32[]{:S(2)}, u32[]{:S(2)}) collective-permute-start(bf16[320,4096]{1,0:T(8,128)(2,1)} %broadcast_select_fusion.u_ref), channel_id=1, source_target_pairs={{0,1},{1,0},{2,3},{3,2},{4,5},{5,4},{6,7},{7,6},{8,9},{9,8},{10,11... | collective-permute-start | bytes 7864328 | tf_op jit(solution)/shard_map/ppermute | solution.py:60
  464.9 16.0 %all-to-all-start.5 = ((bf16[8,320,128]{2,1,0:T(8,128)(2,1)}), bf16[8,320,128]{2,1,0:T(8,128)(2,1)}, u32[]{:S(2)}, u32[]{:S(2)}) async-start(bf16[8,320,128]{2,1,0:T(8,128)(2,1)} %copy-done.83), calls=%async_computation.5 | async-start | bytes 1310720 | tf_op jit(solution)/shard_map/all_to_all | solution.py:893
  492.1 28.3 %all-to-all-start.6 = ((bf16[8,320,384]{2,1,0:T(8,128)(2,1)}), bf16[8,320,384]{2,1,0:T(8,128)(2,1)S(1)}, u32[]{:S(2)}, u32[]{:S(2)}) async-start(bf16[8,320,384]{2,1,0:T(8,128)(2,1)} %bitcast.340), calls=%async_computation.6 | async-start | bytes 3932160 | tf_op jit(solution)/shard_map/all_to_all | solution.py:893
  522.6 19.5 %collective-permute-start.79 = (bf16[8,320,384]{2,1,0:T(8,128)(2,1)S(1)}, bf16[8,320,384]{2,1,0:T(8,128)(2,1)S(1)}, u32[]{:S(2)}, u32[]{:S(2)}) collective-permute-start(bf16[8,320,384]{2,1,0:T(8,128)(2,1)S(1)} %broadcast_select_fusion.2.j_ref), channel_id=1, source_target_pairs={{0,1},{1,0},{2,3},{3,2},{4,5},{5,4},{6,7},{7,6},{8,9},{9,8},{10,11... | collective-permute-start | bytes 5898248 | tf_op jit(solution)/shard_map/ppermute | solution.py:60
  543.3 16.5 %collective-permute-start.82 = (bf16[256,1024]{1,0:T(8,128)(2,1)S(1)}, bf16[256,1024]{1,0:T(8,128)(2,1)S(1)}, u32[]{:S(2)}, u32[]{:S(2)}) collective-permute-start(bf16[256,1024]{1,0:T(8,128)(2,1)S(1)} %fusion.51), channel_id=1, source_target_pairs={{0,4},{1,5},{4,8},{5,9},{8,12},{9,13},{12,14},{13,15},{14,10},{15,... | collective-permute-start | bytes 1572872 | tf_op jit(solution)/shard_map/ppermute | solution.py:586
  560.9 24.7 %collective-permute-start.84 = (bf16[256,1024]{1,0:T(8,128)(2,1)}, bf16[256,1024]{1,0:T(8,128)(2,1)}, u32[]{:S(2)}, u32[]{:S(2)}) collective-permute-start(bf16[256,1024]{1,0:T(8,128)(2,1)} %slice_bitcast_fusion.2), channel_id=1, source_target_pairs={{0,4},{1,5},{4,8},{5,9},{8,12},{9,13},{12,14},{13,15},{14,10},{15,... | collective-permute-start | bytes 1572872 | tf_op jit(solution)/shard_map/ppermute | solution.py:586
  563.0 22.6 %collective-permute-start.85 = (bf16[256,1024]{1,0:T(8,128)(2,1)}, bf16[256,1024]{1,0:T(8,128)(2,1)}, u32[]{:S(2)}, u32[]{:S(2)}) collective-permute-start(bf16[256,1024]{1,0:T(8,128)(2,1)} %slice_bitcast_fusion.1), channel_id=1, source_target_pairs={{0,2},{1,3},{4,0},{5,1},{8,4},{9,5},{12,8},{13,9},{14,12},{15,13},... | collective-permute-start | bytes 1572872 | tf_op jit(solution)/shard_map/ppermute | solution.py:586
  587.2 21.2 %collective-permute-start.86 = (bf16[256,1024]{1,0:T(8,128)(2,1)S(1)}, bf16[256,1024]{1,0:T(8,128)(2,1)S(1)}, u32[]{:S(2)}, u32[]{:S(2)}) collective-permute-start(bf16[256,1024]{1,0:T(8,128)(2,1)S(1)} %fusion.49), channel_id=1, source_target_pairs={{0,4},{1,5},{4,8},{5,9},{8,12},{9,13},{12,14},{13,15},{14,10},{15,... | collective-permute-start | bytes 1572872 | tf_op jit(solution)/shard_map/ppermute | solution.py:586
  589.4 21.0 %collective-permute-start.87 = (bf16[256,1024]{1,0:T(8,128)(2,1)S(1)}, bf16[256,1024]{1,0:T(8,128)(2,1)S(1)}, u32[]{:S(2)}, u32[]{:S(2)}) collective-permute-start(bf16[256,1024]{1,0:T(8,128)(2,1)S(1)} %fusion.48), channel_id=1, source_target_pairs={{0,2},{1,3},{4,0},{5,1},{8,4},{9,5},{12,8},{13,9},{14,12},{15,13},... | collective-permute-start | bytes 1572872 | tf_op jit(solution)/shard_map/ppermute | solution.py:586
  600.4 19.3 %collective-permute-start.104 = (bf16[256,1024]{1,0:T(8,128)(2,1)S(1)}, bf16[256,1024]{1,0:T(8,128)(2,1)S(1)}, u32[]{:S(2)}, u32[]{:S(2)}) collective-permute-start(bf16[256,1024]{1,0:T(8,128)(2,1)S(1)} %fusion.35), channel_id=1, source_target_pairs={{0,4},{1,5},{4,8},{5,9},{8,12},{9,13},{12,14},{13,15},{14,10},{15,... | collective-permute-start | bytes 1572872 | tf_op jit(solution)/shard_map/ppermute | solution.py:586
  602.2 19.5 %collective-permute-start.105 = (bf16[256,1024]{1,0:T(8,128)(2,1)S(1)}, bf16[256,1024]{1,0:T(8,128)(2,1)S(1)}, u32[]{:S(2)}, u32[]{:S(2)}) collective-permute-start(bf16[256,1024]{1,0:T(8,128)(2,1)S(1)} %fusion.34), channel_id=1, source_target_pairs={{0,2},{1,3},{4,0},{5,1},{8,4},{9,5},{12,8},{13,9},{14,12},{15,13},... | collective-permute-start | bytes 1572872 | tf_op jit(solution)/shard_map/ppermute | solution.py:586
  611.7 19.3 %collective-permute-start.88 = (bf16[256,1024]{1,0:T(8,128)(2,1)S(1)}, bf16[256,1024]{1,0:T(8,128)(2,1)S(1)}, u32[]{:S(2)}, u32[]{:S(2)}) collective-permute-start(bf16[256,1024]{1,0:T(8,128)(2,1)S(1)} %fusion.47), channel_id=1, source_target_pairs={{0,4},{1,5},{4,8},{5,9},{8,12},{9,13},{12,14},{13,15},{14,10},{15,... | collective-permute-start | bytes 1572872 | tf_op jit(solution)/shard_map/ppermute | solution.py:586
  614.5 18.4 %collective-permute-start.89 = (bf16[256,1024]{1,0:T(8,128)(2,1)S(1)}, bf16[256,1024]{1,0:T(8,128)(2,1)S(1)}, u32[]{:S(2)}, u32[]{:S(2)}) collective-permute-start(bf16[256,1024]{1,0:T(8,128)(2,1)S(1)} %fusion.46), channel_id=1, source_target_pairs={{0,2},{1,3},{4,0},{5,1},{8,4},{9,5},{12,8},{13,9},{14,12},{15,13},... | collective-permute-start | bytes 1572872 | tf_op jit(solution)/shard_map/ppermute | solution.py:586
  621.9 20.3 %collective-permute-start.106 = (bf16[256,1024]{1,0:T(8,128)(2,1)S(1)}, bf16[256,1024]{1,0:T(8,128)(2,1)S(1)}, u32[]{:S(2)}, u32[]{:S(2)}) collective-permute-start(bf16[256,1024]{1,0:T(8,128)(2,1)S(1)} %fusion.33), channel_id=1, source_target_pairs={{0,4},{1,5},{4,8},{5,9},{8,12},{9,13},{12,14},{13,15},{14,10},{15,... | collective-permute-start | bytes 1572872 | tf_op jit(solution)/shard_map/ppermute | solution.py:586
  623.6 20.5 %collective-permute-start.107 = (bf16[256,1024]{1,0:T(8,128)(2,1)S(1)}, bf16[256,1024]{1,0:T(8,128)(2,1)S(1)}, u32[]{:S(2)}, u32[]{:S(2)}) collective-permute-start(bf16[256,1024]{1,0:T(8,128)(2,1)S(1)} %fusion.32), channel_id=1, source_target_pairs={{0,2},{1,3},{4,0},{5,1},{8,4},{9,5},{12,8},{13,9},{14,12},{15,13},... | collective-permute-start | bytes 1572872 | tf_op jit(solution)/shard_map/ppermute | solution.py:586
  634.1 21.3 %collective-permute-start.91 = (bf16[256,1024]{1,0:T(8,128)(2,1)S(1)}, bf16[256,1024]{1,0:T(8,128)(2,1)S(1)}, u32[]{:S(2)}, u32[]{:S(2)}) collective-permute-start(bf16[256,1024]{1,0:T(8,128)(2,1)S(1)} %fusion.45), channel_id=1, source_target_pairs={{0,4},{1,5},{4,8},{5,9},{8,12},{9,13},{12,14},{13,15},{14,10},{15,... | collective-permute-start | bytes 1572872 | tf_op jit(solution)/shard_map/ppermute | solution.py:586
  635.9 19.5 %collective-permute-start.92 = (bf16[256,1024]{1,0:T(8,128)(2,1)S(1)}, bf16[256,1024]{1,0:T(8,128)(2,1)S(1)}, u32[]{:S(2)}, u32[]{:S(2)}) collective-permute-start(bf16[256,1024]{1,0:T(8,128)(2,1)S(1)} %fusion.44), channel_id=1, source_target_pairs={{0,2},{1,3},{4,0},{5,1},{8,4},{9,5},{12,8},{13,9},{14,12},{15,13},... | collective-permute-start | bytes 1572872 | tf_op jit(solution)/shard_map/ppermute | solution.py:586
  636.5 18.9 %collective-permute-start.93 = (f32[1,112,128]{2,1,0:T(8,128)S(1)}, f32[1,112,128]{2,1,0:T(8,128)S(1)}, u32[]{:S(2)}, u32[]{:S(2)}) collective-permute-start(f32[1,112,128]{2,1,0:T(8,128)S(1)} %add.441), channel_id=1, source_target_pairs={{0,2},{1,3},{2,0},{3,1},{4,6},{5,7},{6,4},{7,5},{8,10},{9,11},{10,... | collective-permute-start | bytes 172040 | tf_op jit(solution)/shard_map/ppermute | solution.py:60
  644.3 21.5 %collective-permute-start.108 = (bf16[256,1024]{1,0:T(8,128)(2,1)S(1)}, bf16[256,1024]{1,0:T(8,128)(2,1)S(1)}, u32[]{:S(2)}, u32[]{:S(2)}) collective-permute-start(bf16[256,1024]{1,0:T(8,128)(2,1)S(1)} %fusion.31), channel_id=1, source_target_pairs={{0,4},{1,5},{4,8},{5,9},{8,12},{9,13},{12,14},{13,15},{14,10},{15,... | collective-permute-start | bytes 1572872 | tf_op jit(solution)/shard_map/ppermute | solution.py:586
  646.1 20.6 %collective-permute-start.109 = (bf16[256,1024]{1,0:T(8,128)(2,1)S(1)}, bf16[256,1024]{1,0:T(8,128)(2,1)S(1)}, u32[]{:S(2)}, u32[]{:S(2)}) collective-permute-start(bf16[256,1024]{1,0:T(8,128)(2,1)S(1)} %fusion.30), channel_id=1, source_target_pairs={{0,2},{1,3},{4,0},{5,1},{8,4},{9,5},{12,8},{13,9},{14,12},{15,13},... | collective-permute-start | bytes 1572872 | tf_op jit(solution)/shard_map/ppermute | solution.py:586
  656.7 22.4 %collective-permute-start.94 = (bf16[256,1024]{1,0:T(8,128)(2,1)S(1)}, bf16[256,1024]{1,0:T(8,128)(2,1)S(1)}, u32[]{:S(2)}, u32[]{:S(2)}) collective-permute-start(bf16[256,1024]{1,0:T(8,128)(2,1)S(1)} %fusion.43), channel_id=1, source_target_pairs={{0,4},{1,5},{4,8},{5,9},{8,12},{9,13},{12,14},{13,15},{14,10},{15,... | collective-permute-start | bytes 1572872 | tf_op jit(solution)/shard_map/ppermute | solution.py:586
  658.6 20.5 %collective-permute-start.95 = (bf16[256,1024]{1,0:T(8,128)(2,1)S(1)}, bf16[256,1024]{1,0:T(8,128)(2,1)S(1)}, u32[]{:S(2)}, u32[]{:S(2)}) collective-permute-start(bf16[256,1024]{1,0:T(8,128)(2,1)S(1)} %fusion.42), channel_id=1, source_target_pairs={{0,2},{1,3},{4,0},{5,1},{8,4},{9,5},{12,8},{13,9},{14,12},{15,13},... | collective-permute-start | bytes 1572872 | tf_op jit(solution)/shard_map/ppermute | solution.py:586
  659.7 19.4 %collective-permute-start.96 = (f32[1,112,128]{2,1,0:T(8,128)S(1)}, f32[1,112,128]{2,1,0:T(8,128)S(1)}, u32[]{:S(2)}, u32[]{:S(2)}) collective-permute-start(f32[1,112,128]{2,1,0:T(8,128)S(1)} %add.444), channel_id=1, source_target_pairs={{0,4},{1,5},{2,6},{3,7},{4,0},{5,1},{6,2},{7,3},{8,12},{9,13},{10,... | collective-permute-start | bytes 172040 | tf_op jit(solution)/shard_map/ppermute | solution.py:60
  666.8 21.5 %collective-permute-start.110 = (bf16[256,1024]{1,0:T(8,128)(2,1)S(1)}, bf16[256,1024]{1,0:T(8,128)(2,1)S(1)}, u32[]{:S(2)}, u32[]{:S(2)}) collective-permute-start(bf16[256,1024]{1,0:T(8,128)(2,1)S(1)} %fusion.29), channel_id=1, source_target_pairs={{0,4},{1,5},{4,8},{5,9},{8,12},{9,13},{12,14},{13,15},{14,10},{15,... | collective-permute-start | bytes 1572872 | tf_op jit(solution)/shard_map/ppermute | solution.py:586
  668.6 21.7 %collective-permute-start.111 = (bf16[256,1024]{1,0:T(8,128)(2,1)S(1)}, bf16[256,1024]{1,0:T(8,128)(2,1)S(1)}, u32[]{:S(2)}, u32[]{:S(2)}) collective-permute-start(bf16[256,1024]{1,0:T(8,128)(2,1)S(1)} %fusion.28), channel_id=1, source_target_pairs={{0,2},{1,3},{4,0},{5,1},{8,4},{9,5},{12,8},{13,9},{14,12},{15,13},... | collective-permute-start | bytes 1572872 | tf_op jit(solution)/shard_map/ppermute | solution.py:586
  680.3 19.7 %collective-permute-start.97 = (bf16[256,1024]{1,0:T(8,128)(2,1)S(1)}, bf16[256,1024]{1,0:T(8,128)(2,1)S(1)}, u32[]{:S(2)}, u32[]{:S(2)}) collective-permute-start(bf16[256,1024]{1,0:T(8,128)(2,1)S(1)} %fusion.41), channel_id=1, source_target_pairs={{0,4},{1,5},{4,8},{5,9},{8,12},{9,13},{12,14},{13,15},{14,10},{15,... | collective-permute-start | bytes 1572872 | tf_op jit(solution)/shard_map/ppermute | solution.py:586
  680.8 19.2 %collective-permute-start.98 = (bf16[256,1024]{1,0:T(8,128)(2,1)S(1)}, bf16[256,1024]{1,0:T(8,128)(2,1)S(1)}, u32[]{:S(2)}, u32[]{:S(2)}) collective-permute-start(bf16[256,1024]{1,0:T(8,128)(2,1)S(1)} %fusion.40), channel_id=1, source_target_pairs={{0,2},{1,3},{4,0},{5,1},{8,4},{9,5},{12,8},{13,9},{14,12},{15,13},... | collective-permute-start | bytes 1572872 | tf_op jit(solution)/shard_map/ppermute | solution.py:586
  682.7 17.3 %collective-permute-start.99 = (f32[1,112,128]{2,1,0:T(8,128)S(1)}, f32[1,112,128]{2,1,0:T(8,128)S(1)}, u32[]{:S(2)}, u32[]{:S(2)}) collective-permute-start(f32[1,112,128]{2,1,0:T(8,128)S(1)} %add.447), channel_id=1, source_target_pairs={{0,8},{1,9},{2,10},{3,11},{4,12},{5,13},{6,14},{7,15},{8,0},{9,1},... | collective-permute-start | bytes 172040 | tf_op jit(solution)/shard_map/ppermute | solution.py:60
  (256 other events, 2148.1 us)

commit v5 on v4

--- a/solution.py
+++ b/solution.py
@@ -383,6 +383,7 @@
         rows_spec((tokens, D)),
         shaped((tokens, D), HIGH),
         (joint_grad, asked_grad, packed),
+        LARGE + 12,
     )
 
 

time: 733 us -> 736 us (level)
    unnamed x424 -> x408, local copies, waits for them, and re-layouts: 73 us -> 69.3 us
  transfers between devices with their start and end apart: 119 -> 119, of which waited for: 55 -> 57; matrix products, arithmetic and copies ran while one was open for 11% -> 11% of each run, Pallas kernels for 12% -> 12%
where the time goes in v5:
time: 736 us; the launch traced here: 724 us
  waiting for transfers between devices  236 us (32%)
  Pallas kernels  185 us (25%)
  starting transfers between devices  113 us (15%)
  local copies, waits for them, and re-layouts  89.4 us (12%)
  other arithmetic  73.9 us (10%)
  matrix products  23.1 us (3%)
    ppermute x56, waiting for transfers between devices, hop(): return lax.ppermute(x, ('section', 'dp'), route)  152 us
    pallas_call x23, Pallas kernels, call(): pl.pallas_call(kernel, grid=grid, in_specs=in_specs, out_specs=out_specs,...  130 us
    unnamed x408, local copies, waits for them, and re-layouts  69.3 us
    ppermute x56, starting transfers between devices, hop(): return lax.ppermute(x, ('section', 'dp'), route)  60.1 us
    ppermute x54, waiting for transfers between devices, swap(): return lax.ppermute(x, ('section', 'dp'), route)  49.9 us
    pallas_call x4, Pallas kernels, assembled(): pl.pallas_call(kernel, grid_spec=pltpu.PrefetchScalarGridSpec(num_scalar_...  29.7 us
    convert_element_type x37, other arithmetic, low(): return v.astype(LOW)  27.9 us
    all_to_all x7, starting transfers between devices, trade(): return lax.all_to_all(x, 'dp', 0, 0, tiled=True, axis_index_groups=members)  26.9 us
  transfers between devices with their start and end apart: 119, of which 57 were waited for; matrix products, arithmetic and copies ran while one was open for 11% of the time, Pallas kernels for 12%

profile of v5, /device:TPU:0, one launch (start us, length us, event | category | flops | bytes accessed | tf_op | source)
XLA Modules:
  0.0 724.4 jit_solution(10441418432920228435)
XLA Ops:
  4.1 3.1 collective-permute-start
  16.2 3.0 collective-permute-done.1.refs_5_
  25.3 7.3 %collective-permute-done.2.refs_8_ = bf16[192,1024]{1,0:T(8,128)(2,1)} collective-permute-done((bf16[192,1024]{1,0:T(8,128)(2,1)S(1)}, bf16[192,1024]{1,0:T(8,128)(2,1)}, u32[]{:S(2)}, u32[]{:S(2)}) %collective-permute-start.2) | collective-permute-done | bytes 393248 | tf_op jit(solution)/shard_map/ppermute | solution.py:587
  40.1 5.0 collective-permute-done.7.refs_12_
  49.9 4.9 collective-permute-done.16
  61.4 7.2 collective-permute-done.21
  73.7 6.2 shard_map.274.refs_16_
  84.6 8.5 %collective-permute-done.26.refs_12_ = bf16[192,1024]{1,0:T(8,128)(2,1)S(1)} collective-permute-done((bf16[192,1024]{1,0:T(8,128)(2,1)}, bf16[192,1024]{1,0:T(8,128)(2,1)S(1)}, u32[]{:S(2)}, u32[]{:S(2)}) %collective-permute-start.26) | collective-permute-done | bytes 393248 | tf_op jit(solution)/shard_map/ppermute | solution.py:587
  101.9 6.1 shard_map.275
  108.1 4.6 copy-done.2
  112.7 4.1 shard_map.276
  118.7 3.7 all-to-all-start
  125.5 24.6 %collective-permute-done.36.refs_8_ = bf16[320,1024]{1,0:T(8,128)(2,1)S(1)} collective-permute-done((bf16[320,1024]{1,0:T(8,128)(2,1)}, bf16[320,1024]{1,0:T(8,128)(2,1)S(1)}, u32[]{:S(2)}, u32[]{:S(2)}) %collective-permute-start.36) | collective-permute-done | bytes 655392 | tf_op jit(solution)/shard_map/ppermute | solution.py:587
  150.9 3.6 all-to-all-start.1
  160.6 8.1 %all-to-all-done.1 = bf16[8,160,384]{2,1,0:T(8,128)(2,1)S(1)} async-done(((bf16[8,160,384]{2,1,0:T(8,128)(2,1)}), bf16[8,160,384]{2,1,0:T(8,128)(2,1)S(1)}, u32[]{:S(2)}, u32[]{:S(2)}) %all-to-all-start.1) | async-done | bytes 983072 | tf_op jit(solution)/shard_map/all_to_all | solution.py:894
  168.7 3.4 all-to-all-start.2
  172.8 10.0 %collective-permute-done.40.refs_12_ = bf16[320,1024]{1,0:T(8,128)(2,1)} collective-permute-done((bf16[320,1024]{1,0:T(8,128)(2,1)}, bf16[320,1024]{1,0:T(8,128)(2,1)}, u32[]{:S(2)}, u32[]{:S(2)}) %collective-permute-start.40) | collective-permute-done | bytes 655392 | tf_op jit(solution)/shard_map/ppermute | solution.py:587
  187.8 3.6 all-to-all-start.3
  191.4 3.7 convolution_bitcast_fusion.4
  196.1 7.2 %all-to-all-done.3 = bf16[8,160,128]{2,1,0:T(8,128)(2,1)S(1)} async-done(((bf16[8,160,128]{2,1,0:T(8,128)(2,1)}), bf16[8,160,128]{2,1,0:T(8,128)(2,1)S(1)}, u32[]{:S(2)}, u32[]{:S(2)}) %all-to-all-start.3) | async-done | bytes 327712 | tf_op jit(solution)/shard_map/all_to_all | solution.py:894
  204.2 3.4 all-to-all-start.4
  210.2 3.7 fusion.87.bias_ref
  215.4 13.1 %collective-permute-done.48.refs_0_ = bf16[320,1024]{1,0:T(8,128)(2,1)} collective-permute-done((bf16[320,1024]{1,0:T(8,128)(2,1)}, bf16[320,1024]{1,0:T(8,128)(2,1)}, u32[]{:S(2)}, u32[]{:S(2)}) %collective-permute-start.48) | collective-permute-done | bytes 655392 | tf_op jit(solution)/shard_map/ppermute | solution.py:587
  230.9 4.6 copy-done.3
  240.6 4.5 collective-permute-done.52.refs_4_
  247.5 10.4 %shard_map.281.refs_12_ = bf16[8,2,640,1024]{3,2,1,0:T(8,128)(2,1)} custom-call(s32[9]{0:T(128)} %pad_add_fusion.order_ref, bf16[320,1024]{1,0:T(8,128)(2,1)} %copy-done.123, bf16[320,1024]{1,0:T(8,128)(2,1)} %copy-done.122, bf16[320,1024]{1,0:T(8,128)(2,1)} %copy-done.130, bf16[320,1024]{1,0:T(8,128)(2,1)} %copy-done.131, bf16[320,1024]{1,0:T(8,128)(2,1)} %copy-done.128, ...), custom_call_target="tpu_custom_call" | custom-call | flops 1 | bytes 1 | tf_op jit(solution)/shard_map/pallas_call | solution.py:645
  265.7 6.9 shard_map.282
  272.7 3.4 shard_map.283
  277.0 10.6 %shard_map.284 = (bf16[320,4096]{1,0:T(8,128)(2,1)S(1)}, bf16[320,4096]{1,0:T(8,128)(2,1)S(1)}, f32[320,1024]{1,0:T(8,128)S(1)}) custom-call(bf16[320,1024]{1,0:T(8,128)(2,1)S(1)} %bitcast.325, bf16[16,640,1024]{2,1,0:T(8,128)(2,1)} %bitcast.345, bf16[16,640,1024]{2,1,0:T(8,128)(2,1)} %bitcast.346), custom_call_target="tpu_custom_call" | custom-call | flops 1 | bytes 1 | tf_op jit(solution)/shard_map/pallas_call | solution.py:196
  291.5 4.3 collective-permute-start.64
  301.2 8.2 %collective-permute-done.64 = bf16[2,160,1024]{2,1,0:T(8,128)(2,1)} collective-permute-done((bf16[2,160,1024]{2,1,0:T(8,128)(2,1)}, bf16[2,160,1024]{2,1,0:T(8,128)(2,1)}, u32[]{:S(2)}, u32[]{:S(2)}) %collective-permute-start.64) | collective-permute-done | bytes 655392 | tf_op jit(solution)/shard_map/ppermute | solution.py:1051
  313.6 4.8 copy-done.4
  318.4 4.1 shard_map.285
  326.9 4.7 shard_map.286
  331.7 3.6 shard_map.288
  337.3 10.6 %shard_map.289 = (bf16[320,4096]{1,0:T(8,128)(2,1)S(1)}, bf16[320,4096]{1,0:T(8,128)(2,1)S(1)}, f32[320,1024]{1,0:T(8,128)S(1)}) custom-call(bf16[320,1024]{1,0:T(8,128)(2,1)S(1)} %bitcast.326, bf16[16,640,1024]{2,1,0:T(8,128)(2,1)} %bitcast.349, bf16[16,640,1024]{2,1,0:T(8,128)(2,1)} %bitcast.350), custom_call_target="tpu_custom_call" | custom-call | flops 1 | bytes 1 | tf_op jit(solution)/shard_map/pallas_call | solution.py:196
  350.4 11.7 %shard_map.290 = (bf16[320,4096]{1,0:T(8,128)(2,1)S(1)}, f32[320,1024]{1,0:T(8,128)S(1)}) custom-call(bf16[320,1024]{1,0:T(8,128)(2,1)S(1)} %bitcast.323, bf16[320,4096]{1,0:T(8,128)(2,1)S(1)} %get-tuple-element.402.upper_ref, bf16[16,640,1024]{2,1,0:T(8,128)(2,1)} %bitcast.351, bf16[16,640,1024]{2,1,0:T(8,128)(2,1)} %bitcast.352), custom_call_target="tpu_custom_call" | custom-call | flops 1 | bytes 1 | tf_op jit(solution)/shard_map/pallas_call | solution.py:196
  365.2 4.4 shard_map.291
  370.5 10.5 %shard_map.292 = (bf16[8,320,384]{2,1,0:T(8,128)(2,1)S(1)}, bf16[8,320,256]{2,1,0:T(8,128)(2,1)}, f32[16,160,320]{2,1,0:T(8,128)S(1)}) custom-call(bf16[8,320,384]{2,1,0:T(8,128)(2,1)S(1)} %get-tuple-element.395.own_ref, bf16[8,320,384]{2,1,0:T(8,128)(2,1)S(1)} %collective-permute-done.65.other_ref, f32[16,160,320]{2,1,0:T(8,128)S(1)} %copy-done.5, ...), custom_call_target="tpu_custom_call" | custom-call | flops 1 | bytes 1 | tf_op jit(solution)/shard_map/pallas_call | solution.py:196
  389.3 4.8 shard_map.293
  399.5 6.7 shard_map.294
  421.6 5.6 shard_map.295
  432.5 7.1 collective-permute-done.67
  441.3 11.9 %shard_map.296 = (bf16[320,4096]{1,0:T(8,128)(2,1)S(1)}, f32[320,1024]{1,0:T(8,128)S(1)}) custom-call(bf16[320,1024]{1,0:T(8,128)(2,1)S(1)} %bitcast.324, bf16[320,4096]{1,0:T(8,128)(2,1)S(1)} %copy-done.45, bf16[16,640,1024]{2,1,0:T(8,128)(2,1)} %bitcast.355, bf16[16,640,1024]{2,1,0:T(8,128)(2,1)} %bitcast.356), custom_call_target="tpu_custom_call" | custom-call | flops 1 | bytes 1 | tf_op jit(solution)/shard_map/pallas_call | solution.py:196
  457.1 4.4 shard_map.297
  463.3 4.7 all-to-all-start.5
  474.2 4.8 shard_map.298
  482.6 6.2 shard_map.299
  490.9 4.5 all-to-all-start.6
  500.6 12.2 %shard_map.300 = (bf16[8,256,1024]{2,1,0:T(8,128)(2,1)S(1)}, bf16[8,256,1024]{2,1,0:T(8,128)(2,1)S(1)}) custom-call(s32[3,8]{1,0:T(4,128)S(1)} %add_add_fusion.4.order_ref, bf16[1024,640]{1,0:T(8,128)(2,1)S(1)} %copy-done.77, bf16[320,4096]{1,0:T(8,128)(2,1)} %broadcast_select_fusion.u_ref, bf16[320,4096]{1,0:T(8,128)(2,1)} %collective-permute-done.73.u2_ref, ...), custom_call_target="tpu_custom_call" | custom-call | flops 1 | bytes 1 | tf_op jit(solution)/shard_map/pallas_call | solution.py:707
  531.4 8.0 %collective-permute-done.75 = bf16[256,1024]{1,0:T(8,128)(2,1)S(1)} collective-permute-done((bf16[256,1024]{1,0:T(8,128)(2,1)S(1)}, bf16[256,1024]{1,0:T(8,128)(2,1)S(1)}, u32[]{:S(2)}, u32[]{:S(2)}) %collective-permute-start.75) | collective-permute-done | bytes 524320 | tf_op jit(solution)/shard_map/ppermute | solution.py:587
  546.4 13.0 %shard_map.301 = (bf16[8,256,1024]{2,1,0:T(8,128)(2,1)S(1)}, bf16[8,256,1024]{2,1,0:T(8,128)(2,1)S(1)}) custom-call(s32[3,8]{1,0:T(4,128)S(1)} %add_add_fusion.4.order_ref, bf16[1024,640]{1,0:T(8,128)(2,1)S(1)} %copy-done.71, bf16[1024,640]{1,0:T(8,128)(2,1)S(1)} %copy-done.73, bf16[1024,640]{1,0:T(8,128)(2,1)S(1)} %copy-done.75, ...), custom_call_target="tpu_custom_call" | custom-call | flops 1 | bytes 1 | tf_op jit(solution)/shard_map/pallas_call | solution.py:707
  564.1 6.7 shard_map.302
  574.8 4.8 fusion.86
  592.4 6.5 collective-permute-done.102
  606.0 4.1 collective-permute-done.86
  617.3 4.0 collective-permute-done.104
  626.5 6.1 collective-permute-done.88
  639.4 4.4 collective-permute-done.106
  649.0 8.1 %collective-permute-done.93 = f32[1,112,128]{2,1,0:T(8,128)S(1)} collective-permute-done((f32[1,112,128]{2,1,0:T(8,128)S(1)}, f32[1,112,128]{2,1,0:T(8,128)S(1)}, u32[]{:S(2)}, u32[]{:S(2)}) %collective-permute-start.93) | collective-permute-done | bytes 57376 | tf_op jit(solution)/shard_map/ppermute | solution.py:60
  662.4 5.1 collective-permute-done.108
  671.4 9.9 %collective-permute-done.96 = f32[1,112,128]{2,1,0:T(8,128)S(1)} collective-permute-done((f32[1,112,128]{2,1,0:T(8,128)S(1)}, f32[1,112,128]{2,1,0:T(8,128)S(1)}, u32[]{:S(2)}, u32[]{:S(2)}) %collective-permute-start.96) | collective-permute-done | bytes 57376 | tf_op jit(solution)/shard_map/ppermute | solution.py:60
  686.7 3.3 collective-permute-done.110
  692.8 9.2 %collective-permute-done.99 = f32[1,112,128]{2,1,0:T(8,128)S(1)} collective-permute-done((f32[1,112,128]{2,1,0:T(8,128)S(1)}, f32[1,112,128]{2,1,0:T(8,128)S(1)}, u32[]{:S(2)}, u32[]{:S(2)}) %collective-permute-start.99) | collective-permute-done | bytes 57376 | tf_op jit(solution)/shard_map/ppermute | solution.py:60
  (801 shorter events, 298.7 us)
Async XLA Ops:
  7.2 18.0 %collective-permute-start.4 = (bf16[192,1024]{1,0:T(8,128)(2,1)S(1)}, bf16[192,1024]{1,0:T(8,128)(2,1)}, u32[]{:S(2)}, u32[]{:S(2)}) collective-permute-start(bf16[192,1024]{1,0:T(8,128)(2,1)S(1)} %bitcast.373), channel_id=1, source_target_pairs={{0,1},{1,0},{2,3},{3,2},{4,5},{5,4},{6,7},{7,6},{8,9},{9,8},{10,11... | collective-permute-start | bytes 1179656 | tf_op jit(solution)/shard_map/ppermute | solution.py:60
  8.0 17.3 %collective-permute-start.5 = (bf16[192,1024]{1,0:T(8,128)(2,1)S(1)}, bf16[192,1024]{1,0:T(8,128)(2,1)}, u32[]{:S(2)}, u32[]{:S(2)}) collective-permute-start(bf16[192,1024]{1,0:T(8,128)(2,1)S(1)} %pad_maximum_fusion.6.refs_1_), channel_id=1, source_target_pairs={{0,1},{1,0},{2,3},{3,2},{4,5},{5,4},{6,7},{7,6},{8,9},{9,8},{10,11... | collective-permute-start | bytes 1179656 | tf_op jit(solution)/shard_map/ppermute | solution.py:60
  23.5 16.2 %collective-permute-start.9 = (bf16[192,1024]{1,0:T(8,128)(2,1)S(1)}, bf16[192,1024]{1,0:T(8,128)(2,1)S(1)}, u32[]{:S(2)}, u32[]{:S(2)}) collective-permute-start(bf16[192,1024]{1,0:T(8,128)(2,1)S(1)} %collective-permute-done.refs_4_), channel_id=1, source_target_pairs={{0,1},{1,0},{2,3},{3,2},{4,5},{5,4},{6,7},{7,6},{8,9},{9,8},{10,11... | collective-permute-start | bytes 1179656 | tf_op jit(solution)/shard_map/ppermute | solution.py:60
  38.9 16.8 %collective-permute-start.14 = (bf16[192,1024]{1,0:T(8,128)(2,1)}, bf16[192,1024]{1,0:T(8,128)(2,1)S(1)}, u32[]{:S(2)}, u32[]{:S(2)}) collective-permute-start(bf16[192,1024]{1,0:T(8,128)(2,1)} %collective-permute-done.2.refs_8_), channel_id=1, source_target_pairs={{0,1},{1,0},{2,3},{3,2},{4,5},{5,4},{6,7},{7,6},{8,9},{9,8},{10,11... | collective-permute-start | bytes 1179656 | tf_op jit(solution)/shard_map/ppermute | solution.py:60
  39.7 16.6 %collective-permute-start.15 = (bf16[192,1024]{1,0:T(8,128)(2,1)}, bf16[192,1024]{1,0:T(8,128)(2,1)}, u32[]{:S(2)}, u32[]{:S(2)}) collective-permute-start(bf16[192,1024]{1,0:T(8,128)(2,1)} %collective-permute-done.3.refs_9_), channel_id=1, source_target_pairs={{0,1},{1,0},{2,3},{3,2},{4,5},{5,4},{6,7},{7,6},{8,9},{9,8},{10,11... | collective-permute-start | bytes 1179656 | tf_op jit(solution)/shard_map/ppermute | solution.py:60
  69.5 15.1 %collective-permute-start.28 = (bf16[192,1024]{1,0:T(8,128)(2,1)}, bf16[192,1024]{1,0:T(8,128)(2,1)}, u32[]{:S(2)}, u32[]{:S(2)}) collective-permute-start(bf16[192,1024]{1,0:T(8,128)(2,1)} %collective-permute-done.17.refs_4_), channel_id=1, source_target_pairs={{0,1},{1,0},{2,3},{3,2},{4,5},{5,4},{6,7},{7,6},{8,9},{9,8},{10,11... | collective-permute-start | bytes 1179656 | tf_op jit(solution)/shard_map/ppermute | solution.py:60
  95.8 21.0 %collective-permute-start.30 = (bf16[320,1024]{1,0:T(8,128)(2,1)S(1)}, bf16[320,1024]{1,0:T(8,128)(2,1)S(1)}, u32[]{:S(2)}, u32[]{:S(2)}) collective-permute-start(bf16[320,1024]{1,0:T(8,128)(2,1)S(1)} %get-tuple-element.553.refs_0_), channel_id=1, source_target_pairs={{0,4},{1,5},{4,8},{5,9},{8,12},{9,13},{12,14},{13,15},{14,10},{15,... | collective-permute-start | bytes 1966088 | tf_op jit(solution)/shard_map/ppermute | solution.py:587
  96.2 20.6 %collective-permute-start.31 = (bf16[320,1024]{1,0:T(8,128)(2,1)S(1)}, bf16[320,1024]{1,0:T(8,128)(2,1)S(1)}, u32[]{:S(2)}, u32[]{:S(2)}) collective-permute-start(bf16[320,1024]{1,0:T(8,128)(2,1)S(1)} %get-tuple-element.552.refs_1_), channel_id=1, source_target_pairs={{0,2},{1,3},{4,0},{5,1},{8,4},{9,5},{12,8},{13,9},{14,12},{15,13},... | collective-permute-start | bytes 1966088 | tf_op jit(solution)/shard_map/ppermute | solution.py:587
  118.7 32.3 %all-to-all-start = ((bf16[8,160,384]{2,1,0:T(8,128)(2,1)}), bf16[8,160,384]{2,1,0:T(8,128)(2,1)S(1)}, u32[]{:S(2)}, u32[]{:S(2)}) async-start(bf16[8,160,384]{2,1,0:T(8,128)(2,1)} %get-tuple-element.547), calls=%async_computation | async-start | bytes 1966080 | tf_op jit(solution)/shard_map/all_to_all | solution.py:894
  123.0 27.1 %collective-permute-start.36 = (bf16[320,1024]{1,0:T(8,128)(2,1)}, bf16[320,1024]{1,0:T(8,128)(2,1)S(1)}, u32[]{:S(2)}, u32[]{:S(2)}) collective-permute-start(bf16[320,1024]{1,0:T(8,128)(2,1)} %copy-done.128), channel_id=1, source_target_pairs={{0,4},{1,5},{4,8},{5,9},{8,12},{9,13},{12,14},{13,15},{14,10},{15,... | collective-permute-start | bytes 1966088 | tf_op jit(solution)/shard_map/ppermute | solution.py:587
  124.8 26.1 %collective-permute-start.37 = (bf16[320,1024]{1,0:T(8,128)(2,1)}, bf16[320,1024]{1,0:T(8,128)(2,1)}, u32[]{:S(2)}, u32[]{:S(2)}) collective-permute-start(bf16[320,1024]{1,0:T(8,128)(2,1)} %copy-done.129), channel_id=1, source_target_pairs={{0,2},{1,3},{4,0},{5,1},{8,4},{9,5},{12,8},{13,9},{14,12},{15,13},... | collective-permute-start | bytes 1966088 | tf_op jit(solution)/shard_map/ppermute | solution.py:587
  150.9 17.7 %all-to-all-start.1 = ((bf16[8,160,384]{2,1,0:T(8,128)(2,1)}), bf16[8,160,384]{2,1,0:T(8,128)(2,1)S(1)}, u32[]{:S(2)}, u32[]{:S(2)}) async-start(bf16[8,160,384]{2,1,0:T(8,128)(2,1)} %get-tuple-element.330), calls=%async_computation.1 | async-start | bytes 1966080 | tf_op jit(solution)/shard_map/all_to_all | solution.py:894
  154.5 18.1 %collective-permute-start.42 = (bf16[320,1024]{1,0:T(8,128)(2,1)}, bf16[320,1024]{1,0:T(8,128)(2,1)}, u32[]{:S(2)}, u32[]{:S(2)}) collective-permute-start(bf16[320,1024]{1,0:T(8,128)(2,1)} %copy-done.128), channel_id=1, source_target_pairs={{0,1},{1,0},{2,3},{3,2},{4,5},{5,4},{6,7},{7,6},{8,9},{9,8},{10,11... | collective-permute-start | bytes 1966088 | tf_op jit(solution)/shard_map/ppermute | solution.py:60
  155.0 17.8 %collective-permute-start.43 = (bf16[320,1024]{1,0:T(8,128)(2,1)}, bf16[320,1024]{1,0:T(8,128)(2,1)}, u32[]{:S(2)}, u32[]{:S(2)}) collective-permute-start(bf16[320,1024]{1,0:T(8,128)(2,1)} %copy-done.129), channel_id=1, source_target_pairs={{0,1},{1,0},{2,3},{3,2},{4,5},{5,4},{6,7},{7,6},{8,9},{9,8},{10,11... | collective-permute-start | bytes 1966088 | tf_op jit(solution)/shard_map/ppermute | solution.py:60
  155.1 27.7 %collective-permute-start.40 = (bf16[320,1024]{1,0:T(8,128)(2,1)}, bf16[320,1024]{1,0:T(8,128)(2,1)}, u32[]{:S(2)}, u32[]{:S(2)}) collective-permute-start(bf16[320,1024]{1,0:T(8,128)(2,1)} %copy-done.132), channel_id=1, source_target_pairs={{0,4},{1,5},{4,8},{5,9},{8,12},{9,13},{12,14},{13,15},{14,10},{15,... | collective-permute-start | bytes 1966088 | tf_op jit(solution)/shard_map/ppermute | solution.py:587
  157.0 25.8 %collective-permute-start.41 = (bf16[320,1024]{1,0:T(8,128)(2,1)}, bf16[320,1024]{1,0:T(8,128)(2,1)}, u32[]{:S(2)}, u32[]{:S(2)}) collective-permute-start(bf16[320,1024]{1,0:T(8,128)(2,1)} %collective-permute-done.37.refs_9_), channel_id=1, source_target_pairs={{0,2},{1,3},{4,0},{5,1},{8,4},{9,5},{12,8},{13,9},{14,12},{15,13},... | collective-permute-start | bytes 1966088 | tf_op jit(solution)/shard_map/ppermute | solution.py:587
  168.7 19.2 %all-to-all-start.2 = ((bf16[8,160,128]{2,1,0:T(8,128)(2,1)}), bf16[8,160,128]{2,1,0:T(8,128)(2,1)S(1)}, u32[]{:S(2)}, u32[]{:S(2)}) async-start(bf16[8,160,128]{2,1,0:T(8,128)(2,1)} %bitcast.26), calls=%async_computation.2 | async-start | bytes 655360 | tf_op jit(solution)/shard_map/all_to_all | solution.py:894
  172.2 35.5 %collective-permute-start.46 = (bf16[320,1024]{1,0:T(8,128)(2,1)}, bf16[320,1024]{1,0:T(8,128)(2,1)}, u32[]{:S(2)}, u32[]{:S(2)}) collective-permute-start(bf16[320,1024]{1,0:T(8,128)(2,1)} %copy-done.132), channel_id=1, source_target_pairs={{0,1},{1,0},{2,3},{3,2},{4,5},{5,4},{6,7},{7,6},{8,9},{9,8},{10,11... | collective-permute-start | bytes 1966088 | tf_op jit(solution)/shard_map/ppermute | solution.py:60
  172.7 35.4 %collective-permute-start.47 = (bf16[320,1024]{1,0:T(8,128)(2,1)}, bf16[320,1024]{1,0:T(8,128)(2,1)}, u32[]{:S(2)}, u32[]{:S(2)}) collective-permute-start(bf16[320,1024]{1,0:T(8,128)(2,1)} %collective-permute-done.37.refs_9_), channel_id=1, source_target_pairs={{0,1},{1,0},{2,3},{3,2},{4,5},{5,4},{6,7},{7,6},{8,9},{9,8},{10,11... | collective-permute-start | bytes 1966088 | tf_op jit(solution)/shard_map/ppermute | solution.py:60
  182.8 25.3 %collective-permute-start.44 = (bf16[320,1024]{1,0:T(8,128)(2,1)}, bf16[320,1024]{1,0:T(8,128)(2,1)}, u32[]{:S(2)}, u32[]{:S(2)}) collective-permute-start(bf16[320,1024]{1,0:T(8,128)(2,1)} %collective-permute-done.40.refs_12_), channel_id=1, source_target_pairs={{0,4},{1,5},{4,8},{5,9},{8,12},{9,13},{12,14},{13,15},{14,10},{15,... | collective-permute-start | bytes 1966088 | tf_op jit(solution)/shard_map/ppermute | solution.py:587
  182.9 25.2 %collective-permute-start.45 = (bf16[320,1024]{1,0:T(8,128)(2,1)}, bf16[320,1024]{1,0:T(8,128)(2,1)}, u32[]{:S(2)}, u32[]{:S(2)}) collective-permute-start(bf16[320,1024]{1,0:T(8,128)(2,1)} %collective-permute-done.41.refs_13_), channel_id=1, source_target_pairs={{0,2},{1,3},{4,0},{5,1},{8,4},{9,5},{12,8},{13,9},{14,12},{15,13},... | collective-permute-start | bytes 1966088 | tf_op jit(solution)/shard_map/ppermute | solution.py:587
  187.8 15.5 %all-to-all-start.3 = ((bf16[8,160,128]{2,1,0:T(8,128)(2,1)}), bf16[8,160,128]{2,1,0:T(8,128)(2,1)S(1)}, u32[]{:S(2)}, u32[]{:S(2)}) async-start(bf16[8,160,128]{2,1,0:T(8,128)(2,1)} %bitcast.27), calls=%async_computation.3 | async-start | bytes 655360 | tf_op jit(solution)/shard_map/all_to_all | solution.py:894
  195.6 19.2 %collective-permute-start.50 = (bf16[320,1024]{1,0:T(8,128)(2,1)}, bf16[320,1024]{1,0:T(8,128)(2,1)}, u32[]{:S(2)}, u32[]{:S(2)}) collective-permute-start(bf16[320,1024]{1,0:T(8,128)(2,1)} %collective-permute-done.40.refs_12_), channel_id=1, source_target_pairs={{0,1},{1,0},{2,3},{3,2},{4,5},{5,4},{6,7},{7,6},{8,9},{9,8},{10,11... | collective-permute-start | bytes 1966088 | tf_op jit(solution)/shard_map/ppermute | solution.py:60
  208.1 20.4 %collective-permute-start.48 = (bf16[320,1024]{1,0:T(8,128)(2,1)}, bf16[320,1024]{1,0:T(8,128)(2,1)}, u32[]{:S(2)}, u32[]{:S(2)}) collective-permute-start(bf16[320,1024]{1,0:T(8,128)(2,1)} %collective-permute-done.44.refs_16_), channel_id=1, source_target_pairs={{0,4},{1,5},{4,8},{5,9},{8,12},{9,13},{12,14},{13,15},{14,10},{15,... | collective-permute-start | bytes 1966088 | tf_op jit(solution)/shard_map/ppermute | solution.py:587
  209.9 18.7 %collective-permute-start.49 = (bf16[320,1024]{1,0:T(8,128)(2,1)}, bf16[320,1024]{1,0:T(8,128)(2,1)}, u32[]{:S(2)}, u32[]{:S(2)}) collective-permute-start(bf16[320,1024]{1,0:T(8,128)(2,1)} %collective-permute-done.45.refs_17_), channel_id=1, source_target_pairs={{0,2},{1,3},{4,0},{5,1},{8,4},{9,5},{12,8},{13,9},{14,12},{15,13},... | collective-permute-start | bytes 1966088 | tf_op jit(solution)/shard_map/ppermute | solution.py:587
  214.0 26.1 %collective-permute-start.54 = (bf16[320,1024]{1,0:T(8,128)(2,1)}, bf16[320,1024]{1,0:T(8,128)(2,1)}, u32[]{:S(2)}, u32[]{:S(2)}) collective-permute-start(bf16[320,1024]{1,0:T(8,128)(2,1)} %collective-permute-done.44.refs_16_), channel_id=1, source_target_pairs={{0,1},{1,0},{2,3},{3,2},{4,5},{5,4},{6,7},{7,6},{8,9},{9,8},{10,11... | collective-permute-start | bytes 1966088 | tf_op jit(solution)/shard_map/ppermute | solution.py:60
  214.8 25.8 %collective-permute-start.55 = (bf16[320,1024]{1,0:T(8,128)(2,1)}, bf16[320,1024]{1,0:T(8,128)(2,1)}, u32[]{:S(2)}, u32[]{:S(2)}) collective-permute-start(bf16[320,1024]{1,0:T(8,128)(2,1)} %collective-permute-done.45.refs_17_), channel_id=1, source_target_pairs={{0,1},{1,0},{2,3},{3,2},{4,5},{5,4},{6,7},{7,6},{8,9},{9,8},{10,11... | collective-permute-start | bytes 1966088 | tf_op jit(solution)/shard_map/ppermute | solution.py:60
  228.5 16.6 %collective-permute-start.52 = (bf16[320,1024]{1,0:T(8,128)(2,1)}, bf16[320,1024]{1,0:T(8,128)(2,1)}, u32[]{:S(2)}, u32[]{:S(2)}) collective-permute-start(bf16[320,1024]{1,0:T(8,128)(2,1)} %collective-permute-done.48.refs_0_), channel_id=1, source_target_pairs={{0,4},{1,5},{4,8},{5,9},{8,12},{9,13},{12,14},{13,15},{14,10},{15,... | collective-permute-start | bytes 1966088 | tf_op jit(solution)/shard_map/ppermute | solution.py:587
  228.9 16.6 %collective-permute-start.53 = (bf16[320,1024]{1,0:T(8,128)(2,1)}, bf16[320,1024]{1,0:T(8,128)(2,1)}, u32[]{:S(2)}, u32[]{:S(2)}) collective-permute-start(bf16[320,1024]{1,0:T(8,128)(2,1)} %collective-permute-done.49.refs_1_), channel_id=1, source_target_pairs={{0,2},{1,3},{4,0},{5,1},{8,4},{9,5},{12,8},{13,9},{14,12},{15,13},... | collective-permute-start | bytes 1966088 | tf_op jit(solution)/shard_map/ppermute | solution.py:587
  230.8 27.1 %collective-permute-start.58 = (bf16[320,1024]{1,0:T(8,128)(2,1)}, bf16[320,1024]{1,0:T(8,128)(2,1)S(1)}, u32[]{:S(2)}, u32[]{:S(2)}) collective-permute-start(bf16[320,1024]{1,0:T(8,128)(2,1)} %collective-permute-done.48.refs_0_), channel_id=1, source_target_pairs={{0,1},{1,0},{2,3},{3,2},{4,5},{5,4},{6,7},{7,6},{8,9},{9,8},{10,11... | collective-permute-start | bytes 1966088 | tf_op jit(solution)/shard_map/ppermute | solution.py:60
  240.1 18.4 %collective-permute-start.59 = (bf16[320,1024]{1,0:T(8,128)(2,1)}, bf16[320,1024]{1,0:T(8,128)(2,1)S(1)}, u32[]{:S(2)}, u32[]{:S(2)}) collective-permute-start(bf16[320,1024]{1,0:T(8,128)(2,1)} %collective-permute-done.49.refs_1_), channel_id=1, source_target_pairs={{0,1},{1,0},{2,3},{3,2},{4,5},{5,4},{6,7},{7,6},{8,9},{9,8},{10,11... | collective-permute-start | bytes 1966088 | tf_op jit(solution)/shard_map/ppermute | solution.py:60
  245.4 15.5 %collective-permute-start.56 = (bf16[320,1024]{1,0:T(8,128)(2,1)}, bf16[320,1024]{1,0:T(8,128)(2,1)S(1)}, u32[]{:S(2)}, u32[]{:S(2)}) collective-permute-start(bf16[320,1024]{1,0:T(8,128)(2,1)} %collective-permute-done.52.refs_4_), channel_id=1, source_target_pairs={{0,4},{1,5},{4,8},{5,9},{8,12},{9,13},{12,14},{13,15},{14,10},{15,... | collective-permute-start | bytes 1966088 | tf_op jit(solution)/shard_map/ppermute | solution.py:587
  246.7 15.1 %collective-permute-start.57 = (bf16[320,1024]{1,0:T(8,128)(2,1)}, bf16[320,1024]{1,0:T(8,128)(2,1)}, u32[]{:S(2)}, u32[]{:S(2)}) collective-permute-start(bf16[320,1024]{1,0:T(8,128)(2,1)} %collective-permute-done.53.refs_5_), channel_id=1, source_target_pairs={{0,2},{1,3},{4,0},{5,1},{8,4},{9,5},{12,8},{13,9},{14,12},{15,13},... | collective-permute-start | bytes 1966088 | tf_op jit(solution)/shard_map/ppermute | solution.py:587
  291.5 17.9 %collective-permute-start.64 = (bf16[2,160,1024]{2,1,0:T(8,128)(2,1)}, bf16[2,160,1024]{2,1,0:T(8,128)(2,1)}, u32[]{:S(2)}, u32[]{:S(2)}) collective-permute-start(bf16[2,160,1024]{2,1,0:T(8,128)(2,1)} %get-tuple-element.567), channel_id=1, source_target_pairs={{0,16},{1,17},{2,18},{3,19},{4,20},{5,21},{6,22},{7,23},{8,24},{9,... | collective-permute-start | bytes 1966088 | tf_op jit(solution)/shard_map/ppermute | solution.py:1051
  412.9 26.7 %collective-permute-start.72 = (bf16[320,4096]{1,0:T(8,128)(2,1)S(1)}, bf16[320,4096]{1,0:T(8,128)(2,1)S(1)}, u32[]{:S(2)}, u32[]{:S(2)}) collective-permute-start(bf16[320,4096]{1,0:T(8,128)(2,1)S(1)} %broadcast_select_fusion.1.a_ref), channel_id=1, source_target_pairs={{0,1},{1,0},{2,3},{3,2},{4,5},{5,4},{6,7},{7,6},{8,9},{9,8},{10,11... | collective-permute-start | bytes 7864328 | tf_op jit(solution)/shard_map/ppermute | solution.py:60
  418.8 20.7 %collective-permute-start.67 = (bf16[2,160,1024]{2,1,0:T(8,128)(2,1)S(1)}, bf16[2,160,1024]{2,1,0:T(8,128)(2,1)S(1)}, u32[]{:S(2)}, u32[]{:S(2)}) collective-permute-start(bf16[2,160,1024]{2,1,0:T(8,128)(2,1)S(1)} %get-tuple-element.414), channel_id=1, source_target_pairs={{16,0},{17,1},{18,2},{19,3},{20,4},{21,5},{22,6},{23,7},{24,8},{25... | collective-permute-start | bytes 1966088 | tf_op jit(solution)/shard_map/ppermute | solution.py:1074
  455.0 24.8 %collective-permute-start.73 = (bf16[320,4096]{1,0:T(8,128)(2,1)}, bf16[320,4096]{1,0:T(8,128)(2,1)}, u32[]{:S(2)}, u32[]{:S(2)}) collective-permute-start(bf16[320,4096]{1,0:T(8,128)(2,1)} %broadcast_select_fusion.u_ref), channel_id=1, source_target_pairs={{0,1},{1,0},{2,3},{3,2},{4,5},{5,4},{6,7},{7,6},{8,9},{9,8},{10,11... | collective-permute-start | bytes 7864328 | tf_op jit(solution)/shard_map/ppermute | solution.py:60
  463.3 16.5 %all-to-all-start.5 = ((bf16[8,320,128]{2,1,0:T(8,128)(2,1)}), bf16[8,320,128]{2,1,0:T(8,128)(2,1)}, u32[]{:S(2)}, u32[]{:S(2)}) async-start(bf16[8,320,128]{2,1,0:T(8,128)(2,1)} %copy-done.80), calls=%async_computation.5 | async-start | bytes 1310720 | tf_op jit(solution)/shard_map/all_to_all | solution.py:894
  490.9 28.8 %all-to-all-start.6 = ((bf16[8,320,384]{2,1,0:T(8,128)(2,1)}), bf16[8,320,384]{2,1,0:T(8,128)(2,1)}, u32[]{:S(2)}, u32[]{:S(2)}) async-start(bf16[8,320,384]{2,1,0:T(8,128)(2,1)} %bitcast.338), calls=%async_computation.6 | async-start | bytes 3932160 | tf_op jit(solution)/shard_map/all_to_all | solution.py:894
  522.2 19.5 %collective-permute-start.79 = (bf16[8,320,384]{2,1,0:T(8,128)(2,1)S(1)}, bf16[8,320,384]{2,1,0:T(8,128)(2,1)S(1)}, u32[]{:S(2)}, u32[]{:S(2)}) collective-permute-start(bf16[8,320,384]{2,1,0:T(8,128)(2,1)S(1)} %broadcast_select_fusion.2.j_ref), channel_id=1, source_target_pairs={{0,1},{1,0},{2,3},{3,2},{4,5},{5,4},{6,7},{7,6},{8,9},{9,8},{10,11... | collective-permute-start | bytes 5898248 | tf_op jit(solution)/shard_map/ppermute | solution.py:60
  542.9 16.5 %collective-permute-start.82 = (bf16[256,1024]{1,0:T(8,128)(2,1)S(1)}, bf16[256,1024]{1,0:T(8,128)(2,1)S(1)}, u32[]{:S(2)}, u32[]{:S(2)}) collective-permute-start(bf16[256,1024]{1,0:T(8,128)(2,1)S(1)} %fusion.51), channel_id=1, source_target_pairs={{0,4},{1,5},{4,8},{5,9},{8,12},{9,13},{12,14},{13,15},{14,10},{15,... | collective-permute-start | bytes 1572872 | tf_op jit(solution)/shard_map/ppermute | solution.py:587
  560.4 26.9 %collective-permute-start.84 = (bf16[256,1024]{1,0:T(8,128)(2,1)}, bf16[256,1024]{1,0:T(8,128)(2,1)}, u32[]{:S(2)}, u32[]{:S(2)}) collective-permute-start(bf16[256,1024]{1,0:T(8,128)(2,1)} %slice_bitcast_fusion.2), channel_id=1, source_target_pairs={{0,4},{1,5},{4,8},{5,9},{8,12},{9,13},{12,14},{13,15},{14,10},{15,... | collective-permute-start | bytes 1572872 | tf_op jit(solution)/shard_map/ppermute | solution.py:587
  563.3 24.0 %collective-permute-start.85 = (bf16[256,1024]{1,0:T(8,128)(2,1)}, bf16[256,1024]{1,0:T(8,128)(2,1)}, u32[]{:S(2)}, u32[]{:S(2)}) collective-permute-start(bf16[256,1024]{1,0:T(8,128)(2,1)} %slice_bitcast_fusion.1), channel_id=1, source_target_pairs={{0,2},{1,3},{4,0},{5,1},{8,4},{9,5},{12,8},{13,9},{14,12},{15,13},... | collective-permute-start | bytes 1572872 | tf_op jit(solution)/shard_map/ppermute | solution.py:587
  588.9 21.2 %collective-permute-start.86 = (bf16[256,1024]{1,0:T(8,128)(2,1)S(1)}, bf16[256,1024]{1,0:T(8,128)(2,1)S(1)}, u32[]{:S(2)}, u32[]{:S(2)}) collective-permute-start(bf16[256,1024]{1,0:T(8,128)(2,1)S(1)} %fusion.49), channel_id=1, source_target_pairs={{0,4},{1,5},{4,8},{5,9},{8,12},{9,13},{12,14},{13,15},{14,10},{15,... | collective-permute-start | bytes 1572872 | tf_op jit(solution)/shard_map/ppermute | solution.py:587
  591.7 21.0 %collective-permute-start.87 = (bf16[256,1024]{1,0:T(8,128)(2,1)S(1)}, bf16[256,1024]{1,0:T(8,128)(2,1)S(1)}, u32[]{:S(2)}, u32[]{:S(2)}) collective-permute-start(bf16[256,1024]{1,0:T(8,128)(2,1)S(1)} %fusion.48), channel_id=1, source_target_pairs={{0,2},{1,3},{4,0},{5,1},{8,4},{9,5},{12,8},{13,9},{14,12},{15,13},... | collective-permute-start | bytes 1572872 | tf_op jit(solution)/shard_map/ppermute | solution.py:587
  602.7 18.6 %collective-permute-start.104 = (bf16[256,1024]{1,0:T(8,128)(2,1)S(1)}, bf16[256,1024]{1,0:T(8,128)(2,1)S(1)}, u32[]{:S(2)}, u32[]{:S(2)}) collective-permute-start(bf16[256,1024]{1,0:T(8,128)(2,1)S(1)} %fusion.35), channel_id=1, source_target_pairs={{0,4},{1,5},{4,8},{5,9},{8,12},{9,13},{12,14},{13,15},{14,10},{15,... | collective-permute-start | bytes 1572872 | tf_op jit(solution)/shard_map/ppermute | solution.py:587
  603.9 20.1 %collective-permute-start.105 = (bf16[256,1024]{1,0:T(8,128)(2,1)S(1)}, bf16[256,1024]{1,0:T(8,128)(2,1)S(1)}, u32[]{:S(2)}, u32[]{:S(2)}) collective-permute-start(bf16[256,1024]{1,0:T(8,128)(2,1)S(1)} %fusion.34), channel_id=1, source_target_pairs={{0,2},{1,3},{4,0},{5,1},{8,4},{9,5},{12,8},{13,9},{14,12},{15,13},... | collective-permute-start | bytes 1572872 | tf_op jit(solution)/shard_map/ppermute | solution.py:587
  614.0 18.6 %collective-permute-start.88 = (bf16[256,1024]{1,0:T(8,128)(2,1)S(1)}, bf16[256,1024]{1,0:T(8,128)(2,1)S(1)}, u32[]{:S(2)}, u32[]{:S(2)}) collective-permute-start(bf16[256,1024]{1,0:T(8,128)(2,1)S(1)} %fusion.47), channel_id=1, source_target_pairs={{0,4},{1,5},{4,8},{5,9},{8,12},{9,13},{12,14},{13,15},{14,10},{15,... | collective-permute-start | bytes 1572872 | tf_op jit(solution)/shard_map/ppermute | solution.py:587
  616.2 19.0 %collective-permute-start.89 = (bf16[256,1024]{1,0:T(8,128)(2,1)S(1)}, bf16[256,1024]{1,0:T(8,128)(2,1)S(1)}, u32[]{:S(2)}, u32[]{:S(2)}) collective-permute-start(bf16[256,1024]{1,0:T(8,128)(2,1)S(1)} %fusion.46), channel_id=1, source_target_pairs={{0,2},{1,3},{4,0},{5,1},{8,4},{9,5},{12,8},{13,9},{14,12},{15,13},... | collective-permute-start | bytes 1572872 | tf_op jit(solution)/shard_map/ppermute | solution.py:587
  624.2 19.6 %collective-permute-start.106 = (bf16[256,1024]{1,0:T(8,128)(2,1)S(1)}, bf16[256,1024]{1,0:T(8,128)(2,1)S(1)}, u32[]{:S(2)}, u32[]{:S(2)}) collective-permute-start(bf16[256,1024]{1,0:T(8,128)(2,1)S(1)} %fusion.33), channel_id=1, source_target_pairs={{0,4},{1,5},{4,8},{5,9},{8,12},{9,13},{12,14},{13,15},{14,10},{15,... | collective-permute-start | bytes 1572872 | tf_op jit(solution)/shard_map/ppermute | solution.py:587
  625.3 21.1 %collective-permute-start.107 = (bf16[256,1024]{1,0:T(8,128)(2,1)S(1)}, bf16[256,1024]{1,0:T(8,128)(2,1)S(1)}, u32[]{:S(2)}, u32[]{:S(2)}) collective-permute-start(bf16[256,1024]{1,0:T(8,128)(2,1)S(1)} %fusion.32), channel_id=1, source_target_pairs={{0,2},{1,3},{4,0},{5,1},{8,4},{9,5},{12,8},{13,9},{14,12},{15,13},... | collective-permute-start | bytes 1572872 | tf_op jit(solution)/shard_map/ppermute | solution.py:587
  636.4 20.6 %collective-permute-start.91 = (bf16[256,1024]{1,0:T(8,128)(2,1)S(1)}, bf16[256,1024]{1,0:T(8,128)(2,1)S(1)}, u32[]{:S(2)}, u32[]{:S(2)}) collective-permute-start(bf16[256,1024]{1,0:T(8,128)(2,1)S(1)} %fusion.45), channel_id=1, source_target_pairs={{0,4},{1,5},{4,8},{5,9},{8,12},{9,13},{12,14},{13,15},{14,10},{15,... | collective-permute-start | bytes 1572872 | tf_op jit(solution)/shard_map/ppermute | solution.py:587
  637.6 20.1 %collective-permute-start.92 = (bf16[256,1024]{1,0:T(8,128)(2,1)S(1)}, bf16[256,1024]{1,0:T(8,128)(2,1)S(1)}, u32[]{:S(2)}, u32[]{:S(2)}) collective-permute-start(bf16[256,1024]{1,0:T(8,128)(2,1)S(1)} %fusion.44), channel_id=1, source_target_pairs={{0,2},{1,3},{4,0},{5,1},{8,4},{9,5},{12,8},{13,9},{14,12},{15,13},... | collective-permute-start | bytes 1572872 | tf_op jit(solution)/shard_map/ppermute | solution.py:587
  638.8 18.3 %collective-permute-start.93 = (f32[1,112,128]{2,1,0:T(8,128)S(1)}, f32[1,112,128]{2,1,0:T(8,128)S(1)}, u32[]{:S(2)}, u32[]{:S(2)}) collective-permute-start(f32[1,112,128]{2,1,0:T(8,128)S(1)} %add.441), channel_id=1, source_target_pairs={{0,2},{1,3},{2,0},{3,1},{4,6},{5,7},{6,4},{7,5},{8,10},{9,11},{10,... | collective-permute-start | bytes 172040 | tf_op jit(solution)/shard_map/ppermute | solution.py:60
  646.6 20.9 %collective-permute-start.108 = (bf16[256,1024]{1,0:T(8,128)(2,1)S(1)}, bf16[256,1024]{1,0:T(8,128)(2,1)S(1)}, u32[]{:S(2)}, u32[]{:S(2)}) collective-permute-start(bf16[256,1024]{1,0:T(8,128)(2,1)S(1)} %fusion.31), channel_id=1, source_target_pairs={{0,4},{1,5},{4,8},{5,9},{8,12},{9,13},{12,14},{13,15},{14,10},{15,... | collective-permute-start | bytes 1572872 | tf_op jit(solution)/shard_map/ppermute | solution.py:587
  647.8 21.1 %collective-permute-start.109 = (bf16[256,1024]{1,0:T(8,128)(2,1)S(1)}, bf16[256,1024]{1,0:T(8,128)(2,1)S(1)}, u32[]{:S(2)}, u32[]{:S(2)}) collective-permute-start(bf16[256,1024]{1,0:T(8,128)(2,1)S(1)} %fusion.30), channel_id=1, source_target_pairs={{0,2},{1,3},{4,0},{5,1},{8,4},{9,5},{12,8},{13,9},{14,12},{15,13},... | collective-permute-start | bytes 1572872 | tf_op jit(solution)/shard_map/ppermute | solution.py:587
  658.9 22.5 %collective-permute-start.94 = (bf16[256,1024]{1,0:T(8,128)(2,1)S(1)}, bf16[256,1024]{1,0:T(8,128)(2,1)S(1)}, u32[]{:S(2)}, u32[]{:S(2)}) collective-permute-start(bf16[256,1024]{1,0:T(8,128)(2,1)S(1)} %fusion.43), channel_id=1, source_target_pairs={{0,4},{1,5},{4,8},{5,9},{8,12},{9,13},{12,14},{13,15},{14,10},{15,... | collective-permute-start | bytes 1572872 | tf_op jit(solution)/shard_map/ppermute | solution.py:587
  660.3 21.1 %collective-permute-start.95 = (bf16[256,1024]{1,0:T(8,128)(2,1)S(1)}, bf16[256,1024]{1,0:T(8,128)(2,1)S(1)}, u32[]{:S(2)}, u32[]{:S(2)}) collective-permute-start(bf16[256,1024]{1,0:T(8,128)(2,1)S(1)} %fusion.42), channel_id=1, source_target_pairs={{0,2},{1,3},{4,0},{5,1},{8,4},{9,5},{12,8},{13,9},{14,12},{15,13},... | collective-permute-start | bytes 1572872 | tf_op jit(solution)/shard_map/ppermute | solution.py:587
  661.5 19.9 %collective-permute-start.96 = (f32[1,112,128]{2,1,0:T(8,128)S(1)}, f32[1,112,128]{2,1,0:T(8,128)S(1)}, u32[]{:S(2)}, u32[]{:S(2)}) collective-permute-start(f32[1,112,128]{2,1,0:T(8,128)S(1)} %add.444), channel_id=1, source_target_pairs={{0,4},{1,5},{2,6},{3,7},{4,0},{5,1},{6,2},{7,3},{8,12},{9,13},{10,... | collective-permute-start | bytes 172040 | tf_op jit(solution)/shard_map/ppermute | solution.py:60
  669.1 20.9 %collective-permute-start.110 = (bf16[256,1024]{1,0:T(8,128)(2,1)S(1)}, bf16[256,1024]{1,0:T(8,128)(2,1)S(1)}, u32[]{:S(2)}, u32[]{:S(2)}) collective-permute-start(bf16[256,1024]{1,0:T(8,128)(2,1)S(1)} %fusion.29), channel_id=1, source_target_pairs={{0,4},{1,5},{4,8},{5,9},{8,12},{9,13},{12,14},{13,15},{14,10},{15,... | collective-permute-start | bytes 1572872 | tf_op jit(solution)/shard_map/ppermute | solution.py:587
  670.3 22.3 %collective-permute-start.111 = (bf16[256,1024]{1,0:T(8,128)(2,1)S(1)}, bf16[256,1024]{1,0:T(8,128)(2,1)S(1)}, u32[]{:S(2)}, u32[]{:S(2)}) collective-permute-start(bf16[256,1024]{1,0:T(8,128)(2,1)S(1)} %fusion.28), channel_id=1, source_target_pairs={{0,2},{1,3},{4,0},{5,1},{8,4},{9,5},{12,8},{13,9},{14,12},{15,13},... | collective-permute-start | bytes 1572872 | tf_op jit(solution)/shard_map/ppermute | solution.py:587
  682.6 19.4 %collective-permute-start.97 = (bf16[256,1024]{1,0:T(8,128)(2,1)S(1)}, bf16[256,1024]{1,0:T(8,128)(2,1)S(1)}, u32[]{:S(2)}, u32[]{:S(2)}) collective-permute-start(bf16[256,1024]{1,0:T(8,128)(2,1)S(1)} %fusion.41), channel_id=1, source_target_pairs={{0,4},{1,5},{4,8},{5,9},{8,12},{9,13},{12,14},{13,15},{14,10},{15,... | collective-permute-start | bytes 1572872 | tf_op jit(solution)/shard_map/ppermute | solution.py:587
  682.9 19.4 %collective-permute-start.98 = (bf16[256,1024]{1,0:T(8,128)(2,1)S(1)}, bf16[256,1024]{1,0:T(8,128)(2,1)S(1)}, u32[]{:S(2)}, u32[]{:S(2)}) collective-permute-start(bf16[256,1024]{1,0:T(8,128)(2,1)S(1)} %fusion.40), channel_id=1, source_target_pairs={{0,2},{1,3},{4,0},{5,1},{8,4},{9,5},{12,8},{13,9},{14,12},{15,13},... | collective-permute-start | bytes 1572872 | tf_op jit(solution)/shard_map/ppermute | solution.py:587
  685.0 17.0 %collective-permute-start.99 = (f32[1,112,128]{2,1,0:T(8,128)S(1)}, f32[1,112,128]{2,1,0:T(8,128)S(1)}, u32[]{:S(2)}, u32[]{:S(2)}) collective-permute-start(f32[1,112,128]{2,1,0:T(8,128)S(1)} %add.447), channel_id=1, source_target_pairs={{0,8},{1,9},{2,10},{3,11},{4,12},{5,13},{6,14},{7,15},{8,0},{9,1},... | collective-permute-start | bytes 172040 | tf_op jit(solution)/shard_map/ppermute | solution.py:60
  (248 other events, 1988.3 us)
